TPU v7x, 32 devices: a whole 2x2x4 slice. The times are simulated.
32 devices in a mesh: dp: 4 (over y, x), fsdp: 8 (over z, core).
Axes of the slice: x: 2, y: 2, z: 4, core: 2. Of those that a mesh axis runs over, the one named last changes fastest.
Arguments:
- tokens: bfloat16 [32768, 768], P(('dp', 'fsdp')), may hold values from -6 to 6
- counts: int32 [32], P(('dp', 'fsdp')), may hold values from 897 to 1024, as said below
- inner_attend: bfloat16 [768, 2304], P(('dp', 'fsdp')), may hold values from -0.21875 to 0.21875
- inner_attend_bias: bfloat16 [2304], P(('dp', 'fsdp')), may hold values from -1.796875 to 1.796875
- inner_merge: bfloat16 [768, 768], P(('dp', 'fsdp')), may hold values from -2.5 to 2.5
- inner_merge_bias: bfloat16 [768], P(('dp', 'fsdp')), may hold values from -1.796875 to 1.796875
- inner_gain: bfloat16 [768], P(('dp', 'fsdp')), may hold values from 0.5 to 1.5
- inner_shift: bfloat16 [768], P(('dp', 'fsdp')), may hold values from -1.796875 to 1.796875
- inner_expand: bfloat16 [768, 3072], P(('dp', 'fsdp')), may hold values from -0.21875 to 0.21875
- inner_expand_bias: bfloat16 [3072], P(('dp', 'fsdp')), may hold values from -1.796875 to 1.796875
- inner_reduce: bfloat16 [3072, 768], P(('dp', 'fsdp')), may hold values from -0.109375 to 0.109375
- inner_reduce_bias: bfloat16 [768], P(('dp', 'fsdp')), may hold values from -1.796875 to 1.796875
- inner_final_gain: bfloat16 [768], P(('dp', 'fsdp')), may hold values from 0.5 to 1.5
- inner_final_shift: bfloat16 [768], P(('dp', 'fsdp')), may hold values from -1.796875 to 1.796875
- outer_attend: bfloat16 [768, 2304], P(('dp', 'fsdp')), may hold values from -0.21875 to 0.21875
- outer_attend_bias: bfloat16 [2304], P(('dp', 'fsdp')), may hold values from -1.796875 to 1.796875
- outer_merge: bfloat16 [768, 768], P(('dp', 'fsdp')), may hold values from -0.625 to 0.625
- outer_merge_bias: bfloat16 [768], P(('dp', 'fsdp')), may hold values from -1.796875 to 1.796875
- outer_gain: bfloat16 [768], P(('dp', 'fsdp')), may hold values from 0.5 to 1.5
- outer_shift: bfloat16 [768], P(('dp', 'fsdp')), may hold values from -1.796875 to 1.796875
- outer_expand: bfloat16 [768, 3072], P(('dp', 'fsdp')), may hold values from -0.21875 to 0.21875
- outer_expand_bias: bfloat16 [3072], P(('dp', 'fsdp')), may hold values from -1.796875 to 1.796875
- outer_reduce: bfloat16 [3072, 768], P(('dp', 'fsdp')), may hold values from -0.109375 to 0.109375
- outer_reduce_bias: bfloat16 [768], P(('dp', 'fsdp')), may hold values from -1.796875 to 1.796875
- outer_final_gain: bfloat16 [768], P(('dp', 'fsdp')), may hold values from 0.5 to 1.5
- outer_final_shift: bfloat16 [768], P(('dp', 'fsdp')), may hold values from -1.796875 to 1.796875
- segment_place: bfloat16 [768, 8], P(('dp', 'fsdp')), may hold values from -3 to 3
- cotangent: bfloat16 [32768, 768], P(('dp', 'fsdp')), may hold values from -6 to 6
Outputs:
- mixed: bfloat16 [32768, 768], P(('dp', 'fsdp'))
- tokens_grad: float32 [32768, 768], P(('dp', 'fsdp'))
- grad_inner_attend: float32 [768, 2304], P(('dp', 'fsdp'))
- grad_inner_attend_bias: float32 [2304], P(('dp', 'fsdp'))
- grad_inner_merge: float32 [768, 768], P(('dp', 'fsdp'))
- grad_inner_merge_bias: float32 [768], P(('dp', 'fsdp'))
- grad_inner_gain: float32 [768], P(('dp', 'fsdp'))
- grad_inner_shift: float32 [768], P(('dp', 'fsdp'))
- grad_inner_expand: float32 [768, 3072], P(('dp', 'fsdp'))
- grad_inner_expand_bias: float32 [3072], P(('dp', 'fsdp'))
- grad_inner_reduce: float32 [3072, 768], P(('dp', 'fsdp'))
- grad_inner_reduce_bias: float32 [768], P(('dp', 'fsdp'))
- grad_inner_final_gain: float32 [768], P(('dp', 'fsdp'))
- grad_inner_final_shift: float32 [768], P(('dp', 'fsdp'))
- grad_outer_attend: float32 [768, 2304], P(('dp', 'fsdp'))
- grad_outer_attend_bias: float32 [2304], P(('dp', 'fsdp'))
- grad_outer_merge: float32 [768, 768], P(('dp', 'fsdp'))
- grad_outer_merge_bias: float32 [768], P(('dp', 'fsdp'))
- grad_outer_gain: float32 [768], P(('dp', 'fsdp'))
- grad_outer_shift: float32 [768], P(('dp', 'fsdp'))
- grad_outer_expand: float32 [768, 3072], P(('dp', 'fsdp'))
- grad_outer_expand_bias: float32 [3072], P(('dp', 'fsdp'))
- grad_outer_reduce: float32 [3072, 768], P(('dp', 'fsdp'))
- grad_outer_reduce_bias: float32 [768], P(('dp', 'fsdp'))
- grad_outer_final_gain: float32 [768], P(('dp', 'fsdp'))
- grad_outer_final_shift: float32 [768], P(('dp', 'fsdp'))
- grad_segment_place: float32 [768, 8], P(('dp', 'fsdp'))
Inputs may be any that keep to these rules, and one draw needn't show every extreme that they name: `counts`: each document fills all its segments but the last, which holds at least one token; some document is full and some holds exactly 897 tokens.
All inputs are finite; a program needn't handle non-finite values.
Results may differ from a plain program's by a relative error of at most 0.025.
Values may be sent and summed in bfloat16 or wider, within the bound.
No kernel may reach another device: no remote copies, remote signals or barrier semaphores. Data moves between devices by JAX's collectives and lax.ppermute only.
A program may use at most 256 MiB of HBM per device.

v0:
```python
from functools import partial

import jax
import jax.numpy as jnp
from jax import lax
from jax.sharding import PartitionSpec as P

D = 768
HEADS = 12
HD = 64
SEG = 128
SLOTS = 1024
SEGS = 8


def norm_apply(rows, norm_gain, norm_shift):
    centre = jnp.mean(rows, axis=-1, keepdims=True)
    centred = rows - centre
    spread = jnp.mean(centred * centred, axis=-1, keepdims=True)
    return centred * lax.rsqrt(spread + 1e-05) * norm_gain + norm_shift


def prepare(group):
    return tuple(
        (
            entry if place_index in (0, 2, 6, 8) else entry.astype(jnp.float32)
            for place_index, entry in enumerate(group)
        )
    )


def cross_rows(left_rows, right_rows):
    return lax.dot_general(
        left_rows, right_rows, (((0,), (0,)), ((), ())), preferred_element_type=jnp.float32
    )


def back_cols(left_rows, right_rows):
    return lax.dot_general(
        left_rows, right_rows, (((1,), (1,)), ((), ())), preferred_element_type=jnp.float32
    )


def block_forward(source, source_float, key_mask, weights):
    (
        attend,
        attend_bias,
        merge,
        merge_bias,
        norm_gain,
        norm_shift,
        expand,
        expand_bias,
        reduce_matrix,
        reduce_bias,
        final_gain,
        final_shift,
    ) = weights
    groups, length, row_width = source.shape
    source_rows = source.reshape(groups * length, row_width)
    projected = (
        jnp.dot(source_rows, attend, preferred_element_type=jnp.float32) + attend_bias
    ).astype(jnp.bfloat16)
    projected = projected.reshape(groups, length, 3, HEADS, HD)
    query_heads = projected[:, :, 0]
    key_heads = projected[:, :, 1]
    value_heads = projected[:, :, 2]
    scores = jnp.einsum(
        "gqhe,gkhe->ghqk", query_heads, key_heads, preferred_element_type=jnp.float32
    ) * HD ** (-0.5)
    if key_mask is not None:
        scores = jnp.where(key_mask[:, None, None, :], scores, -1e30)
    softmax_out = jax.nn.softmax(scores, axis=-1)
    probs_low = softmax_out.astype(jnp.bfloat16)
    context = jnp.einsum(
        "ghqk,gkhe->gqhe", probs_low, value_heads, preferred_element_type=jnp.float32
    )
    context = context.astype(jnp.bfloat16).reshape(groups * length, row_width)
    first_sum = (
        source_float.reshape(groups * length, row_width)
        + jnp.dot(context, merge, preferred_element_type=jnp.float32)
        + merge_bias
    )
    normed = norm_apply(first_sum, norm_gain, norm_shift).astype(jnp.bfloat16)
    hidden = jnp.dot(normed, expand, preferred_element_type=jnp.float32) + expand_bias
    active = jax.nn.gelu(hidden, approximate=False).astype(jnp.bfloat16)
    second_sum = (
        normed.astype(jnp.float32)
        + jnp.dot(active, reduce_matrix, preferred_element_type=jnp.float32)
        + reduce_bias
    )
    result = norm_apply(second_sum, final_gain, final_shift)
    saved = (
        source_rows,
        query_heads,
        key_heads,
        value_heads,
        softmax_out,
        probs_low,
        context,
        first_sum,
        normed,
        hidden,
        active,
        second_sum,
    )
    return (result, saved)


def block_backward(grad_out, saved, weights):
    (
        attend,
        attend_bias,
        merge,
        merge_bias,
        norm_gain,
        norm_shift,
        expand,
        expand_bias,
        reduce_matrix,
        reduce_bias,
        final_gain,
        final_shift,
    ) = weights
    (
        source_rows,
        query_heads,
        key_heads,
        value_heads,
        softmax_out,
        probs_low,
        context,
        first_sum,
        normed,
        hidden,
        active,
        second_sum,
    ) = saved
    groups, length = (query_heads.shape[0], query_heads.shape[1])
    row_width = source_rows.shape[1]
    scale = HD ** (-0.5)
    _, pull_final = jax.vjp(norm_apply, second_sum, final_gain, final_shift)
    grad_second, grad_final_gain, grad_final_shift = pull_final(grad_out)
    grad_branch = grad_second.astype(jnp.bfloat16)
    grad_reduce = cross_rows(active, grad_branch)
    grad_reduce_bias = jnp.sum(grad_branch.astype(jnp.float32), axis=0)
    _, pull_gelu = jax.vjp(partial(jax.nn.gelu, approximate=False), hidden)
    grad_hidden = pull_gelu(back_cols(grad_branch, reduce_matrix))[0].astype(jnp.bfloat16)
    grad_expand = cross_rows(normed, grad_hidden)
    grad_expand_bias = jnp.sum(grad_hidden.astype(jnp.float32), axis=0)
    grad_normed = grad_second + back_cols(grad_hidden, expand)
    _, pull_first = jax.vjp(norm_apply, first_sum, norm_gain, norm_shift)
    grad_first, grad_gain, grad_shift = pull_first(grad_normed)
    grad_attn = grad_first.astype(jnp.bfloat16)
    grad_merge = cross_rows(context, grad_attn)
    grad_merge_bias = jnp.sum(grad_attn.astype(jnp.float32), axis=0)
    grad_context = (
        back_cols(grad_attn, merge).astype(jnp.bfloat16).reshape(groups, length, HEADS, HD)
    )
    grad_values = jnp.einsum(
        "ghqk,gqhe->gkhe", probs_low, grad_context, preferred_element_type=jnp.float32
    )
    grad_probs = jnp.einsum(
        "gqhe,gkhe->ghqk", grad_context, value_heads, preferred_element_type=jnp.float32
    )
    row_total = jnp.sum(grad_probs * softmax_out, axis=-1, keepdims=True)
    grad_scores = (softmax_out * (grad_probs - row_total)).astype(jnp.bfloat16)
    grad_query = (
        jnp.einsum("ghqk,gkhe->gqhe", grad_scores, key_heads, preferred_element_type=jnp.float32)
        * scale
    )
    grad_key = (
        jnp.einsum("ghqk,gqhe->gkhe", grad_scores, query_heads, preferred_element_type=jnp.float32)
        * scale
    )
    grad_projected = jnp.stack([grad_query, grad_key, grad_values], axis=2)
    grad_projected = grad_projected.reshape(groups * length, 3 * row_width).astype(jnp.bfloat16)
    grad_attend = cross_rows(source_rows, grad_projected)
    grad_attend_bias = jnp.sum(grad_projected.astype(jnp.float32), axis=0)
    grad_source = grad_first + back_cols(grad_projected, attend)
    return (
        grad_source,
        (
            grad_attend,
            grad_attend_bias,
            grad_merge,
            grad_merge_bias,
            grad_gain,
            grad_shift,
            grad_expand,
            grad_expand_bias,
            grad_reduce,
            grad_reduce_bias,
            grad_final_gain,
            grad_final_shift,
        ),
    )


def reduce_bucket(bucket):
    return (
        lax.psum_scatter(bucket[0], ("dp", "fsdp"), scatter_dimension=0, tiled=True),
        lax.psum_scatter(bucket[1], ("dp", "fsdp"), scatter_dimension=0, tiled=True),
        lax.psum_scatter(bucket[2], ("dp", "fsdp"), scatter_dimension=0, tiled=True),
        lax.psum_scatter(bucket[3], ("dp", "fsdp"), scatter_dimension=0, tiled=True),
        lax.psum_scatter(bucket[4], ("dp", "fsdp"), scatter_dimension=0, tiled=True),
    )


def on_device(
    tokens,
    counts,
    inner_attend,
    inner_attend_bias,
    inner_merge,
    inner_merge_bias,
    inner_gain,
    inner_shift,
    inner_expand,
    inner_expand_bias,
    inner_reduce,
    inner_reduce_bias,
    inner_final_gain,
    inner_final_shift,
    outer_attend,
    outer_attend_bias,
    outer_merge,
    outer_merge_bias,
    outer_gain,
    outer_shift,
    outer_expand,
    outer_expand_bias,
    outer_reduce,
    outer_reduce_bias,
    outer_final_gain,
    outer_final_shift,
    segment_place,
    cotangent,
):
    gathered = (
        lax.all_gather(inner_attend, ("dp", "fsdp"), axis=0, tiled=True),
        lax.all_gather(inner_attend_bias, ("dp", "fsdp"), axis=0, tiled=True),
        lax.all_gather(inner_merge, ("dp", "fsdp"), axis=0, tiled=True),
        lax.all_gather(inner_merge_bias, ("dp", "fsdp"), axis=0, tiled=True),
        lax.all_gather(inner_gain, ("dp", "fsdp"), axis=0, tiled=True),
        lax.all_gather(inner_shift, ("dp", "fsdp"), axis=0, tiled=True),
        lax.all_gather(inner_expand, ("dp", "fsdp"), axis=0, tiled=True),
        lax.all_gather(inner_expand_bias, ("dp", "fsdp"), axis=0, tiled=True),
        lax.all_gather(inner_reduce, ("dp", "fsdp"), axis=0, tiled=True),
        lax.all_gather(inner_reduce_bias, ("dp", "fsdp"), axis=0, tiled=True),
        lax.all_gather(inner_final_gain, ("dp", "fsdp"), axis=0, tiled=True),
        lax.all_gather(inner_final_shift, ("dp", "fsdp"), axis=0, tiled=True),
        lax.all_gather(outer_attend, ("dp", "fsdp"), axis=0, tiled=True),
        lax.all_gather(outer_attend_bias, ("dp", "fsdp"), axis=0, tiled=True),
        lax.all_gather(outer_merge, ("dp", "fsdp"), axis=0, tiled=True),
        lax.all_gather(outer_merge_bias, ("dp", "fsdp"), axis=0, tiled=True),
        lax.all_gather(outer_gain, ("dp", "fsdp"), axis=0, tiled=True),
        lax.all_gather(outer_shift, ("dp", "fsdp"), axis=0, tiled=True),
        lax.all_gather(outer_expand, ("dp", "fsdp"), axis=0, tiled=True),
        lax.all_gather(outer_expand_bias, ("dp", "fsdp"), axis=0, tiled=True),
        lax.all_gather(outer_reduce, ("dp", "fsdp"), axis=0, tiled=True),
        lax.all_gather(outer_reduce_bias, ("dp", "fsdp"), axis=0, tiled=True),
        lax.all_gather(outer_final_gain, ("dp", "fsdp"), axis=0, tiled=True),
        lax.all_gather(outer_final_shift, ("dp", "fsdp"), axis=0, tiled=True),
        lax.all_gather(segment_place, ("dp", "fsdp"), axis=0, tiled=True),
    )
    inner_weights = prepare(gathered[0:12])
    outer_weights = prepare(gathered[12:24])
    place_table = gathered[24].astype(jnp.float32)
    docs = counts.shape[0]
    keep_mask = jnp.arange(SLOTS)[None, :] < counts[:, None]
    segment_mask = keep_mask.reshape(docs * SEGS, SEG)
    keep_float = segment_mask.astype(jnp.float32)[:, :, None]
    token_groups = tokens.reshape(docs * SEGS, SEG, D)
    inner_out, inner_saved = block_forward(
        token_groups, token_groups.astype(jnp.float32), segment_mask, inner_weights
    )
    inner_rows = inner_out.reshape(docs * SEGS, SEG, D)
    heads_in = (
        inner_rows[:, 0, :].reshape(docs, SEGS, D) + jnp.transpose(place_table)[None]
    ).astype(jnp.bfloat16)
    outer_out, outer_saved = block_forward(
        heads_in, heads_in.astype(jnp.float32), None, outer_weights
    )
    joined = (
        jnp.concatenate([outer_out.reshape(docs * SEGS, 1, D), inner_rows[:, 1:]], axis=1)
        * keep_float
    )
    mixed = joined.reshape(docs * SLOTS, D).astype(jnp.bfloat16)
    regathered = (
        lax.all_gather(inner_attend, ("dp", "fsdp"), axis=0, tiled=True),
        lax.all_gather(inner_attend_bias, ("dp", "fsdp"), axis=0, tiled=True),
        lax.all_gather(inner_merge, ("dp", "fsdp"), axis=0, tiled=True),
        lax.all_gather(inner_merge_bias, ("dp", "fsdp"), axis=0, tiled=True),
        lax.all_gather(inner_gain, ("dp", "fsdp"), axis=0, tiled=True),
        lax.all_gather(inner_shift, ("dp", "fsdp"), axis=0, tiled=True),
        lax.all_gather(inner_expand, ("dp", "fsdp"), axis=0, tiled=True),
        lax.all_gather(inner_expand_bias, ("dp", "fsdp"), axis=0, tiled=True),
        lax.all_gather(inner_reduce, ("dp", "fsdp"), axis=0, tiled=True),
        lax.all_gather(inner_reduce_bias, ("dp", "fsdp"), axis=0, tiled=True),
        lax.all_gather(inner_final_gain, ("dp", "fsdp"), axis=0, tiled=True),
        lax.all_gather(inner_final_shift, ("dp", "fsdp"), axis=0, tiled=True),
        lax.all_gather(outer_attend, ("dp", "fsdp"), axis=0, tiled=True),
        lax.all_gather(outer_attend_bias, ("dp", "fsdp"), axis=0, tiled=True),
        lax.all_gather(outer_merge, ("dp", "fsdp"), axis=0, tiled=True),
        lax.all_gather(outer_merge_bias, ("dp", "fsdp"), axis=0, tiled=True),
        lax.all_gather(outer_gain, ("dp", "fsdp"), axis=0, tiled=True),
        lax.all_gather(outer_shift, ("dp", "fsdp"), axis=0, tiled=True),
        lax.all_gather(outer_expand, ("dp", "fsdp"), axis=0, tiled=True),
        lax.all_gather(outer_expand_bias, ("dp", "fsdp"), axis=0, tiled=True),
        lax.all_gather(outer_reduce, ("dp", "fsdp"), axis=0, tiled=True),
        lax.all_gather(outer_reduce_bias, ("dp", "fsdp"), axis=0, tiled=True),
        lax.all_gather(outer_final_gain, ("dp", "fsdp"), axis=0, tiled=True),
        lax.all_gather(outer_final_shift, ("dp", "fsdp"), axis=0, tiled=True),
        lax.all_gather(segment_place, ("dp", "fsdp"), axis=0, tiled=True),
    )
    inner_back = prepare(regathered[0:12])
    outer_back = prepare(regathered[12:24])
    grad_joined = cotangent.astype(jnp.float32).reshape(docs * SEGS, SEG, D) * keep_float
    grad_heads, outer_grads = block_backward(grad_joined[:, 0, :], outer_saved, outer_back)
    grad_place = jnp.transpose(jnp.sum(grad_heads.reshape(docs, SEGS, D), axis=0))
    grad_inner_rows = jnp.concatenate(
        [grad_heads.reshape(docs * SEGS, 1, D), grad_joined[:, 1:]], axis=1
    )
    tokens_grad, inner_grads = block_backward(
        grad_inner_rows.reshape(docs * SLOTS, D), inner_saved, inner_back
    )
    grad_list = inner_grads + outer_grads + (grad_place,)
    owned = ()
    for bucket_index in range(5):
        owned = owned + tuple(reduce_bucket(grad_list[5 * bucket_index : 5 * bucket_index + 5]))
    return (mixed, tokens_grad) + owned


def solution(mesh):
    return jax.shard_map(
        on_device,
        mesh=mesh,
        in_specs=(
            P(("dp", "fsdp"), None),
            P(("dp", "fsdp")),
            P(("dp", "fsdp"), None),
            P(("dp", "fsdp")),
            P(("dp", "fsdp"), None),
            P(("dp", "fsdp")),
            P(("dp", "fsdp")),
            P(("dp", "fsdp")),
            P(("dp", "fsdp"), None),
            P(("dp", "fsdp")),
            P(("dp", "fsdp"), None),
            P(("dp", "fsdp")),
            P(("dp", "fsdp")),
            P(("dp", "fsdp")),
            P(("dp", "fsdp"), None),
            P(("dp", "fsdp")),
            P(("dp", "fsdp"), None),
            P(("dp", "fsdp")),
            P(("dp", "fsdp")),
            P(("dp", "fsdp")),
            P(("dp", "fsdp"), None),
            P(("dp", "fsdp")),
            P(("dp", "fsdp"), None),
            P(("dp", "fsdp")),
            P(("dp", "fsdp")),
            P(("dp", "fsdp")),
            P(("dp", "fsdp"), None),
            P(("dp", "fsdp"), None),
        ),
        out_specs=(
            P(("dp", "fsdp"), None),
            P(("dp", "fsdp"), None),
            P(("dp", "fsdp"), None),
            P(("dp", "fsdp")),
            P(("dp", "fsdp"), None),
            P(("dp", "fsdp")),
            P(("dp", "fsdp")),
            P(("dp", "fsdp")),
            P(("dp", "fsdp"), None),
            P(("dp", "fsdp")),
            P(("dp", "fsdp"), None),
            P(("dp", "fsdp")),
            P(("dp", "fsdp")),
            P(("dp", "fsdp")),
            P(("dp", "fsdp"), None),
            P(("dp", "fsdp")),
            P(("dp", "fsdp"), None),
            P(("dp", "fsdp")),
            P(("dp", "fsdp")),
            P(("dp", "fsdp")),
            P(("dp", "fsdp"), None),
            P(("dp", "fsdp")),
            P(("dp", "fsdp"), None),
            P(("dp", "fsdp")),
            P(("dp", "fsdp")),
            P(("dp", "fsdp")),
            P(("dp", "fsdp"), None),
        ),
        check_vma=False,
    )
```

profile of v0, /device:TPU:0, one launch (start us, length us, event | category | flops | bytes accessed | tf_op | source)
XLA Modules:
  0.0 1790.0 jit_solution(9081312391397027474)
XLA Ops:
  17.2 2.5 slice_reduce_fusion.1
  24.3 43.5 %all-reduce.34 = (bf16[768]{0:T(1024)(128)(2,1)S(1)}, bf16[2304]{0:T(1024)(128)(2,1)S(1)}, bf16[768]{0:T(1024)(128)(2,1)S(1)}, bf16[768]{0:T(1024)(128)(2,1)S(1)...) all-reduce(bf16[768]{0:T(1024)(128)(2,1)S(1)} %dynamic-update-slice, ...), channel_id=1, replica_groups=mesh['dp'=4,'fsdp'=8] {'dp','fsdp'}, use_global_device_ids=true, to_apply=%add.1 | all-reduce | flops 19968 | bytes 79872
  69.2 40.5 %all-gather = bf16[32,24,8]{1,2,0:T(8,128)(2,1)S(1)} all-gather(bf16[1,24,8]{1,2,0:T(8,128)(2,1)S(1)} %bitcast.224), channel_id=1, replica_groups=mesh['dp'=4,'fsdp'=8] {'dp','fsdp'}, dimensions={0}, use_global_device_ids=true | all-gather | bytes 12672 | tf_op jit(solution)/shard_map/all_gather | solution.py:265
  111.2 7.4 add_convert_fusion.1
  118.6 6.6 copy.135
  125.3 3.6 copy.182
  130.9 2.7 fusion.74
  136.2 2.4 copy.140
  138.6 3.9 fusion.75
  143.1 53.4 %all-gather.14.cloned.1.call-done = bf16[768,3072]{1,0:T(8,128)(2,1)} async-done(((bf16[24,3072]{1,0:T(8,128)(2,1)}), bf16[768,3072]{1,0:T(8,128)(2,1)}) %all-gather.14.cloned.1.call-update) | async-done | bytes 4718608 | tf_op jit(solution)/shard_map/all_gather | solution.py:247
  196.5 36.0 %multiply_convert_fusion = (bf16[1024,3072]{1,0:T(8,128)(2,1)}, f32[1024,3072]{1,0:T(8,128)}, f32[1024,3072]{1,0:T(8,128)}) fusion(f32[3072]{0:T(1024)S(1)} %convert_element_type.225, bf16[768,3072]{1,0:T(8,128)(2,1)} %all-gather.14.cloned.1.call-done, f32[1024,768]{1,0:T(8,128)S(1)} %get-tuple-element.216, f32[768]{0:T(1024)S(1)} %convert_element_type.222, ...), kind=kOutput, calls=%fused_computation.6 | convolution fusion | flops 5043388416 | bytes 39348224 | tf_op jit(solution)/shard_map/dot_general | solution.py:85
  232.5 29.4 %all-gather.16.cloned.1.call-done = bf16[3072,768]{1,0:T(8,128)(2,1)} async-done(((bf16[96,768]{1,0:T(8,128)(2,1)}), bf16[3072,768]{1,0:T(8,128)(2,1)}) %all-gather.16.cloned.1.call-update) | async-done | bytes 4718608 | tf_op jit(solution)/shard_map/all_gather | solution.py:249
  261.8 9.5 fusion.76
  274.2 49.6 %all-gather.18.cloned.1.call-done = bf16[768,2304]{1,0:T(8,128)(2,1)} async-done(((bf16[24,2304]{1,0:T(8,128)(2,1)}), bf16[768,2304]{1,0:T(8,128)(2,1)}) %all-gather.18.cloned.1.call-update) | async-done | bytes 3538960 | tf_op jit(solution)/shard_map/all_gather | solution.py:253
  323.8 2.6 fusion.14
  327.7 52.0 %all-gather.20.cloned.1.call-done = bf16[768,768]{1,0:T(8,128)(2,1)} async-done(((bf16[24,768]{1,0:T(8,128)(2,1)}), bf16[768,768]{1,0:T(8,128)(2,1)}) %all-gather.20.cloned.1.call-update) | async-done | bytes 1179664 | tf_op jit(solution)/shard_map/all_gather | solution.py:255
  382.1 63.3 %all-gather.22.cloned.1.call-done = bf16[768,3072]{1,0:T(8,128)(2,1)} async-done(((bf16[24,3072]{1,0:T(8,128)(2,1)}), bf16[768,3072]{1,0:T(8,128)(2,1)}) %all-gather.22.cloned.1.call-update) | async-done | bytes 4718608 | tf_op jit(solution)/shard_map/all_gather | solution.py:259
  445.3 3.2 multiply_convert_fusion.2
  448.5 62.3 %all-gather.24.cloned.1.call-done = bf16[3072,768]{1,0:T(8,128)(2,1)} async-done(((bf16[96,768]{1,0:T(8,128)(2,1)}), bf16[3072,768]{1,0:T(8,128)(2,1)}) %all-gather.24.cloned.1.call-update) | async-done | bytes 4718608 | tf_op jit(solution)/shard_map/all_gather | solution.py:261
  510.9 3.3 fusion.79
  527.3 3.2 fusion.80
  537.5 19.4 %convert_reduce_fusion = (f32[3072]{0:T(1024)}, bf16[1024,3072]{1,0:T(8,128)(2,1)}) fusion(f32[1024,3072]{1,0:T(8,128)} %get-tuple-element.203, bf16[1024,768]{1,0:T(8,128)(2,1)} %get-tuple-element.187, bf16[3072,768]{1,0:T(8,128)(2,1)} %all-gather.16.cloned.1.call-done, f32[1024,3072]{1,0:T(8,128)} %get-tuple-element.217, f32[3072]{0:T(1024)S(1)} %copy-done.43), kind=kOutput, calls=%fused_computation.4 | convolution fusion | flops 4885312512 | bytes 37773312 | tf_op jit(solution)/shard_map/dot_general | solution.py:39
  556.9 10.2 multiply_reduce_fusion.1
  572.4 2.6 convolution_convert_fusion
  574.9 2.8 copy.157
  579.6 6.3 convolution_bitcast_fusion.1
  586.0 7.1 multiply_reduce_fusion
  593.0 5.0 multiply_convert_fusion.1
  601.7 3.1 convert_reduce_fusion.1
  606.8 4.7 fusion.22
  613.9 11.7 copy.163
  627.7 5.8 convolution_bitcast_fusion
  633.5 8.1 copy.171
  641.9 4.0 fusion.83
  646.0 10.7 fusion.81
  658.1 10.2 fusion.82
  668.4 5.1 fusion.85
  673.9 5.1 fusion.86
  686.0 5.9 add_add_fusion.4
  691.9 65.2 %all-reduce.37.cloned.1.call-done = (f32[2304]{0:T(1024)}, f32[768]{0:T(1024)}, f32[768]{0:T(1024)}, f32[768]{0:T(1024)}, f32[3072]{0:T(1024)}, /*index=5*/f32[7...) async-done(((f32[2304]{0:T(1024)}, f32[768]{0:T(1024)}, ...) | async-done | bytes 104464
  778.7 83.5 %reduce-scatter.12.cloned.1.call-done = f32[24,768]{1,0:T(8,128)} async-done(((f32[768,768]{1,0:T(8,128)}), f32[24,768]{1,0:T(8,128)}) %reduce-scatter.12.cloned.1.call-update) | async-done | bytes 73744 | tf_op jit(solution)/shard_map/reduce_scatter | solution.py:204
  862.2 104.8 %reduce-scatter.20.cloned.1.call-done = f32[24,768]{1,0:T(8,128)} async-done(((f32[768,768]{1,0:T(8,128)}), f32[24,768]{1,0:T(8,128)}) %reduce-scatter.20.cloned.1.call-update) | async-done | bytes 73744 | tf_op jit(solution)/shard_map/reduce_scatter | solution.py:206
  967.0 124.1 %reduce-scatter.26.cloned.1.call-done = f32[24,2304]{1,0:T(8,128)} async-done(((f32[768,2304]{1,0:T(8,128)}), f32[24,2304]{1,0:T(8,128)}) %reduce-scatter.26.cloned.1.call-update) | async-done | bytes 221200
  1091.1 125.6 %reduce-scatter.18.cloned.1.call-done = f32[24,2304]{1,0:T(8,128)} async-done(((f32[768,2304]{1,0:T(8,128)}), f32[24,2304]{1,0:T(8,128)}) %reduce-scatter.18.cloned.1.call-update) | async-done | bytes 221200 | tf_op jit(solution)/shard_map/reduce_scatter | solution.py:204
  1216.7 141.3 %reduce-scatter.14.cloned.1.call-done = f32[24,3072]{1,0:T(8,128)} async-done(((f32[768,3072]{1,0:T(8,128)}), f32[24,3072]{1,0:T(8,128)}) %reduce-scatter.14.cloned.1.call-update) | async-done | bytes 294928 | tf_op jit(solution)/shard_map/reduce_scatter | solution.py:203
  1358.0 142.0 %reduce-scatter.16.cloned.1.call-done = f32[96,768]{1,0:T(8,128)} async-done(((f32[3072,768]{1,0:T(8,128)}), f32[96,768]{1,0:T(8,128)}) %reduce-scatter.16.cloned.1.call-update) | async-done | bytes 294928 | tf_op jit(solution)/shard_map/reduce_scatter | solution.py:205
  1500.1 141.0 %reduce-scatter.22.cloned.1.call-done = f32[24,3072]{1,0:T(8,128)} async-done(((f32[768,3072]{1,0:T(8,128)}), f32[24,3072]{1,0:T(8,128)}) %reduce-scatter.22.cloned.1.call-update) | async-done | bytes 294928 | tf_op jit(solution)/shard_map/reduce_scatter | solution.py:205
  1641.0 142.0 %reduce-scatter.24.cloned.1.call-done = f32[96,768]{1,0:T(8,128)} async-done(((f32[3072,768]{1,0:T(8,128)}), f32[96,768]{1,0:T(8,128)}) %reduce-scatter.24.cloned.1.call-update) | async-done | bytes 294928 | tf_op jit(solution)/shard_map/reduce_scatter | solution.py:202
  (327 shorter events, 95.6 us)
Async XLA Ops:
  7.2 104.0 %all-gather.10.cloned.1.call-start = ((), (), s32[]{:S(2)}) async-start(), calls=%async_computation.8 | async-start | bytes 3649536 | tf_op jit(solution)/shard_map/all_gather | solution.py:241
  7.9 130.7 %all-gather.12.cloned.1.call-start = ((), (), s32[]{:S(2)}) async-start(), calls=%async_computation.9 | async-start | bytes 1216512 | tf_op jit(solution)/shard_map/all_gather | solution.py:243
  8.7 187.8 %all-gather.14.cloned.1.call-start = ((), (), s32[]{:S(2)}) async-start(), calls=%async_computation.10 | async-start | bytes 4866048 | tf_op jit(solution)/shard_map/all_gather | solution.py:247
  9.4 252.4 %all-gather.16.cloned.1.call-start = ((), (), s32[]{:S(2)}) async-start(), calls=%async_computation.11 | async-start | bytes 4866048 | tf_op jit(solution)/shard_map/all_gather | solution.py:249
  10.0 313.8 %all-gather.18.cloned.1.call-start = ((), (), s32[]{:S(2)}) async-start(), calls=%async_computation.12 | async-start | bytes 3649536 | tf_op jit(solution)/shard_map/all_gather | solution.py:253
  10.6 369.1 %all-gather.20.cloned.1.call-start = ((), (), s32[]{:S(2)}) async-start(), calls=%async_computation.13 | async-start | bytes 1216512 | tf_op jit(solution)/shard_map/all_gather | solution.py:255
  11.2 434.2 %all-gather.22.cloned.1.call-start = ((), (), s32[]{:S(2)}) async-start(), calls=%async_computation.14 | async-start | bytes 4866048 | tf_op jit(solution)/shard_map/all_gather | solution.py:259
  11.9 498.9 %all-gather.24.cloned.1.call-start = ((), (), s32[]{:S(2)}) async-start(), calls=%async_computation.15 | async-start | bytes 4866048 | tf_op jit(solution)/shard_map/all_gather | solution.py:261
  12.7 744.5 %all-reduce.37.cloned.1.call-start = ((), (), s32[]{:S(2)}) async-start(), calls=%async_computation.24 | async-start | bytes 245760
  17.1 5.0 copy-start.60
  17.1 5.3 copy-start.61
  17.1 5.5 copy-start.62
  17.2 5.7 copy-start.63
  17.2 5.9 copy-start.64
  17.2 6.2 copy-start.65
  17.2 6.4 copy-start.66
  17.2 6.6 copy-start.67
  17.2 6.9 copy-start.68
  17.2 51.9 %copy-start.45 = (bf16[24,8]{0,1:T(8,128)(2,1)S(1)}, bf16[24,8]{0,1:T(8,128)(2,1)}, u32[]{:S(2)}) copy-start(bf16[24,8]{0,1:T(8,128)(2,1)} %param.54) | copy-start | bytes 1156
  17.2 94.0 %copy-start.50 = (bf16[1024,768]{1,0:T(8,128)(2,1)S(1)}, bf16[1024,768]{1,0:T(8,128)(2,1)}, u32[]{:S(2)}) copy-start(bf16[1024,768]{1,0:T(8,128)(2,1)} %param.28) | copy-start | bytes 4718596
  67.9 128.6 %copy-start.42 = (f32[3072]{0:T(1024)}, f32[3072]{0:T(1024)S(1)}, u32[]{:S(2)}) copy-start(f32[3072]{0:T(1024)S(1)} %convert_element_type.225) | copy-start | bytes 36868
  142.5 89.9 %copy-start = (f32[1024,768]{1,0:T(8,128)}, f32[1024,768]{1,0:T(8,128)S(1)}, u32[]{:S(2)}) copy-start(f32[1024,768]{1,0:T(8,128)S(1)} %get-tuple-element.216) | copy-start | bytes 9437188
  143.1 89.4 %copy-start.33 = (f32[1024]{0:T(1024)}, f32[1024]{0:T(1024)S(1)}, u32[]{:S(2)}) copy-start(f32[1024]{0:T(1024)S(1)} %multiply_reduce_fusion.5) | copy-start | bytes 12292
  326.5 55.1 %copy-start.25 = (bf16[1,8,1,12,64]{4,3,2,1,0:T(8,128)(2,1)}, bf16[1,8,1,12,64]{4,3,2,1,0:T(8,128)(2,1)S(1)}, u32[]{:S(2)}) copy-start(bf16[1,8,1,12,64]{4,3,2,1,0:T(8,128)(2,1)S(1)} %get-tuple-element.210) | copy-start | bytes 36868
  326.5 55.1 %copy-start.38 = (bf16[1,8,1,12,64]{4,3,2,1,0:T(8,128)(2,1)}, bf16[1,8,1,12,64]{4,3,2,1,0:T(8,128)(2,1)S(1)}, u32[]{:S(2)}) copy-start(bf16[1,8,1,12,64]{4,3,2,1,0:T(8,128)(2,1)S(1)} %get-tuple-element.211) | copy-start | bytes 36868
  326.7 54.8 %copy-start.44 = (f32[12,8]{1,0:T(8,128)}, f32[12,8]{1,0:T(8,128)S(1)}, u32[]{:S(2)}) copy-start(f32[12,8]{1,0:T(8,128)S(1)} %get-tuple-element.220) | copy-start | bytes 1156
  327.7 183.2 %copy-start.39 = (f32[768]{0:T(1024)S(1)}, f32[768]{0:T(1024)}, u32[]{:S(2)}) copy-start(f32[768]{0:T(1024)} %convert_element_type.245) | copy-start | bytes 9220
  448.5 65.9 %copy-start.37 = (f32[768]{0:T(1024)S(1)}, f32[768]{0:T(1024)}, u32[]{:S(2)}) copy-start(f32[768]{0:T(1024)} %convert_element_type.246) | copy-start | bytes 9220
  448.5 67.5 %copy-start.40 = (f32[768]{0:T(1024)S(1)}, f32[768]{0:T(1024)}, u32[]{:S(2)}) copy-start(f32[768]{0:T(1024)} %convert_element_type.247) | copy-start | bytes 9220
  510.8 7.4 copy-start.3
  514.2 6.0 copy-start.2
  520.2 6.0 copy-start.26
  520.2 6.2 copy-start.24
  537.5 19.4 %copy-start.1 = (f32[1024,768]{1,0:T(8,128)S(1)}, f32[1024,768]{1,0:T(8,128)}, u32[]{:S(2)}) copy-start(f32[1024,768]{1,0:T(8,128)} %copy-done) | copy-start | bytes 9437188
  556.9 10.2 copy-start.34
  579.6 6.4 copy-start.18
  579.6 13.4 slice-start
  586.0 7.1 slice-start.1
  593.0 5.0 copy-start.7
  606.8 255.4 %reduce-scatter.12.cloned.1.call-start = ((), (), s32[]{:S(2)}) async-start(), calls=%async_computation.16 | async-start | bytes 2433024 | tf_op jit(solution)/shard_map/reduce_scatter | solution.py:204
  611.6 355.4 %reduce-scatter.20.cloned.1.call-start = ((), (), s32[]{:S(2)}) async-start(), calls=%async_computation.20 | async-start | bytes 2433024 | tf_op jit(solution)/shard_map/reduce_scatter | solution.py:206
  613.6 477.6 %reduce-scatter.26.cloned.1.call-start = ((), (), s32[]{:S(2)}) async-start(), calls=%async_computation.23 | async-start | bytes 7299072
  613.8 13.8 copy-start.51
  641.6 575.1 %reduce-scatter.18.cloned.1.call-start = ((), (), s32[]{:S(2)}) async-start(), calls=%async_computation.19 | async-start | bytes 7299072 | tf_op jit(solution)/shard_map/reduce_scatter | solution.py:204
  646.0 712.1 %reduce-scatter.14.cloned.1.call-start = ((), (), s32[]{:S(2)}) async-start(), calls=%async_computation.17 | async-start | bytes 9732096 | tf_op jit(solution)/shard_map/reduce_scatter | solution.py:203
  656.7 843.3 %reduce-scatter.16.cloned.1.call-start = ((), (), s32[]{:S(2)}) async-start(), calls=%async_computation.18 | async-start | bytes 9732096 | tf_op jit(solution)/shard_map/reduce_scatter | solution.py:205
  668.3 972.7 %reduce-scatter.22.cloned.1.call-start = ((), (), s32[]{:S(2)}) async-start(), calls=%async_computation.21 | async-start | bytes 9732096 | tf_op jit(solution)/shard_map/reduce_scatter | solution.py:205
  673.5 1109.5 %reduce-scatter.24.cloned.1.call-start = ((), (), s32[]{:S(2)}) async-start(), calls=%async_computation.22 | async-start | bytes 9732096 | tf_op jit(solution)/shard_map/reduce_scatter | solution.py:202
  (42 other events, 106.6 us)
Sparse Core Ops, SparseCore 0:
  11.1 63.4 all-gather.9
  77.6 53.2 all-gather.11
  133.8 62.5 all-gather.13
  199.3 62.4 all-gather.15
  264.7 59.0 all-gather.17
  326.7 52.9 all-gather.19
  382.7 62.5 all-gather.21
  448.3 62.4 all-gather.23
  606.9 150.1 all-reduce.36
  762.9 99.3 reduce-scatter.11
  869.0 98.0 reduce-scatter.19
  973.1 117.9 reduce-scatter.25
  1098.3 118.3 reduce-scatter.17
  1223.1 134.9 reduce-scatter.13
  1365.4 134.6 reduce-scatter.15
  1506.4 134.5 reduce-scatter.21
  1648.3 134.5 reduce-scatter.23
where the time goes:
time: 1800 us; the launch traced here: 1790 us
  waiting for transfers between devices  1380 us (77%)
  matrix products  182 us (10%)
  blocking collectives  84 us (5%)
  local copies, waits for them, and re-layouts  83.7 us (5%)
  other arithmetic  38 us (2%)
    reduce_scatter x2, waiting for transfers between devices, reduce_bucket(): lax.psum_scatter(bucket[3], ('dp', 'fsdp'), scatter_dimension=0, tiled=True)  283 us
    reduce_scatter x2, waiting for transfers between devices, reduce_bucket(): lax.psum_scatter(bucket[2], ('dp', 'fsdp'), scatter_dimension=0, tiled=True)  209 us
    unnamed x19, waiting for transfers between devices  195 us
    reduce_scatter x1, waiting for transfers between devices, reduce_bucket(): lax.psum_scatter(bucket[0], ('dp', 'fsdp'), scatter_dimension=0, tiled=True)  142 us
    reduce_scatter x1, waiting for transfers between devices, reduce_bucket(): lax.psum_scatter(bucket[1], ('dp', 'fsdp'), scatter_dimension=0, tiled=True)  141 us
    reduce_scatter x1, waiting for transfers between devices, reduce_bucket(): lax.psum_scatter(bucket[4], ('dp', 'fsdp'), scatter_dimension=0, tiled=True)  105 us
    all_gather x1, waiting for transfers between devices, on_device(): lax.all_gather(outer_expand, ('dp', 'fsdp'), axis=0, tiled=True)  63.3 us
    all_gather x1, waiting for transfers between devices, on_device(): lax.all_gather(outer_reduce, ('dp', 'fsdp'), axis=0, tiled=True)  62.3 us
  transfers between devices with their start and end apart: 17, of which 15 were waited for; matrix products, arithmetic and copies ran while one was open for 11% of the time, Pallas kernels for 0%

commit v1 on v0

--- a/solution.py
+++ b/solution.py
@@ -107,7 +107,7 @@
     return (result, saved)
 
 
-def block_backward(grad_out, saved, weights):
+def block_backward(grad_out, saved, weights, factors_only):
     (
         attend,
         attend_bias,
@@ -142,18 +142,12 @@
     _, pull_final = jax.vjp(norm_apply, second_sum, final_gain, final_shift)
     grad_second, grad_final_gain, grad_final_shift = pull_final(grad_out)
     grad_branch = grad_second.astype(jnp.bfloat16)
-    grad_reduce = cross_rows(active, grad_branch)
-    grad_reduce_bias = jnp.sum(grad_branch.astype(jnp.float32), axis=0)
     _, pull_gelu = jax.vjp(partial(jax.nn.gelu, approximate=False), hidden)
     grad_hidden = pull_gelu(back_cols(grad_branch, reduce_matrix))[0].astype(jnp.bfloat16)
-    grad_expand = cross_rows(normed, grad_hidden)
-    grad_expand_bias = jnp.sum(grad_hidden.astype(jnp.float32), axis=0)
     grad_normed = grad_second + back_cols(grad_hidden, expand)
     _, pull_first = jax.vjp(norm_apply, first_sum, norm_gain, norm_shift)
     grad_first, grad_gain, grad_shift = pull_first(grad_normed)
     grad_attn = grad_first.astype(jnp.bfloat16)
-    grad_merge = cross_rows(context, grad_attn)
-    grad_merge_bias = jnp.sum(grad_attn.astype(jnp.float32), axis=0)
     grad_context = (
         back_cols(grad_attn, merge).astype(jnp.bfloat16).reshape(groups, length, HEADS, HD)
     )
@@ -175,36 +169,52 @@
     )
     grad_projected = jnp.stack([grad_query, grad_key, grad_values], axis=2)
     grad_projected = grad_projected.reshape(groups * length, 3 * row_width).astype(jnp.bfloat16)
-    grad_attend = cross_rows(source_rows, grad_projected)
-    grad_attend_bias = jnp.sum(grad_projected.astype(jnp.float32), axis=0)
     grad_source = grad_first + back_cols(grad_projected, attend)
+    if factors_only:
+        return (
+            grad_source,
+            (
+                (source_rows, context, normed, active),
+                (grad_projected, grad_attn, grad_hidden, grad_branch),
+            ),
+            (grad_gain, grad_shift, grad_final_gain, grad_final_shift),
+        )
     return (
         grad_source,
         (
-            grad_attend,
-            grad_attend_bias,
-            grad_merge,
-            grad_merge_bias,
+            cross_rows(source_rows, grad_projected),
+            jnp.sum(grad_projected.astype(jnp.float32), axis=0),
+            cross_rows(context, grad_attn),
+            jnp.sum(grad_attn.astype(jnp.float32), axis=0),
             grad_gain,
             grad_shift,
-            grad_expand,
-            grad_expand_bias,
-            grad_reduce,
-            grad_reduce_bias,
+            cross_rows(normed, grad_hidden),
+            jnp.sum(grad_hidden.astype(jnp.float32), axis=0),
+            cross_rows(active, grad_branch),
+            jnp.sum(grad_branch.astype(jnp.float32), axis=0),
             grad_final_gain,
             grad_final_shift,
         ),
     )
 
 
-def reduce_bucket(bucket):
-    return (
-        lax.psum_scatter(bucket[0], ("dp", "fsdp"), scatter_dimension=0, tiled=True),
-        lax.psum_scatter(bucket[1], ("dp", "fsdp"), scatter_dimension=0, tiled=True),
-        lax.psum_scatter(bucket[2], ("dp", "fsdp"), scatter_dimension=0, tiled=True),
-        lax.psum_scatter(bucket[3], ("dp", "fsdp"), scatter_dimension=0, tiled=True),
-        lax.psum_scatter(bucket[4], ("dp", "fsdp"), scatter_dimension=0, tiled=True),
-    )
+AXES = ("dp", "fsdp")
+
+
+def gather(rows):
+    return lax.all_gather(rows, AXES, axis=0, tiled=True)
+
+
+def scatter(rows):
+    return lax.psum_scatter(rows, AXES, scatter_dimension=0, tiled=True)
+
+
+def split_cols(packed, widths):
+    pieces, start = [], 0
+    for width in widths:
+        pieces.append(packed[..., start : start + width])
+        start += width
+    return pieces
 
 
 def on_device(
@@ -237,36 +247,71 @@
     segment_place,
     cotangent,
 ):
-    gathered = (
-        lax.all_gather(inner_attend, ("dp", "fsdp"), axis=0, tiled=True),
-        lax.all_gather(inner_attend_bias, ("dp", "fsdp"), axis=0, tiled=True),
-        lax.all_gather(inner_merge, ("dp", "fsdp"), axis=0, tiled=True),
-        lax.all_gather(inner_merge_bias, ("dp", "fsdp"), axis=0, tiled=True),
-        lax.all_gather(inner_gain, ("dp", "fsdp"), axis=0, tiled=True),
-        lax.all_gather(inner_shift, ("dp", "fsdp"), axis=0, tiled=True),
-        lax.all_gather(inner_expand, ("dp", "fsdp"), axis=0, tiled=True),
-        lax.all_gather(inner_expand_bias, ("dp", "fsdp"), axis=0, tiled=True),
-        lax.all_gather(inner_reduce, ("dp", "fsdp"), axis=0, tiled=True),
-        lax.all_gather(inner_reduce_bias, ("dp", "fsdp"), axis=0, tiled=True),
-        lax.all_gather(inner_final_gain, ("dp", "fsdp"), axis=0, tiled=True),
-        lax.all_gather(inner_final_shift, ("dp", "fsdp"), axis=0, tiled=True),
-        lax.all_gather(outer_attend, ("dp", "fsdp"), axis=0, tiled=True),
-        lax.all_gather(outer_attend_bias, ("dp", "fsdp"), axis=0, tiled=True),
-        lax.all_gather(outer_merge, ("dp", "fsdp"), axis=0, tiled=True),
-        lax.all_gather(outer_merge_bias, ("dp", "fsdp"), axis=0, tiled=True),
-        lax.all_gather(outer_gain, ("dp", "fsdp"), axis=0, tiled=True),
-        lax.all_gather(outer_shift, ("dp", "fsdp"), axis=0, tiled=True),
-        lax.all_gather(outer_expand, ("dp", "fsdp"), axis=0, tiled=True),
-        lax.all_gather(outer_expand_bias, ("dp", "fsdp"), axis=0, tiled=True),
-        lax.all_gather(outer_reduce, ("dp", "fsdp"), axis=0, tiled=True),
-        lax.all_gather(outer_reduce_bias, ("dp", "fsdp"), axis=0, tiled=True),
-        lax.all_gather(outer_final_gain, ("dp", "fsdp"), axis=0, tiled=True),
-        lax.all_gather(outer_final_shift, ("dp", "fsdp"), axis=0, tiled=True),
-        lax.all_gather(segment_place, ("dp", "fsdp"), axis=0, tiled=True),
-    )
-    inner_weights = prepare(gathered[0:12])
-    outer_weights = prepare(gathered[12:24])
-    place_table = gathered[24].astype(jnp.float32)
+    parts = inner_merge.shape[0]
+    devices = D // parts
+    ratio = inner_reduce.shape[0] // parts
+    here = lax.axis_index(AXES)
+    small_parts = (
+        inner_attend_bias,
+        inner_merge_bias,
+        inner_gain,
+        inner_shift,
+        inner_expand_bias,
+        inner_reduce_bias,
+        inner_final_gain,
+        inner_final_shift,
+        outer_attend_bias,
+        outer_merge_bias,
+        outer_gain,
+        outer_shift,
+        outer_expand_bias,
+        outer_reduce_bias,
+        outer_final_gain,
+        outer_final_shift,
+        segment_place.reshape(parts * SEGS),
+    )
+    small_widths = [part.shape[0] for part in small_parts]
+    small = gather(jnp.concatenate(small_parts)[None])
+    small = [piece.reshape(-1) for piece in split_cols(small, small_widths)]
+    place_table = small[16].reshape(D, SEGS).astype(jnp.float32)
+
+    def rest_pack(merge, expand, reduce_matrix):
+        return jnp.concatenate([merge, expand, fold(reduce_matrix)], axis=1)
+
+    def fold(reduce_rows):
+        return jnp.concatenate(jnp.split(reduce_rows, ratio, axis=0), axis=1)
+
+    def unfold(packed):
+        return jnp.transpose(packed.reshape(devices, parts, ratio, D), (0, 2, 1, 3)).reshape(
+            devices * parts * ratio, D
+        )
+
+    def refold(grad):
+        return jnp.transpose(grad.reshape(devices, ratio, parts, D), (0, 2, 1, 3)).reshape(
+            D, ratio * D
+        )
+
+    wide = inner_expand.shape[1]
+    inner_attend_full = gather(inner_attend)
+    merge_full, expand_full, reduce_full = split_cols(
+        gather(rest_pack(inner_merge, inner_expand, inner_reduce)), (D, wide, ratio * D)
+    )
+    inner_weights = prepare(
+        (inner_attend_full, small[0], merge_full, small[1], small[2], small[3], expand_full)
+        + (small[4], unfold(reduce_full), small[5], small[6], small[7])
+    )
+    attend_full, merge_full, expand_full, reduce_full = split_cols(
+        gather(
+            jnp.concatenate(
+                [outer_attend, rest_pack(outer_merge, outer_expand, outer_reduce)], axis=1
+            )
+        ),
+        (3 * D, D, wide, ratio * D),
+    )
+    outer_weights = prepare(
+        (attend_full, small[8], merge_full, small[9], small[10], small[11], expand_full)
+        + (small[12], unfold(reduce_full), small[13], small[14], small[15])
+    )
     docs = counts.shape[0]
     keep_mask = jnp.arange(SLOTS)[None, :] < counts[:, None]
     segment_mask = keep_mask.reshape(docs * SEGS, SEG)
@@ -287,49 +332,99 @@
         * keep_float
     )
     mixed = joined.reshape(docs * SLOTS, D).astype(jnp.bfloat16)
-    regathered = (
-        lax.all_gather(inner_attend, ("dp", "fsdp"), axis=0, tiled=True),
-        lax.all_gather(inner_attend_bias, ("dp", "fsdp"), axis=0, tiled=True),
-        lax.all_gather(inner_merge, ("dp", "fsdp"), axis=0, tiled=True),
-        lax.all_gather(inner_merge_bias, ("dp", "fsdp"), axis=0, tiled=True),
-        lax.all_gather(inner_gain, ("dp", "fsdp"), axis=0, tiled=True),
-        lax.all_gather(inner_shift, ("dp", "fsdp"), axis=0, tiled=True),
-        lax.all_gather(inner_expand, ("dp", "fsdp"), axis=0, tiled=True),
-        lax.all_gather(inner_expand_bias, ("dp", "fsdp"), axis=0, tiled=True),
-        lax.all_gather(inner_reduce, ("dp", "fsdp"), axis=0, tiled=True),
-        lax.all_gather(inner_reduce_bias, ("dp", "fsdp"), axis=0, tiled=True),
-        lax.all_gather(inner_final_gain, ("dp", "fsdp"), axis=0, tiled=True),
-        lax.all_gather(inner_final_shift, ("dp", "fsdp"), axis=0, tiled=True),
-        lax.all_gather(outer_attend, ("dp", "fsdp"), axis=0, tiled=True),
-        lax.all_gather(outer_attend_bias, ("dp", "fsdp"), axis=0, tiled=True),
-        lax.all_gather(outer_merge, ("dp", "fsdp"), axis=0, tiled=True),
-        lax.all_gather(outer_merge_bias, ("dp", "fsdp"), axis=0, tiled=True),
-        lax.all_gather(outer_gain, ("dp", "fsdp"), axis=0, tiled=True),
-        lax.all_gather(outer_shift, ("dp", "fsdp"), axis=0, tiled=True),
-        lax.all_gather(outer_expand, ("dp", "fsdp"), axis=0, tiled=True),
-        lax.all_gather(outer_expand_bias, ("dp", "fsdp"), axis=0, tiled=True),
-        lax.all_gather(outer_reduce, ("dp", "fsdp"), axis=0, tiled=True),
-        lax.all_gather(outer_reduce_bias, ("dp", "fsdp"), axis=0, tiled=True),
-        lax.all_gather(outer_final_gain, ("dp", "fsdp"), axis=0, tiled=True),
-        lax.all_gather(outer_final_shift, ("dp", "fsdp"), axis=0, tiled=True),
-        lax.all_gather(segment_place, ("dp", "fsdp"), axis=0, tiled=True),
-    )
-    inner_back = prepare(regathered[0:12])
-    outer_back = prepare(regathered[12:24])
     grad_joined = cotangent.astype(jnp.float32).reshape(docs * SEGS, SEG, D) * keep_float
-    grad_heads, outer_grads = block_backward(grad_joined[:, 0, :], outer_saved, outer_back)
+    grad_heads, outer_factors, outer_sums = block_backward(grad_joined[:, 0, :], outer_saved, outer_weights, True)
     grad_place = jnp.transpose(jnp.sum(grad_heads.reshape(docs, SEGS, D), axis=0))
     grad_inner_rows = jnp.concatenate(
         [grad_heads.reshape(docs * SEGS, 1, D), grad_joined[:, 1:]], axis=1
     )
     tokens_grad, inner_grads = block_backward(
-        grad_inner_rows.reshape(docs * SLOTS, D), inner_saved, inner_back
-    )
-    grad_list = inner_grads + outer_grads + (grad_place,)
-    owned = ()
-    for bucket_index in range(5):
-        owned = owned + tuple(reduce_bucket(grad_list[5 * bucket_index : 5 * bucket_index + 5]))
-    return (mixed, tokens_grad) + owned
+        grad_inner_rows.reshape(docs * SLOTS, D), inner_saved, inner_weights, False
+    )
+    left_pack = jnp.concatenate(
+        [factor.reshape(factor.shape[0], devices, -1) for factor in outer_factors[0]], axis=2
+    )
+    left_pack = jnp.transpose(left_pack, (1, 0, 2))
+    left_all = lax.all_to_all(left_pack, AXES, split_axis=0, concat_axis=0, tiled=True)
+    left_all = left_all.reshape(-1, left_all.shape[-1])
+    right_all = gather(jnp.concatenate(outer_factors[1], axis=1))
+    left_pieces = split_cols(left_all, (parts, parts, parts, parts * ratio))
+    right_pieces = split_cols(right_all, (3 * D, D, wide, D))
+    outer_big = [cross_rows(left, right) for left, right in zip(left_pieces, right_pieces)]
+    outer_bias = [
+        lax.dynamic_slice_in_dim(
+            jnp.sum(right.astype(jnp.float32), axis=0), here * width, width, axis=0
+        )
+        for right, width in zip(
+            right_pieces, (3 * parts, parts, wide // devices, parts)
+        )
+    ]
+    (
+        grad_attend,
+        grad_attend_bias,
+        grad_merge,
+        grad_merge_bias,
+        grad_gain,
+        grad_shift,
+        grad_expand,
+        grad_expand_bias,
+        grad_reduce,
+        grad_reduce_bias,
+        grad_final_gain,
+        grad_final_shift,
+    ) = inner_grads
+    tall_pack = scatter(
+        jnp.concatenate([grad_expand, refold(grad_reduce)], axis=1).astype(jnp.bfloat16)
+    ).astype(jnp.float32)
+    head_pack = scatter(
+        jnp.concatenate([grad_attend, grad_merge], axis=1).astype(jnp.bfloat16)
+    ).astype(jnp.float32)
+    row_sums = (
+        grad_attend_bias,
+        grad_merge_bias,
+        grad_gain,
+        grad_shift,
+        grad_expand_bias,
+        grad_reduce_bias,
+        grad_final_gain,
+        grad_final_shift,
+    ) + outer_sums + (grad_place,)
+    sums = scatter(
+        jnp.concatenate([entry.reshape(devices, -1) for entry in row_sums], axis=1)
+    ).reshape(-1)
+    sums = split_cols(sums, [entry.size // devices for entry in row_sums])
+    own_expand, own_reduce = split_cols(tall_pack, (wide, ratio * D))
+    own_reduce = jnp.concatenate(jnp.split(own_reduce, ratio, axis=1), axis=0)
+    own_attend, own_merge = split_cols(head_pack, (3 * D, D))
+    return (
+        mixed,
+        tokens_grad,
+        own_attend,
+        sums[0],
+        own_merge,
+        sums[1],
+        sums[2],
+        sums[3],
+        own_expand,
+        sums[4],
+        own_reduce,
+        sums[5],
+        sums[6],
+        sums[7],
+        outer_big[0],
+        outer_bias[0],
+        outer_big[1],
+        outer_bias[1],
+        sums[8],
+        sums[9],
+        outer_big[2],
+        outer_bias[2],
+        outer_big[3],
+        outer_bias[3],
+        sums[10],
+        sums[11],
+        sums[12].reshape(parts, SEGS),
+    )
 
 
 def solution(mesh):

time: 1800 us -> 854 us (0.47)
  waiting for transfers between devices: 1380 us -> 423 us
  local copies, waits for them, and re-layouts: 83.7 us -> 151 us
  blocking collectives: 84 us -> 42.7 us
  matrix products: 182 us -> 157 us
    reduce_scatter x7 -> x1, waiting for transfers between devices: 880 us -> 127 us  [scatter(): return lax.psum_scatter(rows, AXES, scatter_dimension=0, tiled=True)]
    all_gather x8 -> x4, waiting for transfers between devices: 310 us -> 142 us  [gather(): return lax.all_gather(rows, AXES, axis=0, tiled=True)]
    all_gather x1 -> x0, blocking collectives: 40.5 us -> none  [on_device(): lax.all_gather(segment_place, ('dp', 'fsdp'), axis=0, tiled=True)]
    unnamed x19 -> x9, waiting for transfers between devices: 195 us -> 155 us
    reshape x0 -> x21, local copies, waits for them, and re-layouts: none -> 31.2 us  [the longest x2 19.7 us: unfold(): packed.reshape(devices, parts, ratio, D)]
    dot_general x8, matrix products: 47.6 us -> 28.3 us  [cross_rows(): lax.dot_general(left_rows, right_rows, (((0,), (0,)), ((), ())), preferre...]
    unnamed x198 -> x197, local copies, waits for them, and re-layouts: 56.3 us -> 44.1 us
  transfers between devices with their start and end apart: 17 -> 8, of which waited for: 15 -> 6; matrix products, arithmetic and copies ran while one was open for 11% -> 25% of each run, Pallas kernels for 0% -> 0%
where the time goes in v1:
time: 854 us; the launch traced here: 843 us
  waiting for transfers between devices  423 us (50%)
  matrix products  157 us (18%)
  local copies, waits for them, and re-layouts  151 us (18%)
  other arithmetic  48.1 us (6%)
  blocking collectives  42.7 us (5%)
  between operations  16.8 us (2%)
    unnamed x9, waiting for transfers between devices  155 us
    all_gather x4, waiting for transfers between devices, gather(): return lax.all_gather(rows, AXES, axis=0, tiled=True)  142 us
    reduce_scatter x1, waiting for transfers between devices, scatter(): return lax.psum_scatter(rows, AXES, scatter_dimension=0, tiled=True)  127 us
    dot_general x8, matrix products, back_cols(): lax.dot_general(left_rows, right_rows, (((1,), (1,)), ((), ())), preferre...  48.9 us
    unnamed x197, local copies, waits for them, and re-layouts  44.1 us
    unnamed x1, blocking collectives  42.7 us
    dot_general x2, matrix products, block_forward(): jnp.dot(normed, expand, preferred_element_type=jnp.float32) + expand_bias  40.3 us
    dot_general x8, matrix products, cross_rows(): lax.dot_general(left_rows, right_rows, (((0,), (0,)), ((), ())), preferre...  28.3 us
  transfers between devices with their start and end apart: 8, of which 6 were waited for; matrix products, arithmetic and copies ran while one was open for 25% of the time, Pallas kernels for 0%

profile of v1, /device:TPU:0, one launch (start us, length us, event | category | flops | bytes accessed | tf_op | source)
XLA Modules:
  0.0 842.9 jit_solution(10359287667399623437)
XLA Ops:
  21.0 10.8 %concatenate.37 = bf16[816]{0:T(1024)(128)(2,1)S(1)} concatenate(bf16[72]{0:T(256)(128)(2,1)} %param.31, bf16[24]{0:T(256)(128)(2,1)} %param.33, bf16[24]{0:T(256)(128)(2,1)} %param.34, bf16[24]{0:T(256)(128)(2,1)} %param.35, bf16[96]{0:T(256)(128)(2,1)} %param.37, bf16[24]{0:T(256)(128)(2,1)} %param.39, bf16[24]{0:T(256)(128)(2,1)} %param.40, bf16[24]{0:T(256)(128)(2,1)} %param.41, ...), dimensions={0} | concatenate | bytes 3264 | tf_op jit(solution)/shard_map/concatenate | solution.py:274
  32.0 42.7 %all-reduce = bf16[26112]{0:T(1024)(128)(2,1)S(1)} all-reduce(bf16[26112]{0:T(1024)(128)(2,1)S(1)} %dynamic-update-slice), channel_id=2, replica_groups=mesh['dp'=4,'fsdp'=8] {'dp','fsdp'}, use_global_device_ids=true, to_apply=%add | all-reduce | flops 26112 | bytes 104448
  83.8 3.9 copy_multiply_fusion
  88.5 2.6 slice_reduce_fusion.1
  91.1 8.4 %add_convert_fusion.1 = bf16[1024,2304]{1,0:T(8,128)(2,1)} fusion(bf16[1024,768]{1,0:T(8,128)(2,1)} %param.28, bf16[768,2304]{1,0:T(8,128)(2,1)} %all-gather.6.cloned.1.call-done, f32[2304]{0:T(1024)S(1)} %reshape.604), kind=kOutput, calls=%fused_computation.23 | convolution fusion | flops 3628597248 | bytes 9839616 | tf_op jit(solution)/shard_map/dot_general | solution.py:62
  99.6 6.6 copy.160
  106.2 3.6 copy.215
  111.8 2.9 fusion.122
  118.6 45.0 %all-gather.8.cloned.1.call-done = bf16[768,6912]{1,0:T(8,128)(2,1)} async-done(((bf16[24,6912]{1,0:T(8,128)(2,1)}), bf16[768,6912]{1,0:T(8,128)(2,1)}) %all-gather.8.cloned.1.call-update) | async-done | bytes 10616848 | tf_op jit(solution)/shard_map/all_gather | solution.py:205
  163.6 4.9 slice.296
  168.5 9.8 %reshape.569 = bf16[32,24,4,768]{3,2,1,0:T(4,128)(2,1)} reshape(bf16[768,3072]{1,0:T(8,128)(2,1)} %slice.296) | data formatting | bytes 9437184 | tf_op jit(solution)/shard_map/reshape | solution.py:285
  178.3 3.4 copy.166
  181.7 3.9 fusion.123
  186.2 37.1 %multiply_convert_fusion = (bf16[1024,3072]{1,0:T(8,128)(2,1)S(1)}, f32[1024,3072]{1,0:T(8,128)}, f32[1024,3072]{1,0:T(8,128)}) fusion(f32[3072]{0:T(1024)S(1)} %reshape.608, bf16[768,6912]{1,0:T(8,128)(2,1)} %all-gather.8.cloned.1.call-done, f32[1024,768]{1,0:T(8,128)S(1)} %get-tuple-element.207, f32[768]{0:T(1024)S(1)} %reshape.607, ...), kind=kOutput, calls=%fused_computation.6 | convolution fusion | flops 5043388416 | bytes 39348224 | tf_op jit(solution)/shard_map/dot_general | solution.py:85
  223.4 5.4 fusion.124
  231.6 37.4 %all-gather.10.cloned.1.call-done = bf16[768,9216]{1,0:T(8,128)(2,1)} async-done(((bf16[24,9216]{1,0:T(8,128)(2,1)}), bf16[768,9216]{1,0:T(8,128)(2,1)}) %all-gather.10.cloned.1.call-update) | async-done | bytes 14155792 | tf_op jit(solution)/shard_map/all_gather | solution.py:205
  269.0 2.6 fusion.28
  275.3 4.8 slice.313
  280.1 9.9 %reshape.577 = bf16[32,24,4,768]{3,2,1,0:T(4,128)(2,1)} reshape(bf16[768,3072]{1,0:T(8,128)(2,1)} %slice.313) | data formatting | bytes 9437184 | tf_op jit(solution)/shard_map/reshape | solution.py:285
  290.1 3.2 copy.174
  293.5 3.2 multiply_convert_fusion.2
  302.1 4.3 multiply_reduce_fusion.7
  309.5 3.2 fusion.128
  318.1 18.5 %convert_reduce_fusion = (f32[3072]{0:T(1024)S(1)}, bf16[1024,3072]{1,0:T(8,128)(2,1)}) fusion(f32[1024,3072]{1,0:T(8,128)} %get-tuple-element.164, bf16[1024,768]{1,0:T(8,128)(2,1)} %get-tuple-element.148, bf16[3072,768]{1,0:T(8,128)(2,1)} %bitcast.237, f32[1024,3072]{1,0:T(8,128)} %get-tuple-element.208, f32[3072]{0:T(1024)S(1)} %copy-done.73), kind=kOutput, calls=%fused_computation.4 | convolution fusion | flops 4885312512 | bytes 37773312 | tf_op jit(solution)/shard_map/dot_general | solution.py:39
  336.6 10.1 %multiply_reduce_fusion.1 = (f32[768]{0:T(1024)S(1)}, f32[1024]{0:T(1024)S(1)}, f32[768]{0:T(1024)S(1)}, f32[1024,768]{1,0:T(8,128)S(1)}) fusion(f32[1024,768]{1,0:T(8,128)S(1)} %copy-done.9, f32[1024]{0:T(1024)S(1)} %copy-done.65, f32[1024]{0:T(1024)S(1)} %copy-done.51, f32[768]{0:T(1024)S(1)} %copy-done.60, bf16[1024,3072]{1,0:T(8,128)(2,1)} %get-tuple-element.225, ...), kind=kOutput, calls=%fused_computation.62 | convolution fusion | flops 4839699456 | bytes 20472832 | tf_op jit(solution)/shard_map/dot_general | solution.py:39
  351.4 3.8 convolution_convert_fusion.3
  355.2 3.0 copy.183
  360.1 8.0 multiply_reduce_fusion
  368.1 5.0 multiply_convert_fusion.1
  374.5 2.3 multiply_bitcast_fusion
  376.8 2.3 convolution_bitcast_fusion
  379.1 2.5 fusion.46
  381.6 3.1 convert_reduce_fusion.1
  396.1 11.7 %copy.189 = bf16[8,128,3,12,64]{1,0,4,3,2:T(8,128)(2,1)S(1)} copy(bf16[8,128,3,12,64]{1,4,3,0,2:T(8,128)(2,1)} %get-tuple-element.152) | data formatting | bytes 9437184 | tf_op jit(solution)/shard_map/convert_element_type | solution.py:171
  409.9 4.3 fusion.12
  414.2 2.5 pad_maximum_fusion.1
  416.7 6.6 copy.206
  424.8 7.7 convolution_convert_fusion
  432.6 2.3 copy.191
  437.2 6.3 convolution_convert_fusion.1
  443.5 4.0 pad_maximum_fusion
  452.7 3.6 all-to-all-start
  456.3 2.3 pad_maximum_fusion.2
  462.2 5.9 add_add_fusion.4
  468.1 45.4 %all-reduce.4.cloned.1.call-done = f32[32,600]{1,0:T(8,128)} async-done(((f32[32,600]{1,0:T(8,128)}), f32[32,600]{1,0:T(8,128)}) %all-reduce.4.cloned.1.call-update) | async-done | bytes 76816
  519.1 108.7 %reduce-scatter.7.cloned.1.call-done = bf16[24,3072]{1,0:T(8,128)(2,1)} async-done(((bf16[768,3072]{1,0:T(8,128)(2,1)}), bf16[24,3072]{1,0:T(8,128)(2,1)}) %reduce-scatter.7.cloned.1.call-update) | async-done | bytes 147472
  631.9 59.2 %all-gather.12.cloned.1.call-done = bf16[256,6912]{1,0:T(8,128)(2,1)} async-done(((bf16[8,6912]{1,0:T(8,128)(2,1)}), bf16[256,6912]{1,0:T(8,128)(2,1)}) %all-gather.12.cloned.1.call-update) | async-done | bytes 3538960 | tf_op jit(solution)/shard_map/all_gather | solution.py:205
  705.5 126.9 %reduce-scatter.5.cloned.1.call-done = bf16[24,6144]{1,0:T(8,128)(2,1)} async-done(((bf16[768,6144]{1,0:T(8,128)(2,1)}), bf16[24,6144]{1,0:T(8,128)(2,1)}) %reduce-scatter.5.cloned.1.call-update) | async-done | bytes 294928 | tf_op jit(solution)/shard_map/reduce_scatter | solution.py:209
  (355 shorter events, 110.5 us)
Async XLA Ops:
  7.2 74.0 %copy-start.21 = (bf16[1024,768]{1,0:T(8,128)(2,1)S(1)}, bf16[1024,768]{1,0:T(8,128)(2,1)}, u32[]{:S(2)}) copy-start(bf16[1024,768]{1,0:T(8,128)(2,1)} %param.55) | copy-start | bytes 4718596
  7.2 83.9 %all-gather.6.cloned.1.call-start = ((), (), s32[]{:S(2)}) async-start(), calls=%async_computation.3 | async-start | bytes 3649536 | tf_op jit(solution)/shard_map/all_gather | solution.py:205
  7.9 155.6 %all-gather.8.cloned.1.call-start = ((), (), s32[]{:S(2)}) async-start(), calls=%async_computation.4 | async-start | bytes 10948608 | tf_op jit(solution)/shard_map/all_gather | solution.py:205
  13.6 255.4 %all-gather.10.cloned.1.call-start = ((), (), s32[]{:S(2)}) async-start(), calls=%async_computation.5 | async-start | bytes 14598144 | tf_op jit(solution)/shard_map/all_gather | solution.py:205
  20.1 493.5 %all-reduce.4.cloned.1.call-start = ((), (), s32[]{:S(2)}) async-start(), calls=%async_computation.9 | async-start | bytes 163840
  76.0 147.3 %copy-start.59 = (f32[768]{0:T(1024)}, f32[768]{0:T(1024)S(1)}, u32[]{:S(2)}) copy-start(f32[768]{0:T(1024)S(1)} %reshape.606) | copy-start | bytes 9220
  76.1 147.2 %copy-start.75 = (f32[768]{0:T(1024)}, f32[768]{0:T(1024)S(1)}, u32[]{:S(2)}) copy-start(f32[768]{0:T(1024)S(1)} %reshape.607) | copy-start | bytes 9220
  76.3 109.9 %copy-start.72 = (f32[3072]{0:T(1024)}, f32[3072]{0:T(1024)S(1)}, u32[]{:S(2)}) copy-start(f32[3072]{0:T(1024)S(1)} %reshape.608) | copy-start | bytes 36868
  87.7 11.9 %copy-start.5 = (f32[8,128,768]{2,0,1:T(8,128)}, f32[8,128,768]{2,0,1:T(8,128)S(1)}, u32[]{:S(2)}) copy-start(f32[8,128,768]{2,0,1:T(8,128)S(1)} %copy_multiply_fusion) | copy-start | bytes 9437188
  110.1 4.5 copy-start.16
  118.6 63.1 %copy-start.17 = (bf16[8,128,12,64]{1,0,3,2:T(8,128)(2,1)}, bf16[8,128,12,64]{1,0,3,2:T(8,128)(2,1)S(1)}, u32[]{:S(2)}) copy-start(bf16[8,128,12,64]{1,0,3,2:T(8,128)(2,1)S(1)} %copy.165) | copy-start | bytes 4718596
  181.7 41.7 %copy-start.14 = (bf16[32,4,24,768]{3,2,1,0:T(8,128)(2,1)}, bf16[32,4,24,768]{3,2,1,0:T(8,128)(2,1)S(1)}, u32[]{:S(2)}) copy-start(bf16[32,4,24,768]{3,2,1,0:T(8,128)(2,1)S(1)} %copy.166) | copy-start | bytes 14155780
  185.6 37.7 %copy-start.8 = (f32[1024,768]{1,0:T(8,128)}, f32[1024,768]{1,0:T(8,128)S(1)}, u32[]{:S(2)}) copy-start(f32[1024,768]{1,0:T(8,128)S(1)} %get-tuple-element.207) | copy-start | bytes 9437188
  185.6 37.7 %copy-start.50 = (f32[1024]{0:T(1024)}, f32[1024]{0:T(1024)S(1)}, u32[]{:S(2)}) copy-start(f32[1024]{0:T(1024)S(1)} %broadcast_multiply_fusion.1) | copy-start | bytes 12292
  186.1 37.1 %copy-start.52 = (f32[1024]{0:T(1024)}, f32[1024]{0:T(1024)S(1)}, u32[]{:S(2)}) copy-start(f32[1024]{0:T(1024)S(1)} %multiply_reduce_fusion.5) | copy-start | bytes 12292
  186.2 37.2 %copy-start.64 = (f32[1024]{0:T(1024)}, f32[1024]{0:T(1024)S(1)}, u32[]{:S(2)}) copy-start(f32[1024]{0:T(1024)S(1)} %fusion.104) | copy-start | bytes 12292
  223.3 5.5 copy-start.80
  229.3 42.3 %copy-start.54 = (f32[1024]{0:T(1024)}, f32[1024]{0:T(1024)S(1)}, u32[]{:S(2)}) copy-start(f32[1024]{0:T(1024)S(1)} %multiply_reduce_fusion.4) | copy-start | bytes 12292
  229.9 43.5 %copy-start.63 = (f32[768]{0:T(1024)S(1)}, f32[768]{0:T(1024)}, u32[]{:S(2)}) copy-start(f32[768]{0:T(1024)} %reshape.613) | copy-start | bytes 9220
  271.7 8.4 %copy-start.57 = (bf16[1,8,1,12,64]{4,3,2,1,0:T(8,128)(2,1)}, bf16[1,8,1,12,64]{4,3,2,1,0:T(8,128)(2,1)S(1)}, u32[]{:S(2)}) copy-start(bf16[1,8,1,12,64]{4,3,2,1,0:T(8,128)(2,1)S(1)} %get-tuple-element.176) | copy-start | bytes 36868
  293.4 4.1 copy-start.36
  296.6 4.2 copy-start.34
  300.8 5.7 copy-start.40
  302.1 4.6 copy-start.26
  302.1 6.5 copy-start.49
  302.1 6.5 copy-start.58
  318.1 18.5 %copy-start.9 = (f32[1024,768]{1,0:T(8,128)S(1)}, f32[1024,768]{1,0:T(8,128)}, u32[]{:S(2)}) copy-start(f32[1024,768]{1,0:T(8,128)} %copy-done.8) | copy-start | bytes 9437188
  318.1 18.5 %copy-start.51 = (f32[1024]{0:T(1024)S(1)}, f32[1024]{0:T(1024)}, u32[]{:S(2)}) copy-start(f32[1024]{0:T(1024)} %copy-done.50) | copy-start | bytes 12292
  318.1 18.5 %copy-start.60 = (f32[768]{0:T(1024)S(1)}, f32[768]{0:T(1024)}, u32[]{:S(2)}) copy-start(f32[768]{0:T(1024)} %copy-done.59) | copy-start | bytes 9220
  318.1 18.5 %copy-start.65 = (f32[1024]{0:T(1024)S(1)}, f32[1024]{0:T(1024)}, u32[]{:S(2)}) copy-start(f32[1024]{0:T(1024)} %copy-done.64) | copy-start | bytes 12292
  336.6 10.1 %copy-start.53 = (f32[1024]{0:T(1024)S(1)}, f32[1024]{0:T(1024)}, u32[]{:S(2)}) copy-start(f32[1024]{0:T(1024)} %copy-done.52) | copy-start | bytes 12292
  355.2 4.9 copy-start.44
  360.1 8.0 copy-start.19
  360.1 8.0 slice-start
  360.1 8.0 slice-start.1
  368.1 5.0 copy-start.3
  381.6 7.2 copy-start.71
  395.8 232.0 %reduce-scatter.7.cloned.1.call-start = ((), (), s32[]{:S(2)}) async-start(), calls=%async_computation.8 | async-start | bytes 4866048
  396.0 13.8 %copy-start.79 = (bf16[1024,768]{1,0:T(8,128)(2,1)S(1)}, bf16[1024,768]{1,0:T(8,128)(2,1)}, u32[]{:S(2)}) copy-start(bf16[1024,768]{1,0:T(8,128)(2,1)} %param.28) | copy-start | bytes 4718596
  409.9 4.3 copy-start.24
  423.3 267.8 %all-gather.12.cloned.1.call-start = ((), (), s32[]{:S(2)}) async-start(), calls=%async_computation.7 | async-start | bytes 3649536 | tf_op jit(solution)/shard_map/all_gather | solution.py:205
  424.8 407.6 %reduce-scatter.5.cloned.1.call-start = ((), (), s32[]{:S(2)}) async-start(), calls=%async_computation.6 | async-start | bytes 9732096 | tf_op jit(solution)/shard_map/reduce_scatter | solution.py:209
  447.5 4.1 copy-start.32
  449.4 6.9 copy-start.42
  451.3 8.7 %slice-start.2 = ((s8[4718592]{0:T(1024)(128)(4,1)}), s8[524288]{0:T(1024)(128)(4,1)S(1)}, s32[]{:S(2)}) async-start(s8[4718592]{0:T(1024)(128)(4,1)} %bitcast.239), calls=%async_computation.12 | async-start | bytes 1048576
  452.7 245.3 %all-to-all-start = ((bf16[32,8,168]{2,1,0:T(8,128)(2,1)}), bf16[32,8,168]{2,1,0:T(8,128)(2,1)}, u32[]{:S(2)}, u32[]{:S(2)}) async-start(bf16[32,8,168]{2,1,0:T(8,128)(2,1)} %maximum_bitcast_fusion), calls=%async_computation.1 | async-start | bytes 262144 | tf_op jit(solution)/shard_map/all_to_all | solution.py:348
  456.3 4.8 copy-start.77
  691.1 6.9 copy-start.4
  (47 other events, 98.1 us)
Sparse Core Ops, SparseCore 0:
  11.1 63.2 all-gather.5
  77.3 86.2 all-gather.7
  167.2 101.7 all-gather.9
  395.9 117.5 all-reduce.3
  518.9 108.9 reduce-scatter.6
  631.8 59.3 all-gather.11
  698.0 134.2 reduce-scatter.4

commit v2 on v1

--- a/solution.py
+++ b/solution.py
@@ -3,6 +3,8 @@
 import jax
 import jax.numpy as jnp
 from jax import lax
+from jax.experimental import pallas as pl
+from jax.experimental.pallas import tpu as pltpu
 from jax.sharding import PartitionSpec as P
 
 D = 768
@@ -215,6 +217,227 @@
         pieces.append(packed[..., start : start + width])
         start += width
     return pieces
+
+
+def everyone(rows):
+    devices = lax.axis_size(AXES)
+    padded = jnp.pad(rows, ((0, -rows.shape[0] % 16), (0, 0)))[None]
+    sent = jnp.broadcast_to(padded, (devices,) + padded.shape[1:])
+    return lax.all_to_all(sent, AXES, split_axis=0, concat_axis=0, tiled=True)
+
+
+def sum_rows(rows):
+    devices, size = rows.shape
+    padded = jnp.pad(rows, ((0, 0), (0, -size % 1024))).reshape(devices, -1, 128)
+    got = lax.all_to_all(padded, AXES, split_axis=0, concat_axis=0, tiled=True)
+    return jnp.sum(got, axis=0).reshape(-1)[:size]
+
+
+def hop(array, turn):
+    return lax.ppermute(array, AXES, [(place, turn(place)) for place in range(32)])
+
+
+def over_x(array):
+    return hop(array, lambda place: place ^ 8)
+
+
+def over_y(array):
+    return hop(array, lambda place: place ^ 16)
+
+
+def over_core(array):
+    return hop(array, lambda place: place ^ 1)
+
+
+def over_z(array, step):
+    return hop(array, lambda place: (place & ~6) | ((((place >> 1) + step) & 3) << 1))
+
+
+def place_here():
+    chip = lax.axis_index("fsdp")
+    return lax.axis_index("dp"), chip // 2, chip % 2
+
+
+def half_cols(array, core):
+    width = array.shape[-1] // 2
+    return lax.dynamic_slice_in_dim(array, core * width, width, axis=array.ndim - 1)
+
+
+def fold_rows(array, rows):
+    return jnp.concatenate(jnp.split(array, array.shape[0] // rows, axis=0), axis=1)
+
+
+def unfold_cols(array, width):
+    return jnp.concatenate(jnp.split(array, array.shape[1] // width, axis=1), axis=0)
+
+
+def both_cores(mine, other, core, axis):
+    return jnp.concatenate(
+        [jnp.where(core == 0, mine, other), jnp.where(core == 0, other, mine)], axis=axis
+    )
+
+
+def assemble_kernel(heights, widths, place_ref, *refs):
+    pieces, outs, sems = refs[:10], refs[10:-1], refs[-1]
+    plane, depth, core = place_ref[0], place_ref[1], place_ref[2]
+    slots = ((0, 0, 4), (1, 0, 4), (2, 0, 4), (3, 0, 2), (3, 2, 2))
+    copies = []
+    for side in range(2):
+        column = core if side == 0 else 1 - core
+        for number, (turn, first, count) in enumerate(slots):
+            piece = pieces[5 * side + number]
+            for slot in range(count):
+                chip = (plane ^ turn) * 4 + ((depth + 4 - first - slot) & 3)
+                start = 0
+                for out, height, width in zip(outs, heights, widths):
+                    for group in range(height // 48):
+                        row = pl.multiple_of(chip * height + 48 * group, 48)
+                        lane = pl.multiple_of(column * width, 128)
+                        copies.append(
+                            pltpu.make_async_copy(
+                                piece.at[slot, :, pl.ds(start, width)],
+                                out.at[pl.ds(row, 48), pl.ds(lane, width)],
+                                sems.at[len(copies)],
+                            )
+                        )
+                        start += width
+    for copy in copies:
+        copy.start()
+    for copy in copies:
+        copy.wait()
+
+
+def gather_links(shards):
+    plane, depth, core = place_here()
+    rows = min(shard.shape[0] for shard in shards)
+    mine = jnp.concatenate([fold_rows(half_cols(shard, core), rows) for shard in shards], axis=1)
+    sent = jnp.concatenate(
+        [fold_rows(half_cols(shard, 1 - core), rows) for shard in shards], axis=1
+    )
+    other = over_core(sent)
+    widths = [shard.shape[1] // 2 for shard in shards]
+    heights = [2 * shard.shape[0] for shard in shards]
+    slab, start = [], 0
+    for width, height in zip(widths, heights):
+        span = width * (height // (2 * rows))
+        pair = [unfold_cols(part[:, start : start + span], width) for part in (mine, other)]
+        slab.append(fold_rows(both_cores(pair[0], pair[1], core, 0), 2 * rows))
+        start += span
+    slab = jnp.concatenate(slab, axis=1)
+    line = jnp.stack([slab] + [over_z(slab, step) for step in (1, 2, 3)])
+    line_x, line_y = over_x(line), over_y(line)
+    pieces = [line, line_x, line_y, over_y(line_x[:2]), over_x(line_y[2:])]
+    pieces = pieces + [over_core(piece) for piece in pieces]
+    count = 32 * sum(height // 48 for height in heights)
+    place = jnp.stack([plane, depth, core]).astype(jnp.int32)
+    return pl.pallas_call(
+        partial(assemble_kernel, heights, widths),
+        out_shape=[
+            jax.ShapeDtypeStruct((16 * height, 2 * width), jnp.bfloat16)
+            for height, width in zip(heights, widths)
+        ],
+        in_specs=[pl.BlockSpec(memory_space=pltpu.SMEM)]
+        + [pl.BlockSpec(memory_space=pl.ANY)] * 10,
+        out_specs=[pl.BlockSpec(memory_space=pltpu.VMEM)] * len(shards),
+        scratch_shapes=[pltpu.SemaphoreType.DMA((count,))],
+        compiler_params=pltpu.CompilerParams(vmem_limit_bytes=32 << 20),
+        name="assemble",
+    )(place, *pieces)
+
+
+def scatter_links(grads):
+    plane, depth, core = place_here()
+    low = jnp.bfloat16
+
+    def packed(side):
+        return jnp.concatenate(
+            [
+                jnp.transpose(
+                    half_cols(grad, side).reshape(16, grad.shape[0] // 768, 48, -1), (0, 2, 1, 3)
+                ).reshape(16, 48, -1)
+                for grad in grads
+            ],
+            axis=2,
+        )
+
+    kept = (packed(core) + over_core(packed(1 - core))).reshape(4, 4, 48, -1)
+    here, next_x, next_y, across = [
+        lax.dynamic_index_in_dim(kept, plane ^ turn, axis=0, keepdims=False)
+        for turn in range(4)
+    ]
+    from_y, from_x = over_y(across[:2]), over_x(across[2:])
+    next_x = jnp.concatenate([next_x[:2] + from_y, next_x[2:]], axis=0)
+    next_y = jnp.concatenate([next_y[:2], next_y[2:] + from_x], axis=0)
+    came_x, came_y = over_x(next_x), over_y(next_y)
+    here = (
+        here.astype(jnp.float32) + came_x.astype(jnp.float32) + came_y.astype(jnp.float32)
+    ).astype(low)
+    slabs = [
+        lax.dynamic_index_in_dim(here, (depth + step) & 3, axis=0, keepdims=False)
+        for step in range(4)
+    ]
+    total = slabs[0].astype(jnp.float32)
+    for step in (1, 2, 3):
+        total = total + over_z(slabs[step], step).astype(jnp.float32)
+    mine, sent, start = [], [], 0
+    for grad in grads:
+        width = grad.shape[1] // 2
+        groups = grad.shape[0] // 768
+        rows = unfold_cols(total[:, start : start + groups * width], width)
+        start += groups * width
+        mine.append(fold_rows(lax.dynamic_slice_in_dim(rows, core * 24 * groups, 24 * groups), 24))
+        sent.append(
+            fold_rows(lax.dynamic_slice_in_dim(rows, (1 - core) * 24 * groups, 24 * groups), 24)
+        )
+    other = over_core(jnp.concatenate(sent, axis=1))
+    owned, start = [], 0
+    for grad, part in zip(grads, mine):
+        width = grad.shape[1] // 2
+        pair = [unfold_cols(side, width) for side in (part, other[:, start : start + part.shape[1]])]
+        owned.append(both_cores(pair[0], pair[1], core, 1))
+        start += part.shape[1]
+    return owned
+
+
+def unfold(packed, parts, ratio):
+    width = packed.shape[1] // ratio
+    return jnp.stack(
+        [
+            packed[:, width * group : width * (group + 1)].reshape(-1, parts, width)
+            for group in range(ratio)
+        ],
+        axis=1,
+    ).reshape(-1, width)
+
+
+def gather_flat(shards):
+    parts = min(shard.shape[0] for shard in shards)
+    pieces = split_cols(
+        gather(jnp.concatenate([fold_rows(shard, parts) for shard in shards], axis=1)),
+        [shard.size // parts for shard in shards],
+    )
+    return [
+        unfold(piece, parts, shard.shape[0] // parts) if shard.shape[0] > parts else piece
+        for piece, shard in zip(pieces, shards)
+    ]
+
+
+def scatter_flat(grads):
+    devices = lax.axis_size(AXES)
+    parts = min(grad.shape[0] for grad in grads) // devices
+    packed = jnp.concatenate(
+        [
+            jnp.transpose(grad.reshape(devices, -1, parts, grad.shape[1]), (0, 2, 1, 3)).reshape(
+                devices * parts, -1
+            )
+            for grad in grads
+        ],
+        axis=1,
+    )
+    owned = split_cols(
+        scatter(packed).astype(jnp.float32), [grad.size // (devices * parts) for grad in grads]
+    )
+    return [unfold_cols(piece, grad.shape[1]) for piece, grad in zip(owned, grads)]
 
 
 def on_device(
@@ -271,46 +494,35 @@
         segment_place.reshape(parts * SEGS),
     )
     small_widths = [part.shape[0] for part in small_parts]
-    small = gather(jnp.concatenate(small_parts)[None])
-    small = [piece.reshape(-1) for piece in split_cols(small, small_widths)]
+    spread = everyone(
+        jnp.concatenate(
+            [jnp.pad(part, (0, -part.shape[0] % 128)).reshape(-1, 128) for part in small_parts]
+        )
+    )
+    small, start = [], 0
+    for width in small_widths:
+        rows = -(-width // 128)
+        piece = spread[:, start : start + rows].reshape(devices, -1)[:, :width]
+        small.append(piece.reshape(-1))
+        start += rows
     place_table = small[16].reshape(D, SEGS).astype(jnp.float32)
-
-    def rest_pack(merge, expand, reduce_matrix):
-        return jnp.concatenate([merge, expand, fold(reduce_matrix)], axis=1)
-
-    def fold(reduce_rows):
-        return jnp.concatenate(jnp.split(reduce_rows, ratio, axis=0), axis=1)
-
-    def unfold(packed):
-        return jnp.transpose(packed.reshape(devices, parts, ratio, D), (0, 2, 1, 3)).reshape(
-            devices * parts * ratio, D
-        )
-
-    def refold(grad):
-        return jnp.transpose(grad.reshape(devices, ratio, parts, D), (0, 2, 1, 3)).reshape(
-            D, ratio * D
-        )
-
+    linked = lax.axis_size("dp") == 4 and lax.axis_size("fsdp") == 8
+    gather_inner = gather_links if linked else gather_flat
+    scatter_inner = scatter_links if linked else scatter_flat
     wide = inner_expand.shape[1]
-    inner_attend_full = gather(inner_attend)
-    merge_full, expand_full, reduce_full = split_cols(
-        gather(rest_pack(inner_merge, inner_expand, inner_reduce)), (D, wide, ratio * D)
-    )
+    (attend_full,) = gather_inner([inner_attend])
+    merge_full, expand_full, reduce_full = gather_inner([inner_merge, inner_expand, inner_reduce])
     inner_weights = prepare(
-        (inner_attend_full, small[0], merge_full, small[1], small[2], small[3], expand_full)
-        + (small[4], unfold(reduce_full), small[5], small[6], small[7])
-    )
-    attend_full, merge_full, expand_full, reduce_full = split_cols(
-        gather(
-            jnp.concatenate(
-                [outer_attend, rest_pack(outer_merge, outer_expand, outer_reduce)], axis=1
-            )
-        ),
-        (3 * D, D, wide, ratio * D),
-    )
+        (attend_full, small[0], merge_full, small[1], small[2], small[3], expand_full)
+        + (small[4], reduce_full, small[5], small[6], small[7])
+    )
+    outer_shards = lax.optimization_barrier(
+        (attend_full, outer_attend, outer_merge, outer_expand, outer_reduce)
+    )
+    attend_full, merge_full, expand_full, reduce_full = gather_flat(outer_shards[1:])
     outer_weights = prepare(
         (attend_full, small[8], merge_full, small[9], small[10], small[11], expand_full)
-        + (small[12], unfold(reduce_full), small[13], small[14], small[15])
+        + (small[12], reduce_full, small[13], small[14], small[15])
     )
     docs = counts.shape[0]
     keep_mask = jnp.arange(SLOTS)[None, :] < counts[:, None]
@@ -373,12 +585,12 @@
         grad_final_gain,
         grad_final_shift,
     ) = inner_grads
-    tall_pack = scatter(
-        jnp.concatenate([grad_expand, refold(grad_reduce)], axis=1).astype(jnp.bfloat16)
-    ).astype(jnp.float32)
-    head_pack = scatter(
-        jnp.concatenate([grad_attend, grad_merge], axis=1).astype(jnp.bfloat16)
-    ).astype(jnp.float32)
+    own_expand, own_reduce = scatter_inner(
+        [grad_expand.astype(jnp.bfloat16), grad_reduce.astype(jnp.bfloat16)]
+    )
+    own_attend, own_merge = scatter_inner(
+        [grad_attend.astype(jnp.bfloat16), grad_merge.astype(jnp.bfloat16)]
+    )
     row_sums = (
         grad_attend_bias,
         grad_merge_bias,
@@ -389,13 +601,8 @@
         grad_final_gain,
         grad_final_shift,
     ) + outer_sums + (grad_place,)
-    sums = scatter(
-        jnp.concatenate([entry.reshape(devices, -1) for entry in row_sums], axis=1)
-    ).reshape(-1)
+    sums = sum_rows(jnp.concatenate([entry.reshape(devices, -1) for entry in row_sums], axis=1))
     sums = split_cols(sums, [entry.size // devices for entry in row_sums])
-    own_expand, own_reduce = split_cols(tall_pack, (wide, ratio * D))
-    own_reduce = jnp.concatenate(jnp.split(own_reduce, ratio, axis=1), axis=0)
-    own_attend, own_merge = split_cols(head_pack, (3 * D, D))
     return (
         mixed,
         tokens_grad,

time: 854 us -> 552 us (0.65)
  waiting for transfers between devices: 423 us -> 167 us
  local copies, waits for them, and re-layouts: 151 us -> 77.1 us
  starting transfers between devices: 4.01 us -> 68 us
  blocking collectives: 42.7 us -> 0 us
  other arithmetic: 48.1 us -> 60.2 us
  matrix products: 157 us -> 145 us
    ppermute x0 -> x44, waiting for transfers between devices: none -> 167 us  [hop(): lax.ppermute(array, AXES, [(place, turn(place)) for place in range(32)])]
    unnamed x9 -> x2, waiting for transfers between devices: 155 us -> 0.03 us
    all_gather x4 -> x2, waiting for transfers between devices: 142 us -> 0.02 us  [gather(): return lax.all_gather(rows, AXES, axis=0, tiled=True)]
    reduce_scatter x1 -> x0, waiting for transfers between devices: 127 us -> none  [scatter(): return lax.psum_scatter(rows, AXES, scatter_dimension=0, tiled=True)]
    ppermute x0 -> x44, starting transfers between devices: none -> 44.9 us  [hop(): lax.ppermute(array, AXES, [(place, turn(place)) for place in range(32)])]
    unnamed x1 -> x0, blocking collectives: 42.7 us -> none
    unnamed x197 -> x223, local copies, waits for them, and re-layouts: 44.1 us -> 23.3 us
    all_to_all x0 -> x2, starting transfers between devices: none -> 19.3 us  [the longest x1 14.9 us: sum_rows(): got = lax.all_to_all(padded, AXES, split_axis=0, concat_axis=0, tiled=True)]
  transfers between devices with their start and end apart: 8 -> 49, of which waited for: 6 -> 22; matrix products, arithmetic and copies ran while one was open for 25% -> 28% of each run, Pallas kernels for 0% -> 1%
where the time goes in v2:
time: 552 us; the launch traced here: 542 us
  waiting for transfers between devices  167 us (30%)
  matrix products  145 us (26%)
  local copies, waits for them, and re-layouts  77.1 us (14%)
  starting transfers between devices  68 us (12%)
  other arithmetic  60.2 us (11%)
  between operations  17.3 us (3%)
  Pallas kernels  7.18 us (1%)
    ppermute x44, waiting for transfers between devices, hop(): lax.ppermute(array, AXES, [(place, turn(place)) for place in range(32)])  167 us
    ppermute x44, starting transfers between devices, hop(): lax.ppermute(array, AXES, [(place, turn(place)) for place in range(32)])  44.9 us
    dot_general x8, matrix products, back_cols(): lax.dot_general(left_rows, right_rows, (((1,), (1,)), ((), ())), preferre...  40 us
    dot_general x2, matrix products, block_forward(): jnp.dot(normed, expand, preferred_element_type=jnp.float32) + expand_bias  36.2 us
    dot_general x8, matrix products, cross_rows(): lax.dot_general(left_rows, right_rows, (((0,), (0,)), ((), ())), preferre...  32.3 us
    unnamed x223, local copies, waits for them, and re-layouts  23.3 us
    all_to_all x1, starting transfers between devices, sum_rows(): got = lax.all_to_all(padded, AXES, split_axis=0, concat_axis=0, tiled=True)  14.9 us
  transfers between devices with their start and end apart: 49, of which 22 were waited for; matrix products, arithmetic and copies ran while one was open for 28% of the time, Pallas kernels for 1%

profile of v2, /device:TPU:0, one launch (start us, length us, event | category | flops | bytes accessed | tf_op | source)
XLA Modules:
  0.0 541.7 jit_solution(8364985224743648351)
XLA Ops:
  10.3 3.0 collective-permute-start.1
  13.3 2.6 collective-permute-start.2
  19.2 4.3 collective-permute-done.2
  26.7 9.0 %collective-permute-done.4.refs_1_ = bf16[4,48,1152]{2,1,0:T(8,128)(2,1)S(1)} collective-permute-done((bf16[4,48,1152]{2,1,0:T(8,128)(2,1)S(1)}, bf16[4,48,1152]{2,1,0:T(8,128)(2,1)S(1)}, u32[]{:S(2)}, u32[]{:S(2)}) %collective-permute-start.4) | collective-permute-done | bytes 442400 | tf_op jit(solution)/shard_map/ppermute | solution.py:237
  39.4 2.8 collective-permute-done.6.refs_3_
  55.3 4.4 all-to-all-start
  81.0 2.4 collective-permute-start.15
  85.0 2.6 slice_reduce_fusion.1
  88.8 8.7 %collective-permute-done.14 = bf16[48,3456]{1,0:T(8,128)(2,1)} collective-permute-done((bf16[48,3456]{1,0:T(8,128)(2,1)}, bf16[48,3456]{1,0:T(8,128)(2,1)}, u32[]{:S(2)}, u32[]{:S(2)}) %collective-permute-start.14) | collective-permute-done | bytes 331808 | tf_op jit(solution)/shard_map/ppermute | solution.py:237
  97.5 24.2 %collective-permute-done.15 = bf16[48,3456]{1,0:T(8,128)(2,1)} collective-permute-done((bf16[48,3456]{1,0:T(8,128)(2,1)}, bf16[48,3456]{1,0:T(8,128)(2,1)}, u32[]{:S(2)}, u32[]{:S(2)}) %collective-permute-start.15) | collective-permute-done | bytes 331808 | tf_op jit(solution)/shard_map/ppermute | solution.py:237
  129.0 7.1 %fusion.32 = bf16[288,8,8,128]{3,1,2,0:T(8,128)(2,1)S(1)} fusion(f32[2304]{0:T(1024)S(1)} %reshape.755, bf16[768,2304]{1,0:T(8,128)(2,1)} %copy-done, bf16[1024,768]{1,0:T(8,128)(2,1)} %param.28), kind=kOutput, calls=%fused_computation.87 | convolution fusion | flops 3628597248 | bytes 9839616 | tf_op jit(solution)/shard_map/dot_general | solution.py:64
  137.8 37.0 %collective-permute-done.17.refs_1_ = bf16[4,48,3456]{2,1,0:T(8,128)(2,1)S(1)} collective-permute-done((bf16[4,48,3456]{2,1,0:T(8,128)(2,1)S(1)}, bf16[4,48,3456]{2,1,0:T(8,128)(2,1)S(1)}, u32[]{:S(2)}, u32[]{:S(2)}) %collective-permute-start.17) | collective-permute-done | bytes 1327136 | tf_op jit(solution)/shard_map/ppermute | solution.py:237
  176.3 3.0 collective-permute-done.18.refs_2_
  182.2 2.9 fusion.130
  185.1 9.8 %collective-permute-done.19.refs_3_ = bf16[2,48,3456]{2,1,0:T(8,128)(2,1)S(1)} collective-permute-done((bf16[2,48,3456]{2,1,0:T(8,128)(2,1)S(1)}, bf16[2,48,3456]{2,1,0:T(8,128)(2,1)S(1)}, u32[]{:S(2)}, u32[]{:S(2)}) %collective-permute-start.19) | collective-permute-done | bytes 663584 | tf_op jit(solution)/shard_map/ppermute | solution.py:237
  198.9 5.3 assemble.3
  206.8 35.4 %multiply_convert_fusion = (bf16[1024,3072]{1,0:T(8,128)(2,1)S(1)}, f32[1024,3072]{1,0:T(8,128)}, f32[1024,3072]{1,0:T(8,128)}) fusion(f32[3072]{0:T(1024)S(1)} %reshape.759, bf16[768,3072]{1,0:T(8,128)(2,1)S(1)} %get-tuple-element.35, f32[1024,768]{1,0:T(8,128)S(1)} %get-tuple-element.252, f32[768]{0:T(1024)S(1)} %reshape.758, f32[768]{0:T(1024)S(1)} %reshape.757, ...), kind=kOutput, calls=%fused_computation.6 | convolution fusion | flops 5043388416 | bytes 39348224 | tf_op jit(solution)/shard_map/dot_general | solution.py:87
  242.2 5.4 fusion.132
  251.4 2.6 fusion.21
  256.6 2.8 fusion.122
  260.2 2.8 copy-done.6
  274.6 3.8 fusion.136
  284.6 6.9 %convolution_convert_fusion = bf16[3072,768]{1,0:T(8,128)(2,1)} fusion(bf16[1024,3072]{1,0:T(8,128)(2,1)S(1)} %bitcast.450, bf16[1024,768]{1,0:T(8,128)(2,1)S(1)} %get-tuple-element.135), kind=kOutput, calls=%fused_computation.27 | convolution fusion | flops 4834197504 | bytes 12582912 | tf_op jit(solution)/shard_map/dot_general | solution.py:35
  291.6 17.5 %convert_reduce_fusion = (f32[3072]{0:T(1024)}, bf16[1024,3072]{1,0:T(8,128)(2,1)}) fusion(f32[1024,3072]{1,0:T(8,128)} %get-tuple-element.151, bf16[1024,768]{1,0:T(8,128)(2,1)S(1)} %get-tuple-element.135, bf16[3072,768]{1,0:T(8,128)(2,1)} %copy-done.3, f32[1024,3072]{1,0:T(8,128)} %get-tuple-element.253, f32[3072]{0:T(1024)S(1)} %copy-done.65), kind=kOutput, calls=%fused_computation.4 | convolution fusion | flops 4885312512 | bytes 37773312 | tf_op jit(solution)/shard_map/dot_general | solution.py:41
  309.1 11.1 %convolution_convert_fusion.1 = bf16[768,3072]{1,0:T(8,128)(2,1)} fusion(bf16[1024,3072]{1,0:T(8,128)(2,1)} %get-tuple-element.270, f32[1024,768]{1,0:T(8,128)} %copy-done.14, f32[768]{0:T(1024)S(1)} %copy-done.68, f32[768]{0:T(1024)S(1)} %copy-done.55, f32[1024]{0:T(1024)S(1)} %copy-done.59, f32[1024]{0:T(1024)S(1)} %broadcast_multiply_fusion.1), kind=kOutput, calls=%fused_computation.28 | convolution fusion | flops 4838129664 | bytes 14170112 | tf_op jit(solution)/shard_map/dot_general | solution.py:35
  320.3 6.4 %multiply_reduce_fusion.1 = (f32[768]{0:T(1024)}, f32[1024]{0:T(1024)S(1)}, f32[768]{0:T(1024)}, f32[1024,768]{1,0:T(8,128)S(1)}) fusion(f32[1024,768]{1,0:T(8,128)S(1)} %copy-done.15, f32[1024]{0:T(1024)S(1)} %copy-done.59, f32[1024]{0:T(1024)S(1)} %broadcast_multiply_fusion.1, f32[768]{0:T(1024)S(1)} %copy-done.55, bf16[1024,3072]{1,0:T(8,128)(2,1)S(1)} %copy-done.77, ...), kind=kOutput, calls=%fused_computation.58 | convolution fusion | flops 4839699456 | bytes 20472832 | tf_op jit(solution)/shard_map/dot_general | solution.py:41
  330.3 2.6 convolution_convert_fusion.3
  332.8 3.0 copy.186
  337.8 7.5 %multiply_reduce_fusion = (f32[8,12,128]{2,1,0:T(8,128)S(1)}, f32[8,12,128,128]{2,3,1,0:T(8,128)}) fusion(f32[8,12,128,128]{2,3,1,0:T(8,128)} %copy-done.23, f32[8,12,128]{2,1,0:T(8,128)S(1)} %copy-done.44, bf16[8,128,1,12,64]{1,0,4,3,2:T(8,128)(2,1)S(1)} %copy-done.26, bf16[8,128,12,64]{1,0,3,2:T(8,128)(2,1)S(1)} %bitcast.416), kind=kOutput, calls=%fused_computation.24 | convolution fusion | flops 206032896 | bytes 15826944 | tf_op jit(solution)/shard_map/gqhe,gkhe->ghqk/dot_general | solution.py:159
  345.3 5.0 multiply_convert_fusion.1
  354.0 2.3 convolution_bitcast_fusion
  356.3 2.4 fusion.40
  358.7 2.3 convert_reduce_fusion.1
  361.0 9.2 %copy.192 = bf16[8,128,3,12,64]{1,0,4,3,2:T(8,128)(2,1)S(1)} copy(bf16[8,128,3,12,64]{1,4,3,0,2:T(8,128)(2,1)S(1)} %get-tuple-element.139) | data formatting | bytes 9437184 | tf_op jit(solution)/shard_map/convert_element_type | solution.py:173
  370.2 4.4 convolution_convert_fusion.2
  382.0 2.8 pad_maximum_fusion.1
  385.6 5.8 %add_add_fusion.4 = f32[1024,768]{1,0:T(8,128)} fusion(f32[1024,768]{1,0:T(8,128)S(1)} %get-tuple-element.141, bf16[768,2304]{1,0:T(8,128)(2,1)S(1)} %copy-done.1, bf16[288,8,8,128]{3,2,1,0:T(8,128)(2,1)S(1)} %bitcast.411, f32[1024]{0:T(1024)S(1)} %negate_multiply_fusion.2), kind=kOutput, calls=%fused_computation.77 | convolution fusion | flops 3625451520 | bytes 14553088 | tf_op jit(solution)/shard_map/dot_general | solution.py:41
  405.6 14.9 %all-to-all-start.1 = ((f32[32,8,128]{2,1,0:T(8,128)}), f32[32,8,128]{2,1,0:T(8,128)S(1)}, u32[]{:S(2)}, u32[]{:S(2)}) async-start(f32[32,8,128]{2,1,0:T(8,128)} %bitcast.171), calls=%async_computation.1 | async-start | bytes 262144 | tf_op jit(solution)/shard_map/all_to_all | solution.py:232
  432.3 3.7 all-to-all-start.2
  437.9 4.9 collective-permute-done.28
  446.4 2.4 collective-permute-start.32
  450.5 4.1 maximum_add_fusion
  459.2 15.1 %collective-permute-done.36 = bf16[2,48,3072]{2,1,0:T(8,128)(2,1)S(1)} collective-permute-done((bf16[2,48,3072]{2,1,0:T(8,128)(2,1)S(1)}, bf16[2,48,3072]{2,1,0:T(8,128)(2,1)S(1)}, u32[]{:S(2)}, u32[]{:S(2)}) %collective-permute-start.36) | collective-permute-done | bytes 589856 | tf_op jit(solution)/shard_map/ppermute | solution.py:237
  479.6 21.5 %collective-permute-done.37 = bf16[4,48,3072]{2,1,0:T(8,128)(2,1)S(1)} collective-permute-done((bf16[4,48,3072]{2,1,0:T(8,128)(2,1)S(1)}, bf16[4,48,3072]{2,1,0:T(8,128)(2,1)S(1)}, u32[]{:S(2)}, u32[]{:S(2)}) %collective-permute-start.37) | collective-permute-done | bytes 1179680 | tf_op jit(solution)/shard_map/ppermute | solution.py:237
  502.8 2.9 collective-permute-start.42
  506.3 7.3 %collective-permute-done.40 = bf16[48,3072]{1,0:T(8,128)(2,1)S(1)} collective-permute-done((bf16[48,3072]{1,0:T(8,128)(2,1)S(1)}, bf16[48,3072]{1,0:T(8,128)(2,1)S(1)}, u32[]{:S(2)}, u32[]{:S(2)}) %collective-permute-start.40) | collective-permute-done | bytes 294944 | tf_op jit(solution)/shard_map/ppermute | solution.py:237
  513.6 7.3 %collective-permute-done.41 = bf16[48,3072]{1,0:T(8,128)(2,1)S(1)} collective-permute-done((bf16[48,3072]{1,0:T(8,128)(2,1)S(1)}, bf16[48,3072]{1,0:T(8,128)(2,1)S(1)}, u32[]{:S(2)}, u32[]{:S(2)}) %collective-permute-start.41) | collective-permute-done | bytes 294944 | tf_op jit(solution)/shard_map/ppermute | solution.py:237
  525.5 2.3 fusion.72
  (533 shorter events, 167.1 us)
Async XLA Ops:
  7.2 244.2 %all-gather.3.cloned.1.call-start = ((), (), s32[]{:S(2)}) async-start(), calls=%async_computation.3 | async-start | bytes 14598144 | tf_op jit(solution)/shard_map/all_gather | solution.py:207
  10.3 8.9 %collective-permute-start.1 = (bf16[48,1152]{1,0:T(8,128)(2,1)S(1)}, bf16[48,1152]{1,0:T(8,128)(2,1)S(1)}, u32[]{:S(2)}, u32[]{:S(2)}) collective-permute-start(bf16[48,1152]{1,0:T(8,128)(2,1)S(1)} %get-tuple-element.234), channel_id=1, source_target_pairs={{0,2},{1,3},{2,4},{3,5},{4,6},{5,7},{6,0},{7,1},{8,10},{9,11},{10,... | collective-permute-start | bytes 331784 | tf_op jit(solution)/shard_map/ppermute | solution.py:237
  13.3 10.2 %collective-permute-start.2 = (bf16[48,1152]{1,0:T(8,128)(2,1)S(1)}, bf16[48,1152]{1,0:T(8,128)(2,1)S(1)}, u32[]{:S(2)}, u32[]{:S(2)}) collective-permute-start(bf16[48,1152]{1,0:T(8,128)(2,1)S(1)} %get-tuple-element.234), channel_id=1, source_target_pairs={{0,4},{1,5},{2,6},{3,7},{4,0},{5,1},{6,2},{7,3},{8,12},{9,13},{10,... | collective-permute-start | bytes 331784 | tf_op jit(solution)/shard_map/ppermute | solution.py:237
  15.9 7.7 %collective-permute-start.3 = (bf16[48,1152]{1,0:T(8,128)(2,1)S(1)}, bf16[48,1152]{1,0:T(8,128)(2,1)S(1)}, u32[]{:S(2)}, u32[]{:S(2)}) collective-permute-start(bf16[48,1152]{1,0:T(8,128)(2,1)S(1)} %get-tuple-element.234), channel_id=1, source_target_pairs={{0,6},{1,7},{2,0},{3,1},{4,2},{5,3},{6,4},{7,5},{8,14},{9,15},{10,... | collective-permute-start | bytes 331784 | tf_op jit(solution)/shard_map/ppermute | solution.py:237
  23.6 12.1 %collective-permute-start.4 = (bf16[4,48,1152]{2,1,0:T(8,128)(2,1)S(1)}, bf16[4,48,1152]{2,1,0:T(8,128)(2,1)S(1)}, u32[]{:S(2)}, u32[]{:S(2)}) collective-permute-start(bf16[4,48,1152]{2,1,0:T(8,128)(2,1)S(1)} %pad_maximum_fusion.10.refs_0_), channel_id=1, source_target_pairs={{0,8},{1,9},{2,10},{3,11},{4,12},{5,13},{6,14},{7,15},{8,0},{9,1},... | collective-permute-start | bytes 1327112 | tf_op jit(solution)/shard_map/ppermute | solution.py:237
  25.1 12.1 %collective-permute-start.5 = (bf16[4,48,1152]{2,1,0:T(8,128)(2,1)S(1)}, bf16[4,48,1152]{2,1,0:T(8,128)(2,1)S(1)}, u32[]{:S(2)}, u32[]{:S(2)}) collective-permute-start(bf16[4,48,1152]{2,1,0:T(8,128)(2,1)S(1)} %pad_maximum_fusion.10.refs_0_), channel_id=1, source_target_pairs={{0,16},{1,17},{2,18},{3,19},{4,20},{5,21},{6,22},{7,23},{8,24},{9,... | collective-permute-start | bytes 1327112 | tf_op jit(solution)/shard_map/ppermute | solution.py:237
  26.7 16.9 %collective-permute-start.8 = (bf16[4,48,1152]{2,1,0:T(8,128)(2,1)S(1)}, bf16[4,48,1152]{2,1,0:T(8,128)(2,1)S(1)}, u32[]{:S(2)}, u32[]{:S(2)}) collective-permute-start(bf16[4,48,1152]{2,1,0:T(8,128)(2,1)S(1)} %pad_maximum_fusion.10.refs_0_), channel_id=1, source_target_pairs={{0,1},{1,0},{2,3},{3,2},{4,5},{5,4},{6,7},{7,6},{8,9},{9,8},{10,11... | collective-permute-start | bytes 1327112 | tf_op jit(solution)/shard_map/ppermute | solution.py:237
  35.7 6.5 %collective-permute-start.6 = (bf16[2,48,1152]{2,1,0:T(8,128)(2,1)S(1)}, bf16[2,48,1152]{2,1,0:T(8,128)(2,1)S(1)}, u32[]{:S(2)}, u32[]{:S(2)}) collective-permute-start(bf16[2,48,1152]{2,1,0:T(8,128)(2,1)S(1)} %slice.472), channel_id=1, source_target_pairs={{0,16},{1,17},{2,18},{3,19},{4,20},{5,21},{6,22},{7,23},{8,24},{9,... | collective-permute-start | bytes 663560 | tf_op jit(solution)/shard_map/ppermute | solution.py:237
  37.3 6.2 %collective-permute-start.7 = (bf16[2,48,1152]{2,1,0:T(8,128)(2,1)S(1)}, bf16[2,48,1152]{2,1,0:T(8,128)(2,1)S(1)}, u32[]{:S(2)}, u32[]{:S(2)}) collective-permute-start(bf16[2,48,1152]{2,1,0:T(8,128)(2,1)S(1)} %slice.473), channel_id=1, source_target_pairs={{0,8},{1,9},{2,10},{3,11},{4,12},{5,13},{6,14},{7,15},{8,0},{9,1},... | collective-permute-start | bytes 663560 | tf_op jit(solution)/shard_map/ppermute | solution.py:237
  38.8 6.1 %collective-permute-start.10 = (bf16[4,48,1152]{2,1,0:T(8,128)(2,1)S(1)}, bf16[4,48,1152]{2,1,0:T(8,128)(2,1)S(1)}, u32[]{:S(2)}, u32[]{:S(2)}) collective-permute-start(bf16[4,48,1152]{2,1,0:T(8,128)(2,1)S(1)} %collective-permute-done.5.refs_2_), channel_id=1, source_target_pairs={{0,1},{1,0},{2,3},{3,2},{4,5},{5,4},{6,7},{7,6},{8,9},{9,8},{10,11... | collective-permute-start | bytes 1327112 | tf_op jit(solution)/shard_map/ppermute | solution.py:237
  38.8 6.1 %collective-permute-start.9 = (bf16[4,48,1152]{2,1,0:T(8,128)(2,1)S(1)}, bf16[4,48,1152]{2,1,0:T(8,128)(2,1)S(1)}, u32[]{:S(2)}, u32[]{:S(2)}) collective-permute-start(bf16[4,48,1152]{2,1,0:T(8,128)(2,1)S(1)} %collective-permute-done.4.refs_1_), channel_id=1, source_target_pairs={{0,1},{1,0},{2,3},{3,2},{4,5},{5,4},{6,7},{7,6},{8,9},{9,8},{10,11... | collective-permute-start | bytes 1327112 | tf_op jit(solution)/shard_map/ppermute | solution.py:237
  42.1 1.5 collective-permute-start.11
  43.5 1.5 collective-permute-start.12
  55.3 71.3 %all-to-all-start = ((bf16[32,32,128]{2,1,0:T(8,128)(2,1)}), bf16[32,32,128]{2,1,0:T(8,128)(2,1)S(1)}, u32[]{:S(2)}, u32[]{:S(2)}) async-start(bf16[32,32,128]{2,1,0:T(8,128)(2,1)} %broadcast_in_dim.30), calls=%async_computation | async-start | bytes 524288 | tf_op jit(solution)/shard_map/all_to_all | solution.py:226
  59.7 461.6 %all-gather.5.cloned.1.call-start = ((), (), s32[]{:S(2)}) async-start(), calls=%async_computation.4 | async-start | bytes 3649536 | tf_op jit(solution)/shard_map/all_gather | solution.py:207
  68.0 4.6 collective-permute-start.13
  79.3 18.2 %collective-permute-start.14 = (bf16[48,3456]{1,0:T(8,128)(2,1)}, bf16[48,3456]{1,0:T(8,128)(2,1)}, u32[]{:S(2)}, u32[]{:S(2)}) collective-permute-start(bf16[48,3456]{1,0:T(8,128)(2,1)} %constant_dynamic-update-slice_fusion.5), channel_id=1, source_target_pairs={{0,2},{1,3},{2,4},{3,5},{4,6},{5,7},{6,0},{7,1},{8,10},{9,11},{10,... | collective-permute-start | bytes 995336 | tf_op jit(solution)/shard_map/ppermute | solution.py:237
  81.0 40.7 %collective-permute-start.15 = (bf16[48,3456]{1,0:T(8,128)(2,1)}, bf16[48,3456]{1,0:T(8,128)(2,1)}, u32[]{:S(2)}, u32[]{:S(2)}) collective-permute-start(bf16[48,3456]{1,0:T(8,128)(2,1)} %constant_dynamic-update-slice_fusion.5), channel_id=1, source_target_pairs={{0,4},{1,5},{2,6},{3,7},{4,0},{5,1},{6,2},{7,3},{8,12},{9,13},{10,... | collective-permute-start | bytes 995336 | tf_op jit(solution)/shard_map/ppermute | solution.py:237
  83.4 38.3 %collective-permute-start.16 = (bf16[48,3456]{1,0:T(8,128)(2,1)}, bf16[48,3456]{1,0:T(8,128)(2,1)}, u32[]{:S(2)}, u32[]{:S(2)}) collective-permute-start(bf16[48,3456]{1,0:T(8,128)(2,1)} %constant_dynamic-update-slice_fusion.5), channel_id=1, source_target_pairs={{0,6},{1,7},{2,0},{3,1},{4,2},{5,3},{6,4},{7,5},{8,14},{9,15},{10,... | collective-permute-start | bytes 995336 | tf_op jit(solution)/shard_map/ppermute | solution.py:237
  123.2 51.7 %collective-permute-start.17 = (bf16[4,48,3456]{2,1,0:T(8,128)(2,1)S(1)}, bf16[4,48,3456]{2,1,0:T(8,128)(2,1)S(1)}, u32[]{:S(2)}, u32[]{:S(2)}) collective-permute-start(bf16[4,48,3456]{2,1,0:T(8,128)(2,1)S(1)} %pad_maximum_fusion.5.refs_0_), channel_id=1, source_target_pairs={{0,8},{1,9},{2,10},{3,11},{4,12},{5,13},{6,14},{7,15},{8,0},{9,1},... | collective-permute-start | bytes 3981320 | tf_op jit(solution)/shard_map/ppermute | solution.py:237
  125.2 54.1 %collective-permute-start.18 = (bf16[4,48,3456]{2,1,0:T(8,128)(2,1)S(1)}, bf16[4,48,3456]{2,1,0:T(8,128)(2,1)}, u32[]{:S(2)}, u32[]{:S(2)}) collective-permute-start(bf16[4,48,3456]{2,1,0:T(8,128)(2,1)S(1)} %pad_maximum_fusion.5.refs_0_), channel_id=1, source_target_pairs={{0,16},{1,17},{2,18},{3,19},{4,20},{5,21},{6,22},{7,23},{8,24},{9,... | collective-permute-start | bytes 3981320 | tf_op jit(solution)/shard_map/ppermute | solution.py:237
  126.6 71.0 %collective-permute-start.21 = (bf16[4,48,3456]{2,1,0:T(8,128)(2,1)S(1)}, bf16[4,48,3456]{2,1,0:T(8,128)(2,1)}, u32[]{:S(2)}, u32[]{:S(2)}) collective-permute-start(bf16[4,48,3456]{2,1,0:T(8,128)(2,1)S(1)} %pad_maximum_fusion.5.refs_0_), channel_id=1, source_target_pairs={{0,1},{1,0},{2,3},{3,2},{4,5},{5,4},{6,7},{7,6},{8,9},{9,8},{10,11... | collective-permute-start | bytes 3981320 | tf_op jit(solution)/shard_map/ppermute | solution.py:237
  174.9 20.0 %collective-permute-start.19 = (bf16[2,48,3456]{2,1,0:T(8,128)(2,1)S(1)}, bf16[2,48,3456]{2,1,0:T(8,128)(2,1)S(1)}, u32[]{:S(2)}, u32[]{:S(2)}) collective-permute-start(bf16[2,48,3456]{2,1,0:T(8,128)(2,1)S(1)} %slice.481), channel_id=1, source_target_pairs={{0,16},{1,17},{2,18},{3,19},{4,20},{5,21},{6,22},{7,23},{8,24},{9,... | collective-permute-start | bytes 1990664 | tf_op jit(solution)/shard_map/ppermute | solution.py:237
  180.4 14.5 %collective-permute-start.20 = (bf16[2,48,3456]{2,1,0:T(8,128)(2,1)S(1)}, bf16[2,48,3456]{2,1,0:T(8,128)(2,1)S(1)}, u32[]{:S(2)}, u32[]{:S(2)}) collective-permute-start(bf16[2,48,3456]{2,1,0:T(8,128)(2,1)S(1)} %slice.482), channel_id=1, source_target_pairs={{0,8},{1,9},{2,10},{3,11},{4,12},{5,13},{6,14},{7,15},{8,0},{9,1},... | collective-permute-start | bytes 1990664 | tf_op jit(solution)/shard_map/ppermute | solution.py:237
  181.6 17.3 %collective-permute-start.22 = (bf16[4,48,3456]{2,1,0:T(8,128)(2,1)S(1)}, bf16[4,48,3456]{2,1,0:T(8,128)(2,1)S(1)}, u32[]{:S(2)}, u32[]{:S(2)}) collective-permute-start(bf16[4,48,3456]{2,1,0:T(8,128)(2,1)S(1)} %collective-permute-done.17.refs_1_), channel_id=1, source_target_pairs={{0,1},{1,0},{2,3},{3,2},{4,5},{5,4},{6,7},{7,6},{8,9},{9,8},{10,11... | collective-permute-start | bytes 3981320 | tf_op jit(solution)/shard_map/ppermute | solution.py:237
  181.7 17.2 %collective-permute-start.23 = (bf16[4,48,3456]{2,1,0:T(8,128)(2,1)}, bf16[4,48,3456]{2,1,0:T(8,128)(2,1)S(1)}, u32[]{:S(2)}, u32[]{:S(2)}) collective-permute-start(bf16[4,48,3456]{2,1,0:T(8,128)(2,1)} %collective-permute-done.18.refs_2_), channel_id=1, source_target_pairs={{0,1},{1,0},{2,3},{3,2},{4,5},{5,4},{6,7},{7,6},{8,9},{9,8},{10,11... | collective-permute-start | bytes 3981320 | tf_op jit(solution)/shard_map/ppermute | solution.py:237
  194.9 2.8 collective-permute-start.24
  194.9 4.0 collective-permute-start.25
  377.8 13.7 %collective-permute-start.26 = (bf16[16,48,1536]{2,1,0:T(8,128)(2,1)}, bf16[16,48,1536]{2,1,0:T(8,128)(2,1)S(1)}, u32[]{:S(2)}, u32[]{:S(2)}) collective-permute-start(bf16[16,48,1536]{2,1,0:T(8,128)(2,1)} %pad_maximum_fusion.4), channel_id=1, source_target_pairs={{0,1},{1,0},{2,3},{3,2},{4,5},{5,4},{6,7},{7,6},{8,9},{9,8},{10,11... | collective-permute-start | bytes 7077896 | tf_op jit(solution)/shard_map/ppermute | solution.py:237
  384.8 65.7 %collective-permute-start.35 = (bf16[16,48,3072]{2,1,0:T(8,128)(2,1)}, bf16[16,48,3072]{2,1,0:T(8,128)(2,1)}, u32[]{:S(2)}, u32[]{:S(2)}) collective-permute-start(bf16[16,48,3072]{2,1,0:T(8,128)(2,1)} %pad_maximum_fusion.1), channel_id=1, source_target_pairs={{0,1},{1,0},{2,3},{3,2},{4,5},{5,4},{6,7},{7,6},{8,9},{9,8},{10,11... | collective-permute-start | bytes 14155784 | tf_op jit(solution)/shard_map/ppermute | solution.py:237
  393.1 27.4 %collective-permute-start.27 = (bf16[2,48,1536]{2,1,0:T(8,128)(2,1)}, bf16[2,48,1536]{2,1,0:T(8,128)(2,1)}, u32[]{:S(2)}, u32[]{:S(2)}) collective-permute-start(bf16[2,48,1536]{2,1,0:T(8,128)(2,1)} %get-tuple-element.175), channel_id=1, source_target_pairs={{0,16},{1,17},{2,18},{3,19},{4,20},{5,21},{6,22},{7,23},{8,24},{9,... | collective-permute-start | bytes 884744 | tf_op jit(solution)/shard_map/ppermute | solution.py:237
  394.6 25.9 %collective-permute-start.29 = (bf16[2,48,1536]{2,1,0:T(8,128)(2,1)}, bf16[2,48,1536]{2,1,0:T(8,128)(2,1)}, u32[]{:S(2)}, u32[]{:S(2)}) collective-permute-start(bf16[2,48,1536]{2,1,0:T(8,128)(2,1)} %get-tuple-element.177), channel_id=1, source_target_pairs={{0,8},{1,9},{2,10},{3,11},{4,12},{5,13},{6,14},{7,15},{8,0},{9,1},... | collective-permute-start | bytes 884744 | tf_op jit(solution)/shard_map/ppermute | solution.py:237
  405.6 26.7 %all-to-all-start.1 = ((f32[32,8,128]{2,1,0:T(8,128)}), f32[32,8,128]{2,1,0:T(8,128)S(1)}, u32[]{:S(2)}, u32[]{:S(2)}) async-start(f32[32,8,128]{2,1,0:T(8,128)} %bitcast.171), calls=%async_computation.1 | async-start | bytes 262144 | tf_op jit(solution)/shard_map/all_to_all | solution.py:232
  422.6 20.2 %collective-permute-start.28 = (bf16[4,48,1536]{2,1,0:T(8,128)(2,1)}, bf16[4,48,1536]{2,1,0:T(8,128)(2,1)}, u32[]{:S(2)}, u32[]{:S(2)}) collective-permute-start(bf16[4,48,1536]{2,1,0:T(8,128)(2,1)} %pad_maximum_fusion.8), channel_id=1, source_target_pairs={{0,8},{1,9},{2,10},{3,11},{4,12},{5,13},{6,14},{7,15},{8,0},{9,1},... | collective-permute-start | bytes 1769480 | tf_op jit(solution)/shard_map/ppermute | solution.py:237
  425.3 18.2 %collective-permute-start.30 = (bf16[4,48,1536]{2,1,0:T(8,128)(2,1)}, bf16[4,48,1536]{2,1,0:T(8,128)(2,1)S(1)}, u32[]{:S(2)}, u32[]{:S(2)}) collective-permute-start(bf16[4,48,1536]{2,1,0:T(8,128)(2,1)} %pad_maximum_fusion.9), channel_id=1, source_target_pairs={{0,16},{1,17},{2,18},{3,19},{4,20},{5,21},{6,22},{7,23},{8,24},{9,... | collective-permute-start | bytes 1769480 | tf_op jit(solution)/shard_map/ppermute | solution.py:237
  432.3 89.1 %all-to-all-start.2 = ((bf16[32,8,168]{2,1,0:T(8,128)(2,1)}), bf16[32,8,168]{2,1,0:T(8,128)(2,1)S(1)}, u32[]{:S(2)}, u32[]{:S(2)}) async-start(bf16[32,8,168]{2,1,0:T(8,128)(2,1)} %maximum_bitcast_fusion), calls=%async_computation.2 | async-start | bytes 262144 | tf_op jit(solution)/shard_map/all_to_all | solution.py:560
  445.0 12.5 %collective-permute-start.31 = (bf16[48,1536]{1,0:T(8,128)(2,1)S(1)}, bf16[48,1536]{1,0:T(8,128)(2,1)S(1)}, u32[]{:S(2)}, u32[]{:S(2)}) collective-permute-start(bf16[48,1536]{1,0:T(8,128)(2,1)S(1)} %get-tuple-element.190), channel_id=1, source_target_pairs={{0,2},{1,3},{2,4},{3,5},{4,6},{5,7},{6,0},{7,1},{8,10},{9,11},{10,... | collective-permute-start | bytes 442376 | tf_op jit(solution)/shard_map/ppermute | solution.py:237
  446.4 12.6 %collective-permute-start.32 = (bf16[48,1536]{1,0:T(8,128)(2,1)S(1)}, bf16[48,1536]{1,0:T(8,128)(2,1)S(1)}, u32[]{:S(2)}, u32[]{:S(2)}) collective-permute-start(bf16[48,1536]{1,0:T(8,128)(2,1)S(1)} %get-tuple-element.192), channel_id=1, source_target_pairs={{0,4},{1,5},{2,6},{3,7},{4,0},{5,1},{6,2},{7,3},{8,12},{9,13},{10,... | collective-permute-start | bytes 442376 | tf_op jit(solution)/shard_map/ppermute | solution.py:237
  448.8 10.2 %collective-permute-start.33 = (bf16[48,1536]{1,0:T(8,128)(2,1)S(1)}, bf16[48,1536]{1,0:T(8,128)(2,1)S(1)}, u32[]{:S(2)}, u32[]{:S(2)}) collective-permute-start(bf16[48,1536]{1,0:T(8,128)(2,1)S(1)} %get-tuple-element.191), channel_id=1, source_target_pairs={{0,6},{1,7},{2,0},{3,1},{4,2},{5,3},{6,4},{7,5},{8,14},{9,15},{10,... | collective-permute-start | bytes 442376 | tf_op jit(solution)/shard_map/ppermute | solution.py:237
  454.8 19.6 %collective-permute-start.36 = (bf16[2,48,3072]{2,1,0:T(8,128)(2,1)S(1)}, bf16[2,48,3072]{2,1,0:T(8,128)(2,1)S(1)}, u32[]{:S(2)}, u32[]{:S(2)}) collective-permute-start(bf16[2,48,3072]{2,1,0:T(8,128)(2,1)S(1)} %get-tuple-element.158), channel_id=1, source_target_pairs={{0,16},{1,17},{2,18},{3,19},{4,20},{5,21},{6,22},{7,23},{8,24},{9,... | collective-permute-start | bytes 1769480 | tf_op jit(solution)/shard_map/ppermute | solution.py:237
  456.4 20.0 %collective-permute-start.38 = (bf16[2,48,3072]{2,1,0:T(8,128)(2,1)S(1)}, bf16[2,48,3072]{2,1,0:T(8,128)(2,1)S(1)}, u32[]{:S(2)}, u32[]{:S(2)}) collective-permute-start(bf16[2,48,3072]{2,1,0:T(8,128)(2,1)S(1)} %get-tuple-element.160), channel_id=1, source_target_pairs={{0,8},{1,9},{2,10},{3,11},{4,12},{5,13},{6,14},{7,15},{8,0},{9,1},... | collective-permute-start | bytes 1769480 | tf_op jit(solution)/shard_map/ppermute | solution.py:237
  476.7 24.4 %collective-permute-start.37 = (bf16[4,48,3072]{2,1,0:T(8,128)(2,1)S(1)}, bf16[4,48,3072]{2,1,0:T(8,128)(2,1)S(1)}, u32[]{:S(2)}, u32[]{:S(2)}) collective-permute-start(bf16[4,48,3072]{2,1,0:T(8,128)(2,1)S(1)} %pad_maximum_fusion.6), channel_id=1, source_target_pairs={{0,8},{1,9},{2,10},{3,11},{4,12},{5,13},{6,14},{7,15},{8,0},{9,1},... | collective-permute-start | bytes 3538952 | tf_op jit(solution)/shard_map/ppermute | solution.py:237
  477.4 23.7 %collective-permute-start.39 = (bf16[4,48,3072]{2,1,0:T(8,128)(2,1)S(1)}, bf16[4,48,3072]{2,1,0:T(8,128)(2,1)S(1)}, u32[]{:S(2)}, u32[]{:S(2)}) collective-permute-start(bf16[4,48,3072]{2,1,0:T(8,128)(2,1)S(1)} %pad_maximum_fusion.7), channel_id=1, source_target_pairs={{0,16},{1,17},{2,18},{3,19},{4,20},{5,21},{6,22},{7,23},{8,24},{9,... | collective-permute-start | bytes 3538952 | tf_op jit(solution)/shard_map/ppermute | solution.py:237
  477.5 1.4 collective-permute-start.34
  501.8 11.9 %collective-permute-start.40 = (bf16[48,3072]{1,0:T(8,128)(2,1)S(1)}, bf16[48,3072]{1,0:T(8,128)(2,1)S(1)}, u32[]{:S(2)}, u32[]{:S(2)}) collective-permute-start(bf16[48,3072]{1,0:T(8,128)(2,1)S(1)} %get-tuple-element.179), channel_id=1, source_target_pairs={{0,2},{1,3},{2,4},{3,5},{4,6},{5,7},{6,0},{7,1},{8,10},{9,11},{10,... | collective-permute-start | bytes 884744 | tf_op jit(solution)/shard_map/ppermute | solution.py:237
  502.4 18.5 %collective-permute-start.41 = (bf16[48,3072]{1,0:T(8,128)(2,1)S(1)}, bf16[48,3072]{1,0:T(8,128)(2,1)S(1)}, u32[]{:S(2)}, u32[]{:S(2)}) collective-permute-start(bf16[48,3072]{1,0:T(8,128)(2,1)S(1)} %get-tuple-element.181), channel_id=1, source_target_pairs={{0,4},{1,5},{2,6},{3,7},{4,0},{5,1},{6,2},{7,3},{8,12},{9,13},{10,... | collective-permute-start | bytes 884744 | tf_op jit(solution)/shard_map/ppermute | solution.py:237
  502.8 18.1 %collective-permute-start.42 = (bf16[48,3072]{1,0:T(8,128)(2,1)S(1)}, bf16[48,3072]{1,0:T(8,128)(2,1)S(1)}, u32[]{:S(2)}, u32[]{:S(2)}) collective-permute-start(bf16[48,3072]{1,0:T(8,128)(2,1)S(1)} %get-tuple-element.180), channel_id=1, source_target_pairs={{0,6},{1,7},{2,0},{3,1},{4,2},{5,3},{6,4},{7,5},{8,14},{9,15},{10,... | collective-permute-start | bytes 884744 | tf_op jit(solution)/shard_map/ppermute | solution.py:237
  521.3 11.8 %collective-permute-start.43 = (f32[24,3072]{1,0:T(8,128)S(1)}, f32[24,3072]{1,0:T(8,128)S(1)}, u32[]{:S(2)}, u32[]{:S(2)}) collective-permute-start(f32[24,3072]{1,0:T(8,128)S(1)} %constant_dynamic-update-slice_fusion.17), channel_id=1, source_target_pairs={{0,1},{1,0},{2,3},{3,2},{4,5},{5,4},{6,7},{7,6},{8,9},{9,8},{10,11... | collective-permute-start | bytes 884744 | tf_op jit(solution)/shard_map/ppermute | solution.py:237
  (92 other events, 1197.8 us)
Sparse Core Ops, SparseCore 0:
  49.6 155.0 all-gather.2
  398.3 82.2 all-gather.4

commit v3 on v2

v3 whole, which is shorter than its diff:
```python
from functools import partial

import jax
import jax.numpy as jnp
from jax import lax
from jax.experimental import pallas as pl
from jax.experimental.pallas import tpu as pltpu
from jax.sharding import PartitionSpec as P

D = 768
HEADS = 12
HD = 64
SEG = 128
SLOTS = 1024
SEGS = 8


def cross_rows(left_rows, right_rows):
    return lax.dot_general(
        left_rows, right_rows, (((0,), (0,)), ((), ())), preferred_element_type=jnp.float32
    )


def back_cols(left_rows, right_rows):
    return lax.dot_general(
        left_rows, right_rows, (((1,), (1,)), ((), ())), preferred_element_type=jnp.float32
    )


ROWS = 256
PAIR = 2 * HD
PAIRS = HEADS // 2
F32 = jnp.float32
LOW = jnp.bfloat16


def dot_nn(left, right):
    return jnp.dot(left, right, preferred_element_type=F32)


def centre_rows(rows):
    centred = rows - jnp.mean(rows, axis=-1, keepdims=True)
    spread = lax.rsqrt(jnp.mean(centred * centred, axis=-1, keepdims=True) + 1e-05)
    return centred * spread, spread


def norm_back(grad, unit, spread):
    return spread * (
        grad
        - jnp.mean(grad, axis=-1, keepdims=True)
        - unit * jnp.mean(grad * unit, axis=-1, keepdims=True)
    )


def gelu_pair(hidden):
    size = jnp.abs(hidden)
    bell = jnp.exp(hidden * hidden * -0.5)
    t = 1.0 / (1.0 + (0.3275911 * 0.7071067811865476) * size)
    poly = t * (
        0.127414796
        + t * (-0.142248368 + t * (0.7107068705 + t * (-0.7265760135 + t * 0.5307027145)))
    )
    tail = poly * bell
    phi = jnp.where(hidden >= 0, 1.0 - tail, tail)
    return hidden * phi, phi + hidden * bell * 0.3989422804014327


def two_heads(pair, axis):
    first = lax.broadcasted_iota(jnp.int32, pair.shape, 1) < HD
    zero = jnp.zeros_like(pair)
    return jnp.concatenate([jnp.where(first, pair, zero), jnp.where(first, zero, pair)], axis=axis)


def pair_probs(query, key, valid):
    scores = back_cols(two_heads(query, 0), key) * HD ** (-0.5)
    scores = jnp.where(valid, scores, -1e30)
    weight = jnp.exp(scores - jnp.max(scores, axis=-1, keepdims=True))
    return weight / jnp.sum(weight, axis=-1, keepdims=True)


def side_by_side(stacked):
    half = stacked.shape[0] // 2
    return jnp.concatenate([stacked[:half], stacked[half:]], axis=1)


def valid_keys(count_ref, segment):
    position = lax.broadcasted_iota(jnp.int32, (1, SEG), 1)
    return position < count_ref[0] - segment * SEG


def attend_kernel(count_ref, rows_ref, attend_ref, bias_ref, projected_ref, context_ref):
    step = pl.program_id(0)
    projected_ref[...] = (dot_nn(rows_ref[...], attend_ref[...]) + bias_ref[...]).astype(LOW)
    for local in range(ROWS // SEG):
        valid = valid_keys(count_ref, step * (ROWS // SEG) + local)
        span = slice(local * SEG, (local + 1) * SEG)
        for pair in range(PAIRS):
            query, key, value = [
                projected_ref[span, part * D + pair * PAIR : part * D + (pair + 1) * PAIR]
                for part in range(3)
            ]
            probs = pair_probs(query, key, valid).astype(LOW)
            context_ref[span, pair * PAIR : (pair + 1) * PAIR] = dot_nn(
                side_by_side(probs), two_heads(value, 0)
            ).astype(LOW)


def put_row(ref, place, start, row):
    span = slice(start, start + row.shape[1])
    here = lax.broadcasted_iota(jnp.int32, (ref.shape[0], 1), 0) == place
    ref[:, span] = jnp.where(here, row, ref[:, span])


def get_row(ref, place, span):
    here = lax.broadcasted_iota(jnp.int32, (ref.shape[0], 1), 0) == place
    return jnp.sum(jnp.where(here, ref[:, span], 0.0), axis=0, keepdims=True)


def first_row(rows, segment):
    return rows[segment * SEG : segment * SEG + 16, :].astype(F32)[:1]


def feed_kernel(
    count_ref,
    rows_ref,
    context_ref,
    merge_ref,
    expand_ref,
    expand_bias_ref,
    reduce_ref,
    vectors_ref,
    mixed_ref,
    heads_ref,
    wide_heads_ref,
    first_ref,
    normed_ref,
    active_ref,
    slope_ref,
    second_ref,
):
    step = pl.program_id(0)
    merge_bias, gain, shift, reduce_bias, final_gain, final_shift = [
        vectors_ref[row : row + 1, :] for row in range(6)
    ]
    first = rows_ref[...].astype(F32) + dot_nn(context_ref[...], merge_ref[...]) + merge_bias
    first_ref[...] = first
    normed = (centre_rows(first)[0] * gain + shift).astype(LOW)
    normed_ref[...] = normed
    second = normed.astype(F32) + reduce_bias
    chunk, wide = D, expand_ref.shape[1]
    segments = ROWS // SEG
    for start in range(0, wide, chunk):
        span = slice(start, start + chunk)
        active, slope = gelu_pair(dot_nn(normed, expand_ref[:, span]) + expand_bias_ref[:, span])
        active = active.astype(LOW)
        active_ref[:, span] = active
        slope_ref[:, span] = slope.astype(LOW)
        for local in range(segments):
            head = step * segments + local
            put_row(wide_heads_ref, head, start, slope[local * SEG : local * SEG + 1])
            put_row(wide_heads_ref, head, wide + start, first_row(active, local))
        second = second + dot_nn(active, reduce_ref[span, :])
    second_ref[...] = second
    result = centre_rows(second)[0] * final_gain + final_shift
    for local in range(segments):
        for number, rows in enumerate((result, first, second, normed, context_ref)):
            put_row(heads_ref, step * segments + local, number * D, first_row(rows, local))
    place = lax.broadcasted_iota(jnp.int32, (ROWS, 1), 0) + step * ROWS
    mixed_ref[...] = jnp.where(place < count_ref[0], result, 0.0).astype(LOW)


def feed_back_kernel(
    count_ref,
    cotangent_ref,
    second_ref,
    first_ref,
    slope_ref,
    merge_ref,
    expand_ref,
    reduce_ref,
    vectors_ref,
    branch_ref,
    hidden_ref,
    attn_ref,
    context_ref,
    first_grad_ref,
    sums_ref,
    hidden_sums_ref,
):
    step = pl.program_id(0)
    gain, final_gain = vectors_ref[1:2, :], vectors_ref[4:5, :]
    local = lax.broadcasted_iota(jnp.int32, (ROWS, 1), 0)
    plain = (local + step * ROWS < count_ref[0]) & (local % SEG != 0)
    grad = jnp.where(plain, cotangent_ref[...].astype(F32), 0.0)
    unit, spread = centre_rows(second_ref[...])
    sums = [grad * unit, grad]
    second = norm_back(grad * final_gain, unit, spread)
    branch = second.astype(LOW)
    branch_ref[...] = branch
    sums.append(branch.astype(F32))
    normed = second
    chunk = D

    @pl.when(step == 0)
    def _():
        sums_ref[...] = jnp.zeros_like(sums_ref)
        hidden_sums_ref[...] = jnp.zeros_like(hidden_sums_ref)

    for start in range(0, expand_ref.shape[1], chunk):
        span = slice(start, start + chunk)
        hidden = back_cols(branch, reduce_ref[span, :]) * slope_ref[:, span].astype(F32)
        hidden = hidden.astype(LOW)
        hidden_ref[:, span] = hidden
        hidden_sums_ref[:, span] += jnp.sum(hidden.astype(F32), axis=0, keepdims=True)
        normed = normed + back_cols(hidden, expand_ref[:, span])
    unit, spread = centre_rows(first_ref[...])
    sums += [normed * unit, normed]
    first = norm_back(normed * gain, unit, spread)
    first_grad_ref[...] = first
    attn = first.astype(LOW)
    attn_ref[...] = attn
    sums.append(attn.astype(F32))
    context_ref[...] = back_cols(attn, merge_ref[...]).astype(LOW)
    sums_ref[...] += jnp.concatenate(
        [jnp.sum(entry, axis=0, keepdims=True) for entry in sums]
        + [jnp.zeros((2, D), F32)],
        axis=0,
    )


def attend_back_kernel(
    offset,
    count_ref,
    projected_ref,
    context_ref,
    first_ref,
    mixed_in_ref,
    attend_ref,
    head_context_ref,
    head_first_ref,
    head_out_ref,
    *refs,
):
    grad_ref, tokens_ref, mixed_ref, sums_ref = refs[-4:]
    step = pl.program_id(0)
    segments = ROWS // SEG

    @pl.when(step == 0)
    def _():
        sums_ref[...] = jnp.zeros_like(sums_ref)

    is_head = lax.broadcasted_iota(jnp.int32, (SEG, 1), 0) == 0
    scale = HD ** (-0.5)
    for local in range(segments):
        segment = (step + offset) * segments + local
        valid = valid_keys(count_ref, segment)
        span = slice(local * SEG, (local + 1) * SEG)
        for pair in range(PAIRS):
            columns = [
                slice(part * D + pair * PAIR, part * D + (pair + 1) * PAIR) for part in range(3)
            ]
            query, key, value = [projected_ref[span, column] for column in columns]
            grad = jnp.where(
                is_head,
                get_row(head_context_ref, segment, columns[0]),
                context_ref[span, columns[0]].astype(F32),
            ).astype(LOW)
            grad = two_heads(grad, 0)
            probs = pair_probs(query, key, valid)
            grad_probs = back_cols(grad, value)
            total = jnp.sum(grad_probs * probs, axis=-1, keepdims=True)
            scores = (probs * (grad_probs - total)).astype(LOW)
            grad_ref[span, columns[0]] = (
                dot_nn(side_by_side(scores), two_heads(key, 0)) * scale
            ).astype(LOW)
            grad_ref[span, columns[1]] = (
                cross_rows(scores, two_heads(query, 0)) * scale
            ).astype(LOW)
            grad_ref[span, columns[2]] = cross_rows(probs.astype(LOW), grad).astype(LOW)
        first = jnp.where(is_head, get_row(head_first_ref, segment, slice(0, D)), first_ref[span, :])
        tokens_ref[span, :] = first + back_cols(grad_ref[span, :], attend_ref[...])
        mixed_ref[span, :] = jnp.where(
            is_head, get_row(head_out_ref, segment, slice(0, D)), mixed_in_ref[span, :].astype(F32)
        ).astype(LOW)
    sums_ref[...] += jnp.sum(grad_ref[...].astype(F32), axis=0, keepdims=True)


def by_rows(width, offset=0):
    return pl.BlockSpec((ROWS, width), lambda step: (step + offset, 0))


def entire(array):
    return pl.BlockSpec(array.shape, lambda step: (0,) * array.ndim)


def row_call(kernel, name, operands, specs, outs, flops, steps=None, earlier=()):
    rows = next(operand.shape[0] for operand, spec in zip(operands, specs) if spec is not None)
    shapes = [jax.ShapeDtypeStruct(shape, kind) for shape, kind, _ in outs]
    moved = sum(operand.size * operand.dtype.itemsize for operand in operands)
    moved += sum(shape.size * shape.dtype.itemsize for shape in shapes)
    return pl.pallas_call(
        kernel,
        grid=(rows // ROWS if steps is None else steps,),
        in_specs=[pl.BlockSpec(memory_space=pltpu.SMEM)]
        + [entire(operand) if spec is None else spec for operand, spec in zip(operands[1:], specs[1:])]
        + [pl.BlockSpec(memory_space=pl.ANY)] * len(earlier),
        out_specs=[spec for _, _, spec in outs],
        out_shape=shapes,
        input_output_aliases={len(operands) + place: place for place in range(len(earlier))},
        compiler_params=pltpu.CompilerParams(vmem_limit_bytes=60 << 20),
        cost_estimate=pl.CostEstimate(flops=flops, bytes_accessed=moved, transcendentals=0),
        name=name,
    )(*operands, *earlier)


def whole_block(shape):
    return pl.BlockSpec(shape, lambda step: (0,) * len(shape))


def inner_attention(rows, counts, attend, attend_bias):
    size = rows.shape[0]
    return row_call(
        attend_kernel,
        "attend",
        (counts, rows, attend, attend_bias),
        (None, by_rows(D), None, None),
        [((size, 3 * D), LOW, by_rows(3 * D)), ((size, D), LOW, by_rows(D))],
        2 * size * D * (3 * D + 4 * SEG),
    )


def inner_feed(rows, counts, projected, context, weights):
    attend, merge, expand, reduce_matrix, expand_bias, vectors = weights
    size, wide = rows.shape[0], expand.shape[1]
    mixed, heads, wide_heads, *saved = row_call(
        feed_kernel,
        "feed",
        (counts, rows, context, merge, expand, expand_bias, reduce_matrix, vectors),
        (None, by_rows(D), by_rows(D), None, None, None, None, None),
        [
            ((size, D), LOW, by_rows(D)),
            ((size // SEG, 5 * D), F32, whole_block((size // SEG, 5 * D))),
            ((size // SEG, 2 * wide), F32, whole_block((size // SEG, 2 * wide))),
            ((size, D), F32, by_rows(D)),
            ((size, D), LOW, by_rows(D)),
            ((size, wide), LOW, by_rows(wide)),
            ((size, wide), LOW, by_rows(wide)),
            ((size, D), F32, by_rows(D)),
        ],
        2 * size * D * (D + 2 * wide),
    )
    return mixed, heads, wide_heads, saved


def inner_feed_back(cotangent, counts, saved, weights):
    attend, merge, expand, reduce_matrix, expand_bias, vectors = weights
    first, normed, active, slope, second = saved
    size, wide = cotangent.shape[0], expand.shape[1]
    return row_call(
        feed_back_kernel,
        "feed_back",
        (counts, cotangent, second, first, slope, merge, expand, reduce_matrix, vectors),
        (None, by_rows(D), by_rows(D), by_rows(D), by_rows(wide), None, None, None, None),
        [
            ((size, D), LOW, by_rows(D)),
            ((size, wide), LOW, by_rows(wide)),
            ((size, D), LOW, by_rows(D)),
            ((size, D), LOW, by_rows(D)),
            ((size, D), F32, by_rows(D)),
            ((8, D), F32, whole_block((8, D))),
            ((1, wide), F32, whole_block((1, wide))),
        ],
        2 * size * D * (D + 2 * wide),
    )


def inner_attend_back(counts, operands, attend, head_rows, offset, steps, earlier):
    projected, grad_context, grad_first, mixed = operands
    size = projected.shape[0]
    return row_call(
        partial(attend_back_kernel, offset),
        "attend_back",
        (counts, projected, grad_context, grad_first, mixed, attend, *head_rows),
        (None, by_rows(3 * D, offset), by_rows(D, offset), by_rows(D, offset))
        + (by_rows(D, offset), None, None, None, None),
        [
            ((size, 3 * D), LOW, by_rows(3 * D, offset)),
            ((size, D), F32, by_rows(D, offset)),
            ((size, D), LOW, by_rows(D, offset)),
            ((1, 3 * D), F32, whole_block((1, 3 * D))),
        ],
        2 * steps * ROWS * D * (3 * D + 10 * SEG),
        steps,
        earlier,
    )


AXES = ("dp", "fsdp")


def gather(rows):
    return lax.all_gather(rows, AXES, axis=0, tiled=True)


def scatter(rows):
    return lax.psum_scatter(rows, AXES, scatter_dimension=0, tiled=True)


def split_cols(packed, widths):
    pieces, start = [], 0
    for width in widths:
        pieces.append(packed[..., start : start + width])
        start += width
    return pieces


def pack_kernel(*refs):
    vectors, place_ref, out_ref, rows_ref = refs[:16], refs[16], refs[17], refs[18]
    rows_ref[...] = jnp.zeros_like(rows_ref)
    for row, ref in enumerate(vectors):
        rows_ref[row : row + 1, : ref.shape[1]] = ref[...].astype(F32)
    place = jnp.transpose(place_ref[...].astype(F32))
    rows_ref[16 : 16 + SEGS, : place.shape[1]] = place
    packed = rows_ref[...].astype(LOW)
    out_ref[...] = jnp.broadcast_to(packed[None], out_ref.shape)


def spread_row(rows, size, width):
    devices = rows.shape[0]
    lane = lax.broadcasted_iota(jnp.int32, (128, width), 1)
    owner = lane // size
    pick = (lane - owner * size == lax.broadcasted_iota(jnp.int32, (128, width), 0)).astype(LOW)
    spread = dot_nn(rows, pick)
    row = lax.broadcasted_iota(jnp.int32, (devices, width), 0)
    owner = lax.broadcasted_iota(jnp.int32, (devices, width), 1) // size
    return jnp.sum(jnp.where(row == owner, spread, 0.0), axis=0, keepdims=True)


VECTOR_ROWS = (1, 2, 3, 5, 6, 7)


def unpack_kernel(sizes, got_ref, *outs):
    devices = got_ref.shape[0]
    got = got_ref[...].astype(F32)
    for block in range(2):
        attend_ref, expand_ref, vectors_ref = outs[3 * block : 3 * block + 3]
        for kind in range(8):
            row = 8 * block + kind
            size = sizes[row]
            spread = spread_row(got[:, row, :].astype(LOW), size, size * devices)
            if kind == 0:
                attend_ref[...] = spread
            elif kind == 4:
                expand_ref[...] = spread
            else:
                place = VECTOR_ROWS.index(kind)
                vectors_ref[place : place + 1, :] = spread
        vectors_ref[6:8, :] = jnp.zeros((2, vectors_ref.shape[1]), F32)
    place_ref = outs[6]
    for segment in range(SEGS):
        place_ref[segment : segment + 1, :] = spread_row(
            got[:, 16 + segment, :].astype(LOW), sizes[16], sizes[16] * devices
        )


def share_small(vectors, segment_place):
    devices = lax.axis_size(AXES)
    sizes = [vector.shape[0] for vector in vectors] + [segment_place.shape[0]]
    sent = pl.pallas_call(
        pack_kernel,
        out_shape=jax.ShapeDtypeStruct((devices, 32, 128), LOW),
        scratch_shapes=[pltpu.VMEM((32, 128), F32)],
        name="pack",
    )(*[vector[None] for vector in vectors], segment_place)
    got = lax.all_to_all(sent, AXES, split_axis=0, concat_axis=0, tiled=True)
    shapes = []
    for block in range(2):
        for rows, size in ((1, sizes[8 * block]), (1, sizes[8 * block + 4]), (8, sizes[1])):
            shapes.append(jax.ShapeDtypeStruct((rows, size * devices), F32))
    shapes.append(jax.ShapeDtypeStruct((SEGS, sizes[16] * devices), F32))
    return pl.pallas_call(
        partial(unpack_kernel, sizes),
        out_shape=shapes,
        compiler_params=pltpu.CompilerParams(vmem_limit_bytes=60 << 20),
        name="unpack",
    )(got)


def sum_rows(rows):
    devices, size = rows.shape
    padded = jnp.pad(rows, ((0, 0), (0, -size % 1024))).reshape(devices, -1, 128)
    got = lax.all_to_all(padded, AXES, split_axis=0, concat_axis=0, tiled=True)
    return jnp.sum(got, axis=0).reshape(-1)[:size]


def hop(array, turn):
    return lax.ppermute(array, AXES, [(place, turn(place)) for place in range(32)])


def over_x(array):
    return hop(array, lambda place: place ^ 8)


def over_y(array):
    return hop(array, lambda place: place ^ 16)


def over_core(array):
    return hop(array, lambda place: place ^ 1)


def over_z(array, step):
    return hop(array, lambda place: (place & ~6) | ((((place >> 1) + step) & 3) << 1))


def place_here():
    chip = lax.axis_index("fsdp")
    return lax.axis_index("dp"), chip // 2, chip % 2


def half_cols(array, core):
    width = array.shape[-1] // 2
    return lax.dynamic_slice_in_dim(array, core * width, width, axis=array.ndim - 1)


def fold_rows(array, rows):
    return jnp.concatenate(jnp.split(array, array.shape[0] // rows, axis=0), axis=1)


def unfold_cols(array, width):
    return jnp.concatenate(jnp.split(array, array.shape[1] // width, axis=1), axis=0)


def both_cores(mine, other, core, axis):
    return jnp.concatenate(
        [jnp.where(core == 0, mine, other), jnp.where(core == 0, other, mine)], axis=axis
    )


def assemble_kernel(heights, widths, place_ref, *refs):
    pieces, outs, sems = refs[:10], refs[10:-1], refs[-1]
    plane, depth, core = place_ref[0], place_ref[1], place_ref[2]
    slots = ((0, 0, 4), (1, 0, 4), (2, 0, 4), (3, 0, 2), (3, 2, 2))
    copies = []
    for side in range(2):
        column = core if side == 0 else 1 - core
        for number, (turn, first, count) in enumerate(slots):
            piece = pieces[5 * side + number]
            for slot in range(count):
                chip = (plane ^ turn) * 4 + ((depth + 4 - first - slot) & 3)
                start = 0
                for out, height, width in zip(outs, heights, widths):
                    for group in range(height // 48):
                        row = pl.multiple_of(chip * height + 48 * group, 48)
                        lane = pl.multiple_of(column * width, 128)
                        copies.append(
                            pltpu.make_async_copy(
                                piece.at[slot, :, pl.ds(start, width)],
                                out.at[pl.ds(row, 48), pl.ds(lane, width)],
                                sems.at[len(copies)],
                            )
                        )
                        start += width
    for copy in copies:
        copy.start()
    for copy in copies:
        copy.wait()


def gather_links(shards, gate, gates):
    plane, depth, core = place_here()
    rows = min(shard.shape[0] for shard in shards)
    mine = jnp.concatenate([fold_rows(half_cols(shard, core), rows) for shard in shards], axis=1)
    sent = jnp.concatenate(
        [fold_rows(half_cols(shard, 1 - core), rows) for shard in shards], axis=1
    )
    other = over_core(sent)
    widths = [shard.shape[1] // 2 for shard in shards]
    heights = [2 * shard.shape[0] for shard in shards]
    slab, start = [], 0
    for width, height in zip(widths, heights):
        span = width * (height // (2 * rows))
        pair = [unfold_cols(part[:, start : start + span], width) for part in (mine, other)]
        slab.append(fold_rows(both_cores(pair[0], pair[1], core, 0), 2 * rows))
        start += span
    slab = jnp.concatenate(slab, axis=1)
    line = jnp.stack([slab] + [over_z(slab, step) for step in (1, 2, 3)])
    gates.append(slab)
    line = after(gate, line)
    line_x, line_y = over_x(line), over_y(line)
    pieces = [line, line_x, line_y, over_y(line_x[:2]), over_x(line_y[2:])]
    pieces = pieces + [over_core(piece) for piece in pieces]
    count = 32 * sum(height // 48 for height in heights)
    place = jnp.stack([plane, depth, core]).astype(jnp.int32)
    return pl.pallas_call(
        partial(assemble_kernel, heights, widths),
        out_shape=[
            jax.ShapeDtypeStruct((16 * height, 2 * width), jnp.bfloat16)
            for height, width in zip(heights, widths)
        ],
        in_specs=[pl.BlockSpec(memory_space=pltpu.SMEM)]
        + [pl.BlockSpec(memory_space=pl.ANY)] * 10,
        out_specs=[pl.BlockSpec(memory_space=pltpu.VMEM)] * len(shards),
        scratch_shapes=[pltpu.SemaphoreType.DMA((count,))],
        compiler_params=pltpu.CompilerParams(vmem_limit_bytes=60 << 20),
        name="assemble",
    )(place, *pieces)


def after(first, *later):
    tied = lax.optimization_barrier((first, later))[1]
    return tied[0] if len(tied) == 1 else tied


def first_hops(line, gate):
    core = place_here()[2]
    half = line.shape[0] // 2
    mine = after(gate, lax.dynamic_slice_in_dim(line, core * half, half, axis=0))
    return line, over_x(mine), over_y(mine)


def last_hops(hops, gate):
    line, from_x, from_y = hops
    half = from_x.shape[0] // 2
    sent_y, sent_x = after(gate, from_x[:half], from_y[half:])
    pieces = [from_x, from_y, over_y(sent_y), over_x(sent_x)]
    return [line] + pieces + [over_core(piece) for piece in pieces]


def late_pieces(shard):
    half = shard.shape[0] // 2
    from_x, from_y = over_x(shard), over_y(shard)
    across = jnp.concatenate([over_y(from_x[:half]), over_x(from_y[half:])], axis=0)
    rows = jnp.concatenate([shard, from_x, from_y, across], axis=0)
    return [lax.all_gather(rows, "fsdp", axis=0, tiled=True)]


def join_kernel(all_moves, all_widths, counts, place_ref, *refs):
    total = sum(counts)
    pieces, outs, sems = refs[:total], refs[total:-1], refs[-1]
    waits, first, start, number = [], 0, 0, 0
    for moves, widths, count in zip(all_moves, all_widths, counts):
        targets = outs[number : number + len(widths)]
        waits += start_moves(
            pieces[start : start + count], targets, widths, moves, place_ref, sems, first
        )
        first += len(moves) * len(widths)
        start += count
        number += len(widths)
    for copies in waits:
        wait_all(copies)


def join_pieces(groups, all_widths):
    plane, depth, core = place_here()
    place = jnp.stack([plane, depth, core]).astype(jnp.int32)
    all_moves = [mid_moves_of(pieces) for pieces in groups]
    shapes = [
        jax.ShapeDtypeStruct((4 * pieces[0].shape[0], width), jnp.bfloat16)
        for pieces, widths in zip(groups, all_widths)
        for width in widths
    ]
    sems = sum(len(moves) * len(widths) for moves, widths in zip(all_moves, all_widths))
    pieces = [piece for group in groups for piece in group]
    joined = pl.pallas_call(
        partial(join_kernel, all_moves, all_widths, [len(group) for group in groups]),
        out_shape=shapes,
        in_specs=[pl.BlockSpec(memory_space=pltpu.SMEM)]
        + [pl.BlockSpec(memory_space=pl.ANY)] * len(pieces),
        out_specs=[pl.BlockSpec(memory_space=pltpu.VMEM)] * len(shapes),
        scratch_shapes=[pltpu.SemaphoreType.DMA((sems,))],
        compiler_params=pltpu.CompilerParams(vmem_limit_bytes=60 << 20),
        name="join",
    )(place, *pieces)
    return list(joined)


def along_z(shards):
    return lax.all_gather(jnp.concatenate(shards, axis=1), "fsdp", axis=0, tiled=True)


def start_moves(pieces, outs, widths, moves, place_ref, sems, first):
    plane, core = place_ref[0], place_ref[2]
    groups, start = [], 0
    for out, width in zip(outs, widths):
        copies = []
        for piece, source, rows, turn, quarter, side, offset in moves:
            row = (plane ^ turn) * quarter + offset
            if side is not None:
                row = row + (core if side == 0 else 1 - core) * (quarter // 2)
            copies.append(
                pltpu.make_async_copy(
                    pieces[piece].at[source : source + rows, start : start + width],
                    out.at[pl.ds(pl.multiple_of(row, 48), rows), :],
                    sems.at[first],
                )
            )
            first += 1
        start += width
        groups.append(copies)
    for copies in groups:
        for copy in copies:
            copy.start()
    return groups


def wait_all(copies):
    for copy in copies:
        copy.wait()


def column_sums(rows):
    return jnp.sum(rows, axis=0, keepdims=True)


def feed_rows_back(grad, unit, spread, slope_of, reduce_ref, expand_ref, final_gain):
    second = norm_back(grad * final_gain, unit, spread)
    branch = second.astype(LOW)
    normed, hidden = second, []
    for start in range(0, expand_ref.shape[1], D):
        span = slice(start, start + D)
        part = (back_cols(branch, reduce_ref[span, :]) * slope_of(span)).astype(LOW)
        hidden.append(part)
        normed = normed + back_cols(part, expand_ref[:, span])
    return branch, hidden, normed


def heads_kernel(
    counts,
    mid_moves,
    end_moves,
    place_ref,
    count_ref,
    heads_ref,
    wide_heads_ref,
    table_ref,
    cotangent_ref,
    attend_bias_ref,
    expand_bias_ref,
    vectors_ref,
    inner_vectors_ref,
    *refs,
):
    mid_count, end_count = counts
    mid, refs = refs[:mid_count], refs[mid_count:]
    end, refs = refs[:end_count], refs[end_count:]
    inner_hbm, refs = refs[:3], refs[3:]
    out_ref, grad_ref, left_ref, right_ref, sums_ref = refs[:5]
    branch_ref, hidden_ref, attn_ref, context_ref, first_ref, inner_sums_ref, hidden_sums_ref = refs[5:12]
    attend_ref, merge_ref, expand_ref, reduce_ref = refs[12:16]
    inner_refs, sems = refs[16:19], refs[19]
    wide = expand_ref.shape[1]
    waits = start_moves(
        mid, (attend_ref, merge_ref, expand_ref), (3 * D, D, wide), mid_moves, place_ref, sems, 0
    )
    first_free = 3 * len(mid_moves)
    waits += start_moves(end, (reduce_ref,), (D,), end_moves, place_ref, sems, first_free)
    first_free += len(end_moves)
    inner_waits = [
        pltpu.make_async_copy(source, target, sems.at[first_free + number])
        for number, (source, target) in enumerate(zip(inner_hbm, inner_refs))
    ]
    for copy in inner_waits:
        copy.start()
    merge_bias, gain, shift, reduce_bias, final_gain, final_shift = [
        vectors_ref[row : row + 1, :] for row in range(6)
    ]
    scale = HD ** (-0.5)
    stacked = HEADS * SEGS
    own = (
        lax.broadcasted_iota(jnp.int32, (stacked, D), 1) // HD
        == lax.broadcasted_iota(jnp.int32, (stacked, D), 0) // SEGS
    )

    def by_head(rows):
        return jnp.where(own, jnp.concatenate([rows] * HEADS, axis=0), 0.0).astype(LOW)

    def join_heads(rows):
        rows = jnp.where(own, rows, 0.0)
        return sum(rows[SEGS * head : SEGS * (head + 1)] for head in range(HEADS))

    keep = (
        lax.broadcasted_iota(jnp.int32, (SEGS, 1), 0) * SEG < count_ref[0]
    ).astype(F32)
    source = (heads_ref[:, :D] + table_ref[...]).astype(LOW)
    wait_all(waits[0])
    projected = (dot_nn(source, attend_ref[...]) + attend_bias_ref[...]).astype(LOW)
    query, key, value = projected[:, :D], projected[:, D : 2 * D], projected[:, 2 * D :]
    queries = by_head(query.astype(F32))
    scores = back_cols(queries, key) * scale
    weight = jnp.exp(scores - jnp.max(scores, axis=-1, keepdims=True))
    probs = weight / jnp.sum(weight, axis=-1, keepdims=True)
    probs_low = probs.astype(LOW)
    context = join_heads(dot_nn(probs_low, value)).astype(LOW)
    wait_all(waits[1])
    first = source.astype(F32) + dot_nn(context, merge_ref[...]) + merge_bias
    first_unit, first_spread = centre_rows(first)
    normed = (first_unit * gain + shift).astype(LOW)
    left_ref[:, :D] = source
    left_ref[:, D : 2 * D] = context
    left_ref[:, 2 * D : 3 * D] = normed
    second = normed.astype(F32) + reduce_bias
    slopes = {}
    wait_all(waits[2])
    wait_all(waits[3])
    for start in range(0, wide, D):
        span = slice(start, start + D)
        active, slopes[start] = gelu_pair(
            dot_nn(normed, expand_ref[:, span]) + expand_bias_ref[:, span]
        )
        active = active.astype(LOW)
        left_ref[:, 3 * D + start : 4 * D + start] = active
        second = second + dot_nn(active, reduce_ref[span, :])
    unit, spread = centre_rows(second)
    out_ref[...] = (unit * final_gain + final_shift) * keep
    grad = cotangent_ref[...].astype(F32) * keep
    sums = [column_sums(grad * unit), column_sums(grad)]
    branch, hidden, grad_normed = feed_rows_back(
        grad, unit, spread, lambda span: slopes[span.start], reduce_ref, expand_ref, final_gain
    )
    sums += [column_sums(grad_normed * first_unit), column_sums(grad_normed)]
    grad_first = norm_back(grad_normed * gain, first_unit, first_spread)
    attn = grad_first.astype(LOW)
    grads = by_head(back_cols(attn, merge_ref[...]).astype(LOW).astype(F32))
    grad_probs = back_cols(grads, value)
    total = jnp.sum(grad_probs * probs, axis=-1, keepdims=True)
    grad_scores = (probs * (grad_probs - total)).astype(LOW)
    grad_query = (join_heads(dot_nn(grad_scores, key)) * scale).astype(LOW)
    grad_key = (cross_rows(grad_scores, queries) * scale).astype(LOW)
    grad_value = cross_rows(probs_low, grads).astype(LOW)
    grad_projected = jnp.concatenate([grad_query, grad_key, grad_value], axis=1)
    right_ref[:, : 3 * D] = grad_projected
    right_ref[:, 3 * D : 4 * D] = attn
    for number, part in enumerate(hidden):
        right_ref[:, (4 + number) * D : (5 + number) * D] = part
    right_ref[:, 4 * D + wide :] = branch
    sums_ref[...] = jnp.concatenate(sums + [jnp.zeros((4, D), F32)], axis=0)
    grad = grad_first + back_cols(grad_projected, attend_ref[...])
    grad_ref[...] = grad

    wait_all(inner_waits)
    inner_merge_ref, inner_expand_ref, inner_reduce_ref = inner_refs
    gain, final_gain = inner_vectors_ref[1:2, :], inner_vectors_ref[4:5, :]
    first_unit, first_spread = centre_rows(heads_ref[:, D : 2 * D])
    unit, spread = centre_rows(heads_ref[:, 2 * D : 3 * D])
    sums = [column_sums(grad * unit), column_sums(grad)]
    branch, hidden, grad_normed = feed_rows_back(
        grad,
        unit,
        spread,
        lambda span: wide_heads_ref[:, span],
        inner_reduce_ref,
        inner_expand_ref,
        final_gain,
    )
    branch_ref[...] = branch
    sums.append(column_sums(branch.astype(F32)))
    for number, part in enumerate(hidden):
        span = slice(number * D, (number + 1) * D)
        hidden_ref[:, span] = part
        hidden_sums_ref[:, span] = column_sums(part.astype(F32))
    sums += [column_sums(grad_normed * first_unit), column_sums(grad_normed)]
    grad_first = norm_back(grad_normed * gain, first_unit, first_spread)
    first_ref[...] = grad_first
    attn = grad_first.astype(LOW)
    attn_ref[...] = attn
    sums.append(column_sums(attn.astype(F32)))
    context_ref[...] = back_cols(attn, inner_merge_ref[...]).astype(LOW).astype(F32)
    inner_sums_ref[...] = jnp.concatenate(sums + [jnp.zeros((2, D), F32)], axis=0)


def mid_moves_of(pieces):
    if len(pieces) == 1:
        return [(0, 0, pieces[0].shape[0], 0, 0, None, 0)]
    quarter = pieces[0].shape[0]
    half = quarter // 2
    moves = [(0, 0, quarter, 0, quarter, None, 0)]
    for side in range(2):
        moves += [
            (1 + 4 * side, 0, half, 1, quarter, side, 0),
            (2 + 4 * side, 0, half, 2, quarter, side, 0),
            (3 + 4 * side, 0, half // 2, 3, quarter, side, 0),
            (4 + 4 * side, 0, half // 2, 3, quarter, side, half // 2),
        ]
    return moves


def late_moves_of(piece, linked):
    if not linked:
        return [(0, 0, piece.shape[0], 0, 0, None, 0)]
    rows = piece.shape[0] // 32
    return [
        (0, (4 * slot + turn) * rows, rows, turn, 8 * rows, None, slot * rows)
        for slot in range(8)
        for turn in range(4)
    ]


def heads_step(counts, heads, wide_heads, table, cotangent, small, mid, late, inner, linked):
    attend_bias, expand_bias, vectors, inner_vectors = small
    wide = expand_bias.shape[1]
    mid_moves, end_moves = mid_moves_of(mid), late_moves_of(late, linked)
    plane, depth, core = place_here()
    place = jnp.stack([plane, depth, core]).astype(jnp.int32)
    vmem = pl.BlockSpec(memory_space=pltpu.VMEM)
    smem = pl.BlockSpec(memory_space=pltpu.SMEM)
    outs = [
        ((SEGS, D), F32),
        ((SEGS, D), F32),
        ((SEGS, 3 * D + wide), LOW),
        ((SEGS, 5 * D + wide), LOW),
        ((8, D), F32),
        ((SEGS, D), LOW),
        ((SEGS, wide), LOW),
        ((SEGS, D), LOW),
        ((SEGS, D), F32),
        ((SEGS, D), F32),
        ((8, D), F32),
        ((1, wide), F32),
    ]
    flops = 6 * SEGS * D * (5 * D + 4 * wide)
    moved = 2 * D * (6 * D + 4 * wide)
    return pl.pallas_call(
        partial(heads_kernel, (len(mid), 1), mid_moves, end_moves),
        out_shape=[jax.ShapeDtypeStruct(shape, kind) for shape, kind in outs],
        in_specs=[smem, smem] + [vmem] * 8 + [pl.BlockSpec(memory_space=pl.ANY)] * (len(mid) + 4),
        out_specs=[vmem] * len(outs),
        scratch_shapes=[
            pltpu.VMEM((D, 3 * D), LOW),
            pltpu.VMEM((D, D), LOW),
            pltpu.VMEM((D, wide), LOW),
            pltpu.VMEM((wide, D), LOW),
            pltpu.VMEM((D, D), LOW),
            pltpu.VMEM((D, wide), LOW),
            pltpu.VMEM((wide, D), LOW),
            pltpu.SemaphoreType.DMA((3 * len(mid_moves) + len(end_moves) + 3,)),
        ],
        compiler_params=pltpu.CompilerParams(vmem_limit_bytes=60 << 20),
        cost_estimate=pl.CostEstimate(flops=flops, bytes_accessed=moved, transcendentals=0),
        name="heads",
    )(
        place,
        counts,
        heads,
        wide_heads,
        table,
        cotangent,
        attend_bias,
        expand_bias,
        vectors,
        inner_vectors,
        *mid,
        late,
        *inner,
    )


def scatter_pack(grads):
    core = place_here()[2]

    def packed(side):
        return jnp.concatenate(
            [
                jnp.transpose(
                    half_cols(grad, side).reshape(16, grad.shape[0] // 768, 48, -1), (0, 2, 1, 3)
                ).reshape(16, 48, -1)
                for grad in grads
            ],
            axis=2,
        )

    return packed(core), packed(1 - core)


def scatter_core(kept, sent):
    plane = place_here()[0]
    kept = (kept + over_core(sent)).reshape(4, 4, 48, -1)
    return [
        lax.dynamic_index_in_dim(kept, plane ^ turn, axis=0, keepdims=False)
        for turn in range(4)
    ]


def scatter_across(planes):
    here, next_x, next_y, across = planes
    from_y, from_x = over_y(across[:2]), over_x(across[2:])
    next_x = jnp.concatenate([next_x[:2] + from_y, next_x[2:]], axis=0)
    next_y = jnp.concatenate([next_y[:2], next_y[2:] + from_x], axis=0)
    return here, next_x, next_y


def scatter_next(here, next_x, next_y):
    came_x, came_y = over_x(next_x), over_y(next_y)
    return (
        here.astype(jnp.float32) + came_x.astype(jnp.float32) + came_y.astype(jnp.float32)
    ).astype(jnp.bfloat16)


def scatter_line(here):
    depth = place_here()[1]
    slabs = [
        lax.dynamic_index_in_dim(here, (depth + step) & 3, axis=0, keepdims=False)
        for step in range(4)
    ]
    total = slabs[0].astype(jnp.float32)
    for step in (1, 2, 3):
        total = total + over_z(slabs[step], step).astype(jnp.float32)
    return total


def scatter_end(total, shapes):
    core = place_here()[2]
    mine, sent, start = [], [], 0
    for height, width in shapes:
        width = width // 2
        groups = height // 768
        rows = unfold_cols(total[:, start : start + groups * width], width)
        start += groups * width
        mine.append(fold_rows(lax.dynamic_slice_in_dim(rows, core * 24 * groups, 24 * groups), 24))
        sent.append(
            fold_rows(lax.dynamic_slice_in_dim(rows, (1 - core) * 24 * groups, 24 * groups), 24)
        )
    other = over_core(jnp.concatenate(sent, axis=1))
    owned, start = [], 0
    for (height, width), part in zip(shapes, mine):
        width = width // 2
        pair = [unfold_cols(side, width) for side in (part, other[:, start : start + part.shape[1]])]
        owned.append(both_cores(pair[0], pair[1], core, 1))
        start += part.shape[1]
    return owned


def unfold(packed, parts, ratio):
    width = packed.shape[1] // ratio
    return jnp.stack(
        [
            packed[:, width * group : width * (group + 1)].reshape(-1, parts, width)
            for group in range(ratio)
        ],
        axis=1,
    ).reshape(-1, width)


def gather_flat(shards):
    parts = min(shard.shape[0] for shard in shards)
    pieces = split_cols(
        gather(jnp.concatenate([fold_rows(shard, parts) for shard in shards], axis=1)),
        [shard.size // parts for shard in shards],
    )
    return [
        unfold(piece, parts, shard.shape[0] // parts) if shard.shape[0] > parts else piece
        for piece, shard in zip(pieces, shards)
    ]


def scatter_flat(grads):
    devices = lax.axis_size(AXES)
    parts = min(grad.shape[0] for grad in grads) // devices
    packed = jnp.concatenate(
        [
            jnp.transpose(grad.reshape(devices, -1, parts, grad.shape[1]), (0, 2, 1, 3)).reshape(
                devices * parts, -1
            )
            for grad in grads
        ],
        axis=1,
    )
    owned = split_cols(
        scatter(packed).astype(jnp.float32), [grad.size // (devices * parts) for grad in grads]
    )
    return [unfold_cols(piece, grad.shape[1]) for piece, grad in zip(owned, grads)]


def on_device(
    tokens,
    counts,
    inner_attend,
    inner_attend_bias,
    inner_merge,
    inner_merge_bias,
    inner_gain,
    inner_shift,
    inner_expand,
    inner_expand_bias,
    inner_reduce,
    inner_reduce_bias,
    inner_final_gain,
    inner_final_shift,
    outer_attend,
    outer_attend_bias,
    outer_merge,
    outer_merge_bias,
    outer_gain,
    outer_shift,
    outer_expand,
    outer_expand_bias,
    outer_reduce,
    outer_reduce_bias,
    outer_final_gain,
    outer_final_shift,
    segment_place,
    cotangent,
):
    parts = inner_merge.shape[0]
    devices = D // parts
    ratio = inner_reduce.shape[0] // parts
    here = lax.axis_index(AXES)
    (
        attend_bias,
        expand_bias,
        vectors,
        outer_attend_bias_full,
        outer_expand_bias_full,
        outer_vectors,
        place_rows,
    ) = share_small(
        (
            inner_attend_bias,
            inner_merge_bias,
            inner_gain,
            inner_shift,
            inner_expand_bias,
            inner_reduce_bias,
            inner_final_gain,
            inner_final_shift,
            outer_attend_bias,
            outer_merge_bias,
            outer_gain,
            outer_shift,
            outer_expand_bias,
            outer_reduce_bias,
            outer_final_gain,
            outer_final_shift,
        ),
        segment_place,
    )
    linked = lax.axis_size("dp") == 4 and lax.axis_size("fsdp") == 8
    wide = inner_expand.shape[1]
    inner_rest = [inner_merge, inner_expand, inner_reduce]
    outer_all = [outer_attend, outer_merge, outer_expand, outer_reduce]
    docs = counts.shape[0]
    head_cotangent = cotangent.reshape(docs * SEGS, SEG, D)[:, 0, :]
    if linked:
        gates = []
        inner_full = list(gather_links([inner_attend], place_rows, gates))
        mid_line = along_z(after(gates[0], *inner_rest[:2]))
        end_line = along_z([after(gates[0], inner_rest[2])])
        outer_line = along_z(after(gates[0], *outer_all[:3]))
        projected, context = inner_attention(tokens, counts, inner_full[0], attend_bias)
        mid = first_hops(mid_line, inner_full[0])
        end = first_hops(end_line, (context, mid[1], mid[2]))
        mid = last_hops(mid, context)
        end = last_hops(end, (mid[3], mid[4]))
        outer = first_hops(outer_line, (mid[3], mid[4], end[1], end[2]))
        late = late_pieces(after(context, outer_reduce))
        inner_full += join_pieces([mid, end], [[D, wide], [D]])
    else:
        inner_full = gather_flat([inner_attend]) + gather_flat(inner_rest)
        projected, context = inner_attention(tokens, counts, inner_full[0], attend_bias)
    inner_weights = (*inner_full, expand_bias, vectors)
    mixed, heads, wide_heads, saved = inner_feed(tokens, counts, projected, context, inner_weights)
    if linked:
        outer = last_hops(outer, heads)
    else:
        outer_full = gather_flat(outer_all)
        outer, late = [jnp.concatenate(outer_full[:3], axis=1)], outer_full[3:]
    branch, grad_hidden, grad_attn, grad_context, grad_first, inner_sums, hidden_sums = (
        inner_feed_back(cotangent, counts, saved, inner_weights)
    )
    first, normed, active, slope, second = saved
    low = jnp.bfloat16
    plain_grads = lax.optimization_barrier(
        (
            cross_rows(active, branch).astype(low),
            cross_rows(normed, grad_hidden).astype(low),
            cross_rows(context, grad_attn).astype(low),
        )
    )
    (
        head_out,
        grad_heads,
        left_pack,
        right_pack,
        outer_sums,
        head_branch,
        head_hidden,
        head_attn,
        head_context,
        head_first,
        head_sums,
        head_hidden_sums,
    ) = heads_step(
        counts,
        heads,
        wide_heads,
        place_rows,
        head_cotangent,
        (outer_attend_bias_full, outer_expand_bias_full, outer_vectors, vectors),
        outer,
        late[0],
        inner_full[1:],
        linked,
    )
    grad_place = jnp.transpose(jnp.sum(grad_heads.reshape(docs, SEGS, D), axis=0))
    inner_sums = inner_sums + head_sums
    hidden_sums = hidden_sums + head_hidden_sums
    grad_reduce, grad_expand, grad_merge = [
        (plain.astype(jnp.float32) + cross_rows(left.astype(low), right)).astype(low)
        for plain, left, right in zip(
            plain_grads,
            (wide_heads[:, wide:], heads[:, 3 * D : 4 * D], heads[:, 4 * D :]),
            (head_branch, head_hidden, head_attn),
        )
    ]
    operands = (projected, grad_context, grad_first, mixed)
    head_rows = (head_context, head_first, head_out)
    steps = tokens.shape[0] // ROWS
    if linked:
        kept, sent = scatter_pack([grad_expand, grad_reduce])
        operands = after(sent, *operands)
        part = inner_attend_back(counts, operands, inner_full[0], head_rows, 0, steps // 2, ())
        planes = scatter_core(kept, sent)
        operands = after(planes, *operands)
        rest = inner_attend_back(
            counts, operands, inner_full[0], head_rows, steps // 2, steps - steps // 2, part[:3]
        )
        grad_projected, tokens_grad, mixed = rest[:3]
        attend_sums = part[3] + rest[3]
        tall = scatter_across(planes)
        tall = scatter_next(*tall)
        grad_attend = cross_rows(tokens, grad_projected).astype(low)
        planes = scatter_core(*scatter_pack([grad_attend, grad_merge]))
        tall = scatter_line(tall)
        short = scatter_next(*scatter_across(planes))
        short = scatter_line(short)
        own_expand, own_reduce = scatter_end(tall, [grad_expand.shape, grad_reduce.shape])
        own_attend, own_merge = scatter_end(short, [grad_attend.shape, grad_merge.shape])
    else:
        grad_projected, tokens_grad, mixed, attend_sums = inner_attend_back(
            counts, operands, inner_full[0], head_rows, 0, steps, ()
        )
        grad_attend = cross_rows(tokens, grad_projected).astype(low)
        own_expand, own_reduce = scatter_flat([grad_expand, grad_reduce])
        own_attend, own_merge = scatter_flat([grad_attend, grad_merge])
    left_pack = jnp.concatenate(
        [
            factor.reshape(factor.shape[0], devices, -1)
            for factor in split_cols(left_pack, (D, D, D, wide))
        ],
        axis=2,
    )
    left_pack = jnp.transpose(left_pack, (1, 0, 2))
    left_all = lax.all_to_all(left_pack, AXES, split_axis=0, concat_axis=0, tiled=True)
    left_all = left_all.reshape(-1, left_all.shape[-1])
    right_all = gather(right_pack)
    left_pieces = split_cols(left_all, (parts, parts, parts, parts * ratio))
    right_pieces = split_cols(right_all, (3 * D, D, wide, D))
    outer_big = [cross_rows(left, right) for left, right in zip(left_pieces, right_pieces)]
    outer_bias = [
        lax.dynamic_slice_in_dim(
            jnp.sum(right.astype(jnp.float32), axis=0), here * width, width, axis=0
        )
        for right, width in zip(
            right_pieces, (3 * parts, parts, wide // devices, parts)
        )
    ]
    row_sums = (
        attend_sums,
        inner_sums[5],
        inner_sums[3],
        inner_sums[4],
        hidden_sums,
        inner_sums[2],
        inner_sums[0],
        inner_sums[1],
        outer_sums[2],
        outer_sums[3],
        outer_sums[0],
        outer_sums[1],
        grad_place,
    )
    sums = sum_rows(jnp.concatenate([entry.reshape(devices, -1) for entry in row_sums], axis=1))
    sums = split_cols(sums, [entry.size // devices for entry in row_sums])
    return (
        mixed,
        tokens_grad,
        own_attend,
        sums[0],
        own_merge,
        sums[1],
        sums[2],
        sums[3],
        own_expand,
        sums[4],
        own_reduce,
        sums[5],
        sums[6],
        sums[7],
        outer_big[0],
        outer_bias[0],
        outer_big[1],
        outer_bias[1],
        sums[8],
        sums[9],
        outer_big[2],
        outer_bias[2],
        outer_big[3],
        outer_bias[3],
        sums[10],
        sums[11],
        sums[12].reshape(parts, SEGS),
    )


def solution(mesh):
    return jax.shard_map(
        on_device,
        mesh=mesh,
        in_specs=(
            P(("dp", "fsdp"), None),
            P(("dp", "fsdp")),
            P(("dp", "fsdp"), None),
            P(("dp", "fsdp")),
            P(("dp", "fsdp"), None),
            P(("dp", "fsdp")),
            P(("dp", "fsdp")),
            P(("dp", "fsdp")),
            P(("dp", "fsdp"), None),
            P(("dp", "fsdp")),
            P(("dp", "fsdp"), None),
            P(("dp", "fsdp")),
            P(("dp", "fsdp")),
            P(("dp", "fsdp")),
            P(("dp", "fsdp"), None),
            P(("dp", "fsdp")),
            P(("dp", "fsdp"), None),
            P(("dp", "fsdp")),
            P(("dp", "fsdp")),
            P(("dp", "fsdp")),
            P(("dp", "fsdp"), None),
            P(("dp", "fsdp")),
            P(("dp", "fsdp"), None),
            P(("dp", "fsdp")),
            P(("dp", "fsdp")),
            P(("dp", "fsdp")),
            P(("dp", "fsdp"), None),
            P(("dp", "fsdp"), None),
        ),
        out_specs=(
            P(("dp", "fsdp"), None),
            P(("dp", "fsdp"), None),
            P(("dp", "fsdp"), None),
            P(("dp", "fsdp")),
            P(("dp", "fsdp"), None),
            P(("dp", "fsdp")),
            P(("dp", "fsdp")),
            P(("dp", "fsdp")),
            P(("dp", "fsdp"), None),
            P(("dp", "fsdp")),
            P(("dp", "fsdp"), None),
            P(("dp", "fsdp")),
            P(("dp", "fsdp")),
            P(("dp", "fsdp")),
            P(("dp", "fsdp"), None),
            P(("dp", "fsdp")),
            P(("dp", "fsdp"), None),
            P(("dp", "fsdp")),
            P(("dp", "fsdp")),
            P(("dp", "fsdp")),
            P(("dp", "fsdp"), None),
            P(("dp", "fsdp")),
            P(("dp", "fsdp"), None),
            P(("dp", "fsdp")),
            P(("dp", "fsdp")),
            P(("dp", "fsdp")),
            P(("dp", "fsdp"), None),
        ),
        check_vma=False,
    )
```

time: 552 us -> 483 us (0.88)
  Pallas kernels: 7.18 us -> 140 us
  matrix products: 145 us -> 41.8 us
  local copies, waits for them, and re-layouts: 77.1 us -> 40.7 us
  waiting for transfers between devices: 167 us -> 137 us
  other arithmetic: 60.2 us -> 34.2 us
    pallas_call x0 -> x9, Pallas kernels: none -> 136 us  [the longest x5 105 us: row_call(): pl.pallas_call(kernel, grid=(rows // ROWS if steps is None else steps,),...]
    dot_general x27 -> x0, matrix products: 113 us -> none  [the longest x8 40 us: back_cols(): lax.dot_general(left_rows, right_rows, (((1,), (1,)), ((), ())), preferre...]
    ppermute x44 -> x59, waiting for transfers between devices: 167 us -> 136 us  [hop(): lax.ppermute(array, AXES, [(place, turn(place)) for place in range(32)])]
    reduce_sum x16 -> x0, other arithmetic: 15.8 us -> none  [the longest x5 5.54 us: norm_apply(): return centred * lax.rsqrt(spread + 1e-05) * norm_gain + norm_shift]
    convert_element_type x22 -> x0, local copies, waits for them, and re-layouts: 14.9 us -> none  [the longest x2 9.35 us: block_backward(): grad_projected.reshape(groups * length, 3 * row_width).astype(jnp.bfloat16)]
    all_to_all x1, starting transfers between devices: 14.9 us -> 3.07 us  [sum_rows(): got = lax.all_to_all(padded, AXES, split_axis=0, concat_axis=0, tiled=True)]
    dot_general x8 -> x11, matrix products: 32.3 us -> 41.8 us  [cross_rows(): lax.dot_general(left_rows, right_rows, (((0,), (0,)), ((), ())), preferre...]
    unnamed x223 -> x121, local copies, waits for them, and re-layouts: 23.3 us -> 14.5 us
  transfers between devices with their start and end apart: 49 -> 67, of which waited for: 22 -> 31; matrix products, arithmetic and copies ran while one was open for 28% -> 18% of each run, Pallas kernels for 1% -> 26%
where the time goes in v3:
time: 483 us; the launch traced here: 475 us
  Pallas kernels  140 us (29%)
  waiting for transfers between devices  137 us (28%)
  starting transfers between devices  65.8 us (14%)
  matrix products  41.8 us (9%)
  local copies, waits for them, and re-layouts  40.7 us (8%)
  other arithmetic  34.2 us (7%)
  between operations  15.9 us (3%)
    ppermute x59, waiting for transfers between devices, hop(): lax.ppermute(array, AXES, [(place, turn(place)) for place in range(32)])  136 us
    pallas_call x5, Pallas kernels, row_call(): pl.pallas_call(kernel, grid=(rows // ROWS if steps is None else steps,),...  105 us
    ppermute x59, starting transfers between devices, hop(): lax.ppermute(array, AXES, [(place, turn(place)) for place in range(32)])  49.1 us
    dot_general x11, matrix products, cross_rows(): lax.dot_general(left_rows, right_rows, (((0,), (0,)), ((), ())), preferre...  41.8 us
    pallas_call x1, Pallas kernels, heads_step(): pl.pallas_call(partial(heads_kernel, (len(mid), 1), mid_moves, end_moves)...  17.1 us
    unnamed x121, local copies, waits for them, and re-layouts  14.5 us
  transfers between devices with their start and end apart: 67, of which 31 were waited for; matrix products, arithmetic and copies ran while one was open for 18% of the time, Pallas kernels for 26%

profile of v3, /device:TPU:0, one launch (start us, length us, event | category | flops | bytes accessed | tf_op | source)
XLA Modules:
  0.0 475.4 jit_solution(5557596064204327563)
XLA Ops:
  17.5 7.2 %all-to-all-start = ((bf16[32,32,128]{2,1,0:T(8,128)(2,1)}), bf16[32,32,128]{2,1,0:T(8,128)(2,1)S(1)}, u32[]{:S(2)}, u32[]{:S(2)}) async-start(bf16[32,32,128]{2,1,0:T(8,128)(2,1)} %pack.1), calls=%async_computation | async-start | bytes 524288 | tf_op jit(solution)/shard_map/all_to_all | solution.py:475
  24.7 3.7 collective-permute-start.3
  29.5 12.6 %collective-permute-done.3 = bf16[48,1152]{1,0:T(8,128)(2,1)S(1)} collective-permute-done((bf16[48,1152]{1,0:T(8,128)(2,1)S(1)}, bf16[48,1152]{1,0:T(8,128)(2,1)S(1)}, u32[]{:S(2)}, u32[]{:S(2)}) %collective-permute-start.3) | collective-permute-done | bytes 110624 | tf_op jit(solution)/shard_map/ppermute | solution.py:497
  42.1 10.7 %collective-permute-done.2 = bf16[48,1152]{1,0:T(8,128)(2,1)S(1)} collective-permute-done((bf16[48,1152]{1,0:T(8,128)(2,1)S(1)}, bf16[48,1152]{1,0:T(8,128)(2,1)S(1)}, u32[]{:S(2)}, u32[]{:S(2)}) %collective-permute-start.2) | collective-permute-done | bytes 110624 | tf_op jit(solution)/shard_map/ppermute | solution.py:497
  53.6 3.2 unpack.1
  59.8 9.2 %collective-permute-done.5.refs_2_ = bf16[4,48,1152]{2,1,0:T(8,128)(2,1)S(1)} collective-permute-done((bf16[4,48,1152]{2,1,0:T(8,128)(2,1)S(1)}, bf16[4,48,1152]{2,1,0:T(8,128)(2,1)S(1)}, u32[]{:S(2)}, u32[]{:S(2)}) %collective-permute-start.5) | collective-permute-done | bytes 442400 | tf_op jit(solution)/shard_map/ppermute | solution.py:497
  72.6 3.1 collective-permute-done.7.refs_4_
  80.1 4.8 %assemble.1.attend_ref = bf16[768,2304]{1,0:T(8,128)(2,1)} custom-call(s32[3]{0:T(128)} %pad_add_fusion.place_ref, bf16[4,48,1152]{2,1,0:T(8,128)(2,1)} %copy-done.5, bf16[4,48,1152]{2,1,0:T(8,128)(2,1)} %copy-done.18, bf16[4,48,1152]{2,1,0:T(8,128)(2,1)} %copy-done.17, bf16[2,48,1152]{2,1,0:T(8,128)(2,1)} %copy-done.30, bf16[2,48,1152]{2,1,0:T(8,128)(2,1)} %copy-done.29, ...), custom_call_target="tpu_custom_call" | custom-call | tf_op jit(solution)/shard_map/assemble/pallas_call | solution.py:595
  84.9 12.8 %attend.1 = (bf16[1024,2304]{1,0:T(8,128)(2,1)}, bf16[1024,768]{1,0:T(8,128)(2,1)}) custom-call(s32[1]{0:T(128)S(6)} %copy.94.count_ref, bf16[1024,768]{1,0:T(8,128)(2,1)} %rows_ref.3, bf16[768,2304]{1,0:T(8,128)(2,1)} %assemble.1.attend_ref, f32[1,2304]{1,0:T(1,128)} %get-tuple-element.104.bias_ref), custom_call_target="tpu_custom_call" | custom-call | flops 4429185024 | bytes 11412484 | tf_op jit(solution)/shard_map/attend/pallas_call | solution.py:301
  100.1 3.9 collective-permute-done.38
  110.8 14.5 %collective-permute-done.14.refs_2_ = bf16[96,3840]{1,0:T(8,128)(2,1)S(1)} collective-permute-done((bf16[96,3840]{1,0:T(8,128)(2,1)S(1)}, bf16[96,3840]{1,0:T(8,128)(2,1)S(1)}, u32[]{:S(2)}, u32[]{:S(2)}) %collective-permute-start.14) | collective-permute-done | bytes 737312 | tf_op jit(solution)/shard_map/ppermute | solution.py:497
  130.6 6.9 %collective-permute-done.15.refs_3_ = bf16[48,3840]{1,0:T(8,128)(2,1)} collective-permute-done((bf16[48,3840]{1,0:T(8,128)(2,1)S(1)}, bf16[48,3840]{1,0:T(8,128)(2,1)}, u32[]{:S(2)}, u32[]{:S(2)}) %collective-permute-start.15) | collective-permute-done | bytes 368672 | tf_op jit(solution)/shard_map/ppermute | solution.py:497
  138.5 8.7 %collective-permute-done.22.refs_11_ = bf16[384,768]{1,0:T(8,128)(2,1)S(1)} collective-permute-done((bf16[384,768]{1,0:T(8,128)(2,1)S(1)}, bf16[384,768]{1,0:T(8,128)(2,1)S(1)}, u32[]{:S(2)}, u32[]{:S(2)}) %collective-permute-start.22) | collective-permute-done | bytes 589856 | tf_op jit(solution)/shard_map/ppermute | solution.py:497
  154.8 3.7 collective-permute-done.23.refs_12_
  159.6 2.3 constant_dynamic-slice_fusion.10
  164.3 8.9 %join.1 = (bf16[768,768]{1,0:T(8,128)(2,1)}, bf16[768,3072]{1,0:T(8,128)(2,1)}, bf16[3072,768]{1,0:T(8,128)(2,1)}) custom-call(s32[3]{0:T(128)} %pad_add_fusion.place_ref, bf16[192,3840]{1,0:T(8,128)(2,1)} %all-gather.6.cloned.1.call-done.refs_0_, bf16[96,3840]{1,0:T(8,128)(2,1)} %copy-done.7, bf16[96,3840]{1,0:T(8,128)(2,1)} %copy-done.6, ...), custom_call_target="tpu_custom_call" | custom-call | tf_op jit(solution)/shard_map/join/pallas_call | solution.py:665
  173.3 27.7 %feed.1 = (bf16[1024,768]{1,0:T(8,128)(2,1)}, f32[8,3840]{1,0:T(8,128)}, f32[8,6144]{1,0:T(8,128)}, f32[1024,768]{1,0:T(8,128)}, bf16[1024,768]{1,0:T(8,128)(2,1...) custom-call(s32[1]{0:T(128)S(6)} %copy.94.count_ref, bf16[1024,768]{1,0:T(8,128)(2,1)} %rows_ref.3, ...), custom_call_target="tpu_custom_call" | custom-call | flops 10871635968 | bytes 36139012 | tf_op jit(solution)/shard_map/feed/pallas_call | solution.py:301
  201.0 22.6 %feed_back.1 = (bf16[1024,768]{1,0:T(8,128)(2,1)}, bf16[1024,3072]{1,0:T(8,128)(2,1)}, bf16[1024,768]{1,0:T(8,128)(2,1)}, bf16[1024,768]{1,0:T(8,128)(2,1)}, f32...) custom-call(s32[1]{0:T(128)S(6)} %copy.94.count_ref, bf16[1024,768]{1,0:T(8,128)(2,1)} %cotangent_ref.1, ...), custom_call_target="tpu_custom_call" | custom-call | flops 10871635968 | bytes 38989828 | tf_op jit(solution)/shard_map/feed_back/pallas_call | solution.py:301
  225.9 10.1 %convolution_convert_fusion.1 = bf16[3072,768]{1,0:T(8,128)(2,1)} fusion(bf16[1024,3072]{1,0:T(8,128)(2,1)} %get-tuple-element.120, bf16[1024,768]{1,0:T(8,128)(2,1)S(1)} %copy-done.49), kind=kOutput, calls=%fused_computation.3 | convolution fusion | flops 4834197504 | bytes 12582912 | tf_op jit(solution)/shard_map/dot_general | solution.py:19
  236.5 2.3 collective-permute-done.31.refs_3_
  240.3 7.3 %convolution_convert_fusion = bf16[768,3072]{1,0:T(8,128)(2,1)} fusion(bf16[1024,768]{1,0:T(8,128)(2,1)S(1)} %copy-done.48, bf16[1024,3072]{1,0:T(8,128)(2,1)S(1)} %bitcast.169), kind=kOutput, calls=%fused_computation.2 | convolution fusion | flops 4834197504 | bytes 12582912 | tf_op jit(solution)/shard_map/dot_general | solution.py:19
  248.2 2.5 convolution_convert_fusion.3
  252.6 17.1 %heads.1 = (f32[8,768]{1,0:T(8,128)}, f32[8,768]{1,0:T(8,128)}, bf16[8,5376]{1,0:T(8,128)(2,1)}, bf16[8,6912]{1,0:T(8,128)(2,1)}, f32[8,768]{1,0:T(8,128)}, /*in...) custom-call(s32[3]{0:T(128)} %pad_add_fusion.place_ref, ...), custom_call_target="tpu_custom_call" | custom-call | flops 594542592 | bytes 25952256 | tf_op jit(solution)/shard_map/heads/pallas_call | solution.py:923
  269.8 3.9 add_convert_fusion
  276.4 2.1 add_convert_fusion.1
  279.0 2.8 pad_maximum_fusion
  282.5 2.0 copy.78
  284.5 5.8 %collective-permute-done.41 = bf16[16,48,3072]{2,1,0:T(8,128)(2,1)} collective-permute-done((bf16[16,48,3072]{2,1,0:T(8,128)(2,1)}, bf16[16,48,3072]{2,1,0:T(8,128)(2,1)}, u32[]{:S(2)}, u32[]{:S(2)}) %collective-permute-start.41) | collective-permute-done | bytes 4718624 | tf_op jit(solution)/shard_map/ppermute | solution.py:497
  290.3 4.1 maximum_add_fusion
  294.6 2.0 copy-done
  299.2 13.8 %collective-permute-done.51 = bf16[2,48,3072]{2,1,0:T(8,128)(2,1)S(1)} collective-permute-done((bf16[2,48,3072]{2,1,0:T(8,128)(2,1)S(1)}, bf16[2,48,3072]{2,1,0:T(8,128)(2,1)S(1)}, u32[]{:S(2)}, u32[]{:S(2)}) %collective-permute-start.51) | collective-permute-done | bytes 589856 | tf_op jit(solution)/shard_map/ppermute | solution.py:497
  325.1 20.5 %attend_back.2 = (bf16[1024,2304]{1,0:T(8,128)(2,1)}, f32[1024,768]{1,0:T(8,128)}, bf16[1024,768]{1,0:T(8,128)(2,1)}, f32[1,2304]{1,0:T(1,128)}) custom-call(s32[1]{0:T(128)S(6)} %copy.94.count_ref, bf16[1024,2304]{1,0:T(8,128)(2,1)} %get-tuple-element.152.projected_ref, bf16[1024,768]{1,0:T(8,128)(2,1)} %get-tuple-element.153.context_ref, ...), custom_call_target="tpu_custom_call" | custom-call | flops 2818572288 | bytes 24069124 | tf_op jit(solution)/shard_map/attend_back/pallas_call | solution.py:301
  345.6 2.5 collective-permute-done.54
  348.1 7.1 %collective-permute-done.52 = bf16[4,48,3072]{2,1,0:T(8,128)(2,1)} collective-permute-done((bf16[4,48,3072]{2,1,0:T(8,128)(2,1)}, bf16[4,48,3072]{2,1,0:T(8,128)(2,1)}, u32[]{:S(2)}, u32[]{:S(2)}) %collective-permute-start.52) | collective-permute-done | bytes 1179680 | tf_op jit(solution)/shard_map/ppermute | solution.py:497
  355.2 2.3 add_convert_fusion.2
  357.7 3.8 collective-permute-start.57
  361.5 21.1 %attend_back.3 = (bf16[1024,2304]{1,0:T(8,128)(2,1)}, f32[1024,768]{1,0:T(8,128)}, bf16[1024,768]{1,0:T(8,128)(2,1)}, f32[1,2304]{1,0:T(1,128)}) custom-call(s32[1]{0:T(128)S(6)} %copy.94.count_ref, bf16[1024,2304]{1,0:T(8,128)(2,1)} %get-tuple-element.152.projected_ref, ...), custom_call_target="tpu_custom_call", output_to_operand_aliasing={{0}: (9, {}), {1}: (10, {}), {2}: (11, {})} | custom-call | flops 2818572288 | bytes 24069124 | tf_op jit(solution)/shard_map/attend_back/pallas_call | solution.py:301
  384.2 3.1 all-to-all-start.1
  387.3 6.7 %convolution_convert_fusion.2 = bf16[2304,768]{0,1:T(8,128)(2,1)S(1)} fusion(bf16[1024,2304]{1,0:T(8,128)(2,1)} %get-tuple-element.164, bf16[1024,768]{1,0:T(8,128)(2,1)} %rows_ref.3), kind=kOutput, calls=%fused_computation.4 | convolution fusion | flops 3625648128 | bytes 9830400 | tf_op jit(solution)/shard_map/dot_general | solution.py:19
  397.5 6.3 %all-to-all-start.2 = ((bf16[32,8,168]{2,1,0:T(8,128)(2,1)}), bf16[32,8,168]{2,1,0:T(8,128)(2,1)}, u32[]{:S(2)}, u32[]{:S(2)}) async-start(bf16[32,8,168]{2,1,0:T(8,128)(2,1)} %maximum_bitcast_fusion), calls=%async_computation.2 | async-start | bytes 262144 | tf_op jit(solution)/shard_map/all_to_all | solution.py:1253
  413.5 2.1 convert_reduce_fusion.1
  415.6 2.1 fusion.12
  417.7 2.1 fusion.10
  421.6 2.4 maximum_add_fusion.1
  438.9 10.6 %collective-permute-done.46 = bf16[4,48,1536]{2,1,0:T(8,128)(2,1)S(1)} collective-permute-done((bf16[4,48,1536]{2,1,0:T(8,128)(2,1)S(1)}, bf16[4,48,1536]{2,1,0:T(8,128)(2,1)S(1)}, u32[]{:S(2)}, u32[]{:S(2)}) %collective-permute-start.46) | collective-permute-done | bytes 589856 | tf_op jit(solution)/shard_map/ppermute | solution.py:497
  451.8 2.4 collective-permute-start.49
  455.6 3.4 collective-permute-done.47
  459.0 6.6 %collective-permute-done.48 = bf16[48,1536]{1,0:T(8,128)(2,1)S(1)} collective-permute-done((bf16[48,1536]{1,0:T(8,128)(2,1)S(1)}, bf16[48,1536]{1,0:T(8,128)(2,1)S(1)}, u32[]{:S(2)}, u32[]{:S(2)}) %collective-permute-start.48) | collective-permute-done | bytes 147488 | tf_op jit(solution)/shard_map/ppermute | solution.py:497
  (344 shorter events, 112.1 us)
Async XLA Ops:
  7.2 99.1 %all-gather.6.cloned.1.call-start = ((), (), s32[]{:S(2)}) async-start(), calls=%async_computation.3 | async-start | bytes 1658880 | tf_op jit(solution)/shard_map/all_gather | solution.py:679
  11.9 114.9 %all-gather.8.cloned.1.call-start = ((), (), s32[]{:S(2)}) async-start(), calls=%async_computation.4 | async-start | bytes 1327104 | tf_op jit(solution)/shard_map/all_gather | solution.py:679
  12.7 147.0 %all-gather.10.cloned.1.call-start = ((), (), s32[]{:S(2)}) async-start(), calls=%async_computation.5 | async-start | bytes 2654208 | tf_op jit(solution)/shard_map/all_gather | solution.py:679
  17.5 35.4 %all-to-all-start = ((bf16[32,32,128]{2,1,0:T(8,128)(2,1)}), bf16[32,32,128]{2,1,0:T(8,128)(2,1)S(1)}, u32[]{:S(2)}, u32[]{:S(2)}) async-start(bf16[32,32,128]{2,1,0:T(8,128)(2,1)} %pack.1), calls=%async_computation | async-start | bytes 524288 | tf_op jit(solution)/shard_map/all_to_all | solution.py:475
  24.7 227.9 %all-gather.12.cloned.1.call-start = ((), (), s32[]{:S(2)}) async-start(), calls=%async_computation.6 | async-start | bytes 5308416 | tf_op jit(solution)/shard_map/all_gather | solution.py:635
  24.7 17.3 %collective-permute-start.3 = (bf16[48,1152]{1,0:T(8,128)(2,1)S(1)}, bf16[48,1152]{1,0:T(8,128)(2,1)S(1)}, u32[]{:S(2)}, u32[]{:S(2)}) collective-permute-start(bf16[48,1152]{1,0:T(8,128)(2,1)S(1)} %get-tuple-element.290), channel_id=1, source_target_pairs={{0,6},{1,7},{2,0},{3,1},{4,2},{5,3},{6,4},{7,5},{8,14},{9,15},{10,... | collective-permute-start | bytes 331784 | tf_op jit(solution)/shard_map/ppermute | solution.py:497
  28.4 24.4 %collective-permute-start.2 = (bf16[48,1152]{1,0:T(8,128)(2,1)S(1)}, bf16[48,1152]{1,0:T(8,128)(2,1)S(1)}, u32[]{:S(2)}, u32[]{:S(2)}) collective-permute-start(bf16[48,1152]{1,0:T(8,128)(2,1)S(1)} %get-tuple-element.290), channel_id=1, source_target_pairs={{0,4},{1,5},{2,6},{3,7},{4,0},{5,1},{6,2},{7,3},{8,12},{9,13},{10,... | collective-permute-start | bytes 331784 | tf_op jit(solution)/shard_map/ppermute | solution.py:497
  28.4 24.4 %collective-permute-start.1 = (bf16[48,1152]{1,0:T(8,128)(2,1)S(1)}, bf16[48,1152]{1,0:T(8,128)(2,1)S(1)}, u32[]{:S(2)}, u32[]{:S(2)}) collective-permute-start(bf16[48,1152]{1,0:T(8,128)(2,1)S(1)} %get-tuple-element.290), channel_id=1, source_target_pairs={{0,2},{1,3},{2,4},{3,5},{4,6},{5,7},{6,0},{7,1},{8,10},{9,11},{10,... | collective-permute-start | bytes 331784 | tf_op jit(solution)/shard_map/ppermute | solution.py:497
  56.9 12.1 %collective-permute-start.5 = (bf16[4,48,1152]{2,1,0:T(8,128)(2,1)S(1)}, bf16[4,48,1152]{2,1,0:T(8,128)(2,1)S(1)}, u32[]{:S(2)}, u32[]{:S(2)}) collective-permute-start(bf16[4,48,1152]{2,1,0:T(8,128)(2,1)S(1)} %pad_maximum_fusion.6.refs_0_), channel_id=1, source_target_pairs={{0,16},{1,17},{2,18},{3,19},{4,20},{5,21},{6,22},{7,23},{8,24},{9,... | collective-permute-start | bytes 1327112 | tf_op jit(solution)/shard_map/ppermute | solution.py:497
  58.4 12.2 %collective-permute-start.4 = (bf16[4,48,1152]{2,1,0:T(8,128)(2,1)S(1)}, bf16[4,48,1152]{2,1,0:T(8,128)(2,1)S(1)}, u32[]{:S(2)}, u32[]{:S(2)}) collective-permute-start(bf16[4,48,1152]{2,1,0:T(8,128)(2,1)S(1)} %pad_maximum_fusion.6.refs_0_), channel_id=1, source_target_pairs={{0,8},{1,9},{2,10},{3,11},{4,12},{5,13},{6,14},{7,15},{8,0},{9,1},... | collective-permute-start | bytes 1327112 | tf_op jit(solution)/shard_map/ppermute | solution.py:497
  59.8 18.4 %collective-permute-start.8 = (bf16[4,48,1152]{2,1,0:T(8,128)(2,1)S(1)}, bf16[4,48,1152]{2,1,0:T(8,128)(2,1)S(1)}, u32[]{:S(2)}, u32[]{:S(2)}) collective-permute-start(bf16[4,48,1152]{2,1,0:T(8,128)(2,1)S(1)} %pad_maximum_fusion.6.refs_0_), channel_id=1, source_target_pairs={{0,1},{1,0},{2,3},{3,2},{4,5},{5,4},{6,7},{7,6},{8,9},{9,8},{10,11... | collective-permute-start | bytes 1327112 | tf_op jit(solution)/shard_map/ppermute | solution.py:497
  107.5 17.8 %collective-permute-start.14 = (bf16[96,3840]{1,0:T(8,128)(2,1)S(1)}, bf16[96,3840]{1,0:T(8,128)(2,1)S(1)}, u32[]{:S(2)}, u32[]{:S(2)}) collective-permute-start(bf16[96,3840]{1,0:T(8,128)(2,1)S(1)} %constant_dynamic-slice_fusion.12), channel_id=1, source_target_pairs={{0,16},{1,17},{2,18},{3,19},{4,20},{5,21},{6,22},{7,23},{8,24},{9,... | collective-permute-start | bytes 2211848 | tf_op jit(solution)/shard_map/ppermute | solution.py:497
  108.5 17.3 %collective-permute-start.13 = (bf16[96,3840]{1,0:T(8,128)(2,1)S(1)}, bf16[96,3840]{1,0:T(8,128)(2,1)S(1)}, u32[]{:S(2)}, u32[]{:S(2)}) collective-permute-start(bf16[96,3840]{1,0:T(8,128)(2,1)S(1)} %constant_dynamic-slice_fusion.12), channel_id=1, source_target_pairs={{0,8},{1,9},{2,10},{3,11},{4,12},{5,13},{6,14},{7,15},{8,0},{9,1},... | collective-permute-start | bytes 2211848 | tf_op jit(solution)/shard_map/ppermute | solution.py:497
  110.8 301.0 %all-gather.14.cloned.1.call-start = ((), (), s32[]{:S(2)}) async-start(), calls=%async_computation.7 | async-start | bytes 3649536 | tf_op jit(solution)/shard_map/all_gather | solution.py:402
  125.8 11.7 %collective-permute-start.15 = (bf16[48,3840]{1,0:T(8,128)(2,1)S(1)}, bf16[48,3840]{1,0:T(8,128)(2,1)}, u32[]{:S(2)}, u32[]{:S(2)}) collective-permute-start(bf16[48,3840]{1,0:T(8,128)(2,1)S(1)} %slice.350), channel_id=1, source_target_pairs={{0,16},{1,17},{2,18},{3,19},{4,20},{5,21},{6,22},{7,23},{8,24},{9,... | collective-permute-start | bytes 1105928 | tf_op jit(solution)/shard_map/ppermute | solution.py:497
  128.0 19.2 %collective-permute-start.22 = (bf16[384,768]{1,0:T(8,128)(2,1)S(1)}, bf16[384,768]{1,0:T(8,128)(2,1)S(1)}, u32[]{:S(2)}, u32[]{:S(2)}) collective-permute-start(bf16[384,768]{1,0:T(8,128)(2,1)S(1)} %constant_dynamic-slice_fusion.11), channel_id=1, source_target_pairs={{0,16},{1,17},{2,18},{3,19},{4,20},{5,21},{6,22},{7,23},{8,24},{9,... | collective-permute-start | bytes 1769480 | tf_op jit(solution)/shard_map/ppermute | solution.py:497
  129.1 18.9 %collective-permute-start.21 = (bf16[384,768]{1,0:T(8,128)(2,1)S(1)}, bf16[384,768]{1,0:T(8,128)(2,1)}, u32[]{:S(2)}, u32[]{:S(2)}) collective-permute-start(bf16[384,768]{1,0:T(8,128)(2,1)S(1)} %constant_dynamic-slice_fusion.11), channel_id=1, source_target_pairs={{0,8},{1,9},{2,10},{3,11},{4,12},{5,13},{6,14},{7,15},{8,0},{9,1},... | collective-permute-start | bytes 1769480 | tf_op jit(solution)/shard_map/ppermute | solution.py:497
  130.1 24.1 %collective-permute-start.18 = (bf16[96,3840]{1,0:T(8,128)(2,1)S(1)}, bf16[96,3840]{1,0:T(8,128)(2,1)}, u32[]{:S(2)}, u32[]{:S(2)}) collective-permute-start(bf16[96,3840]{1,0:T(8,128)(2,1)S(1)} %collective-permute-done.14.refs_2_), channel_id=1, source_target_pairs={{0,1},{1,0},{2,3},{3,2},{4,5},{5,4},{6,7},{7,6},{8,9},{9,8},{10,11... | collective-permute-start | bytes 2211848 | tf_op jit(solution)/shard_map/ppermute | solution.py:497
  130.1 24.1 %collective-permute-start.17 = (bf16[96,3840]{1,0:T(8,128)(2,1)S(1)}, bf16[96,3840]{1,0:T(8,128)(2,1)}, u32[]{:S(2)}, u32[]{:S(2)}) collective-permute-start(bf16[96,3840]{1,0:T(8,128)(2,1)S(1)} %collective-permute-done.13.refs_1_), channel_id=1, source_target_pairs={{0,1},{1,0},{2,3},{3,2},{4,5},{5,4},{6,7},{7,6},{8,9},{9,8},{10,11... | collective-permute-start | bytes 2211848 | tf_op jit(solution)/shard_map/ppermute | solution.py:497
  137.5 12.3 %collective-permute-start.16 = (bf16[48,3840]{1,0:T(8,128)(2,1)S(1)}, bf16[48,3840]{1,0:T(8,128)(2,1)S(1)}, u32[]{:S(2)}, u32[]{:S(2)}) collective-permute-start(bf16[48,3840]{1,0:T(8,128)(2,1)S(1)} %slice.351), channel_id=1, source_target_pairs={{0,8},{1,9},{2,10},{3,11},{4,12},{5,13},{6,14},{7,15},{8,0},{9,1},... | collective-permute-start | bytes 1105928 | tf_op jit(solution)/shard_map/ppermute | solution.py:497
  149.8 8.7 %collective-permute-start.23 = (bf16[192,768]{1,0:T(8,128)(2,1)S(1)}, bf16[192,768]{1,0:T(8,128)(2,1)}, u32[]{:S(2)}, u32[]{:S(2)}) collective-permute-start(bf16[192,768]{1,0:T(8,128)(2,1)S(1)} %slice.352), channel_id=1, source_target_pairs={{0,16},{1,17},{2,18},{3,19},{4,20},{5,21},{6,22},{7,23},{8,24},{9,... | collective-permute-start | bytes 884744 | tf_op jit(solution)/shard_map/ppermute | solution.py:497
  154.2 8.7 %collective-permute-start.26 = (bf16[384,768]{1,0:T(8,128)(2,1)S(1)}, bf16[384,768]{1,0:T(8,128)(2,1)}, u32[]{:S(2)}, u32[]{:S(2)}) collective-permute-start(bf16[384,768]{1,0:T(8,128)(2,1)S(1)} %collective-permute-done.22.refs_11_), channel_id=1, source_target_pairs={{0,1},{1,0},{2,3},{3,2},{4,5},{5,4},{6,7},{7,6},{8,9},{9,8},{10,11... | collective-permute-start | bytes 1769480 | tf_op jit(solution)/shard_map/ppermute | solution.py:497
  154.7 9.6 %collective-permute-start.25 = (bf16[384,768]{1,0:T(8,128)(2,1)}, bf16[384,768]{1,0:T(8,128)(2,1)}, u32[]{:S(2)}, u32[]{:S(2)}) collective-permute-start(bf16[384,768]{1,0:T(8,128)(2,1)} %collective-permute-done.21.refs_10_), channel_id=1, source_target_pairs={{0,1},{1,0},{2,3},{3,2},{4,5},{5,4},{6,7},{7,6},{8,9},{9,8},{10,11... | collective-permute-start | bytes 1769480 | tf_op jit(solution)/shard_map/ppermute | solution.py:497
  162.0 61.6 %collective-permute-start.30 = (bf16[96,6144]{1,0:T(8,128)(2,1)}, bf16[96,6144]{1,0:T(8,128)(2,1)S(1)}, u32[]{:S(2)}, u32[]{:S(2)}) collective-permute-start(bf16[96,6144]{1,0:T(8,128)(2,1)} %constant_dynamic-slice_fusion.10), channel_id=1, source_target_pairs={{0,16},{1,17},{2,18},{3,19},{4,20},{5,21},{6,22},{7,23},{8,24},{9,... | collective-permute-start | bytes 3538952 | tf_op jit(solution)/shard_map/ppermute | solution.py:497
  162.9 60.8 %collective-permute-start.29 = (bf16[96,6144]{1,0:T(8,128)(2,1)}, bf16[96,6144]{1,0:T(8,128)(2,1)S(1)}, u32[]{:S(2)}, u32[]{:S(2)}) collective-permute-start(bf16[96,6144]{1,0:T(8,128)(2,1)} %constant_dynamic-slice_fusion.10), channel_id=1, source_target_pairs={{0,8},{1,9},{2,10},{3,11},{4,12},{5,13},{6,14},{7,15},{8,0},{9,1},... | collective-permute-start | bytes 3538952 | tf_op jit(solution)/shard_map/ppermute | solution.py:497
  223.8 15.1 %collective-permute-start.31 = (bf16[48,6144]{1,0:T(8,128)(2,1)S(1)}, bf16[48,6144]{1,0:T(8,128)(2,1)S(1)}, u32[]{:S(2)}, u32[]{:S(2)}) collective-permute-start(bf16[48,6144]{1,0:T(8,128)(2,1)S(1)} %slice.356), channel_id=1, source_target_pairs={{0,16},{1,17},{2,18},{3,19},{4,20},{5,21},{6,22},{7,23},{8,24},{9,... | collective-permute-start | bytes 1769480 | tf_op jit(solution)/shard_map/ppermute | solution.py:497
  225.3 14.9 %collective-permute-start.32 = (bf16[48,6144]{1,0:T(8,128)(2,1)S(1)}, bf16[48,6144]{1,0:T(8,128)(2,1)S(1)}, u32[]{:S(2)}, u32[]{:S(2)}) collective-permute-start(bf16[48,6144]{1,0:T(8,128)(2,1)S(1)} %slice.357), channel_id=1, source_target_pairs={{0,8},{1,9},{2,10},{3,11},{4,12},{5,13},{6,14},{7,15},{8,0},{9,1},... | collective-permute-start | bytes 1769480 | tf_op jit(solution)/shard_map/ppermute | solution.py:497
  236.0 14.7 %collective-permute-start.34 = (bf16[96,6144]{1,0:T(8,128)(2,1)S(1)}, bf16[96,6144]{1,0:T(8,128)(2,1)S(1)}, u32[]{:S(2)}, u32[]{:S(2)}) collective-permute-start(bf16[96,6144]{1,0:T(8,128)(2,1)S(1)} %collective-permute-done.30.refs_2_), channel_id=1, source_target_pairs={{0,1},{1,0},{2,3},{3,2},{4,5},{5,4},{6,7},{7,6},{8,9},{9,8},{10,11... | collective-permute-start | bytes 3538952 | tf_op jit(solution)/shard_map/ppermute | solution.py:497
  236.0 14.7 %collective-permute-start.33 = (bf16[96,6144]{1,0:T(8,128)(2,1)S(1)}, bf16[96,6144]{1,0:T(8,128)(2,1)S(1)}, u32[]{:S(2)}, u32[]{:S(2)}) collective-permute-start(bf16[96,6144]{1,0:T(8,128)(2,1)S(1)} %collective-permute-done.29.refs_1_), channel_id=1, source_target_pairs={{0,1},{1,0},{2,3},{3,2},{4,5},{5,4},{6,7},{7,6},{8,9},{9,8},{10,11... | collective-permute-start | bytes 3538952 | tf_op jit(solution)/shard_map/ppermute | solution.py:497
  238.8 13.0 %collective-permute-start.35 = (bf16[48,6144]{1,0:T(8,128)(2,1)S(1)}, bf16[48,6144]{1,0:T(8,128)(2,1)S(1)}, u32[]{:S(2)}, u32[]{:S(2)}) collective-permute-start(bf16[48,6144]{1,0:T(8,128)(2,1)S(1)} %collective-permute-done.31.refs_3_), channel_id=1, source_target_pairs={{0,1},{1,0},{2,3},{3,2},{4,5},{5,4},{6,7},{7,6},{8,9},{9,8},{10,11... | collective-permute-start | bytes 1769480 | tf_op jit(solution)/shard_map/ppermute | solution.py:497
  240.2 12.4 %collective-permute-start.36 = (bf16[48,6144]{1,0:T(8,128)(2,1)S(1)}, bf16[48,6144]{1,0:T(8,128)(2,1)}, u32[]{:S(2)}, u32[]{:S(2)}) collective-permute-start(bf16[48,6144]{1,0:T(8,128)(2,1)S(1)} %collective-permute-done.32.refs_4_), channel_id=1, source_target_pairs={{0,1},{1,0},{2,3},{3,2},{4,5},{5,4},{6,7},{7,6},{8,9},{9,8},{10,11... | collective-permute-start | bytes 1769480 | tf_op jit(solution)/shard_map/ppermute | solution.py:497
  296.6 16.4 %collective-permute-start.51 = (bf16[2,48,3072]{2,1,0:T(8,128)(2,1)S(1)}, bf16[2,48,3072]{2,1,0:T(8,128)(2,1)S(1)}, u32[]{:S(2)}, u32[]{:S(2)}) collective-permute-start(bf16[2,48,3072]{2,1,0:T(8,128)(2,1)S(1)} %get-tuple-element.247), channel_id=1, source_target_pairs={{0,16},{1,17},{2,18},{3,19},{4,20},{5,21},{6,22},{7,23},{8,24},{9,... | collective-permute-start | bytes 1769480 | tf_op jit(solution)/shard_map/ppermute | solution.py:497
  297.1 16.0 %collective-permute-start.53 = (bf16[2,48,3072]{2,1,0:T(8,128)(2,1)S(1)}, bf16[2,48,3072]{2,1,0:T(8,128)(2,1)S(1)}, u32[]{:S(2)}, u32[]{:S(2)}) collective-permute-start(bf16[2,48,3072]{2,1,0:T(8,128)(2,1)S(1)} %get-tuple-element.249), channel_id=1, source_target_pairs={{0,8},{1,9},{2,10},{3,11},{4,12},{5,13},{6,14},{7,15},{8,0},{9,1},... | collective-permute-start | bytes 1769480 | tf_op jit(solution)/shard_map/ppermute | solution.py:497
  315.7 32.4 %collective-permute-start.54 = (bf16[4,48,3072]{2,1,0:T(8,128)(2,1)}, bf16[4,48,3072]{2,1,0:T(8,128)(2,1)S(1)}, u32[]{:S(2)}, u32[]{:S(2)}) collective-permute-start(bf16[4,48,3072]{2,1,0:T(8,128)(2,1)} %pad_maximum_fusion.3), channel_id=1, source_target_pairs={{0,16},{1,17},{2,18},{3,19},{4,20},{5,21},{6,22},{7,23},{8,24},{9,... | collective-permute-start | bytes 3538952 | tf_op jit(solution)/shard_map/ppermute | solution.py:497
  318.5 36.7 %collective-permute-start.52 = (bf16[4,48,3072]{2,1,0:T(8,128)(2,1)}, bf16[4,48,3072]{2,1,0:T(8,128)(2,1)}, u32[]{:S(2)}, u32[]{:S(2)}) collective-permute-start(bf16[4,48,3072]{2,1,0:T(8,128)(2,1)} %pad_maximum_fusion.2), channel_id=1, source_target_pairs={{0,8},{1,9},{2,10},{3,11},{4,12},{5,13},{6,14},{7,15},{8,0},{9,1},... | collective-permute-start | bytes 3538952 | tf_op jit(solution)/shard_map/ppermute | solution.py:497
  357.6 48.7 %collective-permute-start.55 = (bf16[48,3072]{1,0:T(8,128)(2,1)S(1)}, bf16[48,3072]{1,0:T(8,128)(2,1)S(1)}, u32[]{:S(2)}, u32[]{:S(2)}) collective-permute-start(bf16[48,3072]{1,0:T(8,128)(2,1)S(1)} %get-tuple-element.263), channel_id=1, source_target_pairs={{0,2},{1,3},{2,4},{3,5},{4,6},{5,7},{6,0},{7,1},{8,10},{9,11},{10,... | collective-permute-start | bytes 884744 | tf_op jit(solution)/shard_map/ppermute | solution.py:497
  357.7 48.6 %collective-permute-start.57 = (bf16[48,3072]{1,0:T(8,128)(2,1)S(1)}, bf16[48,3072]{1,0:T(8,128)(2,1)S(1)}, u32[]{:S(2)}, u32[]{:S(2)}) collective-permute-start(bf16[48,3072]{1,0:T(8,128)(2,1)S(1)} %get-tuple-element.264), channel_id=1, source_target_pairs={{0,6},{1,7},{2,0},{3,1},{4,2},{5,3},{6,4},{7,5},{8,14},{9,15},{10,... | collective-permute-start | bytes 884744 | tf_op jit(solution)/shard_map/ppermute | solution.py:497
  361.5 44.8 %collective-permute-start.56 = (bf16[48,3072]{1,0:T(8,128)(2,1)S(1)}, bf16[48,3072]{1,0:T(8,128)(2,1)}, u32[]{:S(2)}, u32[]{:S(2)}) collective-permute-start(bf16[48,3072]{1,0:T(8,128)(2,1)S(1)} %get-tuple-element.265), channel_id=1, source_target_pairs={{0,4},{1,5},{2,6},{3,7},{4,0},{5,1},{6,2},{7,3},{8,12},{9,13},{10,... | collective-permute-start | bytes 884744 | tf_op jit(solution)/shard_map/ppermute | solution.py:497
  384.2 13.2 %all-to-all-start.1 = ((f32[32,8,128]{2,1,0:T(8,128)}), f32[32,8,128]{2,1,0:T(8,128)S(1)}, u32[]{:S(2)}, u32[]{:S(2)}) async-start(f32[32,8,128]{2,1,0:T(8,128)} %bitcast.77), calls=%async_computation.1 | async-start | bytes 262144 | tf_op jit(solution)/shard_map/all_to_all | solution.py:492
  397.4 24.2 %collective-permute-start.42 = (bf16[16,48,1536]{2,1,0:T(8,128)(2,1)}, bf16[16,48,1536]{2,1,0:T(8,128)(2,1)}, u32[]{:S(2)}, u32[]{:S(2)}) collective-permute-start(bf16[16,48,1536]{2,1,0:T(8,128)(2,1)} %pad_maximum_fusion.1), channel_id=1, source_target_pairs={{0,1},{1,0},{2,3},{3,2},{4,5},{5,4},{6,7},{7,6},{8,9},{9,8},{10,11... | collective-permute-start | bytes 7077896 | tf_op jit(solution)/shard_map/ppermute | solution.py:497
  397.5 18.1 %all-to-all-start.2 = ((bf16[32,8,168]{2,1,0:T(8,128)(2,1)}), bf16[32,8,168]{2,1,0:T(8,128)(2,1)}, u32[]{:S(2)}, u32[]{:S(2)}) async-start(bf16[32,8,168]{2,1,0:T(8,128)(2,1)} %maximum_bitcast_fusion), calls=%async_computation.2 | async-start | bytes 262144 | tf_op jit(solution)/shard_map/all_to_all | solution.py:1253
  411.4 25.8 %collective-permute-start.58 = (f32[24,3072]{1,0:T(8,128)}, f32[24,3072]{1,0:T(8,128)}, u32[]{:S(2)}, u32[]{:S(2)}) collective-permute-start(f32[24,3072]{1,0:T(8,128)} %dynamic-slice_dynamic-update-slice_fusion.1), channel_id=1, source_target_pairs={{0,1},{1,0},{2,3},{3,2},{4,5},{5,4},{6,7},{7,6},{8,9},{9,8},{10,11... | collective-permute-start | bytes 884744 | tf_op jit(solution)/shard_map/ppermute | solution.py:497
  424.1 9.3 %collective-permute-start.43 = (bf16[2,48,1536]{2,1,0:T(8,128)(2,1)S(1)}, bf16[2,48,1536]{2,1,0:T(8,128)(2,1)S(1)}, u32[]{:S(2)}, u32[]{:S(2)}) collective-permute-start(bf16[2,48,1536]{2,1,0:T(8,128)(2,1)S(1)} %get-tuple-element.259), channel_id=1, source_target_pairs={{0,16},{1,17},{2,18},{3,19},{4,20},{5,21},{6,22},{7,23},{8,24},{9,... | collective-permute-start | bytes 884744 | tf_op jit(solution)/shard_map/ppermute | solution.py:497
  425.9 9.0 %collective-permute-start.45 = (bf16[2,48,1536]{2,1,0:T(8,128)(2,1)S(1)}, bf16[2,48,1536]{2,1,0:T(8,128)(2,1)S(1)}, u32[]{:S(2)}, u32[]{:S(2)}) collective-permute-start(bf16[2,48,1536]{2,1,0:T(8,128)(2,1)S(1)} %get-tuple-element.261), channel_id=1, source_target_pairs={{0,8},{1,9},{2,10},{3,11},{4,12},{5,13},{6,14},{7,15},{8,0},{9,1},... | collective-permute-start | bytes 884744 | tf_op jit(solution)/shard_map/ppermute | solution.py:497
  435.0 14.5 %collective-permute-start.46 = (bf16[4,48,1536]{2,1,0:T(8,128)(2,1)S(1)}, bf16[4,48,1536]{2,1,0:T(8,128)(2,1)S(1)}, u32[]{:S(2)}, u32[]{:S(2)}) collective-permute-start(bf16[4,48,1536]{2,1,0:T(8,128)(2,1)S(1)} %pad_maximum_fusion.5), channel_id=1, source_target_pairs={{0,16},{1,17},{2,18},{3,19},{4,20},{5,21},{6,22},{7,23},{8,24},{9,... | collective-permute-start | bytes 1769480 | tf_op jit(solution)/shard_map/ppermute | solution.py:497
  435.5 14.5 %collective-permute-start.44 = (bf16[4,48,1536]{2,1,0:T(8,128)(2,1)S(1)}, bf16[4,48,1536]{2,1,0:T(8,128)(2,1)S(1)}, u32[]{:S(2)}, u32[]{:S(2)}) collective-permute-start(bf16[4,48,1536]{2,1,0:T(8,128)(2,1)S(1)} %pad_maximum_fusion.4), channel_id=1, source_target_pairs={{0,8},{1,9},{2,10},{3,11},{4,12},{5,13},{6,14},{7,15},{8,0},{9,1},... | collective-permute-start | bytes 1769480 | tf_op jit(solution)/shard_map/ppermute | solution.py:497
  450.3 8.7 %collective-permute-start.47 = (bf16[48,1536]{1,0:T(8,128)(2,1)S(1)}, bf16[48,1536]{1,0:T(8,128)(2,1)S(1)}, u32[]{:S(2)}, u32[]{:S(2)}) collective-permute-start(bf16[48,1536]{1,0:T(8,128)(2,1)S(1)} %get-tuple-element.274), channel_id=1, source_target_pairs={{0,2},{1,3},{2,4},{3,5},{4,6},{5,7},{6,0},{7,1},{8,10},{9,11},{10,... | collective-permute-start | bytes 442376 | tf_op jit(solution)/shard_map/ppermute | solution.py:497
  454.1 11.5 %collective-permute-start.48 = (bf16[48,1536]{1,0:T(8,128)(2,1)S(1)}, bf16[48,1536]{1,0:T(8,128)(2,1)S(1)}, u32[]{:S(2)}, u32[]{:S(2)}) collective-permute-start(bf16[48,1536]{1,0:T(8,128)(2,1)S(1)} %get-tuple-element.276), channel_id=1, source_target_pairs={{0,4},{1,5},{2,6},{3,7},{4,0},{5,1},{6,2},{7,3},{8,12},{9,13},{10,... | collective-permute-start | bytes 442376 | tf_op jit(solution)/shard_map/ppermute | solution.py:497
  (73 other events, 578.9 us)
Sparse Core Ops, SparseCore 0:
  12.0 37.2 all-gather.5
  51.0 23.6 all-gather.7
  76.9 31.3 all-gather.9
  110.9 49.7 all-gather.11
  297.9 68.2 all-gather.13

commit v4 on v3

--- a/solution.py
+++ b/solution.py
@@ -88,8 +88,47 @@
     return position < count_ref[0] - segment * SEG
 
 
-def attend_kernel(count_ref, rows_ref, attend_ref, bias_ref, projected_ref, context_ref):
+def attend_copies(pieces, target, place_ref, sems):
+    if len(pieces) == 1:
+        return [pltpu.make_async_copy(pieces[0], target, sems.at[0])]
+    plane, depth, core = place_ref[0], place_ref[1], place_ref[2]
+    height, width = pieces[0].shape[1], target.shape[1] // 2
+    slots = ((0, 0, 4), (1, 0, 4), (2, 0, 4), (3, 0, 2), (3, 2, 2))
+    copies = []
+    for side in range(2):
+        lane = pl.multiple_of((core if side == 0 else 1 - core) * width, 128)
+        for number, (turn, first, count) in enumerate(slots):
+            for slot in range(count):
+                chip = (plane ^ turn) * 4 + ((depth + 4 - first - slot) & 3)
+                row = pl.multiple_of(chip * height, 48)
+                copies.append(
+                    pltpu.make_async_copy(
+                        pieces[5 * side + number].at[slot, :, :width],
+                        target.at[pl.ds(row, height), pl.ds(lane, width)],
+                        sems.at[len(copies)],
+                    )
+                )
+    return copies
+
+
+def attend_kernel(count, count_ref, rows_ref, place_ref, bias_ref, *refs):
+    pieces, (projected_ref, context_ref, joined_ref), (attend_ref, sems, out_sem) = (
+        refs[:count],
+        refs[count : count + 3],
+        refs[count + 3 :],
+    )
     step = pl.program_id(0)
+    kept = pltpu.make_async_copy(attend_ref, joined_ref, out_sem)
+
+    @pl.when(step == 0)
+    def _():
+        copies = attend_copies(pieces, attend_ref, place_ref, sems)
+        for copy in copies:
+            copy.start()
+        for copy in copies:
+            copy.wait()
+        kept.start()
+
     projected_ref[...] = (dot_nn(rows_ref[...], attend_ref[...]) + bias_ref[...]).astype(LOW)
     for local in range(ROWS // SEG):
         valid = valid_keys(count_ref, step * (ROWS // SEG) + local)
@@ -104,6 +143,10 @@
                 side_by_side(probs), two_heads(value, 0)
             ).astype(LOW)
 
+    @pl.when(step == pl.num_programs(0) - 1)
+    def _():
+        kept.wait()
+
 
 def put_row(ref, place, start, row):
     span = slice(start, start + row.shape[1])
@@ -121,13 +164,51 @@
 
 
 def feed_kernel(
+    mid_moves,
+    end_moves,
+    counts,
+    count_ref,
+    rows_ref,
+    context_ref,
+    place_ref,
+    expand_bias_ref,
+    vectors_ref,
+    *refs,
+):
+    mid, end, refs = refs[: counts[0]], refs[counts[0] : sum(counts)], refs[sum(counts) :]
+    joined, weights, sems, out_sems = refs[8:11], refs[11:14], refs[14], refs[15]
+    merge_ref, expand_ref, reduce_ref = weights
+    kept = [
+        pltpu.make_async_copy(weight, out, out_sems.at[number])
+        for number, (weight, out) in enumerate(zip(weights, joined))
+    ]
+
+    @pl.when(pl.program_id(0) == 0)
+    def _():
+        widths = (D, expand_ref.shape[1])
+        waits = start_moves(mid, weights[:2], widths, mid_moves, place_ref, sems, 0)
+        waits += start_moves(
+            end, weights[2:], (D,), end_moves, place_ref, sems, 2 * len(mid_moves)
+        )
+        for copies, copy in zip(waits, kept):
+            wait_all(copies)
+            copy.start()
+
+    feed_rows(count_ref, rows_ref, context_ref, *weights, expand_bias_ref, vectors_ref, *refs[:8])
+
+    @pl.when(pl.program_id(0) == pl.num_programs(0) - 1)
+    def _():
+        wait_all(kept)
+
+
+def feed_rows(
     count_ref,
     rows_ref,
     context_ref,
     merge_ref,
     expand_ref,
+    reduce_ref,
     expand_bias_ref,
-    reduce_ref,
     vectors_ref,
     mixed_ref,
     heads_ref,
@@ -249,7 +330,7 @@
     def _():
         sums_ref[...] = jnp.zeros_like(sums_ref)
 
-    is_head = lax.broadcasted_iota(jnp.int32, (SEG, 1), 0) == 0
+    is_head = lax.broadcasted_iota(jnp.int32, (16, 1), 0) == 0
     scale = HD ** (-0.5)
     for local in range(segments):
         segment = (step + offset) * segments + local
@@ -260,11 +341,14 @@
                 slice(part * D + pair * PAIR, part * D + (pair + 1) * PAIR) for part in range(3)
             ]
             query, key, value = [projected_ref[span, column] for column in columns]
-            grad = jnp.where(
+            top = slice(local * SEG, local * SEG + 16)
+            rest = slice(local * SEG + 16, (local + 1) * SEG)
+            replaced = jnp.where(
                 is_head,
                 get_row(head_context_ref, segment, columns[0]),
-                context_ref[span, columns[0]].astype(F32),
+                context_ref[top, columns[0]].astype(F32),
             ).astype(LOW)
+            grad = jnp.concatenate([replaced, context_ref[rest, columns[0]]], axis=0)
             grad = two_heads(grad, 0)
             probs = pair_probs(query, key, valid)
             grad_probs = back_cols(grad, value)
@@ -277,10 +361,17 @@
                 cross_rows(scores, two_heads(query, 0)) * scale
             ).astype(LOW)
             grad_ref[span, columns[2]] = cross_rows(probs.astype(LOW), grad).astype(LOW)
-        first = jnp.where(is_head, get_row(head_first_ref, segment, slice(0, D)), first_ref[span, :])
-        tokens_ref[span, :] = first + back_cols(grad_ref[span, :], attend_ref[...])
-        mixed_ref[span, :] = jnp.where(
-            is_head, get_row(head_out_ref, segment, slice(0, D)), mixed_in_ref[span, :].astype(F32)
+    tokens_ref[...] = first_ref[...] + back_cols(grad_ref[...], attend_ref[...])
+    mixed_ref[...] = mixed_in_ref[...]
+    for local in range(segments):
+        segment = (step + offset) * segments + local
+        top = slice(local * SEG, local * SEG + 16)
+        missing = jnp.where(is_head, get_row(head_first_ref, segment, slice(0, D)), 0.0)
+        tokens_ref[top, :] += missing
+        mixed_ref[top, :] = jnp.where(
+            is_head,
+            get_row(head_out_ref, segment, slice(0, D)),
+            mixed_in_ref[top, :].astype(F32),
         ).astype(LOW)
     sums_ref[...] += jnp.sum(grad_ref[...].astype(F32), axis=0, keepdims=True)
 
@@ -293,7 +384,7 @@
     return pl.BlockSpec(array.shape, lambda step: (0,) * array.ndim)
 
 
-def row_call(kernel, name, operands, specs, outs, flops, steps=None, earlier=()):
+def row_call(kernel, name, operands, specs, outs, flops, steps=None, earlier=(), scratch=()):
     rows = next(operand.shape[0] for operand, spec in zip(operands, specs) if spec is not None)
     shapes = [jax.ShapeDtypeStruct(shape, kind) for shape, kind, _ in outs]
     moved = sum(operand.size * operand.dtype.itemsize for operand in operands)
@@ -307,6 +398,7 @@
         out_specs=[spec for _, _, spec in outs],
         out_shape=shapes,
         input_output_aliases={len(operands) + place: place for place in range(len(earlier))},
+        scratch_shapes=scratch,
         compiler_params=pltpu.CompilerParams(vmem_limit_bytes=60 << 20),
         cost_estimate=pl.CostEstimate(flops=flops, bytes_accessed=moved, transcendentals=0),
         name=name,
@@ -317,26 +409,41 @@
     return pl.BlockSpec(shape, lambda step: (0,) * len(shape))
 
 
-def inner_attention(rows, counts, attend, attend_bias):
+def place_array():
+    return jnp.stack(place_here()).astype(jnp.int32)
+
+
+def inner_attention(rows, counts, pieces, attend_bias):
     size = rows.shape[0]
+    smem, anywhere = pl.BlockSpec(memory_space=pltpu.SMEM), pl.BlockSpec(memory_space=pl.ANY)
     return row_call(
-        attend_kernel,
+        partial(attend_kernel, len(pieces)),
         "attend",
-        (counts, rows, attend, attend_bias),
-        (None, by_rows(D), None, None),
-        [((size, 3 * D), LOW, by_rows(3 * D)), ((size, D), LOW, by_rows(D))],
+        (counts, rows, place_array(), attend_bias, *pieces),
+        (None, by_rows(D), smem, None) + (anywhere,) * len(pieces),
+        [
+            ((size, 3 * D), LOW, by_rows(3 * D)),
+            ((size, D), LOW, by_rows(D)),
+            ((D, 3 * D), LOW, anywhere),
+        ],
         2 * size * D * (3 * D + 4 * SEG),
-    )
-
-
-def inner_feed(rows, counts, projected, context, weights):
-    attend, merge, expand, reduce_matrix, expand_bias, vectors = weights
-    size, wide = rows.shape[0], expand.shape[1]
+        scratch=[
+            pltpu.VMEM((D, 3 * D), LOW),
+            pltpu.SemaphoreType.DMA((32,)),
+            pltpu.SemaphoreType.DMA,
+        ],
+    )
+
+
+def inner_feed(rows, counts, projected, context, mid, end, expand_bias, vectors):
+    size, wide = rows.shape[0], expand_bias.shape[1]
+    mid_moves, end_moves = mid_moves_of(mid), mid_moves_of(end)
+    smem, anywhere = pl.BlockSpec(memory_space=pltpu.SMEM), pl.BlockSpec(memory_space=pl.ANY)
     mixed, heads, wide_heads, *saved = row_call(
-        feed_kernel,
+        partial(feed_kernel, mid_moves, end_moves, (len(mid), len(end))),
         "feed",
-        (counts, rows, context, merge, expand, expand_bias, reduce_matrix, vectors),
-        (None, by_rows(D), by_rows(D), None, None, None, None, None),
+        (counts, rows, context, place_array(), expand_bias, vectors, *mid, *end),
+        (None, by_rows(D), by_rows(D), smem, None, None) + (anywhere,) * (len(mid) + len(end)),
         [
             ((size, D), LOW, by_rows(D)),
             ((size // SEG, 5 * D), F32, whole_block((size // SEG, 5 * D))),
@@ -346,14 +453,24 @@
             ((size, wide), LOW, by_rows(wide)),
             ((size, wide), LOW, by_rows(wide)),
             ((size, D), F32, by_rows(D)),
+            ((D, D), LOW, anywhere),
+            ((D, wide), LOW, anywhere),
+            ((wide, D), LOW, anywhere),
         ],
         2 * size * D * (D + 2 * wide),
-    )
-    return mixed, heads, wide_heads, saved
+        scratch=[
+            pltpu.VMEM((D, D), LOW),
+            pltpu.VMEM((D, wide), LOW),
+            pltpu.VMEM((wide, D), LOW),
+            pltpu.SemaphoreType.DMA((2 * len(mid_moves) + len(end_moves),)),
+            pltpu.SemaphoreType.DMA((3,)),
+        ],
+    )
+    return mixed, heads, wide_heads, saved[:5], saved[5:]
 
 
 def inner_feed_back(cotangent, counts, saved, weights):
-    attend, merge, expand, reduce_matrix, expand_bias, vectors = weights
+    merge, expand, reduce_matrix, vectors = weights
     first, normed, active, slope, second = saved
     size, wide = cotangent.shape[0], expand.shape[1]
     return row_call(
@@ -421,8 +538,16 @@
         rows_ref[row : row + 1, : ref.shape[1]] = ref[...].astype(F32)
     place = jnp.transpose(place_ref[...].astype(F32))
     rows_ref[16 : 16 + SEGS, : place.shape[1]] = place
-    packed = rows_ref[...].astype(LOW)
-    out_ref[...] = jnp.broadcast_to(packed[None], out_ref.shape)
+    out_ref[...] = rows_ref[...].astype(LOW)
+
+
+def pack_small(vectors, segment_place):
+    return pl.pallas_call(
+        pack_kernel,
+        out_shape=jax.ShapeDtypeStruct((16 + SEGS, 128), LOW),
+        scratch_shapes=[pltpu.VMEM((16 + SEGS, 128), F32)],
+        name="pack",
+    )(*[vector[None] for vector in vectors], segment_place)
 
 
 def spread_row(rows, size, width):
@@ -439,9 +564,32 @@
 VECTOR_ROWS = (1, 2, 3, 5, 6, 7)
 
 
-def unpack_kernel(sizes, got_ref, *outs):
-    devices = got_ref.shape[0]
-    got = got_ref[...].astype(F32)
+def unpack_kernel(sizes, place_ref, *refs):
+    outs, got_ref, sems = refs[-9:-2], refs[-2], refs[-1]
+    pieces = refs[:-9]
+    plane, depth = place_ref[0], place_ref[1]
+    if len(pieces) == 1:
+        copies = [pltpu.make_async_copy(pieces[0], got_ref, sems.at[0])]
+    else:
+        copies = []
+        slots = ((0, 0, 4), (1, 0, 4), (2, 0, 4), (3, 0, 2), (3, 2, 2))
+        first_lane = pieces[0].shape[2] - 128
+        for piece, (turn, first, count) in zip(pieces, slots):
+            for slot in range(count):
+                chip = (plane ^ turn) * 4 + ((depth + 4 - first - slot) & 3)
+                copies.append(
+                    pltpu.make_async_copy(
+                        piece.at[slot, :, first_lane : first_lane + 128],
+                        got_ref.at[pl.ds(pl.multiple_of(48 * chip, 48), 48), :],
+                        sems.at[len(copies)],
+                    )
+                )
+    for copy in copies:
+        copy.start()
+    for copy in copies:
+        copy.wait()
+    got = got_ref[...].astype(F32).reshape(-1, 16 + SEGS, 128)
+    devices = got.shape[0]
     for block in range(2):
         attend_ref, expand_ref, vectors_ref = outs[3 * block : 3 * block + 3]
         for kind in range(8):
@@ -456,23 +604,13 @@
                 place = VECTOR_ROWS.index(kind)
                 vectors_ref[place : place + 1, :] = spread
         vectors_ref[6:8, :] = jnp.zeros((2, vectors_ref.shape[1]), F32)
-    place_ref = outs[6]
     for segment in range(SEGS):
-        place_ref[segment : segment + 1, :] = spread_row(
+        outs[6][segment : segment + 1, :] = spread_row(
             got[:, 16 + segment, :].astype(LOW), sizes[16], sizes[16] * devices
         )
 
 
-def share_small(vectors, segment_place):
-    devices = lax.axis_size(AXES)
-    sizes = [vector.shape[0] for vector in vectors] + [segment_place.shape[0]]
-    sent = pl.pallas_call(
-        pack_kernel,
-        out_shape=jax.ShapeDtypeStruct((devices, 32, 128), LOW),
-        scratch_shapes=[pltpu.VMEM((32, 128), F32)],
-        name="pack",
-    )(*[vector[None] for vector in vectors], segment_place)
-    got = lax.all_to_all(sent, AXES, split_axis=0, concat_axis=0, tiled=True)
+def unpack_small(sizes, devices, pieces):
     shapes = []
     for block in range(2):
         for rows, size in ((1, sizes[8 * block]), (1, sizes[8 * block + 4]), (8, sizes[1])):
@@ -481,16 +619,22 @@
     return pl.pallas_call(
         partial(unpack_kernel, sizes),
         out_shape=shapes,
+        in_specs=[pl.BlockSpec(memory_space=pltpu.SMEM)]
+        + [pl.BlockSpec(memory_space=pl.ANY)] * len(pieces),
+        scratch_shapes=[
+            pltpu.VMEM((devices * (16 + SEGS), 128), LOW),
+            pltpu.SemaphoreType.DMA((16,)),
+        ],
         compiler_params=pltpu.CompilerParams(vmem_limit_bytes=60 << 20),
         name="unpack",
-    )(got)
-
-
-def sum_rows(rows):
+    )(place_array(), *pieces)
+
+
+def sum_rows(rows, gate):
     devices, size = rows.shape
     padded = jnp.pad(rows, ((0, 0), (0, -size % 1024))).reshape(devices, -1, 128)
     got = lax.all_to_all(padded, AXES, split_axis=0, concat_axis=0, tiled=True)
-    return jnp.sum(got, axis=0).reshape(-1)[:size]
+    return jnp.sum(after(gate, got), axis=0).reshape(-1)[:size]
 
 
 def hop(array, turn):
@@ -537,74 +681,19 @@
     )
 
 
-def assemble_kernel(heights, widths, place_ref, *refs):
-    pieces, outs, sems = refs[:10], refs[10:-1], refs[-1]
-    plane, depth, core = place_ref[0], place_ref[1], place_ref[2]
-    slots = ((0, 0, 4), (1, 0, 4), (2, 0, 4), (3, 0, 2), (3, 2, 2))
-    copies = []
-    for side in range(2):
-        column = core if side == 0 else 1 - core
-        for number, (turn, first, count) in enumerate(slots):
-            piece = pieces[5 * side + number]
-            for slot in range(count):
-                chip = (plane ^ turn) * 4 + ((depth + 4 - first - slot) & 3)
-                start = 0
-                for out, height, width in zip(outs, heights, widths):
-                    for group in range(height // 48):
-                        row = pl.multiple_of(chip * height + 48 * group, 48)
-                        lane = pl.multiple_of(column * width, 128)
-                        copies.append(
-                            pltpu.make_async_copy(
-                                piece.at[slot, :, pl.ds(start, width)],
-                                out.at[pl.ds(row, 48), pl.ds(lane, width)],
-                                sems.at[len(copies)],
-                            )
-                        )
-                        start += width
-    for copy in copies:
-        copy.start()
-    for copy in copies:
-        copy.wait()
-
-
-def gather_links(shards, gate, gates):
-    plane, depth, core = place_here()
-    rows = min(shard.shape[0] for shard in shards)
-    mine = jnp.concatenate([fold_rows(half_cols(shard, core), rows) for shard in shards], axis=1)
-    sent = jnp.concatenate(
-        [fold_rows(half_cols(shard, 1 - core), rows) for shard in shards], axis=1
-    )
-    other = over_core(sent)
-    widths = [shard.shape[1] // 2 for shard in shards]
-    heights = [2 * shard.shape[0] for shard in shards]
-    slab, start = [], 0
-    for width, height in zip(widths, heights):
-        span = width * (height // (2 * rows))
-        pair = [unfold_cols(part[:, start : start + span], width) for part in (mine, other)]
-        slab.append(fold_rows(both_cores(pair[0], pair[1], core, 0), 2 * rows))
-        start += span
-    slab = jnp.concatenate(slab, axis=1)
-    line = jnp.stack([slab] + [over_z(slab, step) for step in (1, 2, 3)])
-    gates.append(slab)
-    line = after(gate, line)
+def attend_line(shard, small):
+    core = place_here()[2]
+    mine = jnp.concatenate([half_cols(shard, core), small], axis=1)
+    sent = jnp.concatenate([half_cols(shard, 1 - core), small], axis=1)
+    slab = both_cores(mine, over_core(sent), core, 0)
+    hops = [over_z(slab, step) for step in (1, 2, 3)]
+    return slab, jnp.stack([slab] + hops)
+
+
+def attend_pieces(line):
     line_x, line_y = over_x(line), over_y(line)
     pieces = [line, line_x, line_y, over_y(line_x[:2]), over_x(line_y[2:])]
-    pieces = pieces + [over_core(piece) for piece in pieces]
-    count = 32 * sum(height // 48 for height in heights)
-    place = jnp.stack([plane, depth, core]).astype(jnp.int32)
-    return pl.pallas_call(
-        partial(assemble_kernel, heights, widths),
-        out_shape=[
-            jax.ShapeDtypeStruct((16 * height, 2 * width), jnp.bfloat16)
-            for height, width in zip(heights, widths)
-        ],
-        in_specs=[pl.BlockSpec(memory_space=pltpu.SMEM)]
-        + [pl.BlockSpec(memory_space=pl.ANY)] * 10,
-        out_specs=[pl.BlockSpec(memory_space=pltpu.VMEM)] * len(shards),
-        scratch_shapes=[pltpu.SemaphoreType.DMA((count,))],
-        compiler_params=pltpu.CompilerParams(vmem_limit_bytes=60 << 20),
-        name="assemble",
-    )(place, *pieces)
+    return pieces + [over_core(piece) for piece in pieces]
 
 
 def after(first, *later):
@@ -612,67 +701,34 @@
     return tied[0] if len(tied) == 1 else tied
 
 
-def first_hops(line, gate):
-    core = place_here()[2]
+def half_rows(line):
     half = line.shape[0] // 2
-    mine = after(gate, lax.dynamic_slice_in_dim(line, core * half, half, axis=0))
+    return lax.dynamic_slice_in_dim(line, place_here()[2] * half, half, axis=0)
+
+
+def first_hops(line, mine):
     return line, over_x(mine), over_y(mine)
 
 
-def last_hops(hops, gate):
+def last_hops(hops, gate, late_gate=()):
     line, from_x, from_y = hops
     half = from_x.shape[0] // 2
     sent_y, sent_x = after(gate, from_x[:half], from_y[half:])
     pieces = [from_x, from_y, over_y(sent_y), over_x(sent_x)]
-    return [line] + pieces + [over_core(piece) for piece in pieces]
-
-
-def late_pieces(shard):
+    return [line] + pieces + [over_core(piece) for piece in after(late_gate, *pieces)]
+
+
+def late_hops(shard):
+    return shard, over_x(shard), over_y(shard)
+
+
+def late_pieces(hops, gate):
+    shard, from_x, from_y = hops
     half = shard.shape[0] // 2
-    from_x, from_y = over_x(shard), over_y(shard)
-    across = jnp.concatenate([over_y(from_x[:half]), over_x(from_y[half:])], axis=0)
+    sent_y, sent_x = after(gate, from_x[:half], from_y[half:])
+    across = jnp.concatenate([over_y(sent_y), over_x(sent_x)], axis=0)
     rows = jnp.concatenate([shard, from_x, from_y, across], axis=0)
     return [lax.all_gather(rows, "fsdp", axis=0, tiled=True)]
-
-
-def join_kernel(all_moves, all_widths, counts, place_ref, *refs):
-    total = sum(counts)
-    pieces, outs, sems = refs[:total], refs[total:-1], refs[-1]
-    waits, first, start, number = [], 0, 0, 0
-    for moves, widths, count in zip(all_moves, all_widths, counts):
-        targets = outs[number : number + len(widths)]
-        waits += start_moves(
-            pieces[start : start + count], targets, widths, moves, place_ref, sems, first
-        )
-        first += len(moves) * len(widths)
-        start += count
-        number += len(widths)
-    for copies in waits:
-        wait_all(copies)
-
-
-def join_pieces(groups, all_widths):
-    plane, depth, core = place_here()
-    place = jnp.stack([plane, depth, core]).astype(jnp.int32)
-    all_moves = [mid_moves_of(pieces) for pieces in groups]
-    shapes = [
-        jax.ShapeDtypeStruct((4 * pieces[0].shape[0], width), jnp.bfloat16)
-        for pieces, widths in zip(groups, all_widths)
-        for width in widths
-    ]
-    sems = sum(len(moves) * len(widths) for moves, widths in zip(all_moves, all_widths))
-    pieces = [piece for group in groups for piece in group]
-    joined = pl.pallas_call(
-        partial(join_kernel, all_moves, all_widths, [len(group) for group in groups]),
-        out_shape=shapes,
-        in_specs=[pl.BlockSpec(memory_space=pltpu.SMEM)]
-        + [pl.BlockSpec(memory_space=pl.ANY)] * len(pieces),
-        out_specs=[pl.BlockSpec(memory_space=pltpu.VMEM)] * len(shapes),
-        scratch_shapes=[pltpu.SemaphoreType.DMA((sems,))],
-        compiler_params=pltpu.CompilerParams(vmem_limit_bytes=60 << 20),
-        name="join",
-    )(place, *pieces)
-    return list(joined)
 
 
 def along_z(shards):
@@ -955,42 +1011,106 @@
     )
 
 
-def scatter_pack(grads):
-    core = place_here()[2]
-
-    def packed(side):
-        return jnp.concatenate(
-            [
-                jnp.transpose(
-                    half_cols(grad, side).reshape(16, grad.shape[0] // 768, 48, -1), (0, 2, 1, 3)
-                ).reshape(16, 48, -1)
-                for grad in grads
-            ],
-            axis=2,
-        )
-
-    return packed(core), packed(1 - core)
-
-
-def scatter_core(kept, sent):
+UNIT = 384
+
+
+def grads_kernel(jobs, adds, side_ref, *refs):
+    refs, came_ref, out_ref = refs[: -1 - adds], refs[-2], refs[-1]
+    unit = pl.program_id(0)
+
+    def put(chips, units, shape, total):
+        total = total.reshape(shape)
+        if adds:
+            total = total + came_ref[chips, units].astype(F32)
+        out_ref[chips, units] = total.astype(LOW)
+
+    for folded, first, count, number in jobs:
+        (left_ref, right_ref), heads, refs = refs[:2], refs[2:number], refs[number:]
+
+        @pl.when((unit >= first) & (unit < first + count))
+        def _(folded=folded, first=first, left_ref=left_ref, right_ref=right_ref, heads=heads):
+            total = cross_rows(left_ref[...], right_ref[...])
+            if heads:
+                total = total + cross_rows(heads[0][...].astype(LOW), heads[1][...])
+            if folded:
+                chips = pl.ds(4 * (unit - first), 4)
+                put(chips, slice(first, first + 4), (4, 4, 48, UNIT), total)
+            else:
+                put(slice(None), pl.ds(unit, 1), (16, 1, 48, UNIT), total)
+
+
+def half_grads(jobs, side, came=None):
+    rules, operands, specs, first = [], [], [], 0
+    for left, right, head_left, column, head_right in jobs:
+        folded = left.shape[1] > D
+        count = left.shape[1] // D if folded else right.shape[1] // (2 * UNIT)
+        start = first
+
+        def place(unit, start=start, count=count):
+            return lax.min(lax.max(unit - start, 0), count - 1)
+
+        def left_index(unit, side, place=place, folded=folded):
+            return (0, place(unit) if folded else 0)
+
+        def right_index(unit, side, place=place, folded=folded, count=count):
+            return (0, side[0] if folded else side[0] * count + place(unit))
+
+        def head_index(unit, side, place=place, folded=folded, column=column):
+            return (0, column + (place(unit) if folded else 0))
+
+        operands += [left, right]
+        specs += [
+            pl.BlockSpec((left.shape[0], D), left_index),
+            pl.BlockSpec((right.shape[0], UNIT), right_index),
+        ]
+        if head_left is not None:
+            operands += [head_left, head_right]
+            specs += [
+                pl.BlockSpec((SEGS, D), head_index),
+                pl.BlockSpec((SEGS, UNIT), right_index),
+            ]
+        rules.append((folded, first, count, 2 if head_left is None else 4))
+        first += count
+    shape = (16, first, 48, UNIT)
+    whole = pl.BlockSpec(shape, lambda unit, side: (0, 0, 0, 0))
+    if came is not None:
+        operands.append(came)
+        specs.append(whole)
+    size = operands[0].shape[0]
+    return pl.pallas_call(
+        partial(grads_kernel, rules, int(came is not None)),
+        grid_spec=pltpu.PrefetchScalarGridSpec(
+            num_scalar_prefetch=1, grid=(first,), in_specs=specs, out_specs=whole
+        ),
+        out_shape=jax.ShapeDtypeStruct(shape, LOW),
+        compiler_params=pltpu.CompilerParams(vmem_limit_bytes=60 << 20),
+        cost_estimate=pl.CostEstimate(
+            flops=2 * first * size * D * UNIT, bytes_accessed=30 << 20, transcendentals=0
+        ),
+        name="half_grads",
+    )(side.astype(jnp.int32)[None], *operands)
+
+
+def scatter_planes(kept):
     plane = place_here()[0]
-    kept = (kept + over_core(sent)).reshape(4, 4, 48, -1)
+    kept = kept.reshape(4, 4, *kept.shape[1:])
     return [
         lax.dynamic_index_in_dim(kept, plane ^ turn, axis=0, keepdims=False)
         for turn in range(4)
     ]
 
 
-def scatter_across(planes):
+def scatter_across(planes, gate):
     here, next_x, next_y, across = planes
     from_y, from_x = over_y(across[:2]), over_x(across[2:])
+    next_x, next_y = after(gate, next_x, next_y)
     next_x = jnp.concatenate([next_x[:2] + from_y, next_x[2:]], axis=0)
     next_y = jnp.concatenate([next_y[:2], next_y[2:] + from_x], axis=0)
     return here, next_x, next_y
 
 
-def scatter_next(here, next_x, next_y):
-    came_x, came_y = over_x(next_x), over_y(next_y)
+def scatter_next(here, next_x, next_y, gate):
+    came_x, came_y = after(gate, over_x(next_x), over_y(next_y))
     return (
         here.astype(jnp.float32) + came_x.astype(jnp.float32) + came_y.astype(jnp.float32)
     ).astype(jnp.bfloat16)
@@ -1008,14 +1128,29 @@
     return total
 
 
+def scatter_along(here):
+    chips = here.shape[0]
+    groups = [[2 * chip + core for chip in range(chips)] for core in range(2)]
+    total = lax.psum_scatter(
+        here.reshape(-1, here.shape[-1]),
+        "fsdp",
+        scatter_dimension=0,
+        axis_index_groups=groups,
+        tiled=True,
+    )
+    return total.reshape(here.shape[1:]).astype(jnp.float32)
+
+
 def scatter_end(total, shapes):
     core = place_here()[2]
     mine, sent, start = [], [], 0
     for height, width in shapes:
-        width = width // 2
         groups = height // 768
-        rows = unfold_cols(total[:, start : start + groups * width], width)
-        start += groups * width
+        count = groups if groups > 1 else width // (2 * UNIT)
+        rows = jnp.concatenate(
+            [total[unit] for unit in range(start, start + count)], axis=0 if groups > 1 else 1
+        )
+        start += count
         mine.append(fold_rows(lax.dynamic_slice_in_dim(rows, core * 24 * groups, 24 * groups), 24))
         sent.append(
             fold_rows(lax.dynamic_slice_in_dim(rows, (1 - core) * 24 * groups, 24 * groups), 24)
@@ -1105,6 +1240,45 @@
     devices = D // parts
     ratio = inner_reduce.shape[0] // parts
     here = lax.axis_index(AXES)
+    linked = lax.axis_size("dp") == 4 and lax.axis_size("fsdp") == 8
+    wide = inner_expand.shape[1]
+    inner_rest = [inner_merge, inner_expand, inner_reduce]
+    outer_all = [outer_attend, outer_merge, outer_expand, outer_reduce]
+    docs = counts.shape[0]
+    head_cotangent = cotangent.reshape(docs * SEGS, SEG, D)[:, 0, :]
+    small_parts = (
+        inner_attend_bias,
+        inner_merge_bias,
+        inner_gain,
+        inner_shift,
+        inner_expand_bias,
+        inner_reduce_bias,
+        inner_final_gain,
+        inner_final_shift,
+        outer_attend_bias,
+        outer_merge_bias,
+        outer_gain,
+        outer_shift,
+        outer_expand_bias,
+        outer_reduce_bias,
+        outer_final_gain,
+        outer_final_shift,
+    )
+    sizes = [part.shape[0] for part in small_parts] + [parts]
+    small = pack_small(small_parts, segment_place)
+    if linked:
+        slab, line = attend_line(inner_attend, small)
+        late_first = late_hops(after(slab, outer_reduce))
+        line = after(late_first[1:], line)
+        pieces = attend_pieces(line)
+        late = late_pieces(late_first, (pieces[3], pieces[4]))
+        mid_line = along_z(after(line, *inner_rest[:2]))
+        end_line = along_z([after(line, inner_rest[2])])
+        outer_line = along_z(after(line, *outer_all[:3]))
+        small_pieces = pieces[:5]
+    else:
+        pieces = gather_flat([inner_attend])
+        small_pieces = [gather(small)]
     (
         attend_bias,
         expand_bias,
@@ -1113,69 +1287,36 @@
         outer_expand_bias_full,
         outer_vectors,
         place_rows,
-    ) = share_small(
-        (
-            inner_attend_bias,
-            inner_merge_bias,
-            inner_gain,
-            inner_shift,
-            inner_expand_bias,
-            inner_reduce_bias,
-            inner_final_gain,
-            inner_final_shift,
-            outer_attend_bias,
-            outer_merge_bias,
-            outer_gain,
-            outer_shift,
-            outer_expand_bias,
-            outer_reduce_bias,
-            outer_final_gain,
-            outer_final_shift,
-        ),
-        segment_place,
-    )
-    linked = lax.axis_size("dp") == 4 and lax.axis_size("fsdp") == 8
-    wide = inner_expand.shape[1]
-    inner_rest = [inner_merge, inner_expand, inner_reduce]
-    outer_all = [outer_attend, outer_merge, outer_expand, outer_reduce]
-    docs = counts.shape[0]
-    head_cotangent = cotangent.reshape(docs * SEGS, SEG, D)[:, 0, :]
+    ) = unpack_small(sizes, devices, small_pieces)
     if linked:
-        gates = []
-        inner_full = list(gather_links([inner_attend], place_rows, gates))
-        mid_line = along_z(after(gates[0], *inner_rest[:2]))
-        end_line = along_z([after(gates[0], inner_rest[2])])
-        outer_line = along_z(after(gates[0], *outer_all[:3]))
-        projected, context = inner_attention(tokens, counts, inner_full[0], attend_bias)
-        mid = first_hops(mid_line, inner_full[0])
-        end = first_hops(end_line, (context, mid[1], mid[2]))
+        mid_half = half_rows(after((pieces[3], pieces[4], attend_bias), mid_line))
+        attend_bias = after(mid_half, attend_bias)
+    projected, context, attend = inner_attention(tokens, counts, pieces, attend_bias)
+    if linked:
+        mid = first_hops(mid_line, mid_half)
+        end = first_hops(end_line, half_rows(after((context, mid[1], mid[2]), end_line)))
         mid = last_hops(mid, context)
         end = last_hops(end, (mid[3], mid[4]))
-        outer = first_hops(outer_line, (mid[3], mid[4], end[1], end[2]))
-        late = late_pieces(after(context, outer_reduce))
-        inner_full += join_pieces([mid, end], [[D, wide], [D]])
+        outer = first_hops(
+            outer_line, half_rows(after((mid[3], mid[4], end[1], end[2]), outer_line))
+        )
     else:
-        inner_full = gather_flat([inner_attend]) + gather_flat(inner_rest)
-        projected, context = inner_attention(tokens, counts, inner_full[0], attend_bias)
-    inner_weights = (*inner_full, expand_bias, vectors)
-    mixed, heads, wide_heads, saved = inner_feed(tokens, counts, projected, context, inner_weights)
+        rest = gather_flat(inner_rest)
+        mid, end = [jnp.concatenate(rest[:2], axis=1)], rest[2:]
+    mixed, heads, wide_heads, saved, inner_full = inner_feed(
+        tokens, counts, projected, context, mid, end, expand_bias, vectors
+    )
+    inner_weights = (*inner_full, vectors)
+    branch, grad_hidden, grad_attn, grad_context, grad_first, inner_sums, hidden_sums = (
+        inner_feed_back(cotangent, counts, saved, inner_weights)
+    )
     if linked:
-        outer = last_hops(outer, heads)
+        outer = last_hops(outer, heads, inner_sums)
     else:
         outer_full = gather_flat(outer_all)
         outer, late = [jnp.concatenate(outer_full[:3], axis=1)], outer_full[3:]
-    branch, grad_hidden, grad_attn, grad_context, grad_first, inner_sums, hidden_sums = (
-        inner_feed_back(cotangent, counts, saved, inner_weights)
-    )
     first, normed, active, slope, second = saved
     low = jnp.bfloat16
-    plain_grads = lax.optimization_barrier(
-        (
-            cross_rows(active, branch).astype(low),
-            cross_rows(normed, grad_hidden).astype(low),
-            cross_rows(context, grad_attn).astype(low),
-        )
-    )
     (
         head_out,
         grad_heads,
@@ -1198,72 +1339,95 @@
         (outer_attend_bias_full, outer_expand_bias_full, outer_vectors, vectors),
         outer,
         late[0],
-        inner_full[1:],
+        inner_full,
         linked,
     )
     grad_place = jnp.transpose(jnp.sum(grad_heads.reshape(docs, SEGS, D), axis=0))
     inner_sums = inner_sums + head_sums
     hidden_sums = hidden_sums + head_hidden_sums
-    grad_reduce, grad_expand, grad_merge = [
-        (plain.astype(jnp.float32) + cross_rows(left.astype(low), right)).astype(low)
-        for plain, left, right in zip(
-            plain_grads,
-            (wide_heads[:, wide:], heads[:, 3 * D : 4 * D], heads[:, 4 * D :]),
-            (head_branch, head_hidden, head_attn),
-        )
-    ]
     operands = (projected, grad_context, grad_first, mixed)
     head_rows = (head_context, head_first, head_out)
     steps = tokens.shape[0] // ROWS
+    right_all = gather(right_pack)
+
+    def left_factors(left_pack):
+        rows = jnp.concatenate(
+            [
+                factor.reshape(factor.shape[0], devices, -1)
+                for factor in split_cols(left_pack, (D, D, D, wide))
+            ],
+            axis=2,
+        )
+        return jnp.transpose(rows, (1, 0, 2))
+
+    def exchange(rows):
+        return lax.all_to_all(rows, AXES, split_axis=0, concat_axis=0, tiled=True)
+
+    def outer_grads(left_all, right_all):
+        left_all = left_all.reshape(-1, left_all.shape[-1])
+        left_pieces = split_cols(left_all, (parts, parts, parts, parts * ratio))
+        right_pieces = split_cols(right_all, (3 * D, D, wide, D))
+        big = [cross_rows(left, right) for left, right in zip(left_pieces, right_pieces)]
+        bias = [
+            lax.dynamic_slice_in_dim(
+                jnp.sum(right.astype(jnp.float32), axis=0), here * width, width, axis=0
+            )
+            for right, width in zip(right_pieces, (3 * parts, parts, wide // devices, parts))
+        ]
+        return big, bias
+
     if linked:
-        kept, sent = scatter_pack([grad_expand, grad_reduce])
-        operands = after(sent, *operands)
-        part = inner_attend_back(counts, operands, inner_full[0], head_rows, 0, steps // 2, ())
-        planes = scatter_core(kept, sent)
-        operands = after(planes, *operands)
+        core = place_here()[2]
+        jobs = [
+            (normed, grad_hidden, heads, 3, head_hidden),
+            (active, branch, wide_heads, wide // D, head_branch),
+            (context, grad_attn, heads, 4, head_attn),
+        ]
+        sent = half_grads(jobs, 1 - core)
+        left_all = exchange(left_factors(after(sent, left_pack)))
+        part = inner_attend_back(
+            counts, after(sent, *operands), attend, head_rows, 0, 1, ()
+        )
+        kept = half_grads(jobs, after((part[3], left_all), core), over_core(sent))
+        planes = scatter_planes(kept)
+        middle = inner_attend_back(
+            counts, after(planes, *operands), attend, head_rows, 1, 1, part[:3]
+        )
+        tall = scatter_across(planes, middle[3])
         rest = inner_attend_back(
-            counts, operands, inner_full[0], head_rows, steps // 2, steps - steps // 2, part[:3]
+            counts, after(tall, *operands), attend, head_rows, 2, steps - 2, middle[:3]
         )
         grad_projected, tokens_grad, mixed = rest[:3]
-        attend_sums = part[3] + rest[3]
-        tall = scatter_across(planes)
-        tall = scatter_next(*tall)
-        grad_attend = cross_rows(tokens, grad_projected).astype(low)
-        planes = scatter_core(*scatter_pack([grad_attend, grad_merge]))
-        tall = scatter_line(tall)
-        short = scatter_next(*scatter_across(planes))
+        attend_sums = part[3] + middle[3] + rest[3]
+        outer_big, outer_bias = outer_grads(*after(rest[3], left_all, right_all))
+        jobs = [(tokens, grad_projected, None, 0, None)]
+        tall = scatter_next(*tall, (outer_big, outer_bias))
+        sent = half_grads(jobs, after(tall, 1 - core))
+        tall = scatter_along(tall)
+        kept = half_grads(jobs, core, over_core(sent))
+        short = scatter_next(*scatter_across(scatter_planes(kept), ()), ())
+        sums_gate = short
         short = scatter_line(short)
-        own_expand, own_reduce = scatter_end(tall, [grad_expand.shape, grad_reduce.shape])
-        own_attend, own_merge = scatter_end(short, [grad_attend.shape, grad_merge.shape])
+        own_expand, own_reduce, own_merge = scatter_end(tall, [(D, wide), (wide, D), (D, D)])
+        (own_attend,) = scatter_end(short, [(D, 3 * D)])
     else:
+        sums_gate = ()
+        left_all = exchange(left_factors(left_pack))
+        outer_big, outer_bias = outer_grads(left_all, right_all)
         grad_projected, tokens_grad, mixed, attend_sums = inner_attend_back(
-            counts, operands, inner_full[0], head_rows, 0, steps, ()
+            counts, operands, attend, head_rows, 0, steps, ()
         )
         grad_attend = cross_rows(tokens, grad_projected).astype(low)
+        grad_reduce, grad_expand, grad_merge = [
+            (cross_rows(left, right) + cross_rows(head_left.astype(low), head_right)).astype(low)
+            for left, right, head_left, head_right in (
+                (active, branch, wide_heads[:, wide:], head_branch),
+                (normed, grad_hidden, heads[:, 3 * D : 4 * D], head_hidden),
+                (context, grad_attn, heads[:, 4 * D :], head_attn),
+            )
+        ]
         own_expand, own_reduce = scatter_flat([grad_expand, grad_reduce])
         own_attend, own_merge = scatter_flat([grad_attend, grad_merge])
-    left_pack = jnp.concatenate(
-        [
-            factor.reshape(factor.shape[0], devices, -1)
-            for factor in split_cols(left_pack, (D, D, D, wide))
-        ],
-        axis=2,
-    )
-    left_pack = jnp.transpose(left_pack, (1, 0, 2))
-    left_all = lax.all_to_all(left_pack, AXES, split_axis=0, concat_axis=0, tiled=True)
-    left_all = left_all.reshape(-1, left_all.shape[-1])
-    right_all = gather(right_pack)
-    left_pieces = split_cols(left_all, (parts, parts, parts, parts * ratio))
-    right_pieces = split_cols(right_all, (3 * D, D, wide, D))
-    outer_big = [cross_rows(left, right) for left, right in zip(left_pieces, right_pieces)]
-    outer_bias = [
-        lax.dynamic_slice_in_dim(
-            jnp.sum(right.astype(jnp.float32), axis=0), here * width, width, axis=0
-        )
-        for right, width in zip(
-            right_pieces, (3 * parts, parts, wide // devices, parts)
-        )
-    ]
     row_sums = (
         attend_sums,
         inner_sums[5],
@@ -1279,7 +1443,7 @@
         outer_sums[1],
         grad_place,
     )
-    sums = sum_rows(jnp.concatenate([entry.reshape(devices, -1) for entry in row_sums], axis=1))
+    sums = sum_rows(jnp.concatenate([entry.reshape(devices, -1) for entry in row_sums], axis=1), sums_gate)
     sums = split_cols(sums, [entry.size // devices for entry in row_sums])
     return (
         mixed,

time: 483 us -> 413 us (0.86)
  waiting for transfers between devices: 137 us -> 93.8 us
  Pallas kernels: 140 us -> 181 us
  matrix products: 41.8 us -> 4.05 us
  other arithmetic: 34.2 us -> 19.9 us
  starting transfers between devices: 65.8 us -> 56.1 us
    ppermute x59 -> x56, waiting for transfers between devices: 136 us -> 90.3 us  [hop(): lax.ppermute(array, AXES, [(place, turn(place)) for place in range(32)])]
    dot_general x11 -> x4, matrix products: 41.8 us -> 4.05 us  [cross_rows(): lax.dot_general(left_rows, right_rows, (((0,), (0,)), ((), ())), preferre...]
    pallas_call x4 -> x6, Pallas kernels: 18.6 us -> 55 us  [the longest x4 49.5 us: half_grads(): pl.pallas_call(partial(grads_kernel, rules, int(came is not None)), grid_...]
    all_to_all x2 -> x1, starting transfers between devices: 13.5 us -> 3.37 us  [exchange(): return lax.all_to_all(rows, AXES, split_axis=0, concat_axis=0, tiled=True)]
    add x3 -> x1, other arithmetic: 7.23 us -> 0.03 us  [on_device(): attend_sums = part[3] + middle[3] + rest[3]]
    pallas_call x5 -> x6, Pallas kernels: 105 us -> 109 us  [row_call(): pl.pallas_call(kernel, grid=(rows // ROWS if steps is None else steps,),...]
    unnamed x121 -> x102, local copies, waits for them, and re-layouts: 14.5 us -> 11.7 us
    ppermute x59 -> x56, starting transfers between devices: 49.1 us -> 48 us  [hop(): lax.ppermute(array, AXES, [(place, turn(place)) for place in range(32)])]
  transfers between devices with their start and end apart: 67 -> 64, of which waited for: 31 -> 28; matrix products, arithmetic and copies ran while one was open for 18% -> 10% of each run, Pallas kernels for 26% -> 32%
where the time goes in v4:
time: 413 us; the launch traced here: 408 us
  Pallas kernels  181 us (44%)
  waiting for transfers between devices  93.8 us (23%)
  starting transfers between devices  56.1 us (14%)
  local copies, waits for them, and re-layouts  36.5 us (9%)
  other arithmetic  19.9 us (5%)
  between operations  16.2 us (4%)
    pallas_call x6, Pallas kernels, row_call(): pl.pallas_call(kernel, grid=(rows // ROWS if steps is None else steps,),...  109 us
    ppermute x56, waiting for transfers between devices, hop(): lax.ppermute(array, AXES, [(place, turn(place)) for place in range(32)])  90.3 us
    pallas_call x4, Pallas kernels, half_grads(): pl.pallas_call(partial(grads_kernel, rules, int(came is not None)), grid_...  49.5 us
    ppermute x56, starting transfers between devices, hop(): lax.ppermute(array, AXES, [(place, turn(place)) for place in range(32)])  48 us
    pallas_call x1, Pallas kernels, heads_step(): pl.pallas_call(partial(heads_kernel, (len(mid), 1), mid_moves, end_moves)...  17 us
    unnamed x102, local copies, waits for them, and re-layouts  11.7 us
  transfers between devices with their start and end apart: 64, of which 28 were waited for; matrix products, arithmetic and copies ran while one was open for 10% of the time, Pallas kernels for 32%

profile of v4, /device:TPU:0, one launch (start us, length us, event | category | flops | bytes accessed | tf_op | source)
XLA Modules:
  0.0 407.5 jit_solution(8712649762460153016)
XLA Ops:
  9.6 1.5 pack.1
  14.0 5.0 %collective-permute-start.5 = (bf16[48,1280]{1,0:T(8,128)(2,1)S(1)}, bf16[48,1280]{1,0:T(8,128)(2,1)S(1)}, u32[]{:S(2)}, u32[]{:S(2)}) collective-permute-start(bf16[48,1280]{1,0:T(8,128)(2,1)S(1)} %get-tuple-element.329), channel_id=1, source_target_pairs={{0,6},{1,7},{2,0},{3,1},{4,2},{5,3},{6,4},{7,5},{8,14},{9,15},{10,... | collective-permute-start | bytes 368648 | tf_op jit(solution)/shard_map/ppermute | solution.py:641
  21.5 1.5 collective-permute-start.2
  23.0 7.1 %collective-permute-done.4 = bf16[48,1280]{1,0:T(8,128)(2,1)S(1)} collective-permute-done((bf16[48,1280]{1,0:T(8,128)(2,1)S(1)}, bf16[48,1280]{1,0:T(8,128)(2,1)S(1)}, u32[]{:S(2)}, u32[]{:S(2)}) %collective-permute-start.4) | collective-permute-done | bytes 122912 | tf_op jit(solution)/shard_map/ppermute | solution.py:641
  32.6 1.6 collective-permute-start.6
  34.2 1.5 collective-permute-start.8
  35.7 9.7 %collective-permute-done.6.refs_1_ = bf16[4,48,1280]{2,1,0:T(8,128)(2,1)S(1)} collective-permute-done((bf16[4,48,1280]{2,1,0:T(8,128)(2,1)S(1)}, bf16[4,48,1280]{2,1,0:T(8,128)(2,1)S(1)}, u32[]{:S(2)}, u32[]{:S(2)}) %collective-permute-start.6) | collective-permute-done | bytes 491552 | tf_op jit(solution)/shard_map/ppermute | solution.py:641
  45.4 1.6 collective-permute-start.7
  47.0 1.6 collective-permute-start.9
  48.6 3.4 collective-permute-done.7.refs_3_
  55.5 2.3 collective-permute-done.39
  61.0 4.0 unpack.1
  67.3 1.6 collective-permute-start.16
  72.0 14.7 %attend.1 = (bf16[1024,2304]{1,0:T(8,128)(2,1)}, bf16[1024,768]{1,0:T(8,128)(2,1)}, bf16[768,2304]{1,0:T(8,128)(2,1)}) custom-call(s32[1]{0:T(128)S(6)} %copy.89.count_ref, bf16[1024,768]{1,0:T(8,128)(2,1)} %refs_0_.3, s32[3]{0:T(128)} %pad_add_fusion.place_ref, f32[1,2304]{1,0:T(1,128)} %get-tuple-element.143.bias_ref, bf16[4,48,1280]{2,1,0:T(8,128)(2,1)} %copy-done.4, ...), custom_call_target="tpu_custom_call" | custom-call | flops 4429185024 | bytes 15344656 | tf_op jit(solution)/shard_map/attend/pallas_call | solution.py:392
  91.7 1.6 collective-permute-start.24
  93.3 6.2 %collective-permute-done.17.refs_3_ = bf16[48,3840]{1,0:T(8,128)(2,1)S(1)} collective-permute-done((bf16[48,3840]{1,0:T(8,128)(2,1)S(1)}, bf16[48,3840]{1,0:T(8,128)(2,1)S(1)}, u32[]{:S(2)}, u32[]{:S(2)}) %collective-permute-start.17) | collective-permute-done | bytes 368672 | tf_op jit(solution)/shard_map/ppermute | solution.py:641
  100.5 11.1 %collective-permute-done.23.refs_10_ = bf16[384,768]{1,0:T(8,128)(2,1)} collective-permute-done((bf16[384,768]{1,0:T(8,128)(2,1)S(1)}, bf16[384,768]{1,0:T(8,128)(2,1)}, u32[]{:S(2)}, u32[]{:S(2)}) %collective-permute-start.23) | collective-permute-done | bytes 589856 | tf_op jit(solution)/shard_map/ppermute | solution.py:641
  113.6 1.6 collective-permute-start.25
  115.8 5.9 %collective-permute-done.25.refs_12_ = bf16[192,768]{1,0:T(8,128)(2,1)S(1)} collective-permute-done((bf16[192,768]{1,0:T(8,128)(2,1)S(1)}, bf16[192,768]{1,0:T(8,128)(2,1)S(1)}, u32[]{:S(2)}, u32[]{:S(2)}) %collective-permute-start.25) | collective-permute-done | bytes 294944 | tf_op jit(solution)/shard_map/ppermute | solution.py:641
  124.4 1.5 constant_dynamic-slice_fusion.1
  127.7 31.3 %feed.1 = (bf16[1024,768]{1,0:T(8,128)(2,1)}, f32[8,3840]{1,0:T(8,128)}, f32[8,6144]{1,0:T(8,128)}, f32[1024,768]{1,0:T(8,128)}, bf16[1024,768]{1,0:T(8,128)(2,1...) custom-call(s32[1]{0:T(128)S(6)} %copy.89.count_ref, ...), custom_call_target="tpu_custom_call" | custom-call | flops 10871635968 | bytes 46755856 | tf_op jit(solution)/shard_map/feed/pallas_call | solution.py:392
  160.9 1.5 collective-permute-start.33
  163.5 23.1 %feed_back.1 = (bf16[1024,768]{1,0:T(8,128)(2,1)}, bf16[1024,3072]{1,0:T(8,128)(2,1)}, bf16[1024,768]{1,0:T(8,128)(2,1)}, bf16[1024,768]{1,0:T(8,128)(2,1)}, f32...) custom-call(s32[1]{0:T(128)S(6)} %copy.89.count_ref, bf16[1024,768]{1,0:T(8,128)(2,1)} %cotangent_ref.1, ...), custom_call_target="tpu_custom_call" | custom-call | flops 10871635968 | bytes 38989828 | tf_op jit(solution)/shard_map/feed_back/pallas_call | solution.py:392
  190.9 3.1 collective-permute-done.37.refs_7_
  196.6 17.0 %heads.1 = (f32[8,768]{1,0:T(8,128)}, f32[8,768]{1,0:T(8,128)}, bf16[8,5376]{1,0:T(8,128)(2,1)}, bf16[8,6912]{1,0:T(8,128)(2,1)}, f32[8,768]{1,0:T(8,128)}, /*in...) custom-call(s32[3]{0:T(128)} %pad_add_fusion.place_ref, ...), custom_call_target="tpu_custom_call" | custom-call | flops 594542592 | bytes 25952256 | tf_op jit(solution)/shard_map/heads/pallas_call | solution.py:979
  213.6 17.6 %half_grads.4 = bf16[16,9,48,384]{3,2,1,0:T(8,128)(2,1)} custom-call(s32[1]{0:T(128)} %bitcast.side_ref, bf16[1024,768]{1,0:T(8,128)(2,1)} %get-tuple-element.161.refs_0_, bf16[1024,3072]{1,0:T(8,128)(2,1)} %get-tuple-element.168.refs_1_, f32[8,3840]{1,0:T(8,128)} %get-tuple-element.169.heads_ref.refs_2_.refs_10_, ...), custom_call_target="tpu_custom_call" | custom-call | flops 5435817984 | bytes 31457280 | tf_op jit(solution)/shard_map/half_grads/pallas_call | solution.py:1080
  232.9 3.4 all-to-all-start
  236.4 10.8 %attend_back.3 = (bf16[1024,2304]{1,0:T(8,128)(2,1)}, f32[1024,768]{1,0:T(8,128)}, bf16[1024,768]{1,0:T(8,128)(2,1)}, f32[1,2304]{1,0:T(1,128)}) custom-call(s32[1]{0:T(128)S(6)} %copy.89.count_ref, bf16[1024,2304]{1,0:T(8,128)(2,1)} %get-tuple-element.220.projected_ref, bf16[1024,768]{1,0:T(8,128)(2,1)} %get-tuple-element.221.context_ref, ...), custom_call_target="tpu_custom_call" | custom-call | flops 1409286144 | bytes 24069124 | tf_op jit(solution)/shard_map/attend_back/pallas_call | solution.py:392
  247.2 19.3 %half_grads.5 = bf16[16,9,48,384]{3,2,1,0:T(8,128)(2,1)} custom-call(s32[1]{0:T(128)} %bitcast.27.side_ref, bf16[1024,768]{1,0:T(8,128)(2,1)} %get-tuple-element.161.refs_0_, bf16[1024,3072]{1,0:T(8,128)(2,1)} %get-tuple-element.168.refs_1_, f32[8,3840]{1,0:T(8,128)} %get-tuple-element.169.heads_ref.refs_2_.refs_10_, ...), custom_call_target="tpu_custom_call" | custom-call | flops 5435817984 | bytes 31457280 | tf_op jit(solution)/shard_map/half_grads/pallas_call | solution.py:1080
  266.5 2.5 dynamic-slice_bitcast_fusion.3
  269.0 1.8 collective-permute-start.42
  272.2 3.0 dynamic-slice_bitcast_fusion
  275.2 10.8 %attend_back.4 = (bf16[1024,2304]{1,0:T(8,128)(2,1)}, f32[1024,768]{1,0:T(8,128)}, bf16[1024,768]{1,0:T(8,128)(2,1)}, f32[1,2304]{1,0:T(1,128)}) custom-call(s32[1]{0:T(128)S(6)} %copy.89.count_ref, bf16[1024,2304]{1,0:T(8,128)(2,1)} %get-tuple-element.220.projected_ref, ...), custom_call_target="tpu_custom_call", output_to_operand_aliasing={{0}: (9, {}), {1}: (10, {}), {2}: (11, {})} | custom-call | flops 1409286144 | bytes 24069124 | tf_op jit(solution)/shard_map/attend_back/pallas_call | solution.py:392
  286.0 6.7 %collective-permute-done.42 = bf16[2,9,48,384]{3,2,1,0:T(8,128)(2,1)} collective-permute-done((bf16[2,9,48,384]{3,2,1,0:T(8,128)(2,1)}, bf16[2,9,48,384]{3,2,1,0:T(8,128)(2,1)}, u32[]{:S(2)}, u32[]{:S(2)}) %collective-permute-start.42) | collective-permute-done | bytes 663584 | tf_op jit(solution)/shard_map/ppermute | solution.py:641
  294.1 1.6 slice_add_fusion.1
  295.9 1.5 collective-permute-start.44
  299.2 18.3 %attend_back.5 = (bf16[1024,2304]{1,0:T(8,128)(2,1)}, f32[1024,768]{1,0:T(8,128)}, bf16[1024,768]{1,0:T(8,128)(2,1)}, f32[1,2304]{1,0:T(1,128)}) custom-call(s32[1]{0:T(128)S(6)} %copy.89.count_ref, bf16[1024,2304]{1,0:T(8,128)(2,1)} %get-tuple-element.220.projected_ref, ...), custom_call_target="tpu_custom_call", output_to_operand_aliasing={{0}: (9, {}), {1}: (10, {}), {2}: (11, {})} | custom-call | flops 2818572288 | bytes 24069124 | tf_op jit(solution)/shard_map/attend_back/pallas_call | solution.py:392
  322.1 1.7 convert_reduce_fusion
  329.0 3.3 add_convert_fusion
  332.3 6.0 %half_grads.6 = bf16[16,3,48,384]{3,2,1,0:T(8,128)(2,1)} custom-call(s32[1]{0:T(128)} %bitcast.35.side_ref, bf16[1024,768]{1,0:T(8,128)(2,1)} %refs_0_.3, bf16[1024,2304]{1,0:T(8,128)(2,1)} %get-tuple-element.229.refs_1_), custom_call_target="tpu_custom_call" | custom-call | flops 1811939328 | bytes 31457280 | tf_op jit(solution)/shard_map/half_grads/pallas_call | solution.py:1080
  338.4 3.9 collective-permute-done.46.refs_2_
  343.5 6.6 %half_grads.7 = bf16[16,3,48,384]{3,2,1,0:T(8,128)(2,1)} custom-call(s32[1]{0:T(128)} %bitcast.3.side_ref, bf16[1024,768]{1,0:T(8,128)(2,1)} %refs_0_.3, bf16[1024,2304]{1,0:T(8,128)(2,1)} %get-tuple-element.229.refs_1_, bf16[16,3,48,384]{3,2,1,0:T(8,128)(2,1)} %copy-done.5), custom_call_target="tpu_custom_call" | custom-call | flops 1811939328 | bytes 31457280 | tf_op jit(solution)/shard_map/half_grads/pallas_call | solution.py:1080
  353.4 5.5 %collective-permute-done.47 = bf16[2,3,48,384]{3,2,1,0:T(8,128)(2,1)S(1)} collective-permute-done((bf16[2,3,48,384]{3,2,1,0:T(8,128)(2,1)S(1)}, bf16[2,3,48,384]{3,2,1,0:T(8,128)(2,1)S(1)}, u32[]{:S(2)}, u32[]{:S(2)}) %collective-permute-start.47) | collective-permute-done | bytes 221216 | tf_op jit(solution)/shard_map/ppermute | solution.py:641
  363.4 4.5 %all-to-all-start.1 = ((f32[32,8,128]{2,1,0:T(8,128)}), f32[32,8,128]{2,1,0:T(8,128)S(1)}, u32[]{:S(2)}, u32[]{:S(2)}) async-start(f32[32,8,128]{2,1,0:T(8,128)} %bitcast.55), calls=%async_computation.1 | async-start | bytes 262144 | tf_op jit(solution)/shard_map/all_to_all | solution.py:636
  367.9 2.7 collective-permute-done.48
  372.8 3.3 collective-permute-start.53
  377.2 2.7 all-to-all-done.1
  383.0 12.0 %collective-permute-done.52 = bf16[3,48,384]{2,1,0:T(8,128)(2,1)S(1)} collective-permute-done((bf16[3,48,384]{2,1,0:T(8,128)(2,1)S(1)}, bf16[3,48,384]{2,1,0:T(8,128)(2,1)S(1)}, u32[]{:S(2)}, u32[]{:S(2)}) %collective-permute-start.52) | collective-permute-done | bytes 110624 | tf_op jit(solution)/shard_map/ppermute | solution.py:641
  (302 shorter events, 80.9 us)
Async XLA Ops:
  7.3 57.8 %all-gather.6.cloned.1.call-start = ((), (), s32[]{:S(2)}) async-start(), calls=%async_computation.3 | async-start | bytes 1658880 | tf_op jit(solution)/shard_map/all_gather | solution.py:735
  14.0 9.0 %collective-permute-start.5 = (bf16[48,1280]{1,0:T(8,128)(2,1)S(1)}, bf16[48,1280]{1,0:T(8,128)(2,1)S(1)}, u32[]{:S(2)}, u32[]{:S(2)}) collective-permute-start(bf16[48,1280]{1,0:T(8,128)(2,1)S(1)} %get-tuple-element.329), channel_id=1, source_target_pairs={{0,6},{1,7},{2,0},{3,1},{4,2},{5,3},{6,4},{7,5},{8,14},{9,15},{10,... | collective-permute-start | bytes 368648 | tf_op jit(solution)/shard_map/ppermute | solution.py:641
  19.0 11.1 %collective-permute-start.4 = (bf16[48,1280]{1,0:T(8,128)(2,1)S(1)}, bf16[48,1280]{1,0:T(8,128)(2,1)S(1)}, u32[]{:S(2)}, u32[]{:S(2)}) collective-permute-start(bf16[48,1280]{1,0:T(8,128)(2,1)S(1)} %get-tuple-element.329), channel_id=1, source_target_pairs={{0,4},{1,5},{2,6},{3,7},{4,0},{5,1},{6,2},{7,3},{8,12},{9,13},{10,... | collective-permute-start | bytes 368648 | tf_op jit(solution)/shard_map/ppermute | solution.py:641
  19.0 11.1 %collective-permute-start.3 = (bf16[48,1280]{1,0:T(8,128)(2,1)S(1)}, bf16[48,1280]{1,0:T(8,128)(2,1)S(1)}, u32[]{:S(2)}, u32[]{:S(2)}) collective-permute-start(bf16[48,1280]{1,0:T(8,128)(2,1)S(1)} %get-tuple-element.329), channel_id=1, source_target_pairs={{0,2},{1,3},{2,4},{3,5},{4,6},{5,7},{6,0},{7,1},{8,10},{9,11},{10,... | collective-permute-start | bytes 368648 | tf_op jit(solution)/shard_map/ppermute | solution.py:641
  20.0 10.2 %collective-permute-start.1 = (bf16[96,768]{1,0:T(8,128)(2,1)}, bf16[96,768]{1,0:T(8,128)(2,1)S(1)}, u32[]{:S(2)}, u32[]{:S(2)}) collective-permute-start(bf16[96,768]{1,0:T(8,128)(2,1)} %param.50), channel_id=1, source_target_pairs={{0,8},{1,9},{2,10},{3,11},{4,12},{5,13},{6,14},{7,15},{8,0},{9,1},... | collective-permute-start | bytes 442376 | tf_op jit(solution)/shard_map/ppermute | solution.py:641
  21.5 8.7 %collective-permute-start.2 = (bf16[96,768]{1,0:T(8,128)(2,1)}, bf16[96,768]{1,0:T(8,128)(2,1)S(1)}, u32[]{:S(2)}, u32[]{:S(2)}) collective-permute-start(bf16[96,768]{1,0:T(8,128)(2,1)} %param.50), channel_id=1, source_target_pairs={{0,16},{1,17},{2,18},{3,19},{4,20},{5,21},{6,22},{7,23},{8,24},{9,... | collective-permute-start | bytes 442376 | tf_op jit(solution)/shard_map/ppermute | solution.py:641
  31.0 58.6 %all-gather.8.cloned.1.call-start = ((), (), s32[]{:S(2)}) async-start(), calls=%async_computation.4 | async-start | bytes 1327104 | tf_op jit(solution)/shard_map/all_gather | solution.py:735
  31.8 90.6 %all-gather.10.cloned.1.call-start = ((), (), s32[]{:S(2)}) async-start(), calls=%async_computation.5 | async-start | bytes 2654208 | tf_op jit(solution)/shard_map/all_gather | solution.py:735
  32.6 163.0 %all-gather.12.cloned.1.call-start = ((), (), s32[]{:S(2)}) async-start(), calls=%async_computation.6 | async-start | bytes 5308416 | tf_op jit(solution)/shard_map/all_gather | solution.py:731
  32.6 12.7 %collective-permute-start.6 = (bf16[4,48,1280]{2,1,0:T(8,128)(2,1)S(1)}, bf16[4,48,1280]{2,1,0:T(8,128)(2,1)S(1)}, u32[]{:S(2)}, u32[]{:S(2)}) collective-permute-start(bf16[4,48,1280]{2,1,0:T(8,128)(2,1)S(1)} %pad_maximum_fusion.2.refs_0_), channel_id=1, source_target_pairs={{0,8},{1,9},{2,10},{3,11},{4,12},{5,13},{6,14},{7,15},{8,0},{9,1},... | collective-permute-start | bytes 1474568 | tf_op jit(solution)/shard_map/ppermute | solution.py:641
  34.2 12.8 %collective-permute-start.8 = (bf16[4,48,1280]{2,1,0:T(8,128)(2,1)S(1)}, bf16[4,48,1280]{2,1,0:T(8,128)(2,1)S(1)}, u32[]{:S(2)}, u32[]{:S(2)}) collective-permute-start(bf16[4,48,1280]{2,1,0:T(8,128)(2,1)S(1)} %pad_maximum_fusion.2.refs_0_), channel_id=1, source_target_pairs={{0,16},{1,17},{2,18},{3,19},{4,20},{5,21},{6,22},{7,23},{8,24},{9,... | collective-permute-start | bytes 1474568 | tf_op jit(solution)/shard_map/ppermute | solution.py:641
  45.4 6.7 %collective-permute-start.7 = (bf16[2,48,1280]{2,1,0:T(8,128)(2,1)S(1)}, bf16[2,48,1280]{2,1,0:T(8,128)(2,1)S(1)}, u32[]{:S(2)}, u32[]{:S(2)}) collective-permute-start(bf16[2,48,1280]{2,1,0:T(8,128)(2,1)S(1)} %slice.329), channel_id=1, source_target_pairs={{0,16},{1,17},{2,18},{3,19},{4,20},{5,21},{6,22},{7,23},{8,24},{9,... | collective-permute-start | bytes 737288 | tf_op jit(solution)/shard_map/ppermute | solution.py:641
  59.8 257.7 %all-gather.14.cloned.1.call-start = ((), (), s32[]{:S(2)}) async-start(), calls=%async_computation.7 | async-start | bytes 3649536 | tf_op jit(solution)/shard_map/all_gather | solution.py:519
  60.5 8.4 %collective-permute-start.10 = (bf16[4,48,1280]{2,1,0:T(8,128)(2,1)S(1)}, bf16[4,48,1280]{2,1,0:T(8,128)(2,1)S(1)}, u32[]{:S(2)}, u32[]{:S(2)}) collective-permute-start(bf16[4,48,1280]{2,1,0:T(8,128)(2,1)S(1)} %pad_maximum_fusion.2.refs_0_), channel_id=1, source_target_pairs={{0,1},{1,0},{2,3},{3,2},{4,5},{5,4},{6,7},{7,6},{8,9},{9,8},{10,11... | collective-permute-start | bytes 1474568 | tf_op jit(solution)/shard_map/ppermute | solution.py:641
  60.5 8.4 %collective-permute-start.11 = (bf16[4,48,1280]{2,1,0:T(8,128)(2,1)S(1)}, bf16[4,48,1280]{2,1,0:T(8,128)(2,1)}, u32[]{:S(2)}, u32[]{:S(2)}) collective-permute-start(bf16[4,48,1280]{2,1,0:T(8,128)(2,1)S(1)} %collective-permute-done.6.refs_1_), channel_id=1, source_target_pairs={{0,1},{1,0},{2,3},{3,2},{4,5},{5,4},{6,7},{7,6},{8,9},{9,8},{10,11... | collective-permute-start | bytes 1474568 | tf_op jit(solution)/shard_map/ppermute | solution.py:641
  61.0 9.0 %collective-permute-start.12 = (bf16[4,48,1280]{2,1,0:T(8,128)(2,1)S(1)}, bf16[4,48,1280]{2,1,0:T(8,128)(2,1)}, u32[]{:S(2)}, u32[]{:S(2)}) collective-permute-start(bf16[4,48,1280]{2,1,0:T(8,128)(2,1)S(1)} %collective-permute-done.8.refs_2_), channel_id=1, source_target_pairs={{0,1},{1,0},{2,3},{3,2},{4,5},{5,4},{6,7},{7,6},{8,9},{9,8},{10,11... | collective-permute-start | bytes 1474568 | tf_op jit(solution)/shard_map/ppermute | solution.py:641
  66.2 20.5 %collective-permute-start.15 = (bf16[96,3840]{1,0:T(8,128)(2,1)S(1)}, bf16[96,3840]{1,0:T(8,128)(2,1)S(1)}, u32[]{:S(2)}, u32[]{:S(2)}) collective-permute-start(bf16[96,3840]{1,0:T(8,128)(2,1)S(1)} %constant_dynamic-slice_fusion.3), channel_id=1, source_target_pairs={{0,8},{1,9},{2,10},{3,11},{4,12},{5,13},{6,14},{7,15},{8,0},{9,1},... | collective-permute-start | bytes 2211848 | tf_op jit(solution)/shard_map/ppermute | solution.py:641
  67.3 19.5 %collective-permute-start.16 = (bf16[96,3840]{1,0:T(8,128)(2,1)S(1)}, bf16[96,3840]{1,0:T(8,128)(2,1)}, u32[]{:S(2)}, u32[]{:S(2)}) collective-permute-start(bf16[96,3840]{1,0:T(8,128)(2,1)S(1)} %constant_dynamic-slice_fusion.3), channel_id=1, source_target_pairs={{0,16},{1,17},{2,18},{3,19},{4,20},{5,21},{6,22},{7,23},{8,24},{9,... | collective-permute-start | bytes 2211848 | tf_op jit(solution)/shard_map/ppermute | solution.py:641
  88.0 11.5 %collective-permute-start.17 = (bf16[48,3840]{1,0:T(8,128)(2,1)S(1)}, bf16[48,3840]{1,0:T(8,128)(2,1)S(1)}, u32[]{:S(2)}, u32[]{:S(2)}) collective-permute-start(bf16[48,3840]{1,0:T(8,128)(2,1)S(1)} %slice.331), channel_id=1, source_target_pairs={{0,16},{1,17},{2,18},{3,19},{4,20},{5,21},{6,22},{7,23},{8,24},{9,... | collective-permute-start | bytes 1105928 | tf_op jit(solution)/shard_map/ppermute | solution.py:641
  88.5 11.5 %collective-permute-start.18 = (bf16[48,3840]{1,0:T(8,128)(2,1)S(1)}, bf16[48,3840]{1,0:T(8,128)(2,1)S(1)}, u32[]{:S(2)}, u32[]{:S(2)}) collective-permute-start(bf16[48,3840]{1,0:T(8,128)(2,1)S(1)} %slice.332), channel_id=1, source_target_pairs={{0,8},{1,9},{2,10},{3,11},{4,12},{5,13},{6,14},{7,15},{8,0},{9,1},... | collective-permute-start | bytes 1105928 | tf_op jit(solution)/shard_map/ppermute | solution.py:641
  90.7 21.0 %collective-permute-start.23 = (bf16[384,768]{1,0:T(8,128)(2,1)S(1)}, bf16[384,768]{1,0:T(8,128)(2,1)}, u32[]{:S(2)}, u32[]{:S(2)}) collective-permute-start(bf16[384,768]{1,0:T(8,128)(2,1)S(1)} %constant_dynamic-slice_fusion.2), channel_id=1, source_target_pairs={{0,8},{1,9},{2,10},{3,11},{4,12},{5,13},{6,14},{7,15},{8,0},{9,1},... | collective-permute-start | bytes 1769480 | tf_op jit(solution)/shard_map/ppermute | solution.py:641
  91.7 20.9 %collective-permute-start.24 = (bf16[384,768]{1,0:T(8,128)(2,1)S(1)}, bf16[384,768]{1,0:T(8,128)(2,1)}, u32[]{:S(2)}, u32[]{:S(2)}) collective-permute-start(bf16[384,768]{1,0:T(8,128)(2,1)S(1)} %constant_dynamic-slice_fusion.2), channel_id=1, source_target_pairs={{0,16},{1,17},{2,18},{3,19},{4,20},{5,21},{6,22},{7,23},{8,24},{9,... | collective-permute-start | bytes 1769480 | tf_op jit(solution)/shard_map/ppermute | solution.py:641
  100.0 23.6 %collective-permute-start.19 = (bf16[96,3840]{1,0:T(8,128)(2,1)S(1)}, bf16[96,3840]{1,0:T(8,128)(2,1)S(1)}, u32[]{:S(2)}, u32[]{:S(2)}) collective-permute-start(bf16[96,3840]{1,0:T(8,128)(2,1)S(1)} %collective-permute-done.15.refs_1_), channel_id=1, source_target_pairs={{0,1},{1,0},{2,3},{3,2},{4,5},{5,4},{6,7},{7,6},{8,9},{9,8},{10,11... | collective-permute-start | bytes 2211848 | tf_op jit(solution)/shard_map/ppermute | solution.py:641
  100.0 23.0 %collective-permute-start.21 = (bf16[48,3840]{1,0:T(8,128)(2,1)S(1)}, bf16[48,3840]{1,0:T(8,128)(2,1)S(1)}, u32[]{:S(2)}, u32[]{:S(2)}) collective-permute-start(bf16[48,3840]{1,0:T(8,128)(2,1)S(1)} %collective-permute-done.17.refs_3_), channel_id=1, source_target_pairs={{0,1},{1,0},{2,3},{3,2},{4,5},{5,4},{6,7},{7,6},{8,9},{9,8},{10,11... | collective-permute-start | bytes 1105928 | tf_op jit(solution)/shard_map/ppermute | solution.py:641
  100.5 23.0 %collective-permute-start.22 = (bf16[48,3840]{1,0:T(8,128)(2,1)S(1)}, bf16[48,3840]{1,0:T(8,128)(2,1)S(1)}, u32[]{:S(2)}, u32[]{:S(2)}) collective-permute-start(bf16[48,3840]{1,0:T(8,128)(2,1)S(1)} %collective-permute-done.18.refs_4_), channel_id=1, source_target_pairs={{0,1},{1,0},{2,3},{3,2},{4,5},{5,4},{6,7},{7,6},{8,9},{9,8},{10,11... | collective-permute-start | bytes 1105928 | tf_op jit(solution)/shard_map/ppermute | solution.py:641
  113.6 8.0 %collective-permute-start.25 = (bf16[192,768]{1,0:T(8,128)(2,1)S(1)}, bf16[192,768]{1,0:T(8,128)(2,1)S(1)}, u32[]{:S(2)}, u32[]{:S(2)}) collective-permute-start(bf16[192,768]{1,0:T(8,128)(2,1)S(1)} %slice.333), channel_id=1, source_target_pairs={{0,16},{1,17},{2,18},{3,19},{4,20},{5,21},{6,22},{7,23},{8,24},{9,... | collective-permute-start | bytes 884744 | tf_op jit(solution)/shard_map/ppermute | solution.py:641
  115.3 7.7 %collective-permute-start.26 = (bf16[192,768]{1,0:T(8,128)(2,1)S(1)}, bf16[192,768]{1,0:T(8,128)(2,1)}, u32[]{:S(2)}, u32[]{:S(2)}) collective-permute-start(bf16[192,768]{1,0:T(8,128)(2,1)S(1)} %slice.334), channel_id=1, source_target_pairs={{0,8},{1,9},{2,10},{3,11},{4,12},{5,13},{6,14},{7,15},{8,0},{9,1},... | collective-permute-start | bytes 884744 | tf_op jit(solution)/shard_map/ppermute | solution.py:641
  126.0 33.1 %collective-permute-start.31 = (bf16[96,6144]{1,0:T(8,128)(2,1)S(1)}, bf16[96,6144]{1,0:T(8,128)(2,1)S(1)}, u32[]{:S(2)}, u32[]{:S(2)}) collective-permute-start(bf16[96,6144]{1,0:T(8,128)(2,1)S(1)} %constant_dynamic-slice_fusion.1), channel_id=1, source_target_pairs={{0,8},{1,9},{2,10},{3,11},{4,12},{5,13},{6,14},{7,15},{8,0},{9,1},... | collective-permute-start | bytes 3538952 | tf_op jit(solution)/shard_map/ppermute | solution.py:641
  127.0 33.0 %collective-permute-start.32 = (bf16[96,6144]{1,0:T(8,128)(2,1)S(1)}, bf16[96,6144]{1,0:T(8,128)(2,1)S(1)}, u32[]{:S(2)}, u32[]{:S(2)}) collective-permute-start(bf16[96,6144]{1,0:T(8,128)(2,1)S(1)} %constant_dynamic-slice_fusion.1), channel_id=1, source_target_pairs={{0,16},{1,17},{2,18},{3,19},{4,20},{5,21},{6,22},{7,23},{8,24},{9,... | collective-permute-start | bytes 3538952 | tf_op jit(solution)/shard_map/ppermute | solution.py:641
  160.9 25.7 %collective-permute-start.33 = (bf16[48,6144]{1,0:T(8,128)(2,1)}, bf16[48,6144]{1,0:T(8,128)(2,1)S(1)}, u32[]{:S(2)}, u32[]{:S(2)}) collective-permute-start(bf16[48,6144]{1,0:T(8,128)(2,1)} %slice.336), channel_id=1, source_target_pairs={{0,16},{1,17},{2,18},{3,19},{4,20},{5,21},{6,22},{7,23},{8,24},{9,... | collective-permute-start | bytes 1769480 | tf_op jit(solution)/shard_map/ppermute | solution.py:641
  162.4 24.2 %collective-permute-start.34 = (bf16[48,6144]{1,0:T(8,128)(2,1)}, bf16[48,6144]{1,0:T(8,128)(2,1)S(1)}, u32[]{:S(2)}, u32[]{:S(2)}) collective-permute-start(bf16[48,6144]{1,0:T(8,128)(2,1)} %slice.337), channel_id=1, source_target_pairs={{0,8},{1,9},{2,10},{3,11},{4,12},{5,13},{6,14},{7,15},{8,0},{9,1},... | collective-permute-start | bytes 1769480 | tf_op jit(solution)/shard_map/ppermute | solution.py:641
  188.3 6.4 %collective-permute-start.35 = (bf16[96,6144]{1,0:T(8,128)(2,1)S(1)}, bf16[96,6144]{1,0:T(8,128)(2,1)S(1)}, u32[]{:S(2)}, u32[]{:S(2)}) collective-permute-start(bf16[96,6144]{1,0:T(8,128)(2,1)S(1)} %collective-permute-done.31.refs_1_), channel_id=1, source_target_pairs={{0,1},{1,0},{2,3},{3,2},{4,5},{5,4},{6,7},{7,6},{8,9},{9,8},{10,11... | collective-permute-start | bytes 3538952 | tf_op jit(solution)/shard_map/ppermute | solution.py:641
  188.3 7.2 %collective-permute-start.36 = (bf16[96,6144]{1,0:T(8,128)(2,1)S(1)}, bf16[96,6144]{1,0:T(8,128)(2,1)}, u32[]{:S(2)}, u32[]{:S(2)}) collective-permute-start(bf16[96,6144]{1,0:T(8,128)(2,1)S(1)} %collective-permute-done.32.refs_2_), channel_id=1, source_target_pairs={{0,1},{1,0},{2,3},{3,2},{4,5},{5,4},{6,7},{7,6},{8,9},{9,8},{10,11... | collective-permute-start | bytes 3538952 | tf_op jit(solution)/shard_map/ppermute | solution.py:641
  231.3 16.0 %collective-permute-start.41 = (bf16[16,9,48,384]{3,2,1,0:T(8,128)(2,1)}, bf16[16,9,48,384]{3,2,1,0:T(8,128)(2,1)}, u32[]{:S(2)}, u32[]{:S(2)}) collective-permute-start(bf16[16,9,48,384]{3,2,1,0:T(8,128)(2,1)} %half_grads.4), channel_id=1, source_target_pairs={{0,1},{1,0},{2,3},{3,2},{4,5},{5,4},{6,7},{7,6},{8,9},{9,8},{10,11... | collective-permute-start | bytes 15925256 | tf_op jit(solution)/shard_map/ppermute | solution.py:641
  232.9 14.3 %all-to-all-start = ((bf16[32,8,168]{2,1,0:T(8,128)(2,1)}), bf16[32,8,168]{2,1,0:T(8,128)(2,1)S(1)}, u32[]{:S(2)}, u32[]{:S(2)}) async-start(bf16[32,8,168]{2,1,0:T(8,128)(2,1)} %maximum_bitcast_fusion), calls=%async_computation | async-start | bytes 262144 | tf_op jit(solution)/shard_map/all_to_all | solution.py:1364
  236.3 159.0 %reduce-scatter.2.cloned.1.call-start = ((), (), s32[]{:S(2)}) async-start(), calls=%async_computation.8 | async-start | bytes 1658880 | tf_op jit(solution)/shard_map/reduce_scatter | solution.py:1134
  269.0 23.7 %collective-permute-start.42 = (bf16[2,9,48,384]{3,2,1,0:T(8,128)(2,1)}, bf16[2,9,48,384]{3,2,1,0:T(8,128)(2,1)}, u32[]{:S(2)}, u32[]{:S(2)}) collective-permute-start(bf16[2,9,48,384]{3,2,1,0:T(8,128)(2,1)} %get-tuple-element.287), channel_id=1, source_target_pairs={{0,16},{1,17},{2,18},{3,19},{4,20},{5,21},{6,22},{7,23},{8,24},{9,... | collective-permute-start | bytes 1990664 | tf_op jit(solution)/shard_map/ppermute | solution.py:641
  270.7 23.3 %collective-permute-start.43 = (bf16[2,9,48,384]{3,2,1,0:T(8,128)(2,1)}, bf16[2,9,48,384]{3,2,1,0:T(8,128)(2,1)}, u32[]{:S(2)}, u32[]{:S(2)}) collective-permute-start(bf16[2,9,48,384]{3,2,1,0:T(8,128)(2,1)} %get-tuple-element.286), channel_id=1, source_target_pairs={{0,8},{1,9},{2,10},{3,11},{4,12},{5,13},{6,14},{7,15},{8,0},{9,1},... | collective-permute-start | bytes 1990664 | tf_op jit(solution)/shard_map/ppermute | solution.py:641
  295.9 32.6 %collective-permute-start.44 = (bf16[4,9,48,384]{3,2,1,0:T(8,128)(2,1)S(1)}, bf16[4,9,48,384]{3,2,1,0:T(8,128)(2,1)}, u32[]{:S(2)}, u32[]{:S(2)}) collective-permute-start(bf16[4,9,48,384]{3,2,1,0:T(8,128)(2,1)S(1)} %pad_maximum_fusion), channel_id=1, source_target_pairs={{0,8},{1,9},{2,10},{3,11},{4,12},{5,13},{6,14},{7,15},{8,0},{9,1},... | collective-permute-start | bytes 3981320 | tf_op jit(solution)/shard_map/ppermute | solution.py:641
  298.6 30.4 %collective-permute-start.45 = (bf16[4,9,48,384]{3,2,1,0:T(8,128)(2,1)}, bf16[4,9,48,384]{3,2,1,0:T(8,128)(2,1)}, u32[]{:S(2)}, u32[]{:S(2)}) collective-permute-start(bf16[4,9,48,384]{3,2,1,0:T(8,128)(2,1)} %pad_maximum_fusion.1), channel_id=1, source_target_pairs={{0,16},{1,17},{2,18},{3,19},{4,20},{5,21},{6,22},{7,23},{8,24},{9,... | collective-permute-start | bytes 3981320 | tf_op jit(solution)/shard_map/ppermute | solution.py:641
  351.3 7.5 %collective-permute-start.47 = (bf16[2,3,48,384]{3,2,1,0:T(8,128)(2,1)S(1)}, bf16[2,3,48,384]{3,2,1,0:T(8,128)(2,1)S(1)}, u32[]{:S(2)}, u32[]{:S(2)}) collective-permute-start(bf16[2,3,48,384]{3,2,1,0:T(8,128)(2,1)S(1)} %get-tuple-element.292), channel_id=1, source_target_pairs={{0,16},{1,17},{2,18},{3,19},{4,20},{5,21},{6,22},{7,23},{8,24},{9,... | collective-permute-start | bytes 663560 | tf_op jit(solution)/shard_map/ppermute | solution.py:641
  352.7 7.3 %collective-permute-start.49 = (bf16[2,3,48,384]{3,2,1,0:T(8,128)(2,1)S(1)}, bf16[2,3,48,384]{3,2,1,0:T(8,128)(2,1)S(1)}, u32[]{:S(2)}, u32[]{:S(2)}) collective-permute-start(bf16[2,3,48,384]{3,2,1,0:T(8,128)(2,1)S(1)} %get-tuple-element.291), channel_id=1, source_target_pairs={{0,8},{1,9},{2,10},{3,11},{4,12},{5,13},{6,14},{7,15},{8,0},{9,1},... | collective-permute-start | bytes 663560 | tf_op jit(solution)/shard_map/ppermute | solution.py:641
  359.1 11.6 %collective-permute-start.48 = (bf16[4,3,48,384]{3,2,1,0:T(8,128)(2,1)S(1)}, bf16[4,3,48,384]{3,2,1,0:T(8,128)(2,1)}, u32[]{:S(2)}, u32[]{:S(2)}) collective-permute-start(bf16[4,3,48,384]{3,2,1,0:T(8,128)(2,1)S(1)} %pad_maximum_fusion.3), channel_id=1, source_target_pairs={{0,8},{1,9},{2,10},{3,11},{4,12},{5,13},{6,14},{7,15},{8,0},{9,1},... | collective-permute-start | bytes 1327112 | tf_op jit(solution)/shard_map/ppermute | solution.py:641
  360.1 11.3 %collective-permute-start.50 = (bf16[4,3,48,384]{3,2,1,0:T(8,128)(2,1)S(1)}, bf16[4,3,48,384]{3,2,1,0:T(8,128)(2,1)}, u32[]{:S(2)}, u32[]{:S(2)}) collective-permute-start(bf16[4,3,48,384]{3,2,1,0:T(8,128)(2,1)S(1)} %pad_maximum_fusion.4), channel_id=1, source_target_pairs={{0,16},{1,17},{2,18},{3,19},{4,20},{5,21},{6,22},{7,23},{8,24},{9,... | collective-permute-start | bytes 1327112 | tf_op jit(solution)/shard_map/ppermute | solution.py:641
  363.4 16.5 %all-to-all-start.1 = ((f32[32,8,128]{2,1,0:T(8,128)}), f32[32,8,128]{2,1,0:T(8,128)S(1)}, u32[]{:S(2)}, u32[]{:S(2)}) async-start(f32[32,8,128]{2,1,0:T(8,128)} %bitcast.55), calls=%async_computation.1 | async-start | bytes 262144 | tf_op jit(solution)/shard_map/all_to_all | solution.py:636
  372.8 10.2 %collective-permute-start.53 = (bf16[3,48,384]{2,1,0:T(8,128)(2,1)S(1)}, bf16[3,48,384]{2,1,0:T(8,128)(2,1)S(1)}, u32[]{:S(2)}, u32[]{:S(2)}) collective-permute-start(bf16[3,48,384]{2,1,0:T(8,128)(2,1)S(1)} %get-tuple-element.304), channel_id=1, source_target_pairs={{0,6},{1,7},{2,0},{3,1},{4,2},{5,3},{6,4},{7,5},{8,14},{9,15},{10,... | collective-permute-start | bytes 331784 | tf_op jit(solution)/shard_map/ppermute | solution.py:641
  376.1 18.9 %collective-permute-start.52 = (bf16[3,48,384]{2,1,0:T(8,128)(2,1)S(1)}, bf16[3,48,384]{2,1,0:T(8,128)(2,1)S(1)}, u32[]{:S(2)}, u32[]{:S(2)}) collective-permute-start(bf16[3,48,384]{2,1,0:T(8,128)(2,1)S(1)} %get-tuple-element.305), channel_id=1, source_target_pairs={{0,4},{1,5},{2,6},{3,7},{4,0},{5,1},{6,2},{7,3},{8,12},{9,13},{10,... | collective-permute-start | bytes 331784 | tf_op jit(solution)/shard_map/ppermute | solution.py:641
  376.1 18.9 %collective-permute-start.51 = (bf16[3,48,384]{2,1,0:T(8,128)(2,1)S(1)}, bf16[3,48,384]{2,1,0:T(8,128)(2,1)S(1)}, u32[]{:S(2)}, u32[]{:S(2)}) collective-permute-start(bf16[3,48,384]{2,1,0:T(8,128)(2,1)S(1)} %get-tuple-element.303), channel_id=1, source_target_pairs={{0,2},{1,3},{2,4},{3,5},{4,6},{5,7},{6,0},{7,1},{8,10},{9,11},{10,... | collective-permute-start | bytes 331784 | tf_op jit(solution)/shard_map/ppermute | solution.py:641
  (60 other events, 488.4 us)
Sparse Core Ops, SparseCore 0:
  31.1 24.5 all-gather.5
  57.3 22.1 all-gather.7
  81.8 31.3 all-gather.9
  114.7 50.8 all-gather.11
  231.5 64.7 all-gather.13
  352.7 40.4 reduce-scatter.1

commit v5 on v4

--- a/solution.py
+++ b/solution.py
@@ -111,22 +111,23 @@
     return copies
 
 
-def attend_kernel(count, count_ref, rows_ref, place_ref, bias_ref, *refs):
-    pieces, (projected_ref, context_ref, joined_ref), (attend_ref, sems, out_sem) = (
-        refs[:count],
-        refs[count : count + 3],
-        refs[count + 3 :],
-    )
+def attend_kernel(count, small_count, size, count_ref, rows_ref, place_ref, *refs):
+    pieces, small, refs = refs[:count], refs[count : count + small_count], refs[count + small_count :]
+    projected_ref, context_ref, probs_ref, joined_ref = refs[:4]
+    attend_ref, bias_ref, got_ref, sems, small_sems, out_sem = refs[4:]
     step = pl.program_id(0)
     kept = pltpu.make_async_copy(attend_ref, joined_ref, out_sem)
 
     @pl.when(step == 0)
     def _():
+        small_waits = small_copies(small, got_ref, place_ref, small_sems)
         copies = attend_copies(pieces, attend_ref, place_ref, sems)
-        for copy in copies:
+        for copy in small_waits + copies:
             copy.start()
-        for copy in copies:
-            copy.wait()
+        wait_all(small_waits)
+        first_rows = got_ref[...].astype(F32).reshape(-1, 16 + SEGS, 128)[:, 0, :]
+        bias_ref[...] = spread_row(first_rows.astype(LOW), size, bias_ref.shape[1])
+        wait_all(copies)
         kept.start()
 
     projected_ref[...] = (dot_nn(rows_ref[...], attend_ref[...]) + bias_ref[...]).astype(LOW)
@@ -138,9 +139,10 @@
                 projected_ref[span, part * D + pair * PAIR : part * D + (pair + 1) * PAIR]
                 for part in range(3)
             ]
-            probs = pair_probs(query, key, valid).astype(LOW)
+            probs = side_by_side(pair_probs(query, key, valid).astype(LOW))
+            probs_ref[span, pair * 2 * SEG : (pair + 1) * 2 * SEG] = probs
             context_ref[span, pair * PAIR : (pair + 1) * PAIR] = dot_nn(
-                side_by_side(probs), two_heads(value, 0)
+                probs, two_heads(value, 0)
             ).astype(LOW)
 
     @pl.when(step == pl.num_programs(0) - 1)
@@ -311,8 +313,8 @@
 
 def attend_back_kernel(
     offset,
-    count_ref,
     projected_ref,
+    probs_ref,
     context_ref,
     first_ref,
     mixed_in_ref,
@@ -334,7 +336,6 @@
     scale = HD ** (-0.5)
     for local in range(segments):
         segment = (step + offset) * segments + local
-        valid = valid_keys(count_ref, segment)
         span = slice(local * SEG, (local + 1) * SEG)
         for pair in range(PAIRS):
             columns = [
@@ -350,7 +351,9 @@
             ).astype(LOW)
             grad = jnp.concatenate([replaced, context_ref[rest, columns[0]]], axis=0)
             grad = two_heads(grad, 0)
-            probs = pair_probs(query, key, valid)
+            probs = probs_ref[span, pair * 2 * SEG : (pair + 1) * 2 * SEG]
+            probs_low = jnp.concatenate([probs[:, :SEG], probs[:, SEG:]], axis=0)
+            probs = probs_low.astype(F32)
             grad_probs = back_cols(grad, value)
             total = jnp.sum(grad_probs * probs, axis=-1, keepdims=True)
             scores = (probs * (grad_probs - total)).astype(LOW)
@@ -360,7 +363,7 @@
             grad_ref[span, columns[1]] = (
                 cross_rows(scores, two_heads(query, 0)) * scale
             ).astype(LOW)
-            grad_ref[span, columns[2]] = cross_rows(probs.astype(LOW), grad).astype(LOW)
+            grad_ref[span, columns[2]] = cross_rows(probs_low, grad).astype(LOW)
     tokens_ref[...] = first_ref[...] + back_cols(grad_ref[...], attend_ref[...])
     mixed_ref[...] = mixed_in_ref[...]
     for local in range(segments):
@@ -385,15 +388,16 @@
 
 
 def row_call(kernel, name, operands, specs, outs, flops, steps=None, earlier=(), scratch=()):
-    rows = next(operand.shape[0] for operand, spec in zip(operands, specs) if spec is not None)
+    rows = outs[0][0][0]
     shapes = [jax.ShapeDtypeStruct(shape, kind) for shape, kind, _ in outs]
     moved = sum(operand.size * operand.dtype.itemsize for operand in operands)
     moved += sum(shape.size * shape.dtype.itemsize for shape in shapes)
     return pl.pallas_call(
         kernel,
         grid=(rows // ROWS if steps is None else steps,),
-        in_specs=[pl.BlockSpec(memory_space=pltpu.SMEM)]
-        + [entire(operand) if spec is None else spec for operand, spec in zip(operands[1:], specs[1:])]
+        in_specs=[
+            entire(operand) if spec is None else spec for operand, spec in zip(operands, specs)
+        ]
         + [pl.BlockSpec(memory_space=pl.ANY)] * len(earlier),
         out_specs=[spec for _, _, spec in outs],
         out_shape=shapes,
@@ -413,23 +417,28 @@
     return jnp.stack(place_here()).astype(jnp.int32)
 
 
-def inner_attention(rows, counts, pieces, attend_bias):
+def inner_attention(rows, counts, pieces, small_pieces, bias_size):
     size = rows.shape[0]
+    devices = D * 3 // bias_size
     smem, anywhere = pl.BlockSpec(memory_space=pltpu.SMEM), pl.BlockSpec(memory_space=pl.ANY)
     return row_call(
-        partial(attend_kernel, len(pieces)),
+        partial(attend_kernel, len(pieces), len(small_pieces), bias_size),
         "attend",
-        (counts, rows, place_array(), attend_bias, *pieces),
-        (None, by_rows(D), smem, None) + (anywhere,) * len(pieces),
+        (counts, rows, place_array(), *pieces, *small_pieces),
+        (smem, by_rows(D), smem) + (anywhere,) * (len(pieces) + len(small_pieces)),
         [
             ((size, 3 * D), LOW, by_rows(3 * D)),
             ((size, D), LOW, by_rows(D)),
+            ((size, HEADS * SEG), LOW, by_rows(HEADS * SEG)),
             ((D, 3 * D), LOW, anywhere),
         ],
         2 * size * D * (3 * D + 4 * SEG),
         scratch=[
             pltpu.VMEM((D, 3 * D), LOW),
+            pltpu.VMEM((1, 3 * D), F32),
+            pltpu.VMEM((devices * (16 + SEGS), 128), LOW),
             pltpu.SemaphoreType.DMA((32,)),
+            pltpu.SemaphoreType.DMA((16,)),
             pltpu.SemaphoreType.DMA,
         ],
     )
@@ -443,7 +452,7 @@
         partial(feed_kernel, mid_moves, end_moves, (len(mid), len(end))),
         "feed",
         (counts, rows, context, place_array(), expand_bias, vectors, *mid, *end),
-        (None, by_rows(D), by_rows(D), smem, None, None) + (anywhere,) * (len(mid) + len(end)),
+        (smem, by_rows(D), by_rows(D), smem, None, None) + (anywhere,) * (len(mid) + len(end)),
         [
             ((size, D), LOW, by_rows(D)),
             ((size // SEG, 5 * D), F32, whole_block((size // SEG, 5 * D))),
@@ -477,7 +486,8 @@
         feed_back_kernel,
         "feed_back",
         (counts, cotangent, second, first, slope, merge, expand, reduce_matrix, vectors),
-        (None, by_rows(D), by_rows(D), by_rows(D), by_rows(wide), None, None, None, None),
+        (pl.BlockSpec(memory_space=pltpu.SMEM), by_rows(D), by_rows(D), by_rows(D), by_rows(wide))
+        + (None,) * 4,
         [
             ((size, D), LOW, by_rows(D)),
             ((size, wide), LOW, by_rows(wide)),
@@ -491,15 +501,15 @@
     )
 
 
-def inner_attend_back(counts, operands, attend, head_rows, offset, steps, earlier):
-    projected, grad_context, grad_first, mixed = operands
+def inner_attend_back(operands, attend, head_rows, offset, steps, earlier):
+    projected, probs, grad_context, grad_first, mixed = operands
     size = projected.shape[0]
     return row_call(
         partial(attend_back_kernel, offset),
         "attend_back",
-        (counts, projected, grad_context, grad_first, mixed, attend, *head_rows),
-        (None, by_rows(3 * D, offset), by_rows(D, offset), by_rows(D, offset))
-        + (by_rows(D, offset), None, None, None, None),
+        (projected, probs, grad_context, grad_first, mixed, attend, *head_rows),
+        (by_rows(3 * D, offset), by_rows(HEADS * SEG, offset), by_rows(D, offset))
+        + (by_rows(D, offset), by_rows(D, offset), None, None, None, None),
         [
             ((size, 3 * D), LOW, by_rows(3 * D, offset)),
             ((size, D), F32, by_rows(D, offset)),
@@ -564,35 +574,38 @@
 VECTOR_ROWS = (1, 2, 3, 5, 6, 7)
 
 
+def small_copies(pieces, got_ref, place_ref, sems):
+    if len(pieces) == 1:
+        return [pltpu.make_async_copy(pieces[0], got_ref, sems.at[0])]
+    plane, depth = place_ref[0], place_ref[1]
+    copies = []
+    slots = ((0, 0, 4), (1, 0, 4), (2, 0, 4), (3, 0, 2), (3, 2, 2))
+    first_lane = pieces[0].shape[2] - 128
+    for piece, (turn, first, count) in zip(pieces, slots):
+        for slot in range(count):
+            chip = (plane ^ turn) * 4 + ((depth + 4 - first - slot) & 3)
+            copies.append(
+                pltpu.make_async_copy(
+                    piece.at[slot, :, first_lane : first_lane + 128],
+                    got_ref.at[pl.ds(pl.multiple_of(48 * chip, 48), 48), :],
+                    sems.at[len(copies)],
+                )
+            )
+    return copies
+
+
 def unpack_kernel(sizes, place_ref, *refs):
-    outs, got_ref, sems = refs[-9:-2], refs[-2], refs[-1]
-    pieces = refs[:-9]
-    plane, depth = place_ref[0], place_ref[1]
-    if len(pieces) == 1:
-        copies = [pltpu.make_async_copy(pieces[0], got_ref, sems.at[0])]
-    else:
-        copies = []
-        slots = ((0, 0, 4), (1, 0, 4), (2, 0, 4), (3, 0, 2), (3, 2, 2))
-        first_lane = pieces[0].shape[2] - 128
-        for piece, (turn, first, count) in zip(pieces, slots):
-            for slot in range(count):
-                chip = (plane ^ turn) * 4 + ((depth + 4 - first - slot) & 3)
-                copies.append(
-                    pltpu.make_async_copy(
-                        piece.at[slot, :, first_lane : first_lane + 128],
-                        got_ref.at[pl.ds(pl.multiple_of(48 * chip, 48), 48), :],
-                        sems.at[len(copies)],
-                    )
-                )
+    outs, got_ref, sems = (None, *refs[-8:-2]), refs[-2], refs[-1]
+    pieces = refs[:-8]
+    copies = small_copies(pieces, got_ref, place_ref, sems)
     for copy in copies:
         copy.start()
-    for copy in copies:
-        copy.wait()
+    wait_all(copies)
     got = got_ref[...].astype(F32).reshape(-1, 16 + SEGS, 128)
     devices = got.shape[0]
     for block in range(2):
         attend_ref, expand_ref, vectors_ref = outs[3 * block : 3 * block + 3]
-        for kind in range(8):
+        for kind in range(1 - block, 8):
             row = 8 * block + kind
             size = sizes[row]
             spread = spread_row(got[:, row, :].astype(LOW), size, size * devices)
@@ -618,7 +631,7 @@
     shapes.append(jax.ShapeDtypeStruct((SEGS, sizes[16] * devices), F32))
     return pl.pallas_call(
         partial(unpack_kernel, sizes),
-        out_shape=shapes,
+        out_shape=shapes[1:],
         in_specs=[pl.BlockSpec(memory_space=pltpu.SMEM)]
         + [pl.BlockSpec(memory_space=pl.ANY)] * len(pieces),
         scratch_shapes=[
@@ -1280,7 +1293,6 @@
         pieces = gather_flat([inner_attend])
         small_pieces = [gather(small)]
     (
-        attend_bias,
         expand_bias,
         vectors,
         outer_attend_bias_full,
@@ -1289,14 +1301,18 @@
         place_rows,
     ) = unpack_small(sizes, devices, small_pieces)
     if linked:
-        mid_half = half_rows(after((pieces[3], pieces[4], attend_bias), mid_line))
-        attend_bias = after(mid_half, attend_bias)
-    projected, context, attend = inner_attention(tokens, counts, pieces, attend_bias)
+        mid_half = half_rows(after((pieces[3], pieces[4]), mid_line))
+        attend_tokens = after(mid_half, tokens)
+    else:
+        attend_tokens = tokens
+    projected, context, probs, attend = inner_attention(
+        attend_tokens, counts, pieces, small_pieces, sizes[0]
+    )
     if linked:
         mid = first_hops(mid_line, mid_half)
         end = first_hops(end_line, half_rows(after((context, mid[1], mid[2]), end_line)))
         mid = last_hops(mid, context)
-        end = last_hops(end, (mid[3], mid[4]))
+        end = last_hops(end, (mid[3], mid[4], vectors))
         outer = first_hops(
             outer_line, half_rows(after((mid[3], mid[4], end[1], end[2]), outer_line))
         )
@@ -1345,7 +1361,7 @@
     grad_place = jnp.transpose(jnp.sum(grad_heads.reshape(docs, SEGS, D), axis=0))
     inner_sums = inner_sums + head_sums
     hidden_sums = hidden_sums + head_hidden_sums
-    operands = (projected, grad_context, grad_first, mixed)
+    operands = (projected, probs, grad_context, grad_first, mixed)
     head_rows = (head_context, head_first, head_out)
     steps = tokens.shape[0] // ROWS
     right_all = gather(right_pack)
@@ -1381,41 +1397,43 @@
         jobs = [
             (normed, grad_hidden, heads, 3, head_hidden),
             (active, branch, wide_heads, wide // D, head_branch),
-            (context, grad_attn, heads, 4, head_attn),
         ]
         sent = half_grads(jobs, 1 - core)
         left_all = exchange(left_factors(after(sent, left_pack)))
         part = inner_attend_back(
-            counts, after(sent, *operands), attend, head_rows, 0, 1, ()
+            after(sent, *operands), attend, head_rows, 0, 1, ()
         )
         kept = half_grads(jobs, after((part[3], left_all), core), over_core(sent))
         planes = scatter_planes(kept)
         middle = inner_attend_back(
-            counts, after(planes, *operands), attend, head_rows, 1, 1, part[:3]
+            after(planes, *operands), attend, head_rows, 1, steps - 2, part[:3]
         )
         tall = scatter_across(planes, middle[3])
         rest = inner_attend_back(
-            counts, after(tall, *operands), attend, head_rows, 2, steps - 2, middle[:3]
+            after(tall, *operands), attend, head_rows, steps - 1, 1, middle[:3]
         )
         grad_projected, tokens_grad, mixed = rest[:3]
         attend_sums = part[3] + middle[3] + rest[3]
         outer_big, outer_bias = outer_grads(*after(rest[3], left_all, right_all))
-        jobs = [(tokens, grad_projected, None, 0, None)]
+        jobs = [
+            (tokens, grad_projected, None, 0, None),
+            (context, grad_attn, heads, 4, head_attn),
+        ]
         tall = scatter_next(*tall, (outer_big, outer_bias))
         sent = half_grads(jobs, after(tall, 1 - core))
         tall = scatter_along(tall)
         kept = half_grads(jobs, core, over_core(sent))
         short = scatter_next(*scatter_across(scatter_planes(kept), ()), ())
         sums_gate = short
-        short = scatter_line(short)
-        own_expand, own_reduce, own_merge = scatter_end(tall, [(D, wide), (wide, D), (D, D)])
-        (own_attend,) = scatter_end(short, [(D, 3 * D)])
+        short = scatter_line(after(tall, short))
+        own_expand, own_reduce = scatter_end(tall, [(D, wide), (wide, D)])
+        own_attend, own_merge = scatter_end(short, [(D, 3 * D), (D, D)])
     else:
         sums_gate = ()
         left_all = exchange(left_factors(left_pack))
         outer_big, outer_bias = outer_grads(left_all, right_all)
         grad_projected, tokens_grad, mixed, attend_sums = inner_attend_back(
-            counts, operands, attend, head_rows, 0, steps, ()
+            operands, attend, head_rows, 0, steps, ()
         )
         grad_attend = cross_rows(tokens, grad_projected).astype(low)
         grad_reduce, grad_expand, grad_merge = [

time: 413 us -> 398 us (0.964)
  Pallas kernels: 181 us -> 174 us
  waiting for transfers between devices: 93.8 us -> 89.5 us
    ppermute x56, waiting for transfers between devices: 90.3 us -> 80.6 us  [hop(): lax.ppermute(array, AXES, [(place, turn(place)) for place in range(32)])]
    reduce_scatter x1, waiting for transfers between devices: 0.01 us -> 8.14 us  [scatter_along(): lax.psum_scatter(here.reshape(-1, here.shape[-1]), 'fsdp', scatter_dimens...]
    pallas_call x6, Pallas kernels: 109 us -> 102 us  [row_call(): pl.pallas_call(kernel, grid=(rows // ROWS if steps is None else steps,),...]
    unnamed x102 -> x99, local copies, waits for them, and re-layouts: 11.7 us -> 11 us
  transfers between devices with their start and end apart: 64 -> 64, of which waited for: 28 -> 22; matrix products, arithmetic and copies ran while one was open for 10% -> 11% of each run, Pallas kernels for 32% -> 37%
where the time goes in v5:
time: 398 us; the launch traced here: 394 us
  Pallas kernels  174 us (44%)
  waiting for transfers between devices  89.5 us (22%)
  starting transfers between devices  56 us (14%)
  local copies, waits for them, and re-layouts  35.2 us (9%)
  other arithmetic  18.5 us (5%)
  between operations  16.2 us (4%)
  matrix products  4.89 us (1%)
    pallas_call x6, Pallas kernels, row_call(): pl.pallas_call(kernel, grid=(rows // ROWS if steps is None else steps,),...  102 us
    ppermute x56, waiting for transfers between devices, hop(): lax.ppermute(array, AXES, [(place, turn(place)) for place in range(32)])  80.6 us
    pallas_call x4, Pallas kernels, half_grads(): pl.pallas_call(partial(grads_kernel, rules, int(came is not None)), grid_...  49.4 us
    ppermute x56, starting transfers between devices, hop(): lax.ppermute(array, AXES, [(place, turn(place)) for place in range(32)])  48.2 us
    pallas_call x1, Pallas kernels, heads_step(): pl.pallas_call(partial(heads_kernel, (len(mid), 1), mid_moves, end_moves)...  17 us
    unnamed x99, local copies, waits for them, and re-layouts  11 us
    reduce_scatter x1, waiting for transfers between devices, scatter_along(): lax.psum_scatter(here.reshape(-1, here.shape[-1]), 'fsdp', scatter_dimens...  8.14 us
  transfers between devices with their start and end apart: 64, of which 22 were waited for; matrix products, arithmetic and copies ran while one was open for 11% of the time, Pallas kernels for 37%

profile of v5, /device:TPU:0, one launch (start us, length us, event | category | flops | bytes accessed | tf_op | source)
XLA Modules:
  0.0 394.0 jit_solution(5493149123700773803)
XLA Ops:
  9.6 1.5 pack.1
  14.0 5.0 %collective-permute-start.5 = (bf16[48,1280]{1,0:T(8,128)(2,1)S(1)}, bf16[48,1280]{1,0:T(8,128)(2,1)S(1)}, u32[]{:S(2)}, u32[]{:S(2)}) collective-permute-start(bf16[48,1280]{1,0:T(8,128)(2,1)S(1)} %get-tuple-element.333), channel_id=1, source_target_pairs={{0,6},{1,7},{2,0},{3,1},{4,2},{5,3},{6,4},{7,5},{8,14},{9,15},{10,... | collective-permute-start | bytes 368648 | tf_op jit(solution)/shard_map/ppermute | solution.py:654
  20.0 1.5 collective-permute-start.1
  21.5 1.5 collective-permute-start.2
  23.0 7.1 %collective-permute-done.4 = bf16[48,1280]{1,0:T(8,128)(2,1)S(1)} collective-permute-done((bf16[48,1280]{1,0:T(8,128)(2,1)S(1)}, bf16[48,1280]{1,0:T(8,128)(2,1)S(1)}, u32[]{:S(2)}, u32[]{:S(2)}) %collective-permute-start.4) | collective-permute-done | bytes 122912 | tf_op jit(solution)/shard_map/ppermute | solution.py:654
  32.6 1.6 collective-permute-start.6
  34.2 1.5 collective-permute-start.8
  35.7 9.7 %collective-permute-done.6.refs_1_.refs_11_ = bf16[4,48,1280]{2,1,0:T(8,128)(2,1)S(1)} collective-permute-done((bf16[4,48,1280]{2,1,0:T(8,128)(2,1)S(1)}, bf16[4,48,1280]{2,1,0:T(8,128)(2,1)S(1)}, u32[]{:S(2)}, u32[]{:S(2)}) %collective-permute-start.6) | collective-permute-done | bytes 491552 | tf_op jit(solution)/shard_map/ppermute | solution.py:654
  45.4 1.6 collective-permute-start.7
  47.0 1.6 collective-permute-start.9
  48.6 3.4 collective-permute-done.7.refs_3_.refs_13_
  55.5 2.3 collective-permute-done.39
  62.7 1.5 collective-permute-start.16
  67.4 15.3 %attend.1 = (bf16[1024,2304]{1,0:T(8,128)(2,1)}, bf16[1024,768]{1,0:T(8,128)(2,1)}, bf16[1024,1536]{1,0:T(8,128)(2,1)}, bf16[768,2304]{1,0:T(8,128)(2,1)}) custom-call(s32[1]{0:T(128)S(6)} %copy.88.count_ref, bf16[1024,768]{1,0:T(8,128)(2,1)} %refs_0_.3, s32[3]{0:T(128)} %pad_add_fusion.place_ref, bf16[4,48,1280]{2,1,0:T(8,128)(2,1)} %copy-done.4, ...), custom_call_target="tpu_custom_call" | custom-call | flops 4429185024 | bytes 20447248 | tf_op jit(solution)/shard_map/attend/pallas_call | solution.py:395
  87.8 1.5 collective-permute-start.24
  89.3 6.2 %collective-permute-done.17.refs_3_ = bf16[48,3840]{1,0:T(8,128)(2,1)S(1)} collective-permute-done((bf16[48,3840]{1,0:T(8,128)(2,1)S(1)}, bf16[48,3840]{1,0:T(8,128)(2,1)S(1)}, u32[]{:S(2)}, u32[]{:S(2)}) %collective-permute-start.17) | collective-permute-done | bytes 368672 | tf_op jit(solution)/shard_map/ppermute | solution.py:654
  96.6 3.8 unpack.1
  100.4 7.3 %collective-permute-done.23.refs_10_ = bf16[384,768]{1,0:T(8,128)(2,1)} collective-permute-done((bf16[384,768]{1,0:T(8,128)(2,1)S(1)}, bf16[384,768]{1,0:T(8,128)(2,1)}, u32[]{:S(2)}, u32[]{:S(2)}) %collective-permute-start.23) | collective-permute-done | bytes 589856 | tf_op jit(solution)/shard_map/ppermute | solution.py:654
  109.7 1.6 collective-permute-start.25
  111.8 6.0 %collective-permute-done.25.refs_12_ = bf16[192,768]{1,0:T(8,128)(2,1)} collective-permute-done((bf16[192,768]{1,0:T(8,128)(2,1)S(1)}, bf16[192,768]{1,0:T(8,128)(2,1)}, u32[]{:S(2)}, u32[]{:S(2)}) %collective-permute-start.25) | collective-permute-done | bytes 294944 | tf_op jit(solution)/shard_map/ppermute | solution.py:654
  123.7 31.3 %feed.1 = (bf16[1024,768]{1,0:T(8,128)(2,1)}, f32[8,3840]{1,0:T(8,128)}, f32[8,6144]{1,0:T(8,128)}, f32[1024,768]{1,0:T(8,128)}, bf16[1024,768]{1,0:T(8,128)(2,1...) custom-call(s32[1]{0:T(128)S(6)} %copy.88.count_ref, ...), custom_call_target="tpu_custom_call" | custom-call | flops 10871635968 | bytes 46755856 | tf_op jit(solution)/shard_map/feed/pallas_call | solution.py:395
  158.6 23.1 %feed_back.1 = (bf16[1024,768]{1,0:T(8,128)(2,1)}, bf16[1024,3072]{1,0:T(8,128)(2,1)}, bf16[1024,768]{1,0:T(8,128)(2,1)}, bf16[1024,768]{1,0:T(8,128)(2,1)}, f32...) custom-call(s32[1]{0:T(128)S(6)} %copy.88.count_ref, bf16[1024,768]{1,0:T(8,128)(2,1)} %cotangent_ref.1, ...), custom_call_target="tpu_custom_call" | custom-call | flops 10871635968 | bytes 38989828 | tf_op jit(solution)/shard_map/feed_back/pallas_call | solution.py:395
  185.2 3.7 collective-permute-done.37.refs_7_
  191.0 17.0 %heads.1 = (f32[8,768]{1,0:T(8,128)}, f32[8,768]{1,0:T(8,128)}, bf16[8,5376]{1,0:T(8,128)(2,1)}, bf16[8,6912]{1,0:T(8,128)(2,1)}, f32[8,768]{1,0:T(8,128)}, /*in...) custom-call(s32[3]{0:T(128)} %pad_add_fusion.place_ref, ...), custom_call_target="tpu_custom_call" | custom-call | flops 594542592 | bytes 25952256 | tf_op jit(solution)/shard_map/heads/pallas_call | solution.py:992
  208.0 15.0 %half_grads.4 = bf16[16,8,48,384]{3,2,1,0:T(8,128)(2,1)} custom-call(s32[1]{0:T(128)} %bitcast.side_ref, bf16[1024,768]{1,0:T(8,128)(2,1)} %get-tuple-element.163.refs_0_, bf16[1024,3072]{1,0:T(8,128)(2,1)} %get-tuple-element.170.refs_1_, f32[8,3840]{1,0:T(8,128)} %get-tuple-element.171.heads_ref.refs_2_.refs_4_, ...), custom_call_target="tpu_custom_call" | custom-call | flops 4831838208 | bytes 31457280 | tf_op jit(solution)/shard_map/half_grads/pallas_call | solution.py:1093
  224.7 2.8 all-to-all-start
  227.5 8.8 %attend_back.3 = (bf16[1024,2304]{1,0:T(8,128)(2,1)}, f32[1024,768]{1,0:T(8,128)}, bf16[1024,768]{1,0:T(8,128)(2,1)}, f32[1,2304]{1,0:T(1,128)}) custom-call(bf16[1024,2304]{1,0:T(8,128)(2,1)} %get-tuple-element.223.projected_ref, bf16[1024,1536]{1,0:T(8,128)(2,1)} %get-tuple-element.224.probs_ref, bf16[1024,768]{1,0:T(8,128)(2,1)} %get-tuple-element.225.context_ref, ...), custom_call_target="tpu_custom_call" | custom-call | flops 1409286144 | bytes 27214848 | tf_op jit(solution)/shard_map/attend_back/pallas_call | solution.py:395
  236.3 17.0 %half_grads.5 = bf16[16,8,48,384]{3,2,1,0:T(8,128)(2,1)} custom-call(s32[1]{0:T(128)} %bitcast.27.side_ref, bf16[1024,768]{1,0:T(8,128)(2,1)} %get-tuple-element.163.refs_0_, bf16[1024,3072]{1,0:T(8,128)(2,1)} %get-tuple-element.170.refs_1_, f32[8,3840]{1,0:T(8,128)} %get-tuple-element.171.heads_ref.refs_2_.refs_4_, ...), custom_call_target="tpu_custom_call" | custom-call | flops 4831838208 | bytes 31457280 | tf_op jit(solution)/shard_map/half_grads/pallas_call | solution.py:1093
  253.4 2.4 dynamic-slice_bitcast_fusion.3
  255.8 1.7 collective-permute-start.42
  258.9 2.4 dynamic-slice_bitcast_fusion
  261.3 14.5 %attend_back.4 = (bf16[1024,2304]{1,0:T(8,128)(2,1)}, f32[1024,768]{1,0:T(8,128)}, bf16[1024,768]{1,0:T(8,128)(2,1)}, f32[1,2304]{1,0:T(1,128)}) custom-call(bf16[1024,2304]{1,0:T(8,128)(2,1)} %get-tuple-element.223.projected_ref, bf16[1024,1536]{1,0:T(8,128)(2,1)} %get-tuple-element.224.probs_ref, ...), custom_call_target="tpu_custom_call", output_to_operand_aliasing={{0}: (9, {}), {1}: (10, {}), {2}: (11, {})} | custom-call | flops 2818572288 | bytes 27214848 | tf_op jit(solution)/shard_map/attend_back/pallas_call | solution.py:395
  278.5 8.8 %attend_back.5 = (bf16[1024,2304]{1,0:T(8,128)(2,1)}, f32[1024,768]{1,0:T(8,128)}, bf16[1024,768]{1,0:T(8,128)(2,1)}, f32[1,2304]{1,0:T(1,128)}) custom-call(bf16[1024,2304]{1,0:T(8,128)(2,1)} %get-tuple-element.223.projected_ref, bf16[1024,1536]{1,0:T(8,128)(2,1)} %get-tuple-element.224.probs_ref, ...), custom_call_target="tpu_custom_call", output_to_operand_aliasing={{0}: (9, {}), {1}: (10, {}), {2}: (11, {})} | custom-call | flops 1409286144 | bytes 27214848 | tf_op jit(solution)/shard_map/attend_back/pallas_call | solution.py:395
  287.3 1.6 convert_reduce_fusion.1
  292.0 1.7 convert_reduce_fusion
  294.2 1.8 fusion.8
  299.1 6.0 %collective-permute-done.44 = bf16[4,8,48,384]{3,2,1,0:T(8,128)(2,1)} collective-permute-done((bf16[4,8,48,384]{3,2,1,0:T(8,128)(2,1)S(1)}, bf16[4,8,48,384]{3,2,1,0:T(8,128)(2,1)}, u32[]{:S(2)}, u32[]{:S(2)}) %collective-permute-start.44) | collective-permute-done | bytes 1179680 | tf_op jit(solution)/shard_map/ppermute | solution.py:654
  305.5 3.1 add_convert_fusion
  308.7 8.5 %half_grads.6 = bf16[16,4,48,384]{3,2,1,0:T(8,128)(2,1)} custom-call(s32[1]{0:T(128)} %bitcast.35.side_ref, bf16[1024,768]{1,0:T(8,128)(2,1)} %refs_0_.3, bf16[1024,2304]{1,0:T(8,128)(2,1)} %get-tuple-element.233.refs_1_, bf16[1024,768]{1,0:T(8,128)(2,1)} %get-tuple-element.146.context_ref.refs_2_, bf16[1024,768]{1,0:T(8,128)(2,1)} %get-tuple-element.234.refs_3_, ...), custom_call_target="tpu_custom_call" | custom-call | flops 2415919104 | bytes 31457280 | tf_op jit(solution)/shard_map/half_grads/pallas_call | solution.py:1093
  319.8 4.8 %all-to-all-start.1 = ((f32[32,8,128]{2,1,0:T(8,128)}), f32[32,8,128]{2,1,0:T(8,128)S(1)}, u32[]{:S(2)}, u32[]{:S(2)}) async-start(f32[32,8,128]{2,1,0:T(8,128)} %bitcast.57), calls=%async_computation.1 | async-start | bytes 262144 | tf_op jit(solution)/shard_map/all_to_all | solution.py:649
  326.0 9.0 %half_grads.7 = bf16[16,4,48,384]{3,2,1,0:T(8,128)(2,1)} custom-call(s32[1]{0:T(128)} %bitcast.23.side_ref, bf16[1024,768]{1,0:T(8,128)(2,1)} %refs_0_.3, bf16[1024,2304]{1,0:T(8,128)(2,1)} %get-tuple-element.233.refs_1_, bf16[1024,768]{1,0:T(8,128)(2,1)} %get-tuple-element.146.context_ref.refs_2_, bf16[1024,768]{1,0:T(8,128)(2,1)} %get-tuple-element.234.refs_3_, ...), custom_call_target="tpu_custom_call" | custom-call | flops 2415919104 | bytes 31457280 | tf_op jit(solution)/shard_map/half_grads/pallas_call | solution.py:1093
  336.1 1.8 collective-permute-start.47
  339.3 1.5 collective-permute-start.49
  340.8 8.1 %reduce-scatter.2.cloned.1.call-done = bf16[384,384]{1,0:T(8,128)(2,1)} async-done(((bf16[1536,384]{1,0:T(8,128)(2,1)}), bf16[384,384]{1,0:T(8,128)(2,1)}) %reduce-scatter.2.cloned.1.call-update) | async-done | bytes 294928 | tf_op jit(solution)/shard_map/reduce_scatter | solution.py:1147
  350.3 1.5 collective-permute-start.48
  352.0 1.5 collective-permute-start.50
  354.3 11.8 %collective-permute-done.48 = bf16[4,4,48,384]{3,2,1,0:T(8,128)(2,1)S(1)} collective-permute-done((bf16[4,4,48,384]{3,2,1,0:T(8,128)(2,1)S(1)}, bf16[4,4,48,384]{3,2,1,0:T(8,128)(2,1)S(1)}, u32[]{:S(2)}, u32[]{:S(2)}) %collective-permute-start.48) | collective-permute-done | bytes 589856 | tf_op jit(solution)/shard_map/ppermute | solution.py:654
  374.7 9.1 %collective-permute-done.52 = bf16[4,48,384]{2,1,0:T(8,128)(2,1)S(1)} collective-permute-done((bf16[4,48,384]{2,1,0:T(8,128)(2,1)S(1)}, bf16[4,48,384]{2,1,0:T(8,128)(2,1)S(1)}, u32[]{:S(2)}, u32[]{:S(2)}) %collective-permute-start.52) | collective-permute-done | bytes 147488 | tf_op jit(solution)/shard_map/ppermute | solution.py:654
  (302 shorter events, 76.0 us)
Async XLA Ops:
  7.3 53.3 %all-gather.6.cloned.1.call-start = ((), (), s32[]{:S(2)}) async-start(), calls=%async_computation.3 | async-start | bytes 1658880 | tf_op jit(solution)/shard_map/all_gather | solution.py:748
  14.0 9.0 %collective-permute-start.5 = (bf16[48,1280]{1,0:T(8,128)(2,1)S(1)}, bf16[48,1280]{1,0:T(8,128)(2,1)S(1)}, u32[]{:S(2)}, u32[]{:S(2)}) collective-permute-start(bf16[48,1280]{1,0:T(8,128)(2,1)S(1)} %get-tuple-element.333), channel_id=1, source_target_pairs={{0,6},{1,7},{2,0},{3,1},{4,2},{5,3},{6,4},{7,5},{8,14},{9,15},{10,... | collective-permute-start | bytes 368648 | tf_op jit(solution)/shard_map/ppermute | solution.py:654
  19.0 11.1 %collective-permute-start.4 = (bf16[48,1280]{1,0:T(8,128)(2,1)S(1)}, bf16[48,1280]{1,0:T(8,128)(2,1)S(1)}, u32[]{:S(2)}, u32[]{:S(2)}) collective-permute-start(bf16[48,1280]{1,0:T(8,128)(2,1)S(1)} %get-tuple-element.333), channel_id=1, source_target_pairs={{0,4},{1,5},{2,6},{3,7},{4,0},{5,1},{6,2},{7,3},{8,12},{9,13},{10,... | collective-permute-start | bytes 368648 | tf_op jit(solution)/shard_map/ppermute | solution.py:654
  19.0 11.1 %collective-permute-start.3 = (bf16[48,1280]{1,0:T(8,128)(2,1)S(1)}, bf16[48,1280]{1,0:T(8,128)(2,1)S(1)}, u32[]{:S(2)}, u32[]{:S(2)}) collective-permute-start(bf16[48,1280]{1,0:T(8,128)(2,1)S(1)} %get-tuple-element.333), channel_id=1, source_target_pairs={{0,2},{1,3},{2,4},{3,5},{4,6},{5,7},{6,0},{7,1},{8,10},{9,11},{10,... | collective-permute-start | bytes 368648 | tf_op jit(solution)/shard_map/ppermute | solution.py:654
  20.0 10.2 %collective-permute-start.1 = (bf16[96,768]{1,0:T(8,128)(2,1)}, bf16[96,768]{1,0:T(8,128)(2,1)S(1)}, u32[]{:S(2)}, u32[]{:S(2)}) collective-permute-start(bf16[96,768]{1,0:T(8,128)(2,1)} %param.50), channel_id=1, source_target_pairs={{0,8},{1,9},{2,10},{3,11},{4,12},{5,13},{6,14},{7,15},{8,0},{9,1},... | collective-permute-start | bytes 442376 | tf_op jit(solution)/shard_map/ppermute | solution.py:654
  21.5 8.7 %collective-permute-start.2 = (bf16[96,768]{1,0:T(8,128)(2,1)}, bf16[96,768]{1,0:T(8,128)(2,1)S(1)}, u32[]{:S(2)}, u32[]{:S(2)}) collective-permute-start(bf16[96,768]{1,0:T(8,128)(2,1)} %param.50), channel_id=1, source_target_pairs={{0,16},{1,17},{2,18},{3,19},{4,20},{5,21},{6,22},{7,23},{8,24},{9,... | collective-permute-start | bytes 442376 | tf_op jit(solution)/shard_map/ppermute | solution.py:654
  31.0 54.7 %all-gather.8.cloned.1.call-start = ((), (), s32[]{:S(2)}) async-start(), calls=%async_computation.4 | async-start | bytes 1327104 | tf_op jit(solution)/shard_map/all_gather | solution.py:748
  31.8 86.0 %all-gather.10.cloned.1.call-start = ((), (), s32[]{:S(2)}) async-start(), calls=%async_computation.5 | async-start | bytes 2654208 | tf_op jit(solution)/shard_map/all_gather | solution.py:748
  32.6 157.4 %all-gather.12.cloned.1.call-start = ((), (), s32[]{:S(2)}) async-start(), calls=%async_computation.6 | async-start | bytes 5308416 | tf_op jit(solution)/shard_map/all_gather | solution.py:744
  32.6 12.7 %collective-permute-start.6 = (bf16[4,48,1280]{2,1,0:T(8,128)(2,1)S(1)}, bf16[4,48,1280]{2,1,0:T(8,128)(2,1)S(1)}, u32[]{:S(2)}, u32[]{:S(2)}) collective-permute-start(bf16[4,48,1280]{2,1,0:T(8,128)(2,1)S(1)} %pad_maximum_fusion.4.refs_0_.refs_10_), channel_id=1, source_target_pairs={{0,8},{1,9},{2,10},{3,11},{4,12},{5,13},{6,14},{7,15},{8,0},{9,1},... | collective-permute-start | bytes 1474568 | tf_op jit(solution)/shard_map/ppermute | solution.py:654
  34.2 12.8 %collective-permute-start.8 = (bf16[4,48,1280]{2,1,0:T(8,128)(2,1)S(1)}, bf16[4,48,1280]{2,1,0:T(8,128)(2,1)S(1)}, u32[]{:S(2)}, u32[]{:S(2)}) collective-permute-start(bf16[4,48,1280]{2,1,0:T(8,128)(2,1)S(1)} %pad_maximum_fusion.4.refs_0_.refs_10_), channel_id=1, source_target_pairs={{0,16},{1,17},{2,18},{3,19},{4,20},{5,21},{6,22},{7,23},{8,24},{9,... | collective-permute-start | bytes 1474568 | tf_op jit(solution)/shard_map/ppermute | solution.py:654
  45.4 6.7 %collective-permute-start.7 = (bf16[2,48,1280]{2,1,0:T(8,128)(2,1)S(1)}, bf16[2,48,1280]{2,1,0:T(8,128)(2,1)S(1)}, u32[]{:S(2)}, u32[]{:S(2)}) collective-permute-start(bf16[2,48,1280]{2,1,0:T(8,128)(2,1)S(1)} %slice.332), channel_id=1, source_target_pairs={{0,16},{1,17},{2,18},{3,19},{4,20},{5,21},{6,22},{7,23},{8,24},{9,... | collective-permute-start | bytes 737288 | tf_op jit(solution)/shard_map/ppermute | solution.py:654
  47.0 6.4 %collective-permute-start.9 = (bf16[2,48,1280]{2,1,0:T(8,128)(2,1)S(1)}, bf16[2,48,1280]{2,1,0:T(8,128)(2,1)S(1)}, u32[]{:S(2)}, u32[]{:S(2)}) collective-permute-start(bf16[2,48,1280]{2,1,0:T(8,128)(2,1)S(1)} %slice.333), channel_id=1, source_target_pairs={{0,8},{1,9},{2,10},{3,11},{4,12},{5,13},{6,14},{7,15},{8,0},{9,1},... | collective-permute-start | bytes 737288 | tf_op jit(solution)/shard_map/ppermute | solution.py:654
  59.8 227.5 %all-gather.14.cloned.1.call-start = ((), (), s32[]{:S(2)}) async-start(), calls=%async_computation.7 | async-start | bytes 3649536 | tf_op jit(solution)/shard_map/all_gather | solution.py:529
  61.7 21.0 %collective-permute-start.15 = (bf16[96,3840]{1,0:T(8,128)(2,1)S(1)}, bf16[96,3840]{1,0:T(8,128)(2,1)S(1)}, u32[]{:S(2)}, u32[]{:S(2)}) collective-permute-start(bf16[96,3840]{1,0:T(8,128)(2,1)S(1)} %constant_dynamic-slice_fusion.3), channel_id=1, source_target_pairs={{0,8},{1,9},{2,10},{3,11},{4,12},{5,13},{6,14},{7,15},{8,0},{9,1},... | collective-permute-start | bytes 2211848 | tf_op jit(solution)/shard_map/ppermute | solution.py:654
  62.7 20.1 %collective-permute-start.16 = (bf16[96,3840]{1,0:T(8,128)(2,1)S(1)}, bf16[96,3840]{1,0:T(8,128)(2,1)}, u32[]{:S(2)}, u32[]{:S(2)}) collective-permute-start(bf16[96,3840]{1,0:T(8,128)(2,1)S(1)} %constant_dynamic-slice_fusion.3), channel_id=1, source_target_pairs={{0,16},{1,17},{2,18},{3,19},{4,20},{5,21},{6,22},{7,23},{8,24},{9,... | collective-permute-start | bytes 2211848 | tf_op jit(solution)/shard_map/ppermute | solution.py:654
  84.0 11.5 %collective-permute-start.17 = (bf16[48,3840]{1,0:T(8,128)(2,1)S(1)}, bf16[48,3840]{1,0:T(8,128)(2,1)S(1)}, u32[]{:S(2)}, u32[]{:S(2)}) collective-permute-start(bf16[48,3840]{1,0:T(8,128)(2,1)S(1)} %slice.334), channel_id=1, source_target_pairs={{0,16},{1,17},{2,18},{3,19},{4,20},{5,21},{6,22},{7,23},{8,24},{9,... | collective-permute-start | bytes 1105928 | tf_op jit(solution)/shard_map/ppermute | solution.py:654
  84.6 11.5 %collective-permute-start.18 = (bf16[48,3840]{1,0:T(8,128)(2,1)S(1)}, bf16[48,3840]{1,0:T(8,128)(2,1)S(1)}, u32[]{:S(2)}, u32[]{:S(2)}) collective-permute-start(bf16[48,3840]{1,0:T(8,128)(2,1)S(1)} %slice.335), channel_id=1, source_target_pairs={{0,8},{1,9},{2,10},{3,11},{4,12},{5,13},{6,14},{7,15},{8,0},{9,1},... | collective-permute-start | bytes 1105928 | tf_op jit(solution)/shard_map/ppermute | solution.py:654
  86.8 20.8 %collective-permute-start.23 = (bf16[384,768]{1,0:T(8,128)(2,1)S(1)}, bf16[384,768]{1,0:T(8,128)(2,1)}, u32[]{:S(2)}, u32[]{:S(2)}) collective-permute-start(bf16[384,768]{1,0:T(8,128)(2,1)S(1)} %constant_dynamic-slice_fusion.2), channel_id=1, source_target_pairs={{0,8},{1,9},{2,10},{3,11},{4,12},{5,13},{6,14},{7,15},{8,0},{9,1},... | collective-permute-start | bytes 1769480 | tf_op jit(solution)/shard_map/ppermute | solution.py:654
  87.8 20.9 %collective-permute-start.24 = (bf16[384,768]{1,0:T(8,128)(2,1)S(1)}, bf16[384,768]{1,0:T(8,128)(2,1)}, u32[]{:S(2)}, u32[]{:S(2)}) collective-permute-start(bf16[384,768]{1,0:T(8,128)(2,1)S(1)} %constant_dynamic-slice_fusion.2), channel_id=1, source_target_pairs={{0,16},{1,17},{2,18},{3,19},{4,20},{5,21},{6,22},{7,23},{8,24},{9,... | collective-permute-start | bytes 1769480 | tf_op jit(solution)/shard_map/ppermute | solution.py:654
  96.0 23.4 %collective-permute-start.19 = (bf16[96,3840]{1,0:T(8,128)(2,1)S(1)}, bf16[96,3840]{1,0:T(8,128)(2,1)S(1)}, u32[]{:S(2)}, u32[]{:S(2)}) collective-permute-start(bf16[96,3840]{1,0:T(8,128)(2,1)S(1)} %collective-permute-done.15.refs_1_), channel_id=1, source_target_pairs={{0,1},{1,0},{2,3},{3,2},{4,5},{5,4},{6,7},{7,6},{8,9},{9,8},{10,11... | collective-permute-start | bytes 2211848 | tf_op jit(solution)/shard_map/ppermute | solution.py:654
  96.1 22.8 %collective-permute-start.21 = (bf16[48,3840]{1,0:T(8,128)(2,1)S(1)}, bf16[48,3840]{1,0:T(8,128)(2,1)}, u32[]{:S(2)}, u32[]{:S(2)}) collective-permute-start(bf16[48,3840]{1,0:T(8,128)(2,1)S(1)} %collective-permute-done.17.refs_3_), channel_id=1, source_target_pairs={{0,1},{1,0},{2,3},{3,2},{4,5},{5,4},{6,7},{7,6},{8,9},{9,8},{10,11... | collective-permute-start | bytes 1105928 | tf_op jit(solution)/shard_map/ppermute | solution.py:654
  96.6 22.8 %collective-permute-start.22 = (bf16[48,3840]{1,0:T(8,128)(2,1)S(1)}, bf16[48,3840]{1,0:T(8,128)(2,1)}, u32[]{:S(2)}, u32[]{:S(2)}) collective-permute-start(bf16[48,3840]{1,0:T(8,128)(2,1)S(1)} %collective-permute-done.18.refs_4_), channel_id=1, source_target_pairs={{0,1},{1,0},{2,3},{3,2},{4,5},{5,4},{6,7},{7,6},{8,9},{9,8},{10,11... | collective-permute-start | bytes 1105928 | tf_op jit(solution)/shard_map/ppermute | solution.py:654
  109.7 8.1 %collective-permute-start.25 = (bf16[192,768]{1,0:T(8,128)(2,1)S(1)}, bf16[192,768]{1,0:T(8,128)(2,1)}, u32[]{:S(2)}, u32[]{:S(2)}) collective-permute-start(bf16[192,768]{1,0:T(8,128)(2,1)S(1)} %slice.336), channel_id=1, source_target_pairs={{0,16},{1,17},{2,18},{3,19},{4,20},{5,21},{6,22},{7,23},{8,24},{9,... | collective-permute-start | bytes 884744 | tf_op jit(solution)/shard_map/ppermute | solution.py:654
  111.2 7.7 %collective-permute-start.26 = (bf16[192,768]{1,0:T(8,128)(2,1)S(1)}, bf16[192,768]{1,0:T(8,128)(2,1)}, u32[]{:S(2)}, u32[]{:S(2)}) collective-permute-start(bf16[192,768]{1,0:T(8,128)(2,1)S(1)} %slice.337), channel_id=1, source_target_pairs={{0,8},{1,9},{2,10},{3,11},{4,12},{5,13},{6,14},{7,15},{8,0},{9,1},... | collective-permute-start | bytes 884744 | tf_op jit(solution)/shard_map/ppermute | solution.py:654
  121.4 33.6 %collective-permute-start.31 = (bf16[96,6144]{1,0:T(8,128)(2,1)S(1)}, bf16[96,6144]{1,0:T(8,128)(2,1)S(1)}, u32[]{:S(2)}, u32[]{:S(2)}) collective-permute-start(bf16[96,6144]{1,0:T(8,128)(2,1)S(1)} %constant_dynamic-slice_fusion.1), channel_id=1, source_target_pairs={{0,8},{1,9},{2,10},{3,11},{4,12},{5,13},{6,14},{7,15},{8,0},{9,1},... | collective-permute-start | bytes 3538952 | tf_op jit(solution)/shard_map/ppermute | solution.py:654
  122.3 33.7 %collective-permute-start.32 = (bf16[96,6144]{1,0:T(8,128)(2,1)S(1)}, bf16[96,6144]{1,0:T(8,128)(2,1)S(1)}, u32[]{:S(2)}, u32[]{:S(2)}) collective-permute-start(bf16[96,6144]{1,0:T(8,128)(2,1)S(1)} %constant_dynamic-slice_fusion.1), channel_id=1, source_target_pairs={{0,16},{1,17},{2,18},{3,19},{4,20},{5,21},{6,22},{7,23},{8,24},{9,... | collective-permute-start | bytes 3538952 | tf_op jit(solution)/shard_map/ppermute | solution.py:654
  156.0 25.8 %collective-permute-start.33 = (bf16[48,6144]{1,0:T(8,128)(2,1)}, bf16[48,6144]{1,0:T(8,128)(2,1)S(1)}, u32[]{:S(2)}, u32[]{:S(2)}) collective-permute-start(bf16[48,6144]{1,0:T(8,128)(2,1)} %slice.339), channel_id=1, source_target_pairs={{0,16},{1,17},{2,18},{3,19},{4,20},{5,21},{6,22},{7,23},{8,24},{9,... | collective-permute-start | bytes 1769480 | tf_op jit(solution)/shard_map/ppermute | solution.py:654
  157.4 24.4 %collective-permute-start.34 = (bf16[48,6144]{1,0:T(8,128)(2,1)S(1)}, bf16[48,6144]{1,0:T(8,128)(2,1)S(1)}, u32[]{:S(2)}, u32[]{:S(2)}) collective-permute-start(bf16[48,6144]{1,0:T(8,128)(2,1)S(1)} %slice.340), channel_id=1, source_target_pairs={{0,8},{1,9},{2,10},{3,11},{4,12},{5,13},{6,14},{7,15},{8,0},{9,1},... | collective-permute-start | bytes 1769480 | tf_op jit(solution)/shard_map/ppermute | solution.py:654
  182.7 6.4 %collective-permute-start.35 = (bf16[96,6144]{1,0:T(8,128)(2,1)S(1)}, bf16[96,6144]{1,0:T(8,128)(2,1)S(1)}, u32[]{:S(2)}, u32[]{:S(2)}) collective-permute-start(bf16[96,6144]{1,0:T(8,128)(2,1)S(1)} %collective-permute-done.31.refs_1_), channel_id=1, source_target_pairs={{0,1},{1,0},{2,3},{3,2},{4,5},{5,4},{6,7},{7,6},{8,9},{9,8},{10,11... | collective-permute-start | bytes 3538952 | tf_op jit(solution)/shard_map/ppermute | solution.py:654
  182.7 7.3 %collective-permute-start.36 = (bf16[96,6144]{1,0:T(8,128)(2,1)S(1)}, bf16[96,6144]{1,0:T(8,128)(2,1)}, u32[]{:S(2)}, u32[]{:S(2)}) collective-permute-start(bf16[96,6144]{1,0:T(8,128)(2,1)S(1)} %collective-permute-done.32.refs_2_), channel_id=1, source_target_pairs={{0,1},{1,0},{2,3},{3,2},{4,5},{5,4},{6,7},{7,6},{8,9},{9,8},{10,11... | collective-permute-start | bytes 3538952 | tf_op jit(solution)/shard_map/ppermute | solution.py:654
  183.3 5.8 %collective-permute-start.38 = (bf16[48,6144]{1,0:T(8,128)(2,1)}, bf16[48,6144]{1,0:T(8,128)(2,1)S(1)}, u32[]{:S(2)}, u32[]{:S(2)}) collective-permute-start(bf16[48,6144]{1,0:T(8,128)(2,1)} %copy-done.13), channel_id=1, source_target_pairs={{0,1},{1,0},{2,3},{3,2},{4,5},{5,4},{6,7},{7,6},{8,9},{9,8},{10,11... | collective-permute-start | bytes 1769480 | tf_op jit(solution)/shard_map/ppermute | solution.py:654
  223.0 13.3 %collective-permute-start.41 = (bf16[16,8,48,384]{3,2,1,0:T(8,128)(2,1)}, bf16[16,8,48,384]{3,2,1,0:T(8,128)(2,1)}, u32[]{:S(2)}, u32[]{:S(2)}) collective-permute-start(bf16[16,8,48,384]{3,2,1,0:T(8,128)(2,1)} %half_grads.4), channel_id=1, source_target_pairs={{0,1},{1,0},{2,3},{3,2},{4,5},{5,4},{6,7},{7,6},{8,9},{9,8},{10,11... | collective-permute-start | bytes 14155784 | tf_op jit(solution)/shard_map/ppermute | solution.py:654
  224.7 11.7 %all-to-all-start = ((bf16[32,8,168]{2,1,0:T(8,128)(2,1)}), bf16[32,8,168]{2,1,0:T(8,128)(2,1)S(1)}, u32[]{:S(2)}, u32[]{:S(2)}) async-start(bf16[32,8,168]{2,1,0:T(8,128)(2,1)} %maximum_bitcast_fusion), calls=%async_computation | async-start | bytes 262144 | tf_op jit(solution)/shard_map/all_to_all | solution.py:1380
  227.4 121.5 %reduce-scatter.2.cloned.1.call-start = ((), (), s32[]{:S(2)}) async-start(), calls=%async_computation.8 | async-start | bytes 1474560 | tf_op jit(solution)/shard_map/reduce_scatter | solution.py:1147
  255.8 20.0 %collective-permute-start.42 = (bf16[2,8,48,384]{3,2,1,0:T(8,128)(2,1)}, bf16[2,8,48,384]{3,2,1,0:T(8,128)(2,1)}, u32[]{:S(2)}, u32[]{:S(2)}) collective-permute-start(bf16[2,8,48,384]{3,2,1,0:T(8,128)(2,1)} %get-tuple-element.293), channel_id=1, source_target_pairs={{0,16},{1,17},{2,18},{3,19},{4,20},{5,21},{6,22},{7,23},{8,24},{9,... | collective-permute-start | bytes 1769480 | tf_op jit(solution)/shard_map/ppermute | solution.py:654
  257.5 18.3 %collective-permute-start.43 = (bf16[2,8,48,384]{3,2,1,0:T(8,128)(2,1)}, bf16[2,8,48,384]{3,2,1,0:T(8,128)(2,1)}, u32[]{:S(2)}, u32[]{:S(2)}) collective-permute-start(bf16[2,8,48,384]{3,2,1,0:T(8,128)(2,1)} %get-tuple-element.292), channel_id=1, source_target_pairs={{0,8},{1,9},{2,10},{3,11},{4,12},{5,13},{6,14},{7,15},{8,0},{9,1},... | collective-permute-start | bytes 1769480 | tf_op jit(solution)/shard_map/ppermute | solution.py:654
  277.4 27.7 %collective-permute-start.44 = (bf16[4,8,48,384]{3,2,1,0:T(8,128)(2,1)S(1)}, bf16[4,8,48,384]{3,2,1,0:T(8,128)(2,1)}, u32[]{:S(2)}, u32[]{:S(2)}) collective-permute-start(bf16[4,8,48,384]{3,2,1,0:T(8,128)(2,1)S(1)} %pad_maximum_fusion), channel_id=1, source_target_pairs={{0,8},{1,9},{2,10},{3,11},{4,12},{5,13},{6,14},{7,15},{8,0},{9,1},... | collective-permute-start | bytes 3538952 | tf_op jit(solution)/shard_map/ppermute | solution.py:654
  278.2 27.4 %collective-permute-start.45 = (bf16[4,8,48,384]{3,2,1,0:T(8,128)(2,1)S(1)}, bf16[4,8,48,384]{3,2,1,0:T(8,128)(2,1)}, u32[]{:S(2)}, u32[]{:S(2)}) collective-permute-start(bf16[4,8,48,384]{3,2,1,0:T(8,128)(2,1)S(1)} %pad_maximum_fusion.1), channel_id=1, source_target_pairs={{0,16},{1,17},{2,18},{3,19},{4,20},{5,21},{6,22},{7,23},{8,24},{9,... | collective-permute-start | bytes 3538952 | tf_op jit(solution)/shard_map/ppermute | solution.py:654
  317.2 7.4 %collective-permute-start.46 = (bf16[16,4,48,384]{3,2,1,0:T(8,128)(2,1)}, bf16[16,4,48,384]{3,2,1,0:T(8,128)(2,1)S(1)}, u32[]{:S(2)}, u32[]{:S(2)}) collective-permute-start(bf16[16,4,48,384]{3,2,1,0:T(8,128)(2,1)} %half_grads.6), channel_id=1, source_target_pairs={{0,1},{1,0},{2,3},{3,2},{4,5},{5,4},{6,7},{7,6},{8,9},{9,8},{10,11... | collective-permute-start | bytes 7077896 | tf_op jit(solution)/shard_map/ppermute | solution.py:654
  319.8 53.1 %all-to-all-start.1 = ((f32[32,8,128]{2,1,0:T(8,128)}), f32[32,8,128]{2,1,0:T(8,128)S(1)}, u32[]{:S(2)}, u32[]{:S(2)}) async-start(f32[32,8,128]{2,1,0:T(8,128)} %bitcast.57), calls=%async_computation.1 | async-start | bytes 262144 | tf_op jit(solution)/shard_map/all_to_all | solution.py:649
  336.1 14.1 %collective-permute-start.47 = (bf16[2,4,48,384]{3,2,1,0:T(8,128)(2,1)S(1)}, bf16[2,4,48,384]{3,2,1,0:T(8,128)(2,1)S(1)}, u32[]{:S(2)}, u32[]{:S(2)}) collective-permute-start(bf16[2,4,48,384]{3,2,1,0:T(8,128)(2,1)S(1)} %get-tuple-element.298), channel_id=1, source_target_pairs={{0,16},{1,17},{2,18},{3,19},{4,20},{5,21},{6,22},{7,23},{8,24},{9,... | collective-permute-start | bytes 884744 | tf_op jit(solution)/shard_map/ppermute | solution.py:654
  339.3 12.6 %collective-permute-start.49 = (bf16[2,4,48,384]{3,2,1,0:T(8,128)(2,1)S(1)}, bf16[2,4,48,384]{3,2,1,0:T(8,128)(2,1)S(1)}, u32[]{:S(2)}, u32[]{:S(2)}) collective-permute-start(bf16[2,4,48,384]{3,2,1,0:T(8,128)(2,1)S(1)} %get-tuple-element.297), channel_id=1, source_target_pairs={{0,8},{1,9},{2,10},{3,11},{4,12},{5,13},{6,14},{7,15},{8,0},{9,1},... | collective-permute-start | bytes 884744 | tf_op jit(solution)/shard_map/ppermute | solution.py:654
  350.3 15.8 %collective-permute-start.48 = (bf16[4,4,48,384]{3,2,1,0:T(8,128)(2,1)S(1)}, bf16[4,4,48,384]{3,2,1,0:T(8,128)(2,1)S(1)}, u32[]{:S(2)}, u32[]{:S(2)}) collective-permute-start(bf16[4,4,48,384]{3,2,1,0:T(8,128)(2,1)S(1)} %pad_maximum_fusion.2), channel_id=1, source_target_pairs={{0,8},{1,9},{2,10},{3,11},{4,12},{5,13},{6,14},{7,15},{8,0},{9,1},... | collective-permute-start | bytes 1769480 | tf_op jit(solution)/shard_map/ppermute | solution.py:654
  352.0 15.5 %collective-permute-start.50 = (bf16[4,4,48,384]{3,2,1,0:T(8,128)(2,1)S(1)}, bf16[4,4,48,384]{3,2,1,0:T(8,128)(2,1)S(1)}, u32[]{:S(2)}, u32[]{:S(2)}) collective-permute-start(bf16[4,4,48,384]{3,2,1,0:T(8,128)(2,1)S(1)} %pad_maximum_fusion.3), channel_id=1, source_target_pairs={{0,16},{1,17},{2,18},{3,19},{4,20},{5,21},{6,22},{7,23},{8,24},{9,... | collective-permute-start | bytes 1769480 | tf_op jit(solution)/shard_map/ppermute | solution.py:654
  368.9 5.9 %collective-permute-start.53 = (bf16[4,48,384]{2,1,0:T(8,128)(2,1)S(1)}, bf16[4,48,384]{2,1,0:T(8,128)(2,1)S(1)}, u32[]{:S(2)}, u32[]{:S(2)}) collective-permute-start(bf16[4,48,384]{2,1,0:T(8,128)(2,1)S(1)} %get-tuple-element.308), channel_id=1, source_target_pairs={{0,6},{1,7},{2,0},{3,1},{4,2},{5,3},{6,4},{7,5},{8,14},{9,15},{10,... | collective-permute-start | bytes 442376 | tf_op jit(solution)/shard_map/ppermute | solution.py:654
  370.0 13.9 %collective-permute-start.52 = (bf16[4,48,384]{2,1,0:T(8,128)(2,1)S(1)}, bf16[4,48,384]{2,1,0:T(8,128)(2,1)S(1)}, u32[]{:S(2)}, u32[]{:S(2)}) collective-permute-start(bf16[4,48,384]{2,1,0:T(8,128)(2,1)S(1)} %get-tuple-element.309), channel_id=1, source_target_pairs={{0,4},{1,5},{2,6},{3,7},{4,0},{5,1},{6,2},{7,3},{8,12},{9,13},{10,... | collective-permute-start | bytes 442376 | tf_op jit(solution)/shard_map/ppermute | solution.py:654
  371.3 12.6 %collective-permute-start.51 = (bf16[4,48,384]{2,1,0:T(8,128)(2,1)S(1)}, bf16[4,48,384]{2,1,0:T(8,128)(2,1)S(1)}, u32[]{:S(2)}, u32[]{:S(2)}) collective-permute-start(bf16[4,48,384]{2,1,0:T(8,128)(2,1)S(1)} %get-tuple-element.307), channel_id=1, source_target_pairs={{0,2},{1,3},{2,4},{3,5},{4,6},{5,7},{6,0},{7,1},{8,10},{9,11},{10,... | collective-permute-start | bytes 442376 | tf_op jit(solution)/shard_map/ppermute | solution.py:654
  (59 other events, 491.4 us)
Sparse Core Ops, SparseCore 0:
  31.1 24.5 all-gather.5
  57.3 22.1 all-gather.7
  81.8 31.2 all-gather.9
  114.6 50.8 all-gather.11
  208.2 58.3 all-gather.13
  317.4 31.5 reduce-scatter.1

commit v6 on v5

--- a/solution.py
+++ b/solution.py
@@ -707,6 +707,10 @@
     line_x, line_y = over_x(line), over_y(line)
     pieces = [line, line_x, line_y, over_y(line_x[:2]), over_x(line_y[2:])]
     return pieces + [over_core(piece) for piece in pieces]
+
+
+def held(array, first):
+    return array + first.reshape(-1)[:1].reshape((1,) * array.ndim).astype(array.dtype) * 0
 
 
 def after(first, *later):
@@ -1425,7 +1429,8 @@
         kept = half_grads(jobs, core, over_core(sent))
         short = scatter_next(*scatter_across(scatter_planes(kept), ()), ())
         sums_gate = short
-        short = scatter_line(after(tall, short))
+        tall = held(tall, short)
+        short = scatter_line(short)
         own_expand, own_reduce = scatter_end(tall, [(D, wide), (wide, D)])
         own_attend, own_merge = scatter_end(short, [(D, 3 * D), (D, D)])
     else:

time: 398 us -> 394 us (0.990)
  waiting for transfers between devices: 89.5 us -> 83.4 us
    reduce_scatter x1, waiting for transfers between devices: 8.14 us -> 0.02 us  [scatter_along(): lax.psum_scatter(here.reshape(-1, here.shape[-1]), 'fsdp', scatter_dimens...]
    unnamed x99 -> x97, local copies, waits for them, and re-layouts: 11 us -> 10.9 us
  transfers between devices with their start and end apart: 64 -> 64, of which waited for: 22 -> 23; matrix products, arithmetic and copies ran while one was open for 11% -> 11% of each run, Pallas kernels for 37% -> 38%
where the time goes in v6:
time: 394 us; the launch traced here: 390 us
  Pallas kernels  174 us (44%)
  waiting for transfers between devices  83.4 us (21%)
  starting transfers between devices  56.6 us (14%)
  local copies, waits for them, and re-layouts  35.1 us (9%)
  other arithmetic  19.6 us (5%)
  between operations  16.9 us (4%)
  matrix products  4.89 us (1%)
    pallas_call x6, Pallas kernels, row_call(): pl.pallas_call(kernel, grid=(rows // ROWS if steps is None else steps,),...  102 us
    ppermute x56, waiting for transfers between devices, hop(): lax.ppermute(array, AXES, [(place, turn(place)) for place in range(32)])  82.6 us
    pallas_call x4, Pallas kernels, half_grads(): pl.pallas_call(partial(grads_kernel, rules, int(came is not None)), grid_...  49.4 us
    ppermute x56, starting transfers between devices, hop(): lax.ppermute(array, AXES, [(place, turn(place)) for place in range(32)])  49 us
    pallas_call x1, Pallas kernels, heads_step(): pl.pallas_call(partial(heads_kernel, (len(mid), 1), mid_moves, end_moves)...  17 us
    unnamed x97, local copies, waits for them, and re-layouts  10.9 us
  transfers between devices with their start and end apart: 64, of which 23 were waited for; matrix products, arithmetic and copies ran while one was open for 11% of the time, Pallas kernels for 38%

profile of v6, /device:TPU:0, one launch (start us, length us, event | category | flops | bytes accessed | tf_op | source)
XLA Modules:
  0.0 390.0 jit_solution(12438166361042238274)
XLA Ops:
  9.6 1.5 pack.1
  14.0 5.0 %collective-permute-start.5 = (bf16[48,1280]{1,0:T(8,128)(2,1)S(1)}, bf16[48,1280]{1,0:T(8,128)(2,1)S(1)}, u32[]{:S(2)}, u32[]{:S(2)}) collective-permute-start(bf16[48,1280]{1,0:T(8,128)(2,1)S(1)} %get-tuple-element.333), channel_id=1, source_target_pairs={{0,6},{1,7},{2,0},{3,1},{4,2},{5,3},{6,4},{7,5},{8,14},{9,15},{10,... | collective-permute-start | bytes 368648 | tf_op jit(solution)/shard_map/ppermute | solution.py:654
  21.5 1.5 collective-permute-start.2
  23.0 7.1 %collective-permute-done.4 = bf16[48,1280]{1,0:T(8,128)(2,1)S(1)} collective-permute-done((bf16[48,1280]{1,0:T(8,128)(2,1)S(1)}, bf16[48,1280]{1,0:T(8,128)(2,1)S(1)}, u32[]{:S(2)}, u32[]{:S(2)}) %collective-permute-start.4) | collective-permute-done | bytes 122912 | tf_op jit(solution)/shard_map/ppermute | solution.py:654
  32.6 1.6 collective-permute-start.6
  34.2 1.5 collective-permute-start.8
  35.7 9.7 %collective-permute-done.6.refs_1_.refs_11_ = bf16[4,48,1280]{2,1,0:T(8,128)(2,1)S(1)} collective-permute-done((bf16[4,48,1280]{2,1,0:T(8,128)(2,1)S(1)}, bf16[4,48,1280]{2,1,0:T(8,128)(2,1)S(1)}, u32[]{:S(2)}, u32[]{:S(2)}) %collective-permute-start.6) | collective-permute-done | bytes 491552 | tf_op jit(solution)/shard_map/ppermute | solution.py:654
  45.4 1.6 collective-permute-start.7
  47.0 1.6 collective-permute-start.9
  48.6 3.4 collective-permute-done.7.refs_3_.refs_13_
  55.5 2.3 collective-permute-done.39
  67.4 15.3 %attend.1 = (bf16[1024,2304]{1,0:T(8,128)(2,1)}, bf16[1024,768]{1,0:T(8,128)(2,1)}, bf16[1024,1536]{1,0:T(8,128)(2,1)}, bf16[768,2304]{1,0:T(8,128)(2,1)}) custom-call(s32[1]{0:T(128)S(6)} %copy.88.count_ref, bf16[1024,768]{1,0:T(8,128)(2,1)} %refs_0_.3, s32[3]{0:T(128)} %pad_add_fusion.place_ref, bf16[4,48,1280]{2,1,0:T(8,128)(2,1)} %copy-done.4, ...), custom_call_target="tpu_custom_call" | custom-call | flops 4429185024 | bytes 20447248 | tf_op jit(solution)/shard_map/attend/pallas_call | solution.py:395
  87.8 1.5 collective-permute-start.24
  89.3 6.2 %collective-permute-done.17.refs_3_ = bf16[48,3840]{1,0:T(8,128)(2,1)S(1)} collective-permute-done((bf16[48,3840]{1,0:T(8,128)(2,1)S(1)}, bf16[48,3840]{1,0:T(8,128)(2,1)S(1)}, u32[]{:S(2)}, u32[]{:S(2)}) %collective-permute-start.17) | collective-permute-done | bytes 368672 | tf_op jit(solution)/shard_map/ppermute | solution.py:654
  96.5 3.8 unpack.1
  100.4 7.3 %collective-permute-done.23.refs_10_ = bf16[384,768]{1,0:T(8,128)(2,1)} collective-permute-done((bf16[384,768]{1,0:T(8,128)(2,1)S(1)}, bf16[384,768]{1,0:T(8,128)(2,1)}, u32[]{:S(2)}, u32[]{:S(2)}) %collective-permute-start.23) | collective-permute-done | bytes 589856 | tf_op jit(solution)/shard_map/ppermute | solution.py:654
  109.6 1.6 collective-permute-start.25
  111.7 5.9 %collective-permute-done.25.refs_12_ = bf16[192,768]{1,0:T(8,128)(2,1)} collective-permute-done((bf16[192,768]{1,0:T(8,128)(2,1)S(1)}, bf16[192,768]{1,0:T(8,128)(2,1)}, u32[]{:S(2)}, u32[]{:S(2)}) %collective-permute-start.25) | collective-permute-done | bytes 294944 | tf_op jit(solution)/shard_map/ppermute | solution.py:654
  123.7 31.3 %feed.1 = (bf16[1024,768]{1,0:T(8,128)(2,1)}, f32[8,3840]{1,0:T(8,128)}, f32[8,6144]{1,0:T(8,128)}, f32[1024,768]{1,0:T(8,128)}, bf16[1024,768]{1,0:T(8,128)(2,1...) custom-call(s32[1]{0:T(128)S(6)} %copy.88.count_ref, ...), custom_call_target="tpu_custom_call" | custom-call | flops 10871635968 | bytes 46755856 | tf_op jit(solution)/shard_map/feed/pallas_call | solution.py:395
  158.6 23.1 %feed_back.1 = (bf16[1024,768]{1,0:T(8,128)(2,1)}, bf16[1024,3072]{1,0:T(8,128)(2,1)}, bf16[1024,768]{1,0:T(8,128)(2,1)}, bf16[1024,768]{1,0:T(8,128)(2,1)}, f32...) custom-call(s32[1]{0:T(128)S(6)} %copy.88.count_ref, bf16[1024,768]{1,0:T(8,128)(2,1)} %cotangent_ref.1, ...), custom_call_target="tpu_custom_call" | custom-call | flops 10871635968 | bytes 38989828 | tf_op jit(solution)/shard_map/feed_back/pallas_call | solution.py:395
  185.2 3.7 collective-permute-done.37.refs_7_
  190.9 17.0 %heads.1 = (f32[8,768]{1,0:T(8,128)}, f32[8,768]{1,0:T(8,128)}, bf16[8,5376]{1,0:T(8,128)(2,1)}, bf16[8,6912]{1,0:T(8,128)(2,1)}, f32[8,768]{1,0:T(8,128)}, /*in...) custom-call(s32[3]{0:T(128)} %pad_add_fusion.place_ref, ...), custom_call_target="tpu_custom_call" | custom-call | flops 594542592 | bytes 25952256 | tf_op jit(solution)/shard_map/heads/pallas_call | solution.py:996
  208.0 15.0 %half_grads.4 = bf16[16,8,48,384]{3,2,1,0:T(8,128)(2,1)} custom-call(s32[1]{0:T(128)} %bitcast.side_ref, bf16[1024,768]{1,0:T(8,128)(2,1)} %get-tuple-element.163.refs_0_, bf16[1024,3072]{1,0:T(8,128)(2,1)} %get-tuple-element.170.refs_1_, f32[8,3840]{1,0:T(8,128)} %get-tuple-element.171.heads_ref.refs_2_.refs_4_, ...), custom_call_target="tpu_custom_call" | custom-call | flops 4831838208 | bytes 31457280 | tf_op jit(solution)/shard_map/half_grads/pallas_call | solution.py:1097
  224.6 2.8 all-to-all-start
  227.4 8.8 %attend_back.3 = (bf16[1024,2304]{1,0:T(8,128)(2,1)}, f32[1024,768]{1,0:T(8,128)}, bf16[1024,768]{1,0:T(8,128)(2,1)}, f32[1,2304]{1,0:T(1,128)}) custom-call(bf16[1024,2304]{1,0:T(8,128)(2,1)} %get-tuple-element.223.projected_ref, bf16[1024,1536]{1,0:T(8,128)(2,1)} %get-tuple-element.224.probs_ref, bf16[1024,768]{1,0:T(8,128)(2,1)} %get-tuple-element.225.context_ref, ...), custom_call_target="tpu_custom_call" | custom-call | flops 1409286144 | bytes 27214848 | tf_op jit(solution)/shard_map/attend_back/pallas_call | solution.py:395
  236.3 17.0 %half_grads.5 = bf16[16,8,48,384]{3,2,1,0:T(8,128)(2,1)} custom-call(s32[1]{0:T(128)} %bitcast.27.side_ref, bf16[1024,768]{1,0:T(8,128)(2,1)} %get-tuple-element.163.refs_0_, bf16[1024,3072]{1,0:T(8,128)(2,1)} %get-tuple-element.170.refs_1_, f32[8,3840]{1,0:T(8,128)} %get-tuple-element.171.heads_ref.refs_2_.refs_4_, ...), custom_call_target="tpu_custom_call" | custom-call | flops 4831838208 | bytes 31457280 | tf_op jit(solution)/shard_map/half_grads/pallas_call | solution.py:1097
  253.3 2.4 dynamic-slice_bitcast_fusion.3
  255.7 1.7 collective-permute-start.42
  258.8 2.4 dynamic-slice_bitcast_fusion
  261.2 14.5 %attend_back.4 = (bf16[1024,2304]{1,0:T(8,128)(2,1)}, f32[1024,768]{1,0:T(8,128)}, bf16[1024,768]{1,0:T(8,128)(2,1)}, f32[1,2304]{1,0:T(1,128)}) custom-call(bf16[1024,2304]{1,0:T(8,128)(2,1)} %get-tuple-element.223.projected_ref, bf16[1024,1536]{1,0:T(8,128)(2,1)} %get-tuple-element.224.probs_ref, ...), custom_call_target="tpu_custom_call", output_to_operand_aliasing={{0}: (9, {}), {1}: (10, {}), {2}: (11, {})} | custom-call | flops 2818572288 | bytes 27214848 | tf_op jit(solution)/shard_map/attend_back/pallas_call | solution.py:395
  278.4 8.8 %attend_back.5 = (bf16[1024,2304]{1,0:T(8,128)(2,1)}, f32[1024,768]{1,0:T(8,128)}, bf16[1024,768]{1,0:T(8,128)(2,1)}, f32[1,2304]{1,0:T(1,128)}) custom-call(bf16[1024,2304]{1,0:T(8,128)(2,1)} %get-tuple-element.223.projected_ref, bf16[1024,1536]{1,0:T(8,128)(2,1)} %get-tuple-element.224.probs_ref, ...), custom_call_target="tpu_custom_call", output_to_operand_aliasing={{0}: (9, {}), {1}: (10, {}), {2}: (11, {})} | custom-call | flops 1409286144 | bytes 27214848 | tf_op jit(solution)/shard_map/attend_back/pallas_call | solution.py:395
  287.2 1.6 convert_reduce_fusion.1
  291.9 1.7 convert_reduce_fusion
  294.1 1.8 fusion.8
  299.0 6.0 %collective-permute-done.44 = bf16[4,8,48,384]{3,2,1,0:T(8,128)(2,1)} collective-permute-done((bf16[4,8,48,384]{3,2,1,0:T(8,128)(2,1)S(1)}, bf16[4,8,48,384]{3,2,1,0:T(8,128)(2,1)}, u32[]{:S(2)}, u32[]{:S(2)}) %collective-permute-start.44) | collective-permute-done | bytes 1179680 | tf_op jit(solution)/shard_map/ppermute | solution.py:654
  305.5 3.1 add_convert_fusion
  308.6 8.4 %half_grads.6 = bf16[16,4,48,384]{3,2,1,0:T(8,128)(2,1)} custom-call(s32[1]{0:T(128)} %bitcast.35.side_ref, bf16[1024,768]{1,0:T(8,128)(2,1)} %refs_0_.3, bf16[1024,2304]{1,0:T(8,128)(2,1)} %get-tuple-element.233.refs_1_, bf16[1024,768]{1,0:T(8,128)(2,1)} %get-tuple-element.146.context_ref.refs_2_, bf16[1024,768]{1,0:T(8,128)(2,1)} %get-tuple-element.234.refs_3_, ...), custom_call_target="tpu_custom_call" | custom-call | flops 2415919104 | bytes 31457280 | tf_op jit(solution)/shard_map/half_grads/pallas_call | solution.py:1097
  317.1 4.7 %collective-permute-done.46.refs_6_ = bf16[16,4,48,384]{3,2,1,0:T(8,128)(2,1)S(1)} collective-permute-done((bf16[16,4,48,384]{3,2,1,0:T(8,128)(2,1)}, bf16[16,4,48,384]{3,2,1,0:T(8,128)(2,1)S(1)}, u32[]{:S(2)}, u32[]{:S(2)}) %collective-permute-start.46) | collective-permute-done | bytes 2359328 | tf_op jit(solution)/shard_map/ppermute | solution.py:654
  323.2 9.0 %half_grads.7 = bf16[16,4,48,384]{3,2,1,0:T(8,128)(2,1)} custom-call(s32[1]{0:T(128)} %bitcast.23.side_ref, bf16[1024,768]{1,0:T(8,128)(2,1)} %refs_0_.3, bf16[1024,2304]{1,0:T(8,128)(2,1)} %get-tuple-element.233.refs_1_, bf16[1024,768]{1,0:T(8,128)(2,1)} %get-tuple-element.146.context_ref.refs_2_, bf16[1024,768]{1,0:T(8,128)(2,1)} %get-tuple-element.234.refs_3_, ...), custom_call_target="tpu_custom_call" | custom-call | flops 2415919104 | bytes 31457280 | tf_op jit(solution)/shard_map/half_grads/pallas_call | solution.py:1097
  335.3 1.7 collective-permute-start.49
  337.0 5.4 %collective-permute-done.47 = bf16[2,4,48,384]{3,2,1,0:T(8,128)(2,1)S(1)} collective-permute-done((bf16[2,4,48,384]{3,2,1,0:T(8,128)(2,1)S(1)}, bf16[2,4,48,384]{3,2,1,0:T(8,128)(2,1)S(1)}, u32[]{:S(2)}, u32[]{:S(2)}) %collective-permute-start.47) | collective-permute-done | bytes 294944 | tf_op jit(solution)/shard_map/ppermute | solution.py:654
  342.7 1.6 collective-permute-start.48
  344.4 1.7 collective-permute-start.50
  348.6 4.6 %all-to-all-start.1 = ((f32[32,8,128]{2,1,0:T(8,128)}), f32[32,8,128]{2,1,0:T(8,128)S(1)}, u32[]{:S(2)}, u32[]{:S(2)}) async-start(f32[32,8,128]{2,1,0:T(8,128)} %bitcast.58), calls=%async_computation.1 | async-start | bytes 262144 | tf_op jit(solution)/shard_map/all_to_all | solution.py:649
  353.2 4.7 %collective-permute-done.48 = bf16[4,4,48,384]{3,2,1,0:T(8,128)(2,1)S(1)} collective-permute-done((bf16[4,4,48,384]{3,2,1,0:T(8,128)(2,1)S(1)}, bf16[4,4,48,384]{3,2,1,0:T(8,128)(2,1)S(1)}, u32[]{:S(2)}, u32[]{:S(2)}) %collective-permute-start.48) | collective-permute-done | bytes 589856 | tf_op jit(solution)/shard_map/ppermute | solution.py:654
  357.9 1.9 collective-permute-done.50
  365.0 3.9 collective-permute-start.53
  372.7 7.0 %collective-permute-done.52 = bf16[4,48,384]{2,1,0:T(8,128)(2,1)S(1)} collective-permute-done((bf16[4,48,384]{2,1,0:T(8,128)(2,1)S(1)}, bf16[4,48,384]{2,1,0:T(8,128)(2,1)S(1)}, u32[]{:S(2)}, u32[]{:S(2)}) %collective-permute-start.52) | collective-permute-done | bytes 147488 | tf_op jit(solution)/shard_map/ppermute | solution.py:654
  (303 shorter events, 77.6 us)
Async XLA Ops:
  7.3 53.3 %all-gather.6.cloned.1.call-start = ((), (), s32[]{:S(2)}) async-start(), calls=%async_computation.3 | async-start | bytes 1658880 | tf_op jit(solution)/shard_map/all_gather | solution.py:752
  14.0 9.0 %collective-permute-start.5 = (bf16[48,1280]{1,0:T(8,128)(2,1)S(1)}, bf16[48,1280]{1,0:T(8,128)(2,1)S(1)}, u32[]{:S(2)}, u32[]{:S(2)}) collective-permute-start(bf16[48,1280]{1,0:T(8,128)(2,1)S(1)} %get-tuple-element.333), channel_id=1, source_target_pairs={{0,6},{1,7},{2,0},{3,1},{4,2},{5,3},{6,4},{7,5},{8,14},{9,15},{10,... | collective-permute-start | bytes 368648 | tf_op jit(solution)/shard_map/ppermute | solution.py:654
  19.0 11.1 %collective-permute-start.4 = (bf16[48,1280]{1,0:T(8,128)(2,1)S(1)}, bf16[48,1280]{1,0:T(8,128)(2,1)S(1)}, u32[]{:S(2)}, u32[]{:S(2)}) collective-permute-start(bf16[48,1280]{1,0:T(8,128)(2,1)S(1)} %get-tuple-element.333), channel_id=1, source_target_pairs={{0,4},{1,5},{2,6},{3,7},{4,0},{5,1},{6,2},{7,3},{8,12},{9,13},{10,... | collective-permute-start | bytes 368648 | tf_op jit(solution)/shard_map/ppermute | solution.py:654
  19.0 11.1 %collective-permute-start.3 = (bf16[48,1280]{1,0:T(8,128)(2,1)S(1)}, bf16[48,1280]{1,0:T(8,128)(2,1)S(1)}, u32[]{:S(2)}, u32[]{:S(2)}) collective-permute-start(bf16[48,1280]{1,0:T(8,128)(2,1)S(1)} %get-tuple-element.333), channel_id=1, source_target_pairs={{0,2},{1,3},{2,4},{3,5},{4,6},{5,7},{6,0},{7,1},{8,10},{9,11},{10,... | collective-permute-start | bytes 368648 | tf_op jit(solution)/shard_map/ppermute | solution.py:654
  20.0 10.2 %collective-permute-start.1 = (bf16[96,768]{1,0:T(8,128)(2,1)}, bf16[96,768]{1,0:T(8,128)(2,1)S(1)}, u32[]{:S(2)}, u32[]{:S(2)}) collective-permute-start(bf16[96,768]{1,0:T(8,128)(2,1)} %param.50), channel_id=1, source_target_pairs={{0,8},{1,9},{2,10},{3,11},{4,12},{5,13},{6,14},{7,15},{8,0},{9,1},... | collective-permute-start | bytes 442376 | tf_op jit(solution)/shard_map/ppermute | solution.py:654
  21.5 8.7 %collective-permute-start.2 = (bf16[96,768]{1,0:T(8,128)(2,1)}, bf16[96,768]{1,0:T(8,128)(2,1)S(1)}, u32[]{:S(2)}, u32[]{:S(2)}) collective-permute-start(bf16[96,768]{1,0:T(8,128)(2,1)} %param.50), channel_id=1, source_target_pairs={{0,16},{1,17},{2,18},{3,19},{4,20},{5,21},{6,22},{7,23},{8,24},{9,... | collective-permute-start | bytes 442376 | tf_op jit(solution)/shard_map/ppermute | solution.py:654
  31.0 54.7 %all-gather.8.cloned.1.call-start = ((), (), s32[]{:S(2)}) async-start(), calls=%async_computation.4 | async-start | bytes 1327104 | tf_op jit(solution)/shard_map/all_gather | solution.py:752
  31.8 85.9 %all-gather.10.cloned.1.call-start = ((), (), s32[]{:S(2)}) async-start(), calls=%async_computation.5 | async-start | bytes 2654208 | tf_op jit(solution)/shard_map/all_gather | solution.py:752
  32.6 157.3 %all-gather.12.cloned.1.call-start = ((), (), s32[]{:S(2)}) async-start(), calls=%async_computation.6 | async-start | bytes 5308416 | tf_op jit(solution)/shard_map/all_gather | solution.py:748
  32.6 12.7 %collective-permute-start.6 = (bf16[4,48,1280]{2,1,0:T(8,128)(2,1)S(1)}, bf16[4,48,1280]{2,1,0:T(8,128)(2,1)S(1)}, u32[]{:S(2)}, u32[]{:S(2)}) collective-permute-start(bf16[4,48,1280]{2,1,0:T(8,128)(2,1)S(1)} %pad_maximum_fusion.4.refs_0_.refs_10_), channel_id=1, source_target_pairs={{0,8},{1,9},{2,10},{3,11},{4,12},{5,13},{6,14},{7,15},{8,0},{9,1},... | collective-permute-start | bytes 1474568 | tf_op jit(solution)/shard_map/ppermute | solution.py:654
  34.2 12.8 %collective-permute-start.8 = (bf16[4,48,1280]{2,1,0:T(8,128)(2,1)S(1)}, bf16[4,48,1280]{2,1,0:T(8,128)(2,1)S(1)}, u32[]{:S(2)}, u32[]{:S(2)}) collective-permute-start(bf16[4,48,1280]{2,1,0:T(8,128)(2,1)S(1)} %pad_maximum_fusion.4.refs_0_.refs_10_), channel_id=1, source_target_pairs={{0,16},{1,17},{2,18},{3,19},{4,20},{5,21},{6,22},{7,23},{8,24},{9,... | collective-permute-start | bytes 1474568 | tf_op jit(solution)/shard_map/ppermute | solution.py:654
  45.4 6.7 %collective-permute-start.7 = (bf16[2,48,1280]{2,1,0:T(8,128)(2,1)S(1)}, bf16[2,48,1280]{2,1,0:T(8,128)(2,1)S(1)}, u32[]{:S(2)}, u32[]{:S(2)}) collective-permute-start(bf16[2,48,1280]{2,1,0:T(8,128)(2,1)S(1)} %slice.336), channel_id=1, source_target_pairs={{0,16},{1,17},{2,18},{3,19},{4,20},{5,21},{6,22},{7,23},{8,24},{9,... | collective-permute-start | bytes 737288 | tf_op jit(solution)/shard_map/ppermute | solution.py:654
  47.0 6.4 %collective-permute-start.9 = (bf16[2,48,1280]{2,1,0:T(8,128)(2,1)S(1)}, bf16[2,48,1280]{2,1,0:T(8,128)(2,1)S(1)}, u32[]{:S(2)}, u32[]{:S(2)}) collective-permute-start(bf16[2,48,1280]{2,1,0:T(8,128)(2,1)S(1)} %slice.337), channel_id=1, source_target_pairs={{0,8},{1,9},{2,10},{3,11},{4,12},{5,13},{6,14},{7,15},{8,0},{9,1},... | collective-permute-start | bytes 737288 | tf_op jit(solution)/shard_map/ppermute | solution.py:654
  59.8 227.4 %all-gather.14.cloned.1.call-start = ((), (), s32[]{:S(2)}) async-start(), calls=%async_computation.7 | async-start | bytes 3649536 | tf_op jit(solution)/shard_map/all_gather | solution.py:529
  61.7 20.9 %collective-permute-start.15 = (bf16[96,3840]{1,0:T(8,128)(2,1)S(1)}, bf16[96,3840]{1,0:T(8,128)(2,1)S(1)}, u32[]{:S(2)}, u32[]{:S(2)}) collective-permute-start(bf16[96,3840]{1,0:T(8,128)(2,1)S(1)} %constant_dynamic-slice_fusion.3), channel_id=1, source_target_pairs={{0,8},{1,9},{2,10},{3,11},{4,12},{5,13},{6,14},{7,15},{8,0},{9,1},... | collective-permute-start | bytes 2211848 | tf_op jit(solution)/shard_map/ppermute | solution.py:654
  62.7 20.0 %collective-permute-start.16 = (bf16[96,3840]{1,0:T(8,128)(2,1)S(1)}, bf16[96,3840]{1,0:T(8,128)(2,1)}, u32[]{:S(2)}, u32[]{:S(2)}) collective-permute-start(bf16[96,3840]{1,0:T(8,128)(2,1)S(1)} %constant_dynamic-slice_fusion.3), channel_id=1, source_target_pairs={{0,16},{1,17},{2,18},{3,19},{4,20},{5,21},{6,22},{7,23},{8,24},{9,... | collective-permute-start | bytes 2211848 | tf_op jit(solution)/shard_map/ppermute | solution.py:654
  84.0 11.5 %collective-permute-start.17 = (bf16[48,3840]{1,0:T(8,128)(2,1)S(1)}, bf16[48,3840]{1,0:T(8,128)(2,1)S(1)}, u32[]{:S(2)}, u32[]{:S(2)}) collective-permute-start(bf16[48,3840]{1,0:T(8,128)(2,1)S(1)} %slice.338), channel_id=1, source_target_pairs={{0,16},{1,17},{2,18},{3,19},{4,20},{5,21},{6,22},{7,23},{8,24},{9,... | collective-permute-start | bytes 1105928 | tf_op jit(solution)/shard_map/ppermute | solution.py:654
  84.6 11.5 %collective-permute-start.18 = (bf16[48,3840]{1,0:T(8,128)(2,1)S(1)}, bf16[48,3840]{1,0:T(8,128)(2,1)S(1)}, u32[]{:S(2)}, u32[]{:S(2)}) collective-permute-start(bf16[48,3840]{1,0:T(8,128)(2,1)S(1)} %slice.339), channel_id=1, source_target_pairs={{0,8},{1,9},{2,10},{3,11},{4,12},{5,13},{6,14},{7,15},{8,0},{9,1},... | collective-permute-start | bytes 1105928 | tf_op jit(solution)/shard_map/ppermute | solution.py:654
  86.8 20.8 %collective-permute-start.23 = (bf16[384,768]{1,0:T(8,128)(2,1)S(1)}, bf16[384,768]{1,0:T(8,128)(2,1)}, u32[]{:S(2)}, u32[]{:S(2)}) collective-permute-start(bf16[384,768]{1,0:T(8,128)(2,1)S(1)} %constant_dynamic-slice_fusion.2), channel_id=1, source_target_pairs={{0,8},{1,9},{2,10},{3,11},{4,12},{5,13},{6,14},{7,15},{8,0},{9,1},... | collective-permute-start | bytes 1769480 | tf_op jit(solution)/shard_map/ppermute | solution.py:654
  87.8 20.8 %collective-permute-start.24 = (bf16[384,768]{1,0:T(8,128)(2,1)S(1)}, bf16[384,768]{1,0:T(8,128)(2,1)}, u32[]{:S(2)}, u32[]{:S(2)}) collective-permute-start(bf16[384,768]{1,0:T(8,128)(2,1)S(1)} %constant_dynamic-slice_fusion.2), channel_id=1, source_target_pairs={{0,16},{1,17},{2,18},{3,19},{4,20},{5,21},{6,22},{7,23},{8,24},{9,... | collective-permute-start | bytes 1769480 | tf_op jit(solution)/shard_map/ppermute | solution.py:654
  96.0 23.4 %collective-permute-start.19 = (bf16[96,3840]{1,0:T(8,128)(2,1)S(1)}, bf16[96,3840]{1,0:T(8,128)(2,1)S(1)}, u32[]{:S(2)}, u32[]{:S(2)}) collective-permute-start(bf16[96,3840]{1,0:T(8,128)(2,1)S(1)} %collective-permute-done.15.refs_1_), channel_id=1, source_target_pairs={{0,1},{1,0},{2,3},{3,2},{4,5},{5,4},{6,7},{7,6},{8,9},{9,8},{10,11... | collective-permute-start | bytes 2211848 | tf_op jit(solution)/shard_map/ppermute | solution.py:654
  96.0 22.8 %collective-permute-start.21 = (bf16[48,3840]{1,0:T(8,128)(2,1)S(1)}, bf16[48,3840]{1,0:T(8,128)(2,1)}, u32[]{:S(2)}, u32[]{:S(2)}) collective-permute-start(bf16[48,3840]{1,0:T(8,128)(2,1)S(1)} %collective-permute-done.17.refs_3_), channel_id=1, source_target_pairs={{0,1},{1,0},{2,3},{3,2},{4,5},{5,4},{6,7},{7,6},{8,9},{9,8},{10,11... | collective-permute-start | bytes 1105928 | tf_op jit(solution)/shard_map/ppermute | solution.py:654
  96.5 22.8 %collective-permute-start.22 = (bf16[48,3840]{1,0:T(8,128)(2,1)S(1)}, bf16[48,3840]{1,0:T(8,128)(2,1)}, u32[]{:S(2)}, u32[]{:S(2)}) collective-permute-start(bf16[48,3840]{1,0:T(8,128)(2,1)S(1)} %collective-permute-done.18.refs_4_), channel_id=1, source_target_pairs={{0,1},{1,0},{2,3},{3,2},{4,5},{5,4},{6,7},{7,6},{8,9},{9,8},{10,11... | collective-permute-start | bytes 1105928 | tf_op jit(solution)/shard_map/ppermute | solution.py:654
  109.6 8.0 %collective-permute-start.25 = (bf16[192,768]{1,0:T(8,128)(2,1)S(1)}, bf16[192,768]{1,0:T(8,128)(2,1)}, u32[]{:S(2)}, u32[]{:S(2)}) collective-permute-start(bf16[192,768]{1,0:T(8,128)(2,1)S(1)} %slice.340), channel_id=1, source_target_pairs={{0,16},{1,17},{2,18},{3,19},{4,20},{5,21},{6,22},{7,23},{8,24},{9,... | collective-permute-start | bytes 884744 | tf_op jit(solution)/shard_map/ppermute | solution.py:654
  111.2 7.7 %collective-permute-start.26 = (bf16[192,768]{1,0:T(8,128)(2,1)S(1)}, bf16[192,768]{1,0:T(8,128)(2,1)}, u32[]{:S(2)}, u32[]{:S(2)}) collective-permute-start(bf16[192,768]{1,0:T(8,128)(2,1)S(1)} %slice.341), channel_id=1, source_target_pairs={{0,8},{1,9},{2,10},{3,11},{4,12},{5,13},{6,14},{7,15},{8,0},{9,1},... | collective-permute-start | bytes 884744 | tf_op jit(solution)/shard_map/ppermute | solution.py:654
  121.4 33.7 %collective-permute-start.31 = (bf16[96,6144]{1,0:T(8,128)(2,1)S(1)}, bf16[96,6144]{1,0:T(8,128)(2,1)S(1)}, u32[]{:S(2)}, u32[]{:S(2)}) collective-permute-start(bf16[96,6144]{1,0:T(8,128)(2,1)S(1)} %constant_dynamic-slice_fusion.1), channel_id=1, source_target_pairs={{0,8},{1,9},{2,10},{3,11},{4,12},{5,13},{6,14},{7,15},{8,0},{9,1},... | collective-permute-start | bytes 3538952 | tf_op jit(solution)/shard_map/ppermute | solution.py:654
  122.3 33.7 %collective-permute-start.32 = (bf16[96,6144]{1,0:T(8,128)(2,1)S(1)}, bf16[96,6144]{1,0:T(8,128)(2,1)S(1)}, u32[]{:S(2)}, u32[]{:S(2)}) collective-permute-start(bf16[96,6144]{1,0:T(8,128)(2,1)S(1)} %constant_dynamic-slice_fusion.1), channel_id=1, source_target_pairs={{0,16},{1,17},{2,18},{3,19},{4,20},{5,21},{6,22},{7,23},{8,24},{9,... | collective-permute-start | bytes 3538952 | tf_op jit(solution)/shard_map/ppermute | solution.py:654
  156.0 25.7 %collective-permute-start.33 = (bf16[48,6144]{1,0:T(8,128)(2,1)}, bf16[48,6144]{1,0:T(8,128)(2,1)S(1)}, u32[]{:S(2)}, u32[]{:S(2)}) collective-permute-start(bf16[48,6144]{1,0:T(8,128)(2,1)} %slice.343), channel_id=1, source_target_pairs={{0,16},{1,17},{2,18},{3,19},{4,20},{5,21},{6,22},{7,23},{8,24},{9,... | collective-permute-start | bytes 1769480 | tf_op jit(solution)/shard_map/ppermute | solution.py:654
  157.3 24.4 %collective-permute-start.34 = (bf16[48,6144]{1,0:T(8,128)(2,1)S(1)}, bf16[48,6144]{1,0:T(8,128)(2,1)S(1)}, u32[]{:S(2)}, u32[]{:S(2)}) collective-permute-start(bf16[48,6144]{1,0:T(8,128)(2,1)S(1)} %slice.344), channel_id=1, source_target_pairs={{0,8},{1,9},{2,10},{3,11},{4,12},{5,13},{6,14},{7,15},{8,0},{9,1},... | collective-permute-start | bytes 1769480 | tf_op jit(solution)/shard_map/ppermute | solution.py:654
  182.6 6.4 %collective-permute-start.35 = (bf16[96,6144]{1,0:T(8,128)(2,1)S(1)}, bf16[96,6144]{1,0:T(8,128)(2,1)S(1)}, u32[]{:S(2)}, u32[]{:S(2)}) collective-permute-start(bf16[96,6144]{1,0:T(8,128)(2,1)S(1)} %collective-permute-done.31.refs_1_), channel_id=1, source_target_pairs={{0,1},{1,0},{2,3},{3,2},{4,5},{5,4},{6,7},{7,6},{8,9},{9,8},{10,11... | collective-permute-start | bytes 3538952 | tf_op jit(solution)/shard_map/ppermute | solution.py:654
  182.6 7.3 %collective-permute-start.36 = (bf16[96,6144]{1,0:T(8,128)(2,1)S(1)}, bf16[96,6144]{1,0:T(8,128)(2,1)}, u32[]{:S(2)}, u32[]{:S(2)}) collective-permute-start(bf16[96,6144]{1,0:T(8,128)(2,1)S(1)} %collective-permute-done.32.refs_2_), channel_id=1, source_target_pairs={{0,1},{1,0},{2,3},{3,2},{4,5},{5,4},{6,7},{7,6},{8,9},{9,8},{10,11... | collective-permute-start | bytes 3538952 | tf_op jit(solution)/shard_map/ppermute | solution.py:654
  183.2 5.8 %collective-permute-start.38 = (bf16[48,6144]{1,0:T(8,128)(2,1)}, bf16[48,6144]{1,0:T(8,128)(2,1)S(1)}, u32[]{:S(2)}, u32[]{:S(2)}) collective-permute-start(bf16[48,6144]{1,0:T(8,128)(2,1)} %copy-done.12), channel_id=1, source_target_pairs={{0,1},{1,0},{2,3},{3,2},{4,5},{5,4},{6,7},{7,6},{8,9},{9,8},{10,11... | collective-permute-start | bytes 1769480 | tf_op jit(solution)/shard_map/ppermute | solution.py:654
  222.9 13.3 %collective-permute-start.41 = (bf16[16,8,48,384]{3,2,1,0:T(8,128)(2,1)}, bf16[16,8,48,384]{3,2,1,0:T(8,128)(2,1)}, u32[]{:S(2)}, u32[]{:S(2)}) collective-permute-start(bf16[16,8,48,384]{3,2,1,0:T(8,128)(2,1)} %half_grads.4), channel_id=1, source_target_pairs={{0,1},{1,0},{2,3},{3,2},{4,5},{5,4},{6,7},{7,6},{8,9},{9,8},{10,11... | collective-permute-start | bytes 14155784 | tf_op jit(solution)/shard_map/ppermute | solution.py:654
  224.6 11.7 %all-to-all-start = ((bf16[32,8,168]{2,1,0:T(8,128)(2,1)}), bf16[32,8,168]{2,1,0:T(8,128)(2,1)S(1)}, u32[]{:S(2)}, u32[]{:S(2)}) async-start(bf16[32,8,168]{2,1,0:T(8,128)(2,1)} %maximum_bitcast_fusion), calls=%async_computation | async-start | bytes 262144 | tf_op jit(solution)/shard_map/all_to_all | solution.py:1384
  227.4 135.2 %reduce-scatter.2.cloned.1.call-start = ((), (), s32[]{:S(2)}) async-start(), calls=%async_computation.8 | async-start | bytes 1474560 | tf_op jit(solution)/shard_map/reduce_scatter | solution.py:1151
  255.7 20.0 %collective-permute-start.42 = (bf16[2,8,48,384]{3,2,1,0:T(8,128)(2,1)}, bf16[2,8,48,384]{3,2,1,0:T(8,128)(2,1)}, u32[]{:S(2)}, u32[]{:S(2)}) collective-permute-start(bf16[2,8,48,384]{3,2,1,0:T(8,128)(2,1)} %get-tuple-element.293), channel_id=1, source_target_pairs={{0,16},{1,17},{2,18},{3,19},{4,20},{5,21},{6,22},{7,23},{8,24},{9,... | collective-permute-start | bytes 1769480 | tf_op jit(solution)/shard_map/ppermute | solution.py:654
  257.4 18.3 %collective-permute-start.43 = (bf16[2,8,48,384]{3,2,1,0:T(8,128)(2,1)}, bf16[2,8,48,384]{3,2,1,0:T(8,128)(2,1)}, u32[]{:S(2)}, u32[]{:S(2)}) collective-permute-start(bf16[2,8,48,384]{3,2,1,0:T(8,128)(2,1)} %get-tuple-element.292), channel_id=1, source_target_pairs={{0,8},{1,9},{2,10},{3,11},{4,12},{5,13},{6,14},{7,15},{8,0},{9,1},... | collective-permute-start | bytes 1769480 | tf_op jit(solution)/shard_map/ppermute | solution.py:654
  277.3 27.7 %collective-permute-start.44 = (bf16[4,8,48,384]{3,2,1,0:T(8,128)(2,1)S(1)}, bf16[4,8,48,384]{3,2,1,0:T(8,128)(2,1)}, u32[]{:S(2)}, u32[]{:S(2)}) collective-permute-start(bf16[4,8,48,384]{3,2,1,0:T(8,128)(2,1)S(1)} %pad_maximum_fusion), channel_id=1, source_target_pairs={{0,8},{1,9},{2,10},{3,11},{4,12},{5,13},{6,14},{7,15},{8,0},{9,1},... | collective-permute-start | bytes 3538952 | tf_op jit(solution)/shard_map/ppermute | solution.py:654
  278.1 27.4 %collective-permute-start.45 = (bf16[4,8,48,384]{3,2,1,0:T(8,128)(2,1)S(1)}, bf16[4,8,48,384]{3,2,1,0:T(8,128)(2,1)}, u32[]{:S(2)}, u32[]{:S(2)}) collective-permute-start(bf16[4,8,48,384]{3,2,1,0:T(8,128)(2,1)S(1)} %pad_maximum_fusion.1), channel_id=1, source_target_pairs={{0,16},{1,17},{2,18},{3,19},{4,20},{5,21},{6,22},{7,23},{8,24},{9,... | collective-permute-start | bytes 3538952 | tf_op jit(solution)/shard_map/ppermute | solution.py:654
  333.3 9.1 %collective-permute-start.47 = (bf16[2,4,48,384]{3,2,1,0:T(8,128)(2,1)S(1)}, bf16[2,4,48,384]{3,2,1,0:T(8,128)(2,1)S(1)}, u32[]{:S(2)}, u32[]{:S(2)}) collective-permute-start(bf16[2,4,48,384]{3,2,1,0:T(8,128)(2,1)S(1)} %get-tuple-element.298), channel_id=1, source_target_pairs={{0,16},{1,17},{2,18},{3,19},{4,20},{5,21},{6,22},{7,23},{8,24},{9,... | collective-permute-start | bytes 884744 | tf_op jit(solution)/shard_map/ppermute | solution.py:654
  335.3 8.9 %collective-permute-start.49 = (bf16[2,4,48,384]{3,2,1,0:T(8,128)(2,1)S(1)}, bf16[2,4,48,384]{3,2,1,0:T(8,128)(2,1)S(1)}, u32[]{:S(2)}, u32[]{:S(2)}) collective-permute-start(bf16[2,4,48,384]{3,2,1,0:T(8,128)(2,1)S(1)} %get-tuple-element.297), channel_id=1, source_target_pairs={{0,8},{1,9},{2,10},{3,11},{4,12},{5,13},{6,14},{7,15},{8,0},{9,1},... | collective-permute-start | bytes 884744 | tf_op jit(solution)/shard_map/ppermute | solution.py:654
  342.7 15.3 %collective-permute-start.48 = (bf16[4,4,48,384]{3,2,1,0:T(8,128)(2,1)S(1)}, bf16[4,4,48,384]{3,2,1,0:T(8,128)(2,1)S(1)}, u32[]{:S(2)}, u32[]{:S(2)}) collective-permute-start(bf16[4,4,48,384]{3,2,1,0:T(8,128)(2,1)S(1)} %pad_maximum_fusion.2), channel_id=1, source_target_pairs={{0,8},{1,9},{2,10},{3,11},{4,12},{5,13},{6,14},{7,15},{8,0},{9,1},... | collective-permute-start | bytes 1769480 | tf_op jit(solution)/shard_map/ppermute | solution.py:654
  344.4 15.4 %collective-permute-start.50 = (bf16[4,4,48,384]{3,2,1,0:T(8,128)(2,1)S(1)}, bf16[4,4,48,384]{3,2,1,0:T(8,128)(2,1)S(1)}, u32[]{:S(2)}, u32[]{:S(2)}) collective-permute-start(bf16[4,4,48,384]{3,2,1,0:T(8,128)(2,1)S(1)} %pad_maximum_fusion.3), channel_id=1, source_target_pairs={{0,16},{1,17},{2,18},{3,19},{4,20},{5,21},{6,22},{7,23},{8,24},{9,... | collective-permute-start | bytes 1769480 | tf_op jit(solution)/shard_map/ppermute | solution.py:654
  348.6 15.1 %all-to-all-start.1 = ((f32[32,8,128]{2,1,0:T(8,128)}), f32[32,8,128]{2,1,0:T(8,128)S(1)}, u32[]{:S(2)}, u32[]{:S(2)}) async-start(f32[32,8,128]{2,1,0:T(8,128)} %bitcast.58), calls=%async_computation.1 | async-start | bytes 262144 | tf_op jit(solution)/shard_map/all_to_all | solution.py:649
  365.0 7.8 %collective-permute-start.53 = (bf16[4,48,384]{2,1,0:T(8,128)(2,1)S(1)}, bf16[4,48,384]{2,1,0:T(8,128)(2,1)S(1)}, u32[]{:S(2)}, u32[]{:S(2)}) collective-permute-start(bf16[4,48,384]{2,1,0:T(8,128)(2,1)S(1)} %get-tuple-element.312), channel_id=1, source_target_pairs={{0,6},{1,7},{2,0},{3,1},{4,2},{5,3},{6,4},{7,5},{8,14},{9,15},{10,... | collective-permute-start | bytes 442376 | tf_op jit(solution)/shard_map/ppermute | solution.py:654
  368.8 10.9 %collective-permute-start.52 = (bf16[4,48,384]{2,1,0:T(8,128)(2,1)S(1)}, bf16[4,48,384]{2,1,0:T(8,128)(2,1)S(1)}, u32[]{:S(2)}, u32[]{:S(2)}) collective-permute-start(bf16[4,48,384]{2,1,0:T(8,128)(2,1)S(1)} %get-tuple-element.313), channel_id=1, source_target_pairs={{0,4},{1,5},{2,6},{3,7},{4,0},{5,1},{6,2},{7,3},{8,12},{9,13},{10,... | collective-permute-start | bytes 442376 | tf_op jit(solution)/shard_map/ppermute | solution.py:654
  368.8 10.9 %collective-permute-start.51 = (bf16[4,48,384]{2,1,0:T(8,128)(2,1)S(1)}, bf16[4,48,384]{2,1,0:T(8,128)(2,1)S(1)}, u32[]{:S(2)}, u32[]{:S(2)}) collective-permute-start(bf16[4,48,384]{2,1,0:T(8,128)(2,1)S(1)} %get-tuple-element.311), channel_id=1, source_target_pairs={{0,2},{1,3},{2,4},{3,5},{4,6},{5,7},{6,0},{7,1},{8,10},{9,11},{10,... | collective-permute-start | bytes 442376 | tf_op jit(solution)/shard_map/ppermute | solution.py:654
  370.0 10.0 %collective-permute-start.55 = (f32[24,3072]{1,0:T(8,128)S(1)}, f32[24,3072]{1,0:T(8,128)S(1)}, u32[]{:S(2)}, u32[]{:S(2)}) collective-permute-start(f32[24,3072]{1,0:T(8,128)S(1)} %dynamic-slice_dynamic-update-slice_fusion.1), channel_id=1, source_target_pairs={{0,1},{1,0},{2,3},{3,2},{4,5},{5,4},{6,7},{7,6},{8,9},{9,8},{10,11... | collective-permute-start | bytes 884744 | tf_op jit(solution)/shard_map/ppermute | solution.py:654
  (58 other events, 482.9 us)
Sparse Core Ops, SparseCore 0:
  31.1 24.5 all-gather.5
  57.3 22.1 all-gather.7
  81.8 31.4 all-gather.9
  114.7 50.8 all-gather.11
  208.1 58.3 all-gather.13
  317.2 29.3 reduce-scatter.1

commit v7 on v6

--- a/solution.py
+++ b/solution.py
@@ -742,7 +742,7 @@
 def late_pieces(hops, gate):
     shard, from_x, from_y = hops
     half = shard.shape[0] // 2
-    sent_y, sent_x = after(gate, from_x[:half], from_y[half:])
+    sent_y, sent_x = held(from_x[:half], gate), held(from_y[half:], gate)
     across = jnp.concatenate([over_y(sent_y), over_x(sent_x)], axis=0)
     rows = jnp.concatenate([shard, from_x, from_y, across], axis=0)
     return [lax.all_gather(rows, "fsdp", axis=0, tiled=True)]
@@ -1288,7 +1288,6 @@
         late_first = late_hops(after(slab, outer_reduce))
         line = after(late_first[1:], line)
         pieces = attend_pieces(line)
-        late = late_pieces(late_first, (pieces[3], pieces[4]))
         mid_line = along_z(after(line, *inner_rest[:2]))
         end_line = along_z([after(line, inner_rest[2])])
         outer_line = along_z(after(line, *outer_all[:3]))
@@ -1306,6 +1305,7 @@
     ) = unpack_small(sizes, devices, small_pieces)
     if linked:
         mid_half = half_rows(after((pieces[3], pieces[4]), mid_line))
+        late = late_pieces(late_first, mid_half)
         attend_tokens = after(mid_half, tokens)
     else:
         attend_tokens = tokens

time: 394 us -> 404 us (1.025)
    unnamed x97 -> x109, local copies, waits for them, and re-layouts: 10.9 us -> 12.2 us
  transfers between devices with their start and end apart: 64 -> 64, of which waited for: 23 -> 25; matrix products, arithmetic and copies ran while one was open for 11% -> 11% of each run, Pallas kernels for 38% -> 37%
where the time goes in v7:
time: 404 us; the launch traced here: 399 us
  Pallas kernels  174 us (43%)
  waiting for transfers between devices  86 us (21%)
  starting transfers between devices  58.2 us (14%)
  local copies, waits for them, and re-layouts  37 us (9%)
  other arithmetic  21.4 us (5%)
  between operations  17.6 us (4%)
  matrix products  4.89 us (1%)
    pallas_call x6, Pallas kernels, row_call(): pl.pallas_call(kernel, grid=(rows // ROWS if steps is None else steps,),...  102 us
    ppermute x56, waiting for transfers between devices, hop(): lax.ppermute(array, AXES, [(place, turn(place)) for place in range(32)])  82.9 us
    ppermute x56, starting transfers between devices, hop(): lax.ppermute(array, AXES, [(place, turn(place)) for place in range(32)])  50.3 us
    pallas_call x4, Pallas kernels, half_grads(): pl.pallas_call(partial(grads_kernel, rules, int(came is not None)), grid_...  49.4 us
    pallas_call x1, Pallas kernels, heads_step(): pl.pallas_call(partial(heads_kernel, (len(mid), 1), mid_moves, end_moves)...  17 us
    unnamed x109, local copies, waits for them, and re-layouts  12.2 us
  transfers between devices with their start and end apart: 64, of which 25 were waited for; matrix products, arithmetic and copies ran while one was open for 11% of the time, Pallas kernels for 37%

profile of v7, /device:TPU:0, one launch (start us, length us, event | category | flops | bytes accessed | tf_op | source)
XLA Modules:
  0.0 398.7 jit_solution(12780691179628657796)
XLA Ops:
  9.6 1.5 pack.1
  14.0 5.0 %collective-permute-start.5 = (bf16[48,1280]{1,0:T(8,128)(2,1)S(1)}, bf16[48,1280]{1,0:T(8,128)(2,1)S(1)}, u32[]{:S(2)}, u32[]{:S(2)}) collective-permute-start(bf16[48,1280]{1,0:T(8,128)(2,1)S(1)} %get-tuple-element.329), channel_id=1, source_target_pairs={{0,6},{1,7},{2,0},{3,1},{4,2},{5,3},{6,4},{7,5},{8,14},{9,15},{10,... | collective-permute-start | bytes 368648 | tf_op jit(solution)/shard_map/ppermute | solution.py:654
  21.5 1.5 collective-permute-start.2
  23.0 7.1 %collective-permute-done.4 = bf16[48,1280]{1,0:T(8,128)(2,1)S(1)} collective-permute-done((bf16[48,1280]{1,0:T(8,128)(2,1)S(1)}, bf16[48,1280]{1,0:T(8,128)(2,1)S(1)}, u32[]{:S(2)}, u32[]{:S(2)}) %collective-permute-start.4) | collective-permute-done | bytes 122912 | tf_op jit(solution)/shard_map/ppermute | solution.py:654
  32.7 1.6 collective-permute-start.6
  34.2 1.5 collective-permute-start.8
  35.7 9.7 %collective-permute-done.6.refs_1_.refs_11_ = bf16[4,48,1280]{2,1,0:T(8,128)(2,1)S(1)} collective-permute-done((bf16[4,48,1280]{2,1,0:T(8,128)(2,1)S(1)}, bf16[4,48,1280]{2,1,0:T(8,128)(2,1)S(1)}, u32[]{:S(2)}, u32[]{:S(2)}) %collective-permute-start.6) | collective-permute-done | bytes 491552 | tf_op jit(solution)/shard_map/ppermute | solution.py:654
  45.4 1.6 collective-permute-start.7
  47.0 1.6 collective-permute-start.9
  48.7 3.4 collective-permute-done.7.refs_3_.refs_13_
  53.5 2.3 all-gather.6.cloned.1.call-done.refs_0_
  64.3 2.3 collective-permute-done.40
  74.6 15.3 %attend.1 = (bf16[1024,2304]{1,0:T(8,128)(2,1)}, bf16[1024,768]{1,0:T(8,128)(2,1)}, bf16[1024,1536]{1,0:T(8,128)(2,1)}, bf16[768,2304]{1,0:T(8,128)(2,1)}) custom-call(s32[1]{0:T(128)S(6)} %copy.88.count_ref, bf16[1024,768]{1,0:T(8,128)(2,1)} %refs_0_.3, s32[3]{0:T(128)} %pad_add_fusion.place_ref, bf16[4,48,1280]{2,1,0:T(8,128)(2,1)} %copy-done.4, ...), custom_call_target="tpu_custom_call" | custom-call | flops 4429185024 | bytes 20447248 | tf_op jit(solution)/shard_map/attend/pallas_call | solution.py:395
  96.5 6.2 %collective-permute-done.17.refs_3_ = bf16[48,3840]{1,0:T(8,128)(2,1)S(1)} collective-permute-done((bf16[48,3840]{1,0:T(8,128)(2,1)S(1)}, bf16[48,3840]{1,0:T(8,128)(2,1)S(1)}, u32[]{:S(2)}, u32[]{:S(2)}) %collective-permute-start.17) | collective-permute-done | bytes 368672 | tf_op jit(solution)/shard_map/ppermute | solution.py:654
  104.5 3.8 unpack.1
  108.3 7.0 %collective-permute-done.23.refs_10_ = bf16[384,768]{1,0:T(8,128)(2,1)S(1)} collective-permute-done((bf16[384,768]{1,0:T(8,128)(2,1)S(1)}, bf16[384,768]{1,0:T(8,128)(2,1)S(1)}, u32[]{:S(2)}, u32[]{:S(2)}) %collective-permute-start.23) | collective-permute-done | bytes 589856 | tf_op jit(solution)/shard_map/ppermute | solution.py:654
  119.3 5.3 %collective-permute-done.25.refs_12_ = bf16[192,768]{1,0:T(8,128)(2,1)} collective-permute-done((bf16[192,768]{1,0:T(8,128)(2,1)S(1)}, bf16[192,768]{1,0:T(8,128)(2,1)}, u32[]{:S(2)}, u32[]{:S(2)}) %collective-permute-start.25) | collective-permute-done | bytes 294944 | tf_op jit(solution)/shard_map/ppermute | solution.py:654
  128.3 1.5 collective-permute-start.31
  132.5 31.4 %feed.1 = (bf16[1024,768]{1,0:T(8,128)(2,1)}, f32[8,3840]{1,0:T(8,128)}, f32[8,6144]{1,0:T(8,128)}, f32[1024,768]{1,0:T(8,128)}, bf16[1024,768]{1,0:T(8,128)(2,1...) custom-call(s32[1]{0:T(128)S(6)} %copy.88.count_ref, ...), custom_call_target="tpu_custom_call" | custom-call | flops 10871635968 | bytes 46755856 | tf_op jit(solution)/shard_map/feed/pallas_call | solution.py:395
  166.9 23.1 %feed_back.1 = (bf16[1024,768]{1,0:T(8,128)(2,1)}, bf16[1024,3072]{1,0:T(8,128)(2,1)}, bf16[1024,768]{1,0:T(8,128)(2,1)}, bf16[1024,768]{1,0:T(8,128)(2,1)}, f32...) custom-call(s32[1]{0:T(128)S(6)} %copy.88.count_ref, bf16[1024,768]{1,0:T(8,128)(2,1)} %cotangent_ref.1, ...), custom_call_target="tpu_custom_call" | custom-call | flops 10871635968 | bytes 38989828 | tf_op jit(solution)/shard_map/feed_back/pallas_call | solution.py:395
  193.4 3.7 collective-permute-done.37.refs_7_
  199.1 17.0 %heads.1 = (f32[8,768]{1,0:T(8,128)}, f32[8,768]{1,0:T(8,128)}, bf16[8,5376]{1,0:T(8,128)(2,1)}, bf16[8,6912]{1,0:T(8,128)(2,1)}, f32[8,768]{1,0:T(8,128)}, /*in...) custom-call(s32[3]{0:T(128)} %pad_add_fusion.place_ref, ...), custom_call_target="tpu_custom_call" | custom-call | flops 594542592 | bytes 25952256 | tf_op jit(solution)/shard_map/heads/pallas_call | solution.py:996
  216.2 15.0 %half_grads.4 = bf16[16,8,48,384]{3,2,1,0:T(8,128)(2,1)} custom-call(s32[1]{0:T(128)} %bitcast.side_ref, bf16[1024,768]{1,0:T(8,128)(2,1)} %get-tuple-element.161.refs_0_, bf16[1024,3072]{1,0:T(8,128)(2,1)} %get-tuple-element.168.refs_1_, f32[8,3840]{1,0:T(8,128)} %get-tuple-element.169.heads_ref.refs_2_.refs_4_, ...), custom_call_target="tpu_custom_call" | custom-call | flops 4831838208 | bytes 31457280 | tf_op jit(solution)/shard_map/half_grads/pallas_call | solution.py:1097
  232.8 3.1 all-to-all-start
  236.0 8.8 %attend_back.3 = (bf16[1024,2304]{1,0:T(8,128)(2,1)}, f32[1024,768]{1,0:T(8,128)}, bf16[1024,768]{1,0:T(8,128)(2,1)}, f32[1,2304]{1,0:T(1,128)}) custom-call(bf16[1024,2304]{1,0:T(8,128)(2,1)} %get-tuple-element.219.projected_ref, bf16[1024,1536]{1,0:T(8,128)(2,1)} %get-tuple-element.220.probs_ref, bf16[1024,768]{1,0:T(8,128)(2,1)} %get-tuple-element.221.context_ref, ...), custom_call_target="tpu_custom_call" | custom-call | flops 1409286144 | bytes 27214848 | tf_op jit(solution)/shard_map/attend_back/pallas_call | solution.py:395
  244.8 17.0 %half_grads.5 = bf16[16,8,48,384]{3,2,1,0:T(8,128)(2,1)} custom-call(s32[1]{0:T(128)} %bitcast.28.side_ref, bf16[1024,768]{1,0:T(8,128)(2,1)} %get-tuple-element.161.refs_0_, bf16[1024,3072]{1,0:T(8,128)(2,1)} %get-tuple-element.168.refs_1_, f32[8,3840]{1,0:T(8,128)} %get-tuple-element.169.heads_ref.refs_2_.refs_4_, ...), custom_call_target="tpu_custom_call" | custom-call | flops 4831838208 | bytes 31457280 | tf_op jit(solution)/shard_map/half_grads/pallas_call | solution.py:1097
  261.9 2.4 dynamic-slice_bitcast_fusion.3
  264.3 1.7 collective-permute-start.42
  267.4 2.4 dynamic-slice_bitcast_fusion
  269.8 14.5 %attend_back.4 = (bf16[1024,2304]{1,0:T(8,128)(2,1)}, f32[1024,768]{1,0:T(8,128)}, bf16[1024,768]{1,0:T(8,128)(2,1)}, f32[1,2304]{1,0:T(1,128)}) custom-call(bf16[1024,2304]{1,0:T(8,128)(2,1)} %get-tuple-element.219.projected_ref, bf16[1024,1536]{1,0:T(8,128)(2,1)} %get-tuple-element.220.probs_ref, ...), custom_call_target="tpu_custom_call", output_to_operand_aliasing={{0}: (9, {}), {1}: (10, {}), {2}: (11, {})} | custom-call | flops 2818572288 | bytes 27214848 | tf_op jit(solution)/shard_map/attend_back/pallas_call | solution.py:395
  287.0 8.8 %attend_back.5 = (bf16[1024,2304]{1,0:T(8,128)(2,1)}, f32[1024,768]{1,0:T(8,128)}, bf16[1024,768]{1,0:T(8,128)(2,1)}, f32[1,2304]{1,0:T(1,128)}) custom-call(bf16[1024,2304]{1,0:T(8,128)(2,1)} %get-tuple-element.219.projected_ref, bf16[1024,1536]{1,0:T(8,128)(2,1)} %get-tuple-element.220.probs_ref, ...), custom_call_target="tpu_custom_call", output_to_operand_aliasing={{0}: (9, {}), {1}: (10, {}), {2}: (11, {})} | custom-call | flops 1409286144 | bytes 27214848 | tf_op jit(solution)/shard_map/attend_back/pallas_call | solution.py:395
  295.8 1.6 convert_reduce_fusion.1
  300.5 1.7 convert_reduce_fusion
  302.7 1.8 fusion.8
  307.6 6.0 %collective-permute-done.44 = bf16[4,8,48,384]{3,2,1,0:T(8,128)(2,1)} collective-permute-done((bf16[4,8,48,384]{3,2,1,0:T(8,128)(2,1)S(1)}, bf16[4,8,48,384]{3,2,1,0:T(8,128)(2,1)}, u32[]{:S(2)}, u32[]{:S(2)}) %collective-permute-start.44) | collective-permute-done | bytes 1179680 | tf_op jit(solution)/shard_map/ppermute | solution.py:654
  314.1 3.1 add_convert_fusion
  317.2 8.4 %half_grads.6 = bf16[16,4,48,384]{3,2,1,0:T(8,128)(2,1)} custom-call(s32[1]{0:T(128)} %bitcast.36.side_ref, bf16[1024,768]{1,0:T(8,128)(2,1)} %refs_0_.3, bf16[1024,2304]{1,0:T(8,128)(2,1)} %get-tuple-element.229.refs_1_, bf16[1024,768]{1,0:T(8,128)(2,1)} %get-tuple-element.144.context_ref.refs_2_, bf16[1024,768]{1,0:T(8,128)(2,1)} %get-tuple-element.230.refs_3_, ...), custom_call_target="tpu_custom_call" | custom-call | flops 2415919104 | bytes 31457280 | tf_op jit(solution)/shard_map/half_grads/pallas_call | solution.py:1097
  325.6 4.7 %collective-permute-done.46.refs_6_ = bf16[16,4,48,384]{3,2,1,0:T(8,128)(2,1)S(1)} collective-permute-done((bf16[16,4,48,384]{3,2,1,0:T(8,128)(2,1)}, bf16[16,4,48,384]{3,2,1,0:T(8,128)(2,1)S(1)}, u32[]{:S(2)}, u32[]{:S(2)}) %collective-permute-start.46) | collective-permute-done | bytes 2359328 | tf_op jit(solution)/shard_map/ppermute | solution.py:654
  331.8 9.0 %half_grads.7 = bf16[16,4,48,384]{3,2,1,0:T(8,128)(2,1)} custom-call(s32[1]{0:T(128)} %bitcast.23.side_ref, bf16[1024,768]{1,0:T(8,128)(2,1)} %refs_0_.3, bf16[1024,2304]{1,0:T(8,128)(2,1)} %get-tuple-element.229.refs_1_, bf16[1024,768]{1,0:T(8,128)(2,1)} %get-tuple-element.144.context_ref.refs_2_, bf16[1024,768]{1,0:T(8,128)(2,1)} %get-tuple-element.230.refs_3_, ...), custom_call_target="tpu_custom_call" | custom-call | flops 2415919104 | bytes 31457280 | tf_op jit(solution)/shard_map/half_grads/pallas_call | solution.py:1097
  343.9 1.7 collective-permute-start.49
  345.6 5.4 %collective-permute-done.47 = bf16[2,4,48,384]{3,2,1,0:T(8,128)(2,1)S(1)} collective-permute-done((bf16[2,4,48,384]{3,2,1,0:T(8,128)(2,1)S(1)}, bf16[2,4,48,384]{3,2,1,0:T(8,128)(2,1)S(1)}, u32[]{:S(2)}, u32[]{:S(2)}) %collective-permute-start.47) | collective-permute-done | bytes 294944 | tf_op jit(solution)/shard_map/ppermute | solution.py:654
  351.2 1.6 collective-permute-start.48
  353.0 1.7 collective-permute-start.50
  357.2 4.6 %all-to-all-start.1 = ((f32[32,8,128]{2,1,0:T(8,128)}), f32[32,8,128]{2,1,0:T(8,128)S(1)}, u32[]{:S(2)}, u32[]{:S(2)}) async-start(f32[32,8,128]{2,1,0:T(8,128)} %bitcast.59), calls=%async_computation.1 | async-start | bytes 262144 | tf_op jit(solution)/shard_map/all_to_all | solution.py:649
  361.8 4.7 %collective-permute-done.48 = bf16[4,4,48,384]{3,2,1,0:T(8,128)(2,1)S(1)} collective-permute-done((bf16[4,4,48,384]{3,2,1,0:T(8,128)(2,1)S(1)}, bf16[4,4,48,384]{3,2,1,0:T(8,128)(2,1)S(1)}, u32[]{:S(2)}, u32[]{:S(2)}) %collective-permute-start.48) | collective-permute-done | bytes 589856 | tf_op jit(solution)/shard_map/ppermute | solution.py:654
  366.5 1.9 collective-permute-done.50
  373.6 3.9 collective-permute-start.53
  381.3 7.0 %collective-permute-done.52 = bf16[4,48,384]{2,1,0:T(8,128)(2,1)S(1)} collective-permute-done((bf16[4,48,384]{2,1,0:T(8,128)(2,1)S(1)}, bf16[4,48,384]{2,1,0:T(8,128)(2,1)S(1)}, u32[]{:S(2)}, u32[]{:S(2)}) %collective-permute-start.52) | collective-permute-done | bytes 147488 | tf_op jit(solution)/shard_map/ppermute | solution.py:654
  (317 shorter events, 85.3 us)
Async XLA Ops:
  7.3 48.5 %all-gather.6.cloned.1.call-start = ((), (), s32[]{:S(2)}) async-start(), calls=%async_computation.3 | async-start | bytes 1658880 | tf_op jit(solution)/shard_map/all_gather | solution.py:752
  14.0 9.0 %collective-permute-start.5 = (bf16[48,1280]{1,0:T(8,128)(2,1)S(1)}, bf16[48,1280]{1,0:T(8,128)(2,1)S(1)}, u32[]{:S(2)}, u32[]{:S(2)}) collective-permute-start(bf16[48,1280]{1,0:T(8,128)(2,1)S(1)} %get-tuple-element.329), channel_id=1, source_target_pairs={{0,6},{1,7},{2,0},{3,1},{4,2},{5,3},{6,4},{7,5},{8,14},{9,15},{10,... | collective-permute-start | bytes 368648 | tf_op jit(solution)/shard_map/ppermute | solution.py:654
  19.0 11.1 %collective-permute-start.4 = (bf16[48,1280]{1,0:T(8,128)(2,1)S(1)}, bf16[48,1280]{1,0:T(8,128)(2,1)S(1)}, u32[]{:S(2)}, u32[]{:S(2)}) collective-permute-start(bf16[48,1280]{1,0:T(8,128)(2,1)S(1)} %get-tuple-element.329), channel_id=1, source_target_pairs={{0,4},{1,5},{2,6},{3,7},{4,0},{5,1},{6,2},{7,3},{8,12},{9,13},{10,... | collective-permute-start | bytes 368648 | tf_op jit(solution)/shard_map/ppermute | solution.py:654
  19.0 11.1 %collective-permute-start.3 = (bf16[48,1280]{1,0:T(8,128)(2,1)S(1)}, bf16[48,1280]{1,0:T(8,128)(2,1)S(1)}, u32[]{:S(2)}, u32[]{:S(2)}) collective-permute-start(bf16[48,1280]{1,0:T(8,128)(2,1)S(1)} %get-tuple-element.329), channel_id=1, source_target_pairs={{0,2},{1,3},{2,4},{3,5},{4,6},{5,7},{6,0},{7,1},{8,10},{9,11},{10,... | collective-permute-start | bytes 368648 | tf_op jit(solution)/shard_map/ppermute | solution.py:654
  20.0 10.2 %collective-permute-start.1 = (bf16[96,768]{1,0:T(8,128)(2,1)}, bf16[96,768]{1,0:T(8,128)(2,1)S(1)}, u32[]{:S(2)}, u32[]{:S(2)}) collective-permute-start(bf16[96,768]{1,0:T(8,128)(2,1)} %param.50), channel_id=1, source_target_pairs={{0,8},{1,9},{2,10},{3,11},{4,12},{5,13},{6,14},{7,15},{8,0},{9,1},... | collective-permute-start | bytes 442376 | tf_op jit(solution)/shard_map/ppermute | solution.py:654
  21.5 8.7 %collective-permute-start.2 = (bf16[96,768]{1,0:T(8,128)(2,1)}, bf16[96,768]{1,0:T(8,128)(2,1)S(1)}, u32[]{:S(2)}, u32[]{:S(2)}) collective-permute-start(bf16[96,768]{1,0:T(8,128)(2,1)} %param.50), channel_id=1, source_target_pairs={{0,16},{1,17},{2,18},{3,19},{4,20},{5,21},{6,22},{7,23},{8,24},{9,... | collective-permute-start | bytes 442376 | tf_op jit(solution)/shard_map/ppermute | solution.py:654
  31.0 62.2 %all-gather.8.cloned.1.call-start = ((), (), s32[]{:S(2)}) async-start(), calls=%async_computation.4 | async-start | bytes 1327104 | tf_op jit(solution)/shard_map/all_gather | solution.py:752
  31.8 92.8 %all-gather.10.cloned.1.call-start = ((), (), s32[]{:S(2)}) async-start(), calls=%async_computation.5 | async-start | bytes 2654208 | tf_op jit(solution)/shard_map/all_gather | solution.py:752
  32.6 165.5 %all-gather.12.cloned.1.call-start = ((), (), s32[]{:S(2)}) async-start(), calls=%async_computation.6 | async-start | bytes 5308416 | tf_op jit(solution)/shard_map/all_gather | solution.py:748
  32.7 12.7 %collective-permute-start.6 = (bf16[4,48,1280]{2,1,0:T(8,128)(2,1)S(1)}, bf16[4,48,1280]{2,1,0:T(8,128)(2,1)S(1)}, u32[]{:S(2)}, u32[]{:S(2)}) collective-permute-start(bf16[4,48,1280]{2,1,0:T(8,128)(2,1)S(1)} %pad_maximum_fusion.4.refs_0_.refs_10_), channel_id=1, source_target_pairs={{0,8},{1,9},{2,10},{3,11},{4,12},{5,13},{6,14},{7,15},{8,0},{9,1},... | collective-permute-start | bytes 1474568 | tf_op jit(solution)/shard_map/ppermute | solution.py:654
  34.2 12.8 %collective-permute-start.8 = (bf16[4,48,1280]{2,1,0:T(8,128)(2,1)S(1)}, bf16[4,48,1280]{2,1,0:T(8,128)(2,1)S(1)}, u32[]{:S(2)}, u32[]{:S(2)}) collective-permute-start(bf16[4,48,1280]{2,1,0:T(8,128)(2,1)S(1)} %pad_maximum_fusion.4.refs_0_.refs_10_), channel_id=1, source_target_pairs={{0,16},{1,17},{2,18},{3,19},{4,20},{5,21},{6,22},{7,23},{8,24},{9,... | collective-permute-start | bytes 1474568 | tf_op jit(solution)/shard_map/ppermute | solution.py:654
  45.4 6.7 %collective-permute-start.7 = (bf16[2,48,1280]{2,1,0:T(8,128)(2,1)S(1)}, bf16[2,48,1280]{2,1,0:T(8,128)(2,1)S(1)}, u32[]{:S(2)}, u32[]{:S(2)}) collective-permute-start(bf16[2,48,1280]{2,1,0:T(8,128)(2,1)S(1)} %slice.341), channel_id=1, source_target_pairs={{0,16},{1,17},{2,18},{3,19},{4,20},{5,21},{6,22},{7,23},{8,24},{9,... | collective-permute-start | bytes 737288 | tf_op jit(solution)/shard_map/ppermute | solution.py:654
  47.0 6.4 %collective-permute-start.9 = (bf16[2,48,1280]{2,1,0:T(8,128)(2,1)S(1)}, bf16[2,48,1280]{2,1,0:T(8,128)(2,1)S(1)}, u32[]{:S(2)}, u32[]{:S(2)}) collective-permute-start(bf16[2,48,1280]{2,1,0:T(8,128)(2,1)S(1)} %slice.342), channel_id=1, source_target_pairs={{0,8},{1,9},{2,10},{3,11},{4,12},{5,13},{6,14},{7,15},{8,0},{9,1},... | collective-permute-start | bytes 737288 | tf_op jit(solution)/shard_map/ppermute | solution.py:654
  67.5 228.3 %all-gather.14.cloned.1.call-start = ((), (), s32[]{:S(2)}) async-start(), calls=%async_computation.7 | async-start | bytes 3649536 | tf_op jit(solution)/shard_map/all_gather | solution.py:529
  68.2 21.7 %collective-permute-start.15 = (bf16[96,3840]{1,0:T(8,128)(2,1)S(1)}, bf16[96,3840]{1,0:T(8,128)(2,1)S(1)}, u32[]{:S(2)}, u32[]{:S(2)}) collective-permute-start(bf16[96,3840]{1,0:T(8,128)(2,1)S(1)} %constant_dynamic-slice_fusion.3), channel_id=1, source_target_pairs={{0,8},{1,9},{2,10},{3,11},{4,12},{5,13},{6,14},{7,15},{8,0},{9,1},... | collective-permute-start | bytes 2211848 | tf_op jit(solution)/shard_map/ppermute | solution.py:654
  69.7 20.3 %collective-permute-start.16 = (bf16[96,3840]{1,0:T(8,128)(2,1)S(1)}, bf16[96,3840]{1,0:T(8,128)(2,1)}, u32[]{:S(2)}, u32[]{:S(2)}) collective-permute-start(bf16[96,3840]{1,0:T(8,128)(2,1)S(1)} %constant_dynamic-slice_fusion.3), channel_id=1, source_target_pairs={{0,16},{1,17},{2,18},{3,19},{4,20},{5,21},{6,22},{7,23},{8,24},{9,... | collective-permute-start | bytes 2211848 | tf_op jit(solution)/shard_map/ppermute | solution.py:654
  91.2 11.5 %collective-permute-start.17 = (bf16[48,3840]{1,0:T(8,128)(2,1)S(1)}, bf16[48,3840]{1,0:T(8,128)(2,1)S(1)}, u32[]{:S(2)}, u32[]{:S(2)}) collective-permute-start(bf16[48,3840]{1,0:T(8,128)(2,1)S(1)} %slice.343), channel_id=1, source_target_pairs={{0,16},{1,17},{2,18},{3,19},{4,20},{5,21},{6,22},{7,23},{8,24},{9,... | collective-permute-start | bytes 1105928 | tf_op jit(solution)/shard_map/ppermute | solution.py:654
  92.4 11.6 %collective-permute-start.18 = (bf16[48,3840]{1,0:T(8,128)(2,1)S(1)}, bf16[48,3840]{1,0:T(8,128)(2,1)}, u32[]{:S(2)}, u32[]{:S(2)}) collective-permute-start(bf16[48,3840]{1,0:T(8,128)(2,1)S(1)} %slice.344), channel_id=1, source_target_pairs={{0,8},{1,9},{2,10},{3,11},{4,12},{5,13},{6,14},{7,15},{8,0},{9,1},... | collective-permute-start | bytes 1105928 | tf_op jit(solution)/shard_map/ppermute | solution.py:654
  94.4 20.9 %collective-permute-start.23 = (bf16[384,768]{1,0:T(8,128)(2,1)S(1)}, bf16[384,768]{1,0:T(8,128)(2,1)S(1)}, u32[]{:S(2)}, u32[]{:S(2)}) collective-permute-start(bf16[384,768]{1,0:T(8,128)(2,1)S(1)} %constant_dynamic-slice_fusion.2), channel_id=1, source_target_pairs={{0,8},{1,9},{2,10},{3,11},{4,12},{5,13},{6,14},{7,15},{8,0},{9,1},... | collective-permute-start | bytes 1769480 | tf_op jit(solution)/shard_map/ppermute | solution.py:654
  95.6 19.7 %collective-permute-start.24 = (bf16[384,768]{1,0:T(8,128)(2,1)S(1)}, bf16[384,768]{1,0:T(8,128)(2,1)}, u32[]{:S(2)}, u32[]{:S(2)}) collective-permute-start(bf16[384,768]{1,0:T(8,128)(2,1)S(1)} %constant_dynamic-slice_fusion.2), channel_id=1, source_target_pairs={{0,16},{1,17},{2,18},{3,19},{4,20},{5,21},{6,22},{7,23},{8,24},{9,... | collective-permute-start | bytes 1769480 | tf_op jit(solution)/shard_map/ppermute | solution.py:654
  104.0 22.4 %collective-permute-start.19 = (bf16[96,3840]{1,0:T(8,128)(2,1)S(1)}, bf16[96,3840]{1,0:T(8,128)(2,1)S(1)}, u32[]{:S(2)}, u32[]{:S(2)}) collective-permute-start(bf16[96,3840]{1,0:T(8,128)(2,1)S(1)} %collective-permute-done.15.refs_1_), channel_id=1, source_target_pairs={{0,1},{1,0},{2,3},{3,2},{4,5},{5,4},{6,7},{7,6},{8,9},{9,8},{10,11... | collective-permute-start | bytes 2211848 | tf_op jit(solution)/shard_map/ppermute | solution.py:654
  104.0 21.8 %collective-permute-start.21 = (bf16[48,3840]{1,0:T(8,128)(2,1)S(1)}, bf16[48,3840]{1,0:T(8,128)(2,1)}, u32[]{:S(2)}, u32[]{:S(2)}) collective-permute-start(bf16[48,3840]{1,0:T(8,128)(2,1)S(1)} %collective-permute-done.17.refs_3_), channel_id=1, source_target_pairs={{0,1},{1,0},{2,3},{3,2},{4,5},{5,4},{6,7},{7,6},{8,9},{9,8},{10,11... | collective-permute-start | bytes 1105928 | tf_op jit(solution)/shard_map/ppermute | solution.py:654
  104.5 21.8 %collective-permute-start.22 = (bf16[48,3840]{1,0:T(8,128)(2,1)}, bf16[48,3840]{1,0:T(8,128)(2,1)}, u32[]{:S(2)}, u32[]{:S(2)}) collective-permute-start(bf16[48,3840]{1,0:T(8,128)(2,1)} %collective-permute-done.18.refs_4_), channel_id=1, source_target_pairs={{0,1},{1,0},{2,3},{3,2},{4,5},{5,4},{6,7},{7,6},{8,9},{9,8},{10,11... | collective-permute-start | bytes 1105928 | tf_op jit(solution)/shard_map/ppermute | solution.py:654
  116.5 8.0 %collective-permute-start.25 = (bf16[192,768]{1,0:T(8,128)(2,1)S(1)}, bf16[192,768]{1,0:T(8,128)(2,1)}, u32[]{:S(2)}, u32[]{:S(2)}) collective-permute-start(bf16[192,768]{1,0:T(8,128)(2,1)S(1)} %slice.345), channel_id=1, source_target_pairs={{0,16},{1,17},{2,18},{3,19},{4,20},{5,21},{6,22},{7,23},{8,24},{9,... | collective-permute-start | bytes 884744 | tf_op jit(solution)/shard_map/ppermute | solution.py:654
  117.8 8.0 %collective-permute-start.26 = (bf16[192,768]{1,0:T(8,128)(2,1)S(1)}, bf16[192,768]{1,0:T(8,128)(2,1)}, u32[]{:S(2)}, u32[]{:S(2)}) collective-permute-start(bf16[192,768]{1,0:T(8,128)(2,1)S(1)} %slice.346), channel_id=1, source_target_pairs={{0,8},{1,9},{2,10},{3,11},{4,12},{5,13},{6,14},{7,15},{8,0},{9,1},... | collective-permute-start | bytes 884744 | tf_op jit(solution)/shard_map/ppermute | solution.py:654
  128.3 35.7 %collective-permute-start.31 = (bf16[96,6144]{1,0:T(8,128)(2,1)S(1)}, bf16[96,6144]{1,0:T(8,128)(2,1)S(1)}, u32[]{:S(2)}, u32[]{:S(2)}) collective-permute-start(bf16[96,6144]{1,0:T(8,128)(2,1)S(1)} %constant_dynamic-slice_fusion.1), channel_id=1, source_target_pairs={{0,8},{1,9},{2,10},{3,11},{4,12},{5,13},{6,14},{7,15},{8,0},{9,1},... | collective-permute-start | bytes 3538952 | tf_op jit(solution)/shard_map/ppermute | solution.py:654
  129.8 35.1 %collective-permute-start.32 = (bf16[96,6144]{1,0:T(8,128)(2,1)S(1)}, bf16[96,6144]{1,0:T(8,128)(2,1)S(1)}, u32[]{:S(2)}, u32[]{:S(2)}) collective-permute-start(bf16[96,6144]{1,0:T(8,128)(2,1)S(1)} %constant_dynamic-slice_fusion.1), channel_id=1, source_target_pairs={{0,16},{1,17},{2,18},{3,19},{4,20},{5,21},{6,22},{7,23},{8,24},{9,... | collective-permute-start | bytes 3538952 | tf_op jit(solution)/shard_map/ppermute | solution.py:654
  164.9 25.0 %collective-permute-start.33 = (bf16[48,6144]{1,0:T(8,128)(2,1)}, bf16[48,6144]{1,0:T(8,128)(2,1)S(1)}, u32[]{:S(2)}, u32[]{:S(2)}) collective-permute-start(bf16[48,6144]{1,0:T(8,128)(2,1)} %slice.348), channel_id=1, source_target_pairs={{0,16},{1,17},{2,18},{3,19},{4,20},{5,21},{6,22},{7,23},{8,24},{9,... | collective-permute-start | bytes 1769480 | tf_op jit(solution)/shard_map/ppermute | solution.py:654
  166.0 23.9 %collective-permute-start.34 = (bf16[48,6144]{1,0:T(8,128)(2,1)S(1)}, bf16[48,6144]{1,0:T(8,128)(2,1)S(1)}, u32[]{:S(2)}, u32[]{:S(2)}) collective-permute-start(bf16[48,6144]{1,0:T(8,128)(2,1)S(1)} %slice.349), channel_id=1, source_target_pairs={{0,8},{1,9},{2,10},{3,11},{4,12},{5,13},{6,14},{7,15},{8,0},{9,1},... | collective-permute-start | bytes 1769480 | tf_op jit(solution)/shard_map/ppermute | solution.py:654
  190.9 6.4 %collective-permute-start.35 = (bf16[96,6144]{1,0:T(8,128)(2,1)S(1)}, bf16[96,6144]{1,0:T(8,128)(2,1)S(1)}, u32[]{:S(2)}, u32[]{:S(2)}) collective-permute-start(bf16[96,6144]{1,0:T(8,128)(2,1)S(1)} %collective-permute-done.31.refs_1_), channel_id=1, source_target_pairs={{0,1},{1,0},{2,3},{3,2},{4,5},{5,4},{6,7},{7,6},{8,9},{9,8},{10,11... | collective-permute-start | bytes 3538952 | tf_op jit(solution)/shard_map/ppermute | solution.py:654
  190.9 7.2 %collective-permute-start.36 = (bf16[96,6144]{1,0:T(8,128)(2,1)S(1)}, bf16[96,6144]{1,0:T(8,128)(2,1)}, u32[]{:S(2)}, u32[]{:S(2)}) collective-permute-start(bf16[96,6144]{1,0:T(8,128)(2,1)S(1)} %collective-permute-done.32.refs_2_), channel_id=1, source_target_pairs={{0,1},{1,0},{2,3},{3,2},{4,5},{5,4},{6,7},{7,6},{8,9},{9,8},{10,11... | collective-permute-start | bytes 3538952 | tf_op jit(solution)/shard_map/ppermute | solution.py:654
  191.4 5.8 %collective-permute-start.38 = (bf16[48,6144]{1,0:T(8,128)(2,1)}, bf16[48,6144]{1,0:T(8,128)(2,1)S(1)}, u32[]{:S(2)}, u32[]{:S(2)}) collective-permute-start(bf16[48,6144]{1,0:T(8,128)(2,1)} %copy-done.12), channel_id=1, source_target_pairs={{0,1},{1,0},{2,3},{3,2},{4,5},{5,4},{6,7},{7,6},{8,9},{9,8},{10,11... | collective-permute-start | bytes 1769480 | tf_op jit(solution)/shard_map/ppermute | solution.py:654
  231.2 13.7 %collective-permute-start.41 = (bf16[16,8,48,384]{3,2,1,0:T(8,128)(2,1)}, bf16[16,8,48,384]{3,2,1,0:T(8,128)(2,1)}, u32[]{:S(2)}, u32[]{:S(2)}) collective-permute-start(bf16[16,8,48,384]{3,2,1,0:T(8,128)(2,1)} %half_grads.4), channel_id=1, source_target_pairs={{0,1},{1,0},{2,3},{3,2},{4,5},{5,4},{6,7},{7,6},{8,9},{9,8},{10,11... | collective-permute-start | bytes 14155784 | tf_op jit(solution)/shard_map/ppermute | solution.py:654
  232.8 12.0 %all-to-all-start = ((bf16[32,8,168]{2,1,0:T(8,128)(2,1)}), bf16[32,8,168]{2,1,0:T(8,128)(2,1)S(1)}, u32[]{:S(2)}, u32[]{:S(2)}) async-start(bf16[32,8,168]{2,1,0:T(8,128)(2,1)} %maximum_bitcast_fusion), calls=%async_computation | async-start | bytes 262144 | tf_op jit(solution)/shard_map/all_to_all | solution.py:1384
  235.9 135.2 %reduce-scatter.2.cloned.1.call-start = ((), (), s32[]{:S(2)}) async-start(), calls=%async_computation.8 | async-start | bytes 1474560 | tf_op jit(solution)/shard_map/reduce_scatter | solution.py:1151
  264.3 20.0 %collective-permute-start.42 = (bf16[2,8,48,384]{3,2,1,0:T(8,128)(2,1)}, bf16[2,8,48,384]{3,2,1,0:T(8,128)(2,1)}, u32[]{:S(2)}, u32[]{:S(2)}) collective-permute-start(bf16[2,8,48,384]{3,2,1,0:T(8,128)(2,1)} %get-tuple-element.289), channel_id=1, source_target_pairs={{0,16},{1,17},{2,18},{3,19},{4,20},{5,21},{6,22},{7,23},{8,24},{9,... | collective-permute-start | bytes 1769480 | tf_op jit(solution)/shard_map/ppermute | solution.py:654
  266.0 18.3 %collective-permute-start.43 = (bf16[2,8,48,384]{3,2,1,0:T(8,128)(2,1)}, bf16[2,8,48,384]{3,2,1,0:T(8,128)(2,1)}, u32[]{:S(2)}, u32[]{:S(2)}) collective-permute-start(bf16[2,8,48,384]{3,2,1,0:T(8,128)(2,1)} %get-tuple-element.288), channel_id=1, source_target_pairs={{0,8},{1,9},{2,10},{3,11},{4,12},{5,13},{6,14},{7,15},{8,0},{9,1},... | collective-permute-start | bytes 1769480 | tf_op jit(solution)/shard_map/ppermute | solution.py:654
  285.9 27.7 %collective-permute-start.44 = (bf16[4,8,48,384]{3,2,1,0:T(8,128)(2,1)S(1)}, bf16[4,8,48,384]{3,2,1,0:T(8,128)(2,1)}, u32[]{:S(2)}, u32[]{:S(2)}) collective-permute-start(bf16[4,8,48,384]{3,2,1,0:T(8,128)(2,1)S(1)} %pad_maximum_fusion), channel_id=1, source_target_pairs={{0,8},{1,9},{2,10},{3,11},{4,12},{5,13},{6,14},{7,15},{8,0},{9,1},... | collective-permute-start | bytes 3538952 | tf_op jit(solution)/shard_map/ppermute | solution.py:654
  286.7 27.4 %collective-permute-start.45 = (bf16[4,8,48,384]{3,2,1,0:T(8,128)(2,1)S(1)}, bf16[4,8,48,384]{3,2,1,0:T(8,128)(2,1)}, u32[]{:S(2)}, u32[]{:S(2)}) collective-permute-start(bf16[4,8,48,384]{3,2,1,0:T(8,128)(2,1)S(1)} %pad_maximum_fusion.1), channel_id=1, source_target_pairs={{0,16},{1,17},{2,18},{3,19},{4,20},{5,21},{6,22},{7,23},{8,24},{9,... | collective-permute-start | bytes 3538952 | tf_op jit(solution)/shard_map/ppermute | solution.py:654
  341.9 9.1 %collective-permute-start.47 = (bf16[2,4,48,384]{3,2,1,0:T(8,128)(2,1)S(1)}, bf16[2,4,48,384]{3,2,1,0:T(8,128)(2,1)S(1)}, u32[]{:S(2)}, u32[]{:S(2)}) collective-permute-start(bf16[2,4,48,384]{3,2,1,0:T(8,128)(2,1)S(1)} %get-tuple-element.294), channel_id=1, source_target_pairs={{0,16},{1,17},{2,18},{3,19},{4,20},{5,21},{6,22},{7,23},{8,24},{9,... | collective-permute-start | bytes 884744 | tf_op jit(solution)/shard_map/ppermute | solution.py:654
  343.9 8.9 %collective-permute-start.49 = (bf16[2,4,48,384]{3,2,1,0:T(8,128)(2,1)S(1)}, bf16[2,4,48,384]{3,2,1,0:T(8,128)(2,1)S(1)}, u32[]{:S(2)}, u32[]{:S(2)}) collective-permute-start(bf16[2,4,48,384]{3,2,1,0:T(8,128)(2,1)S(1)} %get-tuple-element.293), channel_id=1, source_target_pairs={{0,8},{1,9},{2,10},{3,11},{4,12},{5,13},{6,14},{7,15},{8,0},{9,1},... | collective-permute-start | bytes 884744 | tf_op jit(solution)/shard_map/ppermute | solution.py:654
  351.2 15.3 %collective-permute-start.48 = (bf16[4,4,48,384]{3,2,1,0:T(8,128)(2,1)S(1)}, bf16[4,4,48,384]{3,2,1,0:T(8,128)(2,1)S(1)}, u32[]{:S(2)}, u32[]{:S(2)}) collective-permute-start(bf16[4,4,48,384]{3,2,1,0:T(8,128)(2,1)S(1)} %pad_maximum_fusion.2), channel_id=1, source_target_pairs={{0,8},{1,9},{2,10},{3,11},{4,12},{5,13},{6,14},{7,15},{8,0},{9,1},... | collective-permute-start | bytes 1769480 | tf_op jit(solution)/shard_map/ppermute | solution.py:654
  353.0 15.4 %collective-permute-start.50 = (bf16[4,4,48,384]{3,2,1,0:T(8,128)(2,1)S(1)}, bf16[4,4,48,384]{3,2,1,0:T(8,128)(2,1)S(1)}, u32[]{:S(2)}, u32[]{:S(2)}) collective-permute-start(bf16[4,4,48,384]{3,2,1,0:T(8,128)(2,1)S(1)} %pad_maximum_fusion.3), channel_id=1, source_target_pairs={{0,16},{1,17},{2,18},{3,19},{4,20},{5,21},{6,22},{7,23},{8,24},{9,... | collective-permute-start | bytes 1769480 | tf_op jit(solution)/shard_map/ppermute | solution.py:654
  357.2 15.1 %all-to-all-start.1 = ((f32[32,8,128]{2,1,0:T(8,128)}), f32[32,8,128]{2,1,0:T(8,128)S(1)}, u32[]{:S(2)}, u32[]{:S(2)}) async-start(f32[32,8,128]{2,1,0:T(8,128)} %bitcast.59), calls=%async_computation.1 | async-start | bytes 262144 | tf_op jit(solution)/shard_map/all_to_all | solution.py:649
  373.6 7.8 %collective-permute-start.53 = (bf16[4,48,384]{2,1,0:T(8,128)(2,1)S(1)}, bf16[4,48,384]{2,1,0:T(8,128)(2,1)S(1)}, u32[]{:S(2)}, u32[]{:S(2)}) collective-permute-start(bf16[4,48,384]{2,1,0:T(8,128)(2,1)S(1)} %get-tuple-element.308), channel_id=1, source_target_pairs={{0,6},{1,7},{2,0},{3,1},{4,2},{5,3},{6,4},{7,5},{8,14},{9,15},{10,... | collective-permute-start | bytes 442376 | tf_op jit(solution)/shard_map/ppermute | solution.py:654
  377.4 10.9 %collective-permute-start.52 = (bf16[4,48,384]{2,1,0:T(8,128)(2,1)S(1)}, bf16[4,48,384]{2,1,0:T(8,128)(2,1)S(1)}, u32[]{:S(2)}, u32[]{:S(2)}) collective-permute-start(bf16[4,48,384]{2,1,0:T(8,128)(2,1)S(1)} %get-tuple-element.309), channel_id=1, source_target_pairs={{0,4},{1,5},{2,6},{3,7},{4,0},{5,1},{6,2},{7,3},{8,12},{9,13},{10,... | collective-permute-start | bytes 442376 | tf_op jit(solution)/shard_map/ppermute | solution.py:654
  377.4 10.9 %collective-permute-start.51 = (bf16[4,48,384]{2,1,0:T(8,128)(2,1)S(1)}, bf16[4,48,384]{2,1,0:T(8,128)(2,1)S(1)}, u32[]{:S(2)}, u32[]{:S(2)}) collective-permute-start(bf16[4,48,384]{2,1,0:T(8,128)(2,1)S(1)} %get-tuple-element.307), channel_id=1, source_target_pairs={{0,2},{1,3},{2,4},{3,5},{4,6},{5,7},{6,0},{7,1},{8,10},{9,11},{10,... | collective-permute-start | bytes 442376 | tf_op jit(solution)/shard_map/ppermute | solution.py:654
  378.6 10.1 %collective-permute-start.55 = (f32[24,3072]{1,0:T(8,128)S(1)}, f32[24,3072]{1,0:T(8,128)S(1)}, u32[]{:S(2)}, u32[]{:S(2)}) collective-permute-start(f32[24,3072]{1,0:T(8,128)S(1)} %dynamic-slice_dynamic-update-slice_fusion.1), channel_id=1, source_target_pairs={{0,1},{1,0},{2,3},{3,2},{4,5},{5,4},{6,7},{7,6},{8,9},{9,8},{10,11... | collective-permute-start | bytes 884744 | tf_op jit(solution)/shard_map/ppermute | solution.py:654
  (64 other events, 524.7 us)
Sparse Core Ops, SparseCore 0:
  31.2 24.5 all-gather.5
  57.4 22.1 all-gather.7
  81.8 31.3 all-gather.9
  114.7 50.8 all-gather.11
  216.3 58.7 all-gather.13
  325.8 29.3 reduce-scatter.1
